TPU v7x, 32 devices: a whole 2x2x4 slice. The times are simulated.
32 devices in a mesh: dp: 4 (over y, x), ctx: 8 (over z, core).
Axes of the slice: x: 2, y: 2, z: 4, core: 2. Of those that a mesh axis runs over, the one named last changes fastest.
Arguments:
- tokens: bfloat16 [16384, 2048], P(('dp', 'ctx')), may hold values from -6 to 6
- cotangent: bfloat16 [16384, 2048], P(('dp', 'ctx')), may hold values from -6 to 6
- wqkv: bfloat16 [2048, 6144], P('dp'), may hold values from -0.125 to 0.125
- wo: bfloat16 [2048, 2048], P('dp'), may hold values from -1 to 1
- attn_gain: bfloat16 [2048], P('dp'), may hold values from 0.25 to 1.75
- query_gain: bfloat16 [2048], P('dp'), may hold values from 0.25 to 1.75
- key_gain: bfloat16 [2048], P('dp'), may hold values from 0.25 to 1.75
- moe_gain: bfloat16 [2048], P('dp'), may hold values from 0.25 to 1.75
- w_gate: bfloat16 [16, 2048, 1024], P('ctx', 'dp'), may hold values from -0.125 to 0.125
- w_up: bfloat16 [16, 2048, 1024], P('ctx', 'dp'), may hold values from -0.125 to 0.125
- w_down: bfloat16 [16, 1024, 2048], P('ctx', 'dp'), may hold values from -0.375 to 0.375
- expert_ids: int32 [16384, 8], P(('dp', 'ctx')), may hold values from 0 to 15, all different within a row
- gates: float32 [16384, 8], P(('dp', 'ctx')), may hold values from 0.25 to 0.6
- slot_order: int32 [16384, 8], P(('dp', 'ctx')), may hold values from 0 to 4095, as said below
- block_assign: int32 [4, 16], P('dp'), may hold values from 0 to 15, each once within a row
- segment_ids: int32 [4, 2048], P('dp'), may hold values from 0 to 7, never falling along the last dimension, each value on 1 to 512 neighbouring positions
Outputs:
- output: bfloat16 [16384, 2048], P(('dp', 'ctx'))
- input_grad: bfloat16 [16384, 2048], P(('dp', 'ctx'))
- grad_wqkv: float32 [2048, 6144], P('dp')
- grad_wo: float32 [2048, 2048], P('dp')
- grad_attn_gain: float32 [2048], P('dp')
- grad_query_gain: float32 [2048], P('dp')
- grad_key_gain: float32 [2048], P('dp')
- grad_moe_gain: float32 [2048], P('dp')
- grad_w_gate: float32 [16, 2048, 1024], P('ctx', 'dp')
- grad_w_up: float32 [16, 2048, 1024], P('ctx', 'dp')
- grad_w_down: float32 [16, 1024, 2048], P('ctx', 'dp')
Inputs may be any that keep to these rules, and one draw needn't show every extreme that they name: `slot_order`: within each aligned block of 512 rows, the 4096 entries are each of 0 to 4095 once. `block_assign`: each row is a permutation. `segment_ids`: never falling along a row; each continuation has 1 to 512 tokens. `expert_ids`: each row names 8 different experts.
All inputs are finite; a program needn't handle non-finite values.
Results may differ from a plain program's by a relative error of at most 0.023.
Values may be sent and summed in bfloat16 or wider, within the bound.
No kernel may reach another device: no remote copies, remote signals or barrier semaphores. Data moves between devices by JAX's collectives and lax.ppermute only.
A program may use at most 512 MiB of HBM per device.

v0:
```python
import jax
import jax.numpy as jnp
from jax import lax
from jax.sharding import PartitionSpec as P

HEADS = 16
TOP = 8
BLK_DEV = 2


epsilon = 1e-06
masked_value = -1e30
highest = lax.Precision.HIGHEST


def rms_scale(values_in):
    return lax.rsqrt(jnp.mean(values_in * values_in, axis=-1, keepdims=True) + epsilon)


def rms_back(grad_hat, normed, scale_rows):
    return scale_rows * (grad_hat - normed * jnp.mean(grad_hat * normed, axis=-1, keepdims=True))


def take_rows(array, start, length):
    return lax.dynamic_slice_in_dim(array, start, length, 0)


def layout(assign_row, segment_row, block_len):
    count_blocks = assign_row.shape[0]
    offsets = jnp.arange(block_len, dtype=jnp.int32)
    logical = (assign_row[:, None] * block_len + offsets[None, :]).reshape(-1)
    prompt_len = count_blocks * block_len - segment_row.shape[0]
    segment_full = jnp.concatenate([jnp.full((prompt_len,), -1, jnp.int32), segment_row]).reshape(
        count_blocks, block_len
    )
    stored = jnp.take(segment_full, assign_row, axis=0).reshape(-1)
    return (logical, stored)


def visible(query_pos, query_seg, key_pos, key_seg):
    causal = key_pos[None, :] <= query_pos[:, None]
    same_doc = (key_seg[None, :] == query_seg[:, None]) & causal
    prompt_key = (key_seg[None, :] < 0) & (query_seg[:, None] >= 0)
    return same_doc | prompt_key


def scores_of(queries, keys, allowed, scale):
    raw_scores = (
        jnp.einsum("thd,khd->htk", queries, keys, preferred_element_type=jnp.float32) * scale
    )
    return jnp.where(allowed[None], raw_scores, masked_value)


def probs_and_grads(
    queries, grad_attn, lse, query_pos, query_seg, keys, values, key_pos, key_seg, scale
):
    allowed = visible(query_pos, query_seg, key_pos, key_seg)
    probs = jnp.exp(scores_of(queries, keys, allowed, scale) - lse[..., None])
    dprobs = jnp.einsum("thd,khd->htk", grad_attn, values, preferred_element_type=jnp.float32)
    return (probs, dprobs)


def attention_forward(
    queries, query_pos, query_seg, keys, values, key_pos, key_seg, scale, key_block
):
    head_count = queries.shape[1]
    count_rows = queries.shape[0]
    count_blocks = keys.shape[0] // key_block

    def first_pass(carry, block_index):
        running_max, running_sum = carry
        start = block_index * key_block
        allowed = visible(
            query_pos,
            query_seg,
            take_rows(key_pos, start, key_block),
            take_rows(key_seg, start, key_block),
        )
        scores = scores_of(queries, take_rows(keys, start, key_block), allowed, scale)
        new_max = jnp.maximum(running_max, jnp.max(scores, axis=-1))
        terms = jnp.where(allowed[None], jnp.exp(scores - new_max[..., None]), 0.0)
        return (
            (new_max, running_sum * jnp.exp(running_max - new_max) + jnp.sum(terms, axis=-1)),
            None,
        )

    start_max = jnp.full((head_count, count_rows), masked_value, jnp.float32)
    start_sum = jnp.zeros((head_count, count_rows), jnp.float32)
    (largest, totals), unused = lax.scan(
        first_pass, (start_max, start_sum), jnp.arange(count_blocks)
    )
    lse = largest + jnp.log(totals)

    def second_pass(running, block_index):
        start = block_index * key_block
        allowed = visible(
            query_pos,
            query_seg,
            take_rows(key_pos, start, key_block),
            take_rows(key_seg, start, key_block),
        )
        probs = jnp.exp(
            scores_of(queries, take_rows(keys, start, key_block), allowed, scale) - lse[..., None]
        )
        part = jnp.einsum(
            "htk,khd->thd",
            probs.astype(jnp.bfloat16),
            take_rows(values, start, key_block),
            preferred_element_type=jnp.float32,
        )
        return (running + part, None)

    attended, unused = lax.scan(
        second_pass, jnp.zeros(queries.shape, jnp.float32), jnp.arange(count_blocks)
    )
    return (attended, lse)


def delta_pass(
    queries, grad_attn, lse, query_pos, query_seg, keys, values, key_pos, key_seg, scale, key_block
):
    count_blocks = keys.shape[0] // key_block

    def delta_step(running, block_index):
        start = block_index * key_block
        probs, dprobs = probs_and_grads(
            queries,
            grad_attn,
            lse,
            query_pos,
            query_seg,
            take_rows(keys, start, key_block),
            take_rows(values, start, key_block),
            take_rows(key_pos, start, key_block),
            take_rows(key_seg, start, key_block),
            scale,
        )
        return (running + jnp.sum(probs * dprobs, axis=-1), None)

    delta, unused = lax.scan(
        delta_step, jnp.zeros(lse.shape, jnp.float32), jnp.arange(count_blocks)
    )
    return delta


def query_grads(
    queries,
    grad_attn,
    lse,
    delta,
    query_pos,
    query_seg,
    keys,
    values,
    key_pos,
    key_seg,
    scale,
    key_block,
):
    count_blocks = keys.shape[0] // key_block

    def query_step(running, block_index):
        start = block_index * key_block
        keys_here = take_rows(keys, start, key_block)
        probs, dprobs = probs_and_grads(
            queries,
            grad_attn,
            lse,
            query_pos,
            query_seg,
            keys_here,
            take_rows(values, start, key_block),
            take_rows(key_pos, start, key_block),
            take_rows(key_seg, start, key_block),
            scale,
        )
        dscores = (probs * (dprobs - delta[..., None])).astype(jnp.bfloat16)
        return (
            running
            + jnp.einsum("htk,khd->thd", dscores, keys_here, preferred_element_type=jnp.float32)
            * scale,
            None,
        )

    grad_queries, unused = lax.scan(
        query_step, jnp.zeros(queries.shape, jnp.float32), jnp.arange(count_blocks)
    )
    return grad_queries


def own_key_grads(
    every_query,
    every_grad,
    every_lse,
    every_delta,
    every_pos,
    every_seg,
    keys,
    values,
    key_pos,
    key_seg,
    scale,
    query_block,
):
    count_blocks = every_query.shape[0] // query_block

    def own_step(carry, block_index):
        key_total, value_total = carry
        start = block_index * query_block
        query_here = take_rows(every_query, start, query_block)
        grad_here = take_rows(every_grad, start, query_block)
        lse_here = take_rows(every_lse, start, query_block).T
        delta_here = take_rows(every_delta, start, query_block).T
        probs, dprobs = probs_and_grads(
            query_here,
            grad_here,
            lse_here,
            take_rows(every_pos, start, query_block),
            take_rows(every_seg, start, query_block),
            keys,
            values,
            key_pos,
            key_seg,
            scale,
        )
        dscores = (probs * (dprobs - delta_here[..., None])).astype(jnp.bfloat16)
        key_total = (
            key_total
            + jnp.einsum("htk,thd->khd", dscores, query_here, preferred_element_type=jnp.float32)
            * scale
        )
        value_total = value_total + jnp.einsum(
            "htk,thd->khd",
            probs.astype(jnp.bfloat16),
            grad_here,
            preferred_element_type=jnp.float32,
        )
        return ((key_total, value_total), None)

    empty = jnp.zeros(keys.shape, jnp.float32)
    (key_total, value_total), unused = lax.scan(own_step, (empty, empty), jnp.arange(count_blocks))
    return (key_total, value_total)


def slot_positions(expert_rows, order_rows, count_experts, capacity):
    pair_count = expert_rows.shape[0] * expert_rows.shape[1]
    flat_expert = expert_rows.reshape(pair_count)
    flat_order = order_rows.reshape(pair_count)
    by_order = jnp.zeros((pair_count,), jnp.int32).at[flat_order].set(flat_expert)
    matched = (by_order[:, None] == jnp.arange(count_experts, dtype=jnp.int32)[None, :]).astype(
        jnp.int32
    )
    earlier = jnp.cumsum(matched, axis=0) - matched
    slot_sorted = jnp.sum(earlier * matched, axis=1)
    slot_pair = jnp.take(slot_sorted, flat_order)
    position = jnp.where(slot_pair < capacity, flat_expert * capacity + slot_pair, -1)
    return position.reshape(expert_rows.shape)


def on_device(
    tokens,
    cotangent,
    wqkv,
    wo,
    attn_gain,
    query_gain,
    key_gain,
    moe_gain,
    w_gate,
    w_up,
    w_down,
    expert_ids,
    gates,
    slot_order,
    block_assign,
    segment_ids,
):
    count_rows, width = tokens.shape
    head_dim = width // HEADS
    scale = head_dim ** (-0.5)
    peers = lax.axis_size("ctx")
    full_wqkv, full_wo, gain_attn, gain_query, gain_key, gain_moe = (
        lax.all_gather(wqkv, "dp", axis=0, tiled=True),
        lax.all_gather(wo, "dp", axis=0, tiled=True),
        lax.all_gather(attn_gain, "dp", axis=0, tiled=True),
        lax.all_gather(query_gain, "dp", axis=0, tiled=True),
        lax.all_gather(key_gain, "dp", axis=0, tiled=True),
        lax.all_gather(moe_gain, "dp", axis=0, tiled=True),
    )
    gain_attn = gain_attn.astype(jnp.float32)
    gain_query = gain_query.astype(jnp.float32)
    gain_key = gain_key.astype(jnp.float32)
    gain_moe = gain_moe.astype(jnp.float32)
    block_len = count_rows // BLK_DEV
    key_pos, key_seg = layout(block_assign[0], segment_ids[0], block_len)
    total_keys = key_pos.shape[0]
    key_block = min(1024, total_keys)
    first_row = lax.axis_index("ctx") * count_rows
    query_pos = lax.dynamic_slice_in_dim(key_pos, first_row, count_rows, 0)
    query_seg = lax.dynamic_slice_in_dim(key_seg, first_row, count_rows, 0)
    inputs = tokens.astype(jnp.float32)
    inv_in = rms_scale(inputs)
    hat_in = inputs * inv_in
    normed = (hat_in * gain_attn).astype(jnp.bfloat16)
    qkv = jnp.dot(normed, full_wqkv, preferred_element_type=jnp.float32)
    query_raw = qkv[:, :width]
    key_raw = qkv[:, width : 2 * width]
    inv_query = rms_scale(query_raw)
    hat_query = query_raw * inv_query
    inv_key = rms_scale(key_raw)
    hat_key = key_raw * inv_key
    queries = (hat_query * gain_query).astype(jnp.bfloat16)
    keys = (hat_key * gain_key).astype(jnp.bfloat16)
    values = qkv[:, 2 * width :].astype(jnp.bfloat16)
    all_keys, all_values = (
        lax.all_gather(keys, "ctx", axis=0, tiled=True),
        lax.all_gather(values, "ctx", axis=0, tiled=True),
    )
    query_heads = queries.reshape(count_rows, HEADS, head_dim)
    key_heads = all_keys.reshape(total_keys, HEADS, head_dim)
    value_heads = all_values.reshape(total_keys, HEADS, head_dim)
    attended, lse_heads = attention_forward(
        query_heads,
        query_pos,
        query_seg,
        key_heads,
        value_heads,
        key_pos,
        key_seg,
        scale,
        key_block,
    )
    attn_low = attended.reshape(count_rows, width).astype(jnp.bfloat16)
    state = inputs + jnp.dot(attn_low, full_wo, preferred_element_type=jnp.float32)
    inv_state = rms_scale(state)
    hat_state = state * inv_state
    normed_moe = (hat_state * gain_moe).astype(jnp.bfloat16)
    local_experts = w_gate.shape[0]
    count_experts = local_experts * peers
    capacity = 9 * count_rows * TOP // (8 * count_experts)
    slots = count_experts * capacity
    position = slot_positions(expert_ids, slot_order, count_experts, capacity)
    kept = position >= 0
    slot_ids = jnp.arange(slots, dtype=jnp.int32)
    matches = position[None, :, :] == slot_ids[:, None, None]
    dispatch = jnp.sum(matches.astype(jnp.int32), axis=2).astype(jnp.bfloat16)
    weighting = jnp.sum(jnp.where(matches, gates[None, :, :], 0.0), axis=2)
    send_rows = (
        jnp.dot(dispatch, normed_moe, preferred_element_type=jnp.float32)
        .astype(jnp.bfloat16)
        .reshape(count_experts, capacity, width)
    )
    full_gate, full_up, full_down = (
        lax.all_gather(w_gate, "dp", axis=1, tiled=True),
        lax.all_gather(w_up, "dp", axis=1, tiled=True),
        lax.all_gather(w_down, "dp", axis=1, tiled=True),
    )
    hidden_width = full_gate.shape[2]
    received = lax.all_to_all(send_rows, "ctx", split_axis=0, concat_axis=0, tiled=True)
    shaped = received.reshape(peers, local_experts, -1, width)
    gate_pre = jnp.einsum("sncd,ndf->sncf", shaped, full_gate, preferred_element_type=jnp.float32)
    up_pre = jnp.einsum("sncd,ndf->sncf", shaped, full_up, preferred_element_type=jnp.float32)
    hidden = (jax.nn.silu(gate_pre) * up_pre).astype(jnp.bfloat16)
    out_rows = jnp.einsum(
        "sncf,nfd->sncd", hidden, full_down, preferred_element_type=jnp.float32
    ).astype(jnp.bfloat16)
    returned = lax.all_to_all(
        out_rows.reshape(count_experts, -1, width), "ctx", split_axis=0, concat_axis=0, tiled=True
    )
    returned, received, gate_pre, up_pre = (
        returned,
        received,
        gate_pre.reshape(count_experts, -1, hidden_width),
        up_pre.reshape(count_experts, -1, hidden_width),
    )
    target = jnp.where(kept, position, slots).reshape(-1)
    padded_out = jnp.concatenate(
        [returned.reshape(slots, width), jnp.zeros((1, width), jnp.bfloat16)], axis=0
    )
    picked = jnp.take(padded_out, target, axis=0).reshape(count_rows, TOP, width)
    mixed = jnp.sum(picked.astype(jnp.float32) * gates[..., None], axis=1)
    output = (state + mixed).astype(jnp.bfloat16)
    grad_out = cotangent.astype(jnp.float32)
    grad_rows = (
        jnp.dot(weighting, grad_out, precision=highest)
        .astype(jnp.bfloat16)
        .reshape(count_experts, capacity, width)
    )
    grad_received = lax.all_to_all(
        grad_rows, "ctx", split_axis=0, concat_axis=0, tiled=True
    ).reshape(peers, local_experts, capacity, width)
    gate_four = gate_pre.reshape(peers, local_experts, capacity, hidden_width)
    up_four = up_pre.reshape(peers, local_experts, capacity, hidden_width)
    received_four = received.reshape(peers, local_experts, capacity, width)
    sigmoid_gate = jax.nn.sigmoid(gate_four)
    silu_gate = jax.nn.silu(gate_four)
    hidden = (silu_gate * up_four).astype(jnp.bfloat16)
    grad_hidden = jnp.einsum(
        "sncd,nfd->sncf", grad_received, full_down, preferred_element_type=jnp.float32
    )
    grad_gate_pre = (
        grad_hidden * up_four * sigmoid_gate * (1.0 + gate_four * (1.0 - sigmoid_gate))
    ).astype(jnp.bfloat16)
    grad_up_pre = (grad_hidden * silu_gate).astype(jnp.bfloat16)
    grad_down = jnp.einsum(
        "sncf,sncd->nfd", hidden, grad_received, preferred_element_type=jnp.float32
    )
    grad_gate = jnp.einsum(
        "sncd,sncf->ndf", received_four, grad_gate_pre, preferred_element_type=jnp.float32
    )
    grad_up = jnp.einsum(
        "sncd,sncf->ndf", received_four, grad_up_pre, preferred_element_type=jnp.float32
    )
    grad_in_rows = jnp.einsum(
        "sncf,ndf->sncd", grad_gate_pre, full_gate, preferred_element_type=jnp.float32
    )
    grad_in_rows = grad_in_rows + jnp.einsum(
        "sncf,ndf->sncd", grad_up_pre, full_up, preferred_element_type=jnp.float32
    )
    grad_in_rows = grad_in_rows.astype(jnp.bfloat16).reshape(count_experts, capacity, width)
    rows_back = lax.all_to_all(
        grad_in_rows, "ctx", split_axis=0, concat_axis=0, tiled=True
    ).reshape(slots, width)
    grad_normed_moe = lax.dot_general(
        dispatch, rows_back, (((0,), (0,)), ((), ())), preferred_element_type=jnp.float32
    )
    moe_gain_term = jnp.sum(grad_normed_moe * hat_state, axis=0)
    grad_state = grad_out + rms_back(grad_normed_moe * gain_moe, hat_state, inv_state)
    grad_branch = grad_state.astype(jnp.bfloat16)
    grad_attn = lax.dot_general(
        grad_branch, full_wo, (((1,), (1,)), ((), ())), preferred_element_type=jnp.float32
    ).astype(jnp.bfloat16)
    grad_attn_heads = grad_attn.reshape(count_rows, HEADS, head_dim)
    delta = delta_pass(
        query_heads,
        grad_attn_heads,
        lse_heads,
        query_pos,
        query_seg,
        key_heads,
        value_heads,
        key_pos,
        key_seg,
        scale,
        key_block,
    )
    grad_query_heads = query_grads(
        query_heads,
        grad_attn_heads,
        lse_heads,
        delta,
        query_pos,
        query_seg,
        key_heads,
        value_heads,
        key_pos,
        key_seg,
        scale,
        key_block,
    )
    every_query, every_grad, every_lse, every_delta = (
        lax.all_gather(queries.astype(jnp.float32), "ctx", axis=0, tiled=True).astype(
            queries.dtype
        ),
        lax.all_gather(grad_attn.astype(jnp.float32), "ctx", axis=0, tiled=True).astype(
            grad_attn.dtype
        ),
        lax.all_gather(lse_heads.T, "ctx", axis=0, tiled=True),
        lax.all_gather(delta.T, "ctx", axis=0, tiled=True),
    )
    own_keys = keys.reshape(count_rows, HEADS, head_dim)
    own_values = values.reshape(count_rows, HEADS, head_dim)
    key_total, value_total = own_key_grads(
        every_query.reshape(total_keys, HEADS, head_dim),
        every_grad.reshape(total_keys, HEADS, head_dim),
        every_lse,
        every_delta,
        key_pos,
        key_seg,
        own_keys,
        own_values,
        query_pos,
        query_seg,
        scale,
        key_block,
    )
    grad_keys = key_total.reshape(count_rows, width)
    grad_values = value_total.reshape(count_rows, width)
    grad_queries = grad_query_heads.reshape(count_rows, width)
    query_gain_term = jnp.sum(grad_queries * hat_query, axis=0)
    key_gain_term = jnp.sum(grad_keys * hat_key, axis=0)
    grad_query_raw = rms_back(grad_queries * gain_query, hat_query, inv_query)
    grad_key_raw = rms_back(grad_keys * gain_key, hat_key, inv_key)
    grad_qkv = jnp.concatenate([grad_query_raw, grad_key_raw, grad_values], axis=1).astype(
        jnp.bfloat16
    )
    grad_normed = lax.dot_general(
        grad_qkv, full_wqkv, (((1,), (1,)), ((), ())), preferred_element_type=jnp.float32
    )
    attn_gain_term = jnp.sum(grad_normed * hat_in, axis=0)
    input_grad = (grad_state + rms_back(grad_normed * gain_attn, hat_in, inv_in)).astype(
        jnp.bfloat16
    )
    part_qkv = lax.dot_general(
        normed, grad_qkv, (((0,), (0,)), ((), ())), preferred_element_type=jnp.float32
    )
    part_out = lax.dot_general(
        attn_low, grad_branch, (((0,), (0,)), ((), ())), preferred_element_type=jnp.float32
    )
    weight_shard = lax.psum_scatter(
        jnp.concatenate([part_qkv, part_out], axis=1).astype(jnp.bfloat16),
        "dp",
        scatter_dimension=0,
        tiled=True,
    )
    gain_terms = jnp.stack([attn_gain_term, query_gain_term, key_gain_term, moe_gain_term])
    gate_shard, up_shard, down_shard, gain_shard = (
        lax.psum_scatter(
            grad_gate.astype(jnp.bfloat16), "dp", scatter_dimension=1, tiled=True
        ).astype(jnp.float32),
        lax.psum_scatter(
            grad_up.astype(jnp.bfloat16), "dp", scatter_dimension=1, tiled=True
        ).astype(jnp.float32),
        lax.psum_scatter(
            grad_down.astype(jnp.bfloat16), "dp", scatter_dimension=1, tiled=True
        ).astype(jnp.float32),
        lax.psum_scatter(
            gain_terms.astype(jnp.bfloat16), "dp", scatter_dimension=1, tiled=True
        ).astype(jnp.float32),
    )
    weight_total, gain_total = (
        lax.psum(weight_shard, "ctx").astype(jnp.float32),
        lax.psum(gain_shard.astype(jnp.bfloat16), "ctx").astype(jnp.float32),
    )
    return (
        output,
        input_grad,
        weight_total[:, : 3 * width],
        weight_total[:, 3 * width :],
        gain_total[0],
        gain_total[1],
        gain_total[2],
        gain_total[3],
        gate_shard,
        up_shard,
        down_shard,
    )


def solution(mesh):
    placed = (
        P(("dp", "ctx"), None),
        P(("dp", "ctx"), None),
        P("dp", None),
        P("dp", None),
        P("dp"),
        P("dp"),
        P("dp"),
        P("dp"),
        P("ctx", "dp", None),
        P("ctx", "dp", None),
        P("ctx", "dp", None),
        P(("dp", "ctx"), None),
        P(("dp", "ctx"), None),
        P(("dp", "ctx"), None),
        P("dp", None),
        P("dp", None),
    )
    return jax.shard_map(
        on_device,
        mesh=mesh,
        in_specs=placed,
        out_specs=(
            P(("dp", "ctx"), None),
            P(("dp", "ctx"), None),
            P("dp", None),
            P("dp", None),
            P("dp"),
            P("dp"),
            P("dp"),
            P("dp"),
            P("ctx", "dp", None),
            P("ctx", "dp", None),
            P("ctx", "dp", None),
        ),
        check_vma=False,
    )
```

profile of v0, /device:TPU:0, one launch (start us, length us, event | category | flops | bytes accessed | tf_op | source)
XLA Modules:
  0.0 4246.6 jit_solution(13553801058493736749)
XLA Ops:
  33.3 207.1 %all-gather.14.cloned.1.call-done = bf16[2048,6144]{1,0:T(8,128)(2,1)} async-done(((bf16[512,6144]{1,0:T(8,128)(2,1)}), bf16[2048,6144]{1,0:T(8,128)(2,1)}) %all-gather.14.cloned.1.call-update) | async-done | bytes 25165840 | tf_op jit(solution)/shard_map/all_gather | solution.py:283
  322.6 51.3 %convert_reduce_fusion = s32[4608,512]{1,0:T(8,128)} fusion(s32[512,8]{0,1:T(8,128)S(1)} %get-tuple-element.968), kind=kLoop, calls=%fused_computation.94 | loop fusion | flops 54263808 | bytes 9453568 | tf_op jit(solution)/shard_map/reduce_sum | solution.py:346
  383.0 39.2 all-gather.18.cloned.1.call-done
  437.0 133.2 %while.59 = (s32[]{:T(128)}, f32[16,512]{1,0:T(8,128)S(1)}, f32[16,512]{1,0:T(8,128)S(1)}, s32[4]{0:T(128)S(1)}, s32[4096]{0:T(1024)S(1)}, /*index=5*/s32[512]{0...) while((s32[]{:T(128)}, f32[16,512]{1,0:T(8,128)S(1)}, ...), condition=%wide.region_6.7_spmd.clone, body=%wide.region_3.0_spmd.clone.sunk | while | flops 2217256448 | bytes 75433168 | solution.py:89
  589.9 92.4 %while.60 = (s32[]{:T(128)}, f32[512,16,128]{0,2,1:T(8,128)}, s32[4]{0:T(128)S(1)}, bf16[4096,16,128]{2,1,0:T(8,128)(2,1)}, s32[4096]{0:T(1024)S(1)}, /*index=5*...) while((s32[]{:T(128)}, f32[512,16,128]{0,2,1:T(8,128)}, ...), condition=%wide.region_8.9_spmd.clone, body=%wide.region_7.8_spmd.clone.sunk | while | flops 4333241856 | bytes 28378336 | solution.py:113
  723.6 51.8 %select_reduce_fusion.1 = f32[4608,512]{1,0:T(8,128)} fusion(f32[512,8]{0,1:T(8,128)S(1)} %copy-done.32, s32[512,8]{0,1:T(8,128)S(1)} %copy-done.26), kind=kLoop, calls=%fused_computation.93 | loop fusion | flops 54263808 | bytes 9469952 | tf_op jit(solution)/shard_map/reduce_sum | solution.py:347
  775.4 33.6 convolution_convert_fusion.1
  809.0 322.6 %all-to-all-done = bf16[16,288,2048]{2,1,0:T(8,128)(2,1)} async-done(((bf16[16,288,2048]{2,1,0:T(8,128)(2,1)}), bf16[16,288,2048]{2,1,0:T(8,128)(2,1)}, u32[]{:S(2)}, u32[]{:S(2)}) %all-to-all-start) | async-done | bytes 18874400 | tf_op jit(solution)/shard_map/all_to_all | solution.py:359
  1138.9 27.6 fusion.100
  1166.5 62.5 %all-gather.24.cloned.1.call-done = bf16[2,2048,1024]{2,1,0:T(8,128)(2,1)} async-done(((bf16[2,512,1024]{2,1,0:T(8,128)(2,1)}), bf16[2,2048,1024]{2,1,0:T(8,128)(2,1)}) %all-gather.24.cloned.1.call-update) | async-done | bytes 8388624 | tf_op jit(solution)/shard_map/all_gather | solution.py:355
  1229.0 27.2 fusion.98
  1256.2 62.3 %all-gather.26.cloned.1.call-done = bf16[2,1024,2048]{2,1,0:T(8,128)(2,1)} async-done(((bf16[2,256,2048]{2,1,0:T(8,128)(2,1)}), bf16[2,1024,2048]{2,1,0:T(8,128)(2,1)}) %all-gather.26.cloned.1.call-update) | async-done | bytes 8388624 | tf_op jit(solution)/shard_map/all_gather | solution.py:356
  1318.5 227.6 %all-to-all-done.2 = bf16[16,288,2048]{2,1,0:T(8,128)(2,1)} async-done(((bf16[16,288,2048]{2,1,0:T(8,128)(2,1)}), bf16[16,288,2048]{2,1,0:T(8,128)(2,1)}, u32[]{:S(2)}, u32[]{:S(2)}) %all-to-all-start.2) | async-done | bytes 18874400 | tf_op jit(solution)/shard_map/all_to_all | solution.py:389
  1546.1 37.5 fusion.88
  1583.6 29.2 fusion.108
  1612.8 32.3 fusion.84
  1668.7 27.2 convert_bitcast_fusion
  1712.9 498.5 %all-to-all-done.3 = bf16[16,288,2048]{2,1,0:T(8,128)(2,1)} async-done(((bf16[16,288,2048]{2,1,0:T(8,128)(2,1)}), bf16[16,288,2048]{2,1,0:T(8,128)(2,1)}, u32[]{:S(2)}, u32[]{:S(2)}) %all-to-all-start.3) | async-done | bytes 18874400 | tf_op jit(solution)/shard_map/all_to_all | solution.py:421
  2242.0 391.9 %all_gather.57 = f32[4096,16]{0,1:T(8,128)} all-gather(f32[512,16]{0,1:T(8,128)} %bitcast.37), channel_id=1, replica_groups=mesh['dp'=4,'ctx'=8] {'ctx'}, dimensions={0}, use_global_device_ids=true | all-gather | bytes 294912 | tf_op jit(solution)/shard_map/all_gather | solution.py:468
  2675.4 40.1 gather_fusion.2
  2751.0 148.3 %while.61 = (s32[]{:T(128)}, f32[16,512]{1,0:T(8,128)S(1)}, s32[4]{0:T(128)S(1)}, s32[4096]{0:T(1024)S(1)}, s32[512]{0:T(512)S(1)}, /*index=5*/s32[4096]{0:T(102...) while((s32[]{:T(128)}, f32[16,512]{1,0:T(8,128)S(1)}, ...), condition=%wide.region_20.21_spmd.clone, body=%wide.region_18.20_spmd.clone.sunk | while | flops 4339541504 | bytes 80938208 | solution.py:140
  2899.3 158.1 %while.62 = (s32[]{:T(128)}, f32[512,16,128]{0,2,1:T(8,128)}, s32[4]{0:T(128)S(1)}, bf16[4096,16,128]{2,0,1:T(8,128)(2,1)}, s32[4096]{0:T(1024)S(1)}, /*index=5*...) while((s32[]{:T(128)}, f32[512,16,128]{0,2,1:T(8,128)}, ...), condition=%wide.region_22.23_spmd.clone, body=%wide.region_21.22_spmd.clone.sunk | while | flops 6498551296 | bytes 93424368 | solution.py:185
  3101.2 294.5 %while.63 = (s32[]{:T(128)}, f32[512,16,128]{0,2,1:T(8,128)}, f32[512,16,128]{0,2,1:T(8,128)}, s32[4]{0:T(128)S(1)}, bf16[4096,16,128]{2,1,0:T(8,128)(2,1)}, /*i...) while((s32[]{:T(128)}, f32[512,16,128]{0,2,1:T(8,128)}, ...), condition=%wide.region_25.26_spmd.clone, body=%wide.region_24.25_spmd.clone.sunk | while | flops 8681687040 | bytes 157254912 | solution.py:241
  3221.2 26.5 bitcast_add_fusion.10
  3463.2 26.8 bitcast_convert_fusion.2
  3490.1 27.5 bitcast_convert_fusion.1
  3517.7 27.3 bitcast_convert_fusion
  3571.0 181.7 %reduce-scatter.18.cloned.1.call-done = bf16[512,8192]{1,0:T(8,128)(2,1)} async-done(((bf16[2048,8192]{1,0:T(8,128)(2,1)}), bf16[512,8192]{1,0:T(8,128)(2,1)}) %reduce-scatter.18.cloned.1.call-update) | async-done | bytes 8388624
  3752.7 90.3 %reduce-scatter.10.cloned.1.call-done = bf16[2,512,1024]{2,1,0:T(8,128)(2,1)} async-done(((bf16[2,2048,1024]{2,1,0:T(8,128)(2,1)}), bf16[2,512,1024]{2,1,0:T(8,128)(2,1)}) %reduce-scatter.10.cloned.1.call-update) | async-done | bytes 2097168 | tf_op jit(solution)/shard_map/reduce_scatter | solution.py:518
  3847.1 85.3 %reduce-scatter.12.cloned.1.call-done = bf16[2,512,1024]{2,1,0:T(8,128)(2,1)} async-done(((bf16[2,2048,1024]{2,1,0:T(8,128)(2,1)}), bf16[2,512,1024]{2,1,0:T(8,128)(2,1)}) %reduce-scatter.12.cloned.1.call-update) | async-done | bytes 2097168 | tf_op jit(solution)/shard_map/reduce_scatter | solution.py:521
  3936.5 85.7 %reduce-scatter.14.cloned.1.call-done = bf16[2,256,2048]{2,1,0:T(8,128)(2,1)} async-done(((bf16[2,1024,2048]{2,1,0:T(8,128)(2,1)}), bf16[2,256,2048]{2,1,0:T(8,128)(2,1)}) %reduce-scatter.14.cloned.1.call-update) | async-done | bytes 2097168 | tf_op jit(solution)/shard_map/reduce_scatter | solution.py:524
  4067.9 159.9 %all-reduce.5.cloned.1.call-done = bf16[512,8192]{1,0:T(8,128)(2,1)} async-done(((bf16[512,8192]{1,0:T(8,128)(2,1)}), bf16[512,8192]{1,0:T(8,128)(2,1)}) %all-reduce.5.cloned.1.call-update) | async-done | bytes 8388624 | tf_op jit(solution)/shard_map/psum | solution.py:532
  (463 shorter events, 1335.3 us)
Async XLA Ops:
  7.2 233.2 %all-gather.14.cloned.1.call-start = ((), (), s32[]{:S(2)}) async-start(), calls=%async_computation.9 | async-start | bytes 31457280 | tf_op jit(solution)/shard_map/all_gather | solution.py:283
  8.0 414.3 %all-gather.18.cloned.1.call-start = ((), (), s32[]{:S(2)}) async-start(), calls=%async_computation.11 | async-start | bytes 18874368 | tf_op jit(solution)/shard_map/all_gather | solution.py:316
  17.6 243.7 %copy-start.40 = (f32[4,1,512]{2,1,0:T(1,128)}, f32[4,1,512]{2,1,0:T(1,128)S(1)}, u32[]{:S(2)}) copy-start(f32[4,1,512]{2,1,0:T(1,128)S(1)} %convert_element_type.188) | copy-start | bytes 24580
  25.7 239.7 %copy-start.28 = (f32[4,1,512]{2,1,0:T(1,128)}, f32[4,1,512]{2,1,0:T(1,128)S(1)}, u32[]{:S(2)}) copy-start(f32[4,1,512]{2,1,0:T(1,128)S(1)} %convert_element_type.189) | copy-start | bytes 24580
  32.8 232.5 %copy-start.30 = (f32[4,1,512]{2,1,0:T(1,128)}, f32[4,1,512]{2,1,0:T(1,128)S(1)}, u32[]{:S(2)}) copy-start(f32[4,1,512]{2,1,0:T(1,128)S(1)} %convert_element_type.190) | copy-start | bytes 24580
  33.3 227.9 %copy-start.48 = (f32[512]{0:T(512)}, f32[512]{0:T(512)S(1)}, u32[]{:S(2)}) copy-start(f32[512]{0:T(512)S(1)} %add_rsqrt_fusion.3) | copy-start | bytes 6148
  271.1 302.8 %all-gather.16.cloned.1.call-start = ((), (), s32[]{:S(2)}) async-start(), calls=%async_computation.10 | async-start | bytes 18874368 | tf_op jit(solution)/shard_map/all_gather | solution.py:317
  275.0 412.0 %all-gather.20.cloned.1.call-start = ((), (), s32[]{:S(2)}) async-start(), calls=%async_computation.12 | async-start | bytes 10485760 | tf_op jit(solution)/shard_map/all_gather | solution.py:284
  322.6 51.3 %copy-start.58 = (bf16[512]{0:T(512)(128)(2,1)S(1)}, bf16[512]{0:T(512)(128)(2,1)}, u32[]{:S(2)}) copy-start(bf16[512]{0:T(512)(128)(2,1)} %param.33) | copy-start | bytes 3076
  322.6 59.9 %copy-start.10 = (bf16[64,16,8,128]{3,2,1,0:T(8,128)(2,1)S(1)}, bf16[64,16,8,128]{3,2,1,0:T(8,128)(2,1)}, u32[]{:S(2)}) copy-start(bf16[64,16,8,128]{3,2,1,0:T(8,128)(2,1)} %get-tuple-element.979) | copy-start | bytes 6291460
  716.9 414.7 %all-to-all-start = ((bf16[16,288,2048]{2,1,0:T(8,128)(2,1)}), bf16[16,288,2048]{2,1,0:T(8,128)(2,1)}, u32[]{:S(2)}, u32[]{:S(2)}) async-start(bf16[16,288,2048]{2,1,0:T(8,128)(2,1)} %bitcast.323), calls=%async_computation | async-start | bytes 37748736 | tf_op jit(solution)/shard_map/all_to_all | solution.py:359
  723.0 415.9 %all-gather.22.cloned.1.call-start = ((), (), s32[]{:S(2)}) async-start(), calls=%async_computation.13 | async-start | bytes 10485760 | tf_op jit(solution)/shard_map/all_gather | solution.py:354
  723.6 51.8 %copy-start.17 = (bf16[512,2048]{1,0:T(8,128)(2,1)S(1)}, bf16[512,2048]{1,0:T(8,128)(2,1)}, u32[]{:S(2)}) copy-start(bf16[512,2048]{1,0:T(8,128)(2,1)} %param.27) | copy-start | bytes 6291460
  1131.6 414.5 %all-to-all-start.2 = ((bf16[16,288,2048]{2,1,0:T(8,128)(2,1)}), bf16[16,288,2048]{2,1,0:T(8,128)(2,1)}, u32[]{:S(2)}, u32[]{:S(2)}) async-start(bf16[16,288,2048]{2,1,0:T(8,128)(2,1)} %bitcast.322), calls=%async_computation.2 | async-start | bytes 37748736 | tf_op jit(solution)/shard_map/all_to_all | solution.py:389
  1137.5 91.5 %all-gather.24.cloned.1.call-start = ((), (), s32[]{:S(2)}) async-start(), calls=%async_computation.14 | async-start | bytes 10485760 | tf_op jit(solution)/shard_map/all_gather | solution.py:355
  1138.1 180.4 %all-gather.26.cloned.1.call-start = ((), (), s32[]{:S(2)}) async-start(), calls=%async_computation.15 | async-start | bytes 10485760 | tf_op jit(solution)/shard_map/all_gather | solution.py:356
  1662.1 549.3 %all-to-all-start.3 = ((bf16[16,288,2048]{2,1,0:T(8,128)(2,1)}), bf16[16,288,2048]{2,1,0:T(8,128)(2,1)}, u32[]{:S(2)}, u32[]{:S(2)}) async-start(bf16[16,288,2048]{2,1,0:T(8,128)(2,1)} %bitcast.318), calls=%async_computation.3 | async-start | bytes 37748736 | tf_op jit(solution)/shard_map/all_to_all | solution.py:421
  1668.0 556.1 %all-gather.28.cloned.1.call-start = ((), (), s32[]{:S(2)}) async-start(), calls=%async_computation.16 | async-start | bytes 18874368 | tf_op jit(solution)/shard_map/all_gather | solution.py:462
  2211.4 447.1 %all-to-all-start.1 = ((bf16[16,288,2048]{2,1,0:T(8,128)(2,1)}), bf16[16,288,2048]{2,1,0:T(8,128)(2,1)}, u32[]{:S(2)}, u32[]{:S(2)}) async-start(bf16[16,288,2048]{2,1,0:T(8,128)(2,1)} %bitcast.317), calls=%async_computation.1 | async-start | bytes 37748736 | tf_op jit(solution)/shard_map/all_to_all | solution.py:367
  2217.4 868.5 %all-gather.30.cloned.1.call-start = ((), (), s32[]{:S(2)}) async-start(), calls=%async_computation.17 | async-start | bytes 18874368 | tf_op jit(solution)/shard_map/all_gather | solution.py:465
  2224.1 409.8 %slice-start = ((s8[16777216]{0:T(1024)(128)(4,1)}), s8[4194304]{0:T(1024)(128)(4,1)S(1)}, s32[]{:S(2)}) async-start(s8[16777216]{0:T(1024)(128)(4,1)} %bitcast.320), calls=%async_computation.24 | async-start | bytes 8388608
  2224.1 409.8 %slice-start.1 = ((s8[16777216]{0:T(1024)(128)(4,1)}), s8[4194304]{0:T(1024)(128)(4,1)S(1)}, s32[]{:S(2)}) async-start(s8[16777216]{0:T(1024)(128)(4,1)} %bitcast.320), calls=%async_computation.25 | async-start | bytes 8388608
  2224.1 409.8 %slice-start.2 = ((s8[16777216]{0:T(1024)(128)(4,1)}), s8[4194304]{0:T(1024)(128)(4,1)S(1)}, s32[]{:S(2)}) async-start(s8[16777216]{0:T(1024)(128)(4,1)} %bitcast.320), calls=%async_computation.26 | async-start | bytes 8388608
  2224.1 409.8 %slice-start.3 = ((s8[16777216]{0:T(1024)(128)(4,1)}), s8[4194304]{0:T(1024)(128)(4,1)S(1)}, s32[]{:S(2)}) async-start(s8[16777216]{0:T(1024)(128)(4,1)} %bitcast.320), calls=%async_computation.27 | async-start | bytes 8388608
  2224.1 417.6 %slice-start.4 = ((s8[9437184]{0:T(1024)(128)(4,1)}), s8[4194304]{0:T(1024)(128)(4,1)S(1)}, s32[]{:S(2)}) async-start(s8[9437184]{0:T(1024)(128)(4,1)} %bitcast.326), calls=%async_computation.28 | async-start | bytes 8388608
  2224.1 417.6 %slice-start.5 = ((s8[9437184]{0:T(1024)(128)(4,1)}), s8[4194304]{0:T(1024)(128)(4,1)S(1)}, s32[]{:S(2)}) async-start(s8[9437184]{0:T(1024)(128)(4,1)} %bitcast.326), calls=%async_computation.29 | async-start | bytes 8388608
  2750.9 1001.8 %reduce-scatter.18.cloned.1.call-start = ((), (), s32[]{:S(2)}) async-start(), calls=%async_computation.23 | async-start | bytes 41943040
  3463.2 379.9 %reduce-scatter.10.cloned.1.call-start = ((), (), s32[]{:S(2)}) async-start(), calls=%async_computation.19 | async-start | bytes 10485760 | tf_op jit(solution)/shard_map/reduce_scatter | solution.py:518
  3490.0 442.4 %reduce-scatter.12.cloned.1.call-start = ((), (), s32[]{:S(2)}) async-start(), calls=%async_computation.20 | async-start | bytes 10485760 | tf_op jit(solution)/shard_map/reduce_scatter | solution.py:521
  3517.6 504.6 %reduce-scatter.14.cloned.1.call-start = ((), (), s32[]{:S(2)}) async-start(), calls=%async_computation.21 | async-start | bytes 10485760 | tf_op jit(solution)/shard_map/reduce_scatter | solution.py:524
  3545.0 504.7 %reduce-scatter.16.cloned.1.call-start = ((), (), s32[]{:S(2)}) async-start(), calls=%async_computation.22 | async-start | bytes 655360
  3570.9 656.8 %all-reduce.5.cloned.1.call-start = ((), (), s32[]{:S(2)}) async-start(), calls=%async_computation.18 | async-start | bytes 16777216 | tf_op jit(solution)/shard_map/psum | solution.py:532
  (54 other events, 541.1 us)
Sparse Core Ops, SparseCore 0:
  9.9 230.4 all-gather.13
  271.1 151.1 all-gather.17
  424.5 149.3 all-gather.15
  575.5 85.8 all-gather.19
  725.4 89.0 all-gather.21
  1139.9 89.0 all-gather.23
  1230.8 87.6 all-gather.25
  1671.0 290.4 all-gather.27
  2751.0 151.6 all-gather.29
  3463.3 289.3 reduce-scatter.17
  3756.6 86.3 reduce-scatter.9
  3846.0 86.4 reduce-scatter.11
  3935.8 86.3 reduce-scatter.13
  4024.9 24.7 reduce-scatter.15
  4052.1 175.6 all-reduce.4
where the time goes:
time: 4260 us; the launch traced here: 4250 us
  waiting for transfers between devices  2050 us (48%)
  matrix products  1090 us (26%)
  blocking collectives  455 us (11%)
  local copies, waits for them, and re-layouts  318 us (7%)
  other arithmetic  281 us (7%)
    all_to_all x1, waiting for transfers between devices, on_device(): lax.all_to_all(grad_in_rows, 'ctx', split_axis=0, concat_axis=0, tiled=True)  498 us
    all_gather x1, blocking collectives, on_device(): lax.all_gather(lse_heads.T, 'ctx', axis=0, tiled=True)  392 us
    all_to_all x1, waiting for transfers between devices, on_device(): lax.all_to_all(send_rows, 'ctx', split_axis=0, concat_axis=0, tiled=True)  323 us
    dot_general x16, matrix products, scores_of(): jnp.einsum('thd,khd->htk', queries, keys, preferred_element_type=jnp.floa...  250 us
    all_to_all x1, waiting for transfers between devices, on_device(): lax.all_to_all(grad_rows, 'ctx', split_axis=0, concat_axis=0, tiled=True)  228 us
    all_gather x1, waiting for transfers between devices, on_device(): lax.all_gather(wqkv, 'dp', axis=0, tiled=True)  207 us
    unnamed x17, waiting for transfers between devices  204 us
    psum x1, waiting for transfers between devices, on_device(): lax.psum(weight_shard, 'ctx').astype(jnp.float32)  160 us
  transfers between devices with their start and end apart: 19, of which 14 were waited for; matrix products, arithmetic and copies ran while one was open for 24% of the time, Pallas kernels for 0%

commit v1 on v0

v1 whole, which is shorter than its diff:
```python
import functools

import jax
import jax.numpy as jnp
from jax import lax
from jax.experimental import pallas as pl
from jax.experimental.pallas import tpu as pltpu
from jax.sharding import PartitionSpec as P

HEADS = 16
TOP = 8
BLK_DEV = 2
LOG2E = 1.4426950408889634

epsilon = 1e-06
masked_value = -1e30
f32 = jnp.float32
bf16 = jnp.bfloat16
NT = (((1,), (1,)), ((), ()))
TN = (((0,), (0,)), ((), ()))


def rms_scale(values_in):
    return lax.rsqrt(jnp.mean(values_in * values_in, axis=-1, keepdims=True) + epsilon)


def rms_back(grad_hat, normed, scale_rows):
    return scale_rows * (grad_hat - normed * jnp.mean(grad_hat * normed, axis=-1, keepdims=True))


def tile_mask(seg_col, seg_row, key_first, query_first):
    rows, columns = seg_col.shape[0], seg_row.shape[1]
    key_pos = key_first + lax.broadcasted_iota(jnp.int32, (rows, columns), 0)
    query_pos = query_first + lax.broadcasted_iota(jnp.int32, (rows, columns), 1)
    return (seg_col == seg_row) & (key_pos <= query_pos)


def forward_kernel(
    tile,
    prompt_tiles,
    block_len,
    scale,
    place,
    first_tile,
    raw_q,
    raw_k,
    raw_v,
    inv,
    gain_q,
    gain_k,
    seg_col,
    seg_row,
    out,
    lse,
    queries,
    keys,
    values,
    values_t,
    out_logical,
):
    group, width = raw_q.shape
    tiles = group // tile
    blocks = group // block_len

    def bring(block, carry):
        source = pl.ds(pl.multiple_of(place[block] * block_len, block_len), block_len)
        target = pl.ds(pl.multiple_of(block * block_len, block_len), block_len)
        scales = inv[source, :]
        queries[target, :] = (raw_q[source, :] * scales[:, 0:1] * gain_q[...]).astype(bf16)
        keys[target, :] = (raw_k[source, :] * scales[:, 1:2] * gain_k[...]).astype(bf16)
        values[target, :] = raw_v[source, :].astype(bf16)
        return carry

    lax.fori_loop(0, blocks, bring, 0)
    for index in range(tiles):
        values_t[:, index * tile : (index + 1) * tile] = values[
            index * tile : (index + 1) * tile, :
        ].T

    def query_tile(index, carry):
        first = pl.multiple_of(index * tile, tile)
        query = queries[pl.ds(first, tile), :]
        seg_query = seg_row[pl.ds(index, 1), :]

        def step(is_masked, at, state):
            largest, total, running = state
            key_first = pl.multiple_of(at * tile, tile)
            scores = lax.dot_general(
                keys[pl.ds(key_first, tile), :], query, NT, preferred_element_type=f32
            ) * (scale * LOG2E)
            if is_masked:
                allowed = tile_mask(seg_col[pl.ds(key_first, tile), :], seg_query, key_first, first)
                scores = jnp.where(allowed, scores, masked_value)
            new_largest = jnp.maximum(largest, jnp.max(scores, axis=0, keepdims=True))
            shrink = jnp.exp2(largest - new_largest)
            terms = jnp.exp2(scores - new_largest)
            total = total * shrink + jnp.sum(terms, axis=0, keepdims=True)
            running = running * shrink + jnp.dot(
                values_t[:, pl.ds(key_first, tile)], terms.astype(bf16), preferred_element_type=f32
            )
            return (new_largest, total, running)

        state = (
            jnp.full((1, tile), masked_value, f32),
            jnp.zeros((1, tile), f32),
            jnp.zeros((width, tile), f32),
        )
        state = lax.fori_loop(
            0, jnp.minimum(index, prompt_tiles), functools.partial(step, False), state
        )
        state = lax.fori_loop(first_tile[index], index + 1, functools.partial(step, True), state)
        largest, total, running = state
        lse[pl.ds(index, 1), :] = largest + jnp.log2(total)
        out_logical[pl.ds(first, tile), :] = (running / total).T
        return carry

    lax.fori_loop(0, tiles, query_tile, 0)

    def send(block, carry):
        target = pl.ds(pl.multiple_of(place[block] * block_len, block_len), block_len)
        source = pl.ds(pl.multiple_of(block * block_len, block_len), block_len)
        out[target, :] = out_logical[source, :].astype(bf16)
        return carry

    lax.fori_loop(0, blocks, send, 0)


def backward_kernel(
    tile,
    prompt_tiles,
    block_len,
    scale,
    place,
    first_tile,
    queries,
    keys,
    values,
    lse,
    out,
    grad_out,
    seg_col,
    seg_row,
    grad_q,
    grad_k,
    grad_v,
    keys_t,
    grad_here,
    delta,
    total_q,
    total_k,
    total_v,
):
    group, width = queries.shape
    tiles = group // tile
    blocks = group // block_len

    def bring(block, carry):
        source = pl.ds(pl.multiple_of(place[block] * block_len, block_len), block_len)
        target = pl.ds(pl.multiple_of(block * block_len, block_len), block_len)
        grad_here[target, :] = grad_out[source, :]
        total_q[target, :] = out[source, :].astype(f32) * grad_out[source, :].astype(f32)
        return carry

    lax.fori_loop(0, blocks, bring, 0)
    for index in range(tiles):
        rows = slice(index * tile, (index + 1) * tile)
        keys_t[:, rows] = keys[rows, :].T
        delta[index : index + 1, :] = jnp.sum(total_q[rows, :].T, axis=0, keepdims=True)
    total_k[...] = jnp.zeros_like(total_k)
    total_v[...] = jnp.zeros_like(total_v)

    def query_tile(index, carry):
        first = pl.multiple_of(index * tile, tile)
        query = queries[pl.ds(first, tile), :]
        grad_tile = grad_here[pl.ds(first, tile), :]
        seg_query = seg_row[pl.ds(index, 1), :]
        lse_tile = lse[pl.ds(index, 1), :]
        delta_tile = delta[pl.ds(index, 1), :]

        def step(is_masked, at, running):
            key_first = pl.multiple_of(at * tile, tile)
            here = pl.ds(key_first, tile)
            scores = lax.dot_general(keys[here, :], query, NT, preferred_element_type=f32) * (
                scale * LOG2E
            )
            probs = jnp.exp2(scores - lse_tile)
            if is_masked:
                allowed = tile_mask(seg_col[here, :], seg_query, key_first, first)
                probs = jnp.where(allowed, probs, 0.0)
            dprobs = lax.dot_general(values[here, :], grad_tile, NT, preferred_element_type=f32)
            dscores = (probs * (dprobs - delta_tile)).astype(bf16)
            total_v[here, :] += jnp.dot(probs.astype(bf16), grad_tile, preferred_element_type=f32)
            total_k[here, :] += jnp.dot(dscores, query, preferred_element_type=f32)
            return running + jnp.dot(keys_t[:, here], dscores, preferred_element_type=f32)

        running = jnp.zeros((width, tile), f32)
        running = lax.fori_loop(
            0, jnp.minimum(index, prompt_tiles), functools.partial(step, False), running
        )
        running = lax.fori_loop(
            first_tile[index], index + 1, functools.partial(step, True), running
        )
        total_q[pl.ds(first, tile), :] = running.T
        return carry

    lax.fori_loop(0, tiles, query_tile, 0)

    def send(block, carry):
        target = pl.ds(pl.multiple_of(place[block] * block_len, block_len), block_len)
        source = pl.ds(pl.multiple_of(block * block_len, block_len), block_len)
        grad_q[target, :] = total_q[source, :] * scale
        grad_k[target, :] = total_k[source, :] * scale
        grad_v[target, :] = total_v[source, :].astype(bf16)
        return carry

    lax.fori_loop(0, blocks, send, 0)


def attention_forward(
    raw, inv, gain_q, gain_k, seg_col, seg_row, place, first_tile, tile, block_len, scale
):
    group, width = raw.shape[0], raw.shape[1] // 3
    head_dim = 128
    heads = width // head_dim
    tiles = group // tile
    prompt_tiles = tiles // 2

    def part(which):
        return pl.BlockSpec((group, head_dim), lambda h, *_: (0, which * heads + h))

    def whole(shape):
        return pl.BlockSpec(shape, lambda h, *_: (0,) * len(shape))

    head = pl.BlockSpec((group, head_dim), lambda h, *_: (0, h))
    return pl.pallas_call(
        functools.partial(forward_kernel, tile, prompt_tiles, block_len, scale),
        grid_spec=pltpu.PrefetchScalarGridSpec(
            num_scalar_prefetch=2,
            grid=(heads,),
            in_specs=[
                part(0),
                part(1),
                part(2),
                whole((group, 2)),
                pl.BlockSpec((1, head_dim), lambda h, *_: (0, h)),
                pl.BlockSpec((1, head_dim), lambda h, *_: (0, h)),
                whole((group, 1)),
                whole((tiles, tile)),
            ],
            out_specs=[
                head,
                pl.BlockSpec((None, tiles, tile), lambda h, *_: (h, 0, 0)),
                head,
                head,
                head,
            ],
            scratch_shapes=[
                pltpu.VMEM((head_dim, group), bf16),
                pltpu.VMEM((group, head_dim), f32),
            ],
        ),
        out_shape=[
            jax.ShapeDtypeStruct((group, width), bf16),
            jax.ShapeDtypeStruct((heads, tiles, tile), f32),
            jax.ShapeDtypeStruct((group, width), bf16),
            jax.ShapeDtypeStruct((group, width), bf16),
            jax.ShapeDtypeStruct((group, width), bf16),
        ],
        compiler_params=pltpu.CompilerParams(vmem_limit_bytes=56 * 2**20),
        cost_estimate=pl.CostEstimate(
            flops=2 * heads * group * group * head_dim * 2,
            bytes_accessed=32 * group * width,
            transcendentals=0,
        ),
        name="attention_forward",
    )(place, first_tile, raw, raw, raw, inv, gain_q, gain_k, seg_col, seg_row)


def attention_backward(
    queries, keys, values, lse, out, grad_out, seg_col, seg_row, place, first_tile, tile, block_len, scale
):
    group, width = queries.shape
    head_dim = 128
    heads = width // head_dim
    tiles = group // tile
    prompt_tiles = tiles // 2

    def whole(shape):
        return pl.BlockSpec(shape, lambda h, *_: (0,) * len(shape))

    head = pl.BlockSpec((group, head_dim), lambda h, *_: (0, h))
    return pl.pallas_call(
        functools.partial(backward_kernel, tile, prompt_tiles, block_len, scale),
        grid_spec=pltpu.PrefetchScalarGridSpec(
            num_scalar_prefetch=2,
            grid=(heads,),
            in_specs=[
                head,
                head,
                head,
                pl.BlockSpec((None, tiles, tile), lambda h, *_: (h, 0, 0)),
                head,
                head,
                whole((group, 1)),
                whole((tiles, tile)),
            ],
            out_specs=[head, head, head],
            scratch_shapes=[
                pltpu.VMEM((head_dim, group), bf16),
                pltpu.VMEM((group, head_dim), bf16),
                pltpu.VMEM((tiles, tile), f32),
                pltpu.VMEM((group, head_dim), f32),
                pltpu.VMEM((group, head_dim), f32),
                pltpu.VMEM((group, head_dim), f32),
            ],
        ),
        out_shape=[
            jax.ShapeDtypeStruct((group, width), f32),
            jax.ShapeDtypeStruct((group, width), f32),
            jax.ShapeDtypeStruct((group, width), bf16),
        ],
        compiler_params=pltpu.CompilerParams(vmem_limit_bytes=56 * 2**20),
        cost_estimate=pl.CostEstimate(
            flops=5 * heads * group * group * head_dim,
            bytes_accessed=32 * group * width,
            transcendentals=0,
        ),
        name="attention_backward",
    )(place, first_tile, queries, keys, values, lse, out, grad_out, seg_col, seg_row)


def slot_table(expert_rows, order_rows, gate_rows, count_experts, capacity):
    chosen = expert_rows.T[None, :, :] == jnp.arange(count_experts, dtype=jnp.int32)[:, None, None]
    holds = jnp.any(chosen, axis=1)
    order = jnp.sum(jnp.where(chosen, order_rows.T[None], 0), axis=1)
    gate = jnp.sum(jnp.where(chosen, gate_rows.T[None], 0.0), axis=1)
    earlier = holds[:, None, :] & (order[:, None, :] < order[:, :, None])
    slot = jnp.sum(earlier.astype(jnp.int32), axis=2)
    return (jnp.where(holds & (slot < capacity), slot, -1), gate)


def on_device(
    tokens,
    cotangent,
    wqkv,
    wo,
    attn_gain,
    query_gain,
    key_gain,
    moe_gain,
    w_gate,
    w_up,
    w_down,
    expert_ids,
    gates,
    slot_order,
    block_assign,
    segment_ids,
):
    count_rows, width = tokens.shape
    head_dim = width // HEADS
    scale = head_dim ** (-0.5)
    peers = lax.axis_size("ctx")
    groups = lax.axis_size("dp")
    me = lax.axis_index("ctx")
    my_dp = lax.axis_index("dp")
    group_rows = count_rows * peers
    rep = max(1, peers // HEADS)
    own_heads = max(1, HEADS // peers)
    own_width = own_heads * head_dim
    first_head = (me // rep) * own_heads
    block_len = count_rows // BLK_DEV
    tile = 512

    gain_all = lax.all_gather(
        jnp.stack([attn_gain, query_gain, key_gain, moe_gain]), "dp", axis=1, tiled=True
    ).astype(f32)
    gain_attn, gain_moe = gain_all[0:1], gain_all[3:4]
    gain_own = lax.dynamic_slice_in_dim(gain_all, first_head * head_dim, own_width, 1)
    gain_q, gain_k = gain_own[1:2], gain_own[2:3]

    assign = block_assign[0]
    count_blocks = assign.shape[0]
    place = jnp.argmax(
        assign[None, :] == jnp.arange(count_blocks, dtype=jnp.int32)[:, None], axis=1
    ).astype(jnp.int32)
    cont = segment_ids[0]
    prompt_len = group_rows - cont.shape[0]
    seg_logical = jnp.concatenate([jnp.full((prompt_len,), -1, jnp.int32), cont])
    tiles = group_rows // tile
    tile_seg = seg_logical.reshape(tiles, tile)[:, 0]
    first_tile = jnp.where(
        tile_seg < 0,
        jnp.arange(tiles, dtype=jnp.int32),
        jnp.sum((seg_logical[None, :] < tile_seg[:, None]).astype(jnp.int32), axis=1) // tile,
    ).astype(jnp.int32)
    seg_col = seg_logical[:, None]
    seg_row = seg_logical.reshape(tiles, tile)

    inputs = tokens.astype(f32)
    inv_in = rms_scale(inputs)
    hat_in = inputs * inv_in
    normed = (hat_in * gain_attn).astype(bf16)
    normed_all = lax.all_gather(normed, "ctx", axis=0, tiled=True)
    w_own = lax.dynamic_slice_in_dim(
        wqkv.reshape(wqkv.shape[0], 3, HEADS, head_dim), first_head, own_heads, 2
    ).reshape(wqkv.shape[0], 3 * own_width)
    w_own = lax.all_gather(w_own, "dp", axis=0, tiled=True)
    raw = jnp.dot(normed_all, w_own, preferred_element_type=f32)
    square = raw[:, : 2 * own_width].reshape(group_rows, 2, own_width)
    square = lax.psum(jnp.sum(square * square, axis=2).T, "ctx") * (1.0 / rep)
    inv_qk = lax.rsqrt(square / width + epsilon).T
    attended, lse, queries, keys, values = attention_forward(
        raw, inv_qk, gain_q, gain_k, seg_col, seg_row, place, first_tile, tile, block_len, scale
    )
    attn_low = lax.all_to_all(
        attended.reshape(peers, count_rows, own_width), "ctx", split_axis=0, concat_axis=0, tiled=True
    )[::rep]
    attn_low = attn_low.transpose(1, 0, 2).reshape(count_rows, width)
    full_wo = lax.all_gather(wo, "dp", axis=0, tiled=True)
    state = inputs + jnp.dot(attn_low, full_wo, preferred_element_type=f32)
    inv_state = rms_scale(state)
    hat_state = state * inv_state
    normed_moe = (hat_state * gain_moe).astype(bf16)

    local_experts = w_gate.shape[0]
    count_experts = local_experts * peers
    capacity = 9 * count_rows * TOP // (8 * count_experts)
    slot, gate = slot_table(expert_ids, slot_order, gates, count_experts, capacity)
    slot = lax.all_to_all(
        slot.reshape(peers, local_experts, count_rows), "ctx", split_axis=0, concat_axis=0, tiled=True
    )
    gate = lax.all_to_all(
        gate.reshape(peers, local_experts, count_rows), "ctx", split_axis=0, concat_axis=0, tiled=True
    )
    picks = slot[:, :, None, :] == jnp.arange(capacity, dtype=jnp.int32)[:, None]
    slot_gate = jnp.sum(jnp.where(picks, gate[:, :, None, :], 0.0), axis=3)[..., None]
    picks = picks.astype(bf16)

    full_gate = lax.all_gather(w_gate, "dp", axis=1, tiled=True)
    full_up = lax.all_gather(w_up, "dp", axis=1, tiled=True)
    full_down = lax.all_gather(w_down, "dp", axis=1, tiled=True)

    cot_all = lax.all_gather(cotangent, "ctx", axis=0, tiled=True).reshape(peers, count_rows, width)
    grad_rows = (
        jnp.einsum("sncr,srd->sncd", picks, cot_all, preferred_element_type=f32) * slot_gate
    ).astype(bf16)
    grad_hidden = jnp.einsum("sncd,nfd->sncf", grad_rows, full_down, preferred_element_type=f32)

    moe_all = lax.all_gather(normed_moe, "ctx", axis=0, tiled=True).reshape(
        peers, count_rows, width
    )
    expert_in = jnp.einsum("sncr,srd->sncd", picks, moe_all, preferred_element_type=f32).astype(
        bf16
    )
    gate_pre = jnp.einsum("sncd,ndf->sncf", expert_in, full_gate, preferred_element_type=f32)
    up_pre = jnp.einsum("sncd,ndf->sncf", expert_in, full_up, preferred_element_type=f32)
    sigmoid = jax.nn.sigmoid(gate_pre)
    silu = gate_pre * sigmoid
    hidden = (silu * up_pre).astype(bf16)
    grad_gate_pre = (
        grad_hidden * up_pre * sigmoid * (1.0 + gate_pre * (1.0 - sigmoid))
    ).astype(bf16)
    grad_up_pre = (grad_hidden * silu).astype(bf16)
    grad_in = (
        jnp.einsum("sncf,ndf->sncd", grad_gate_pre, full_gate, preferred_element_type=f32)
        + jnp.einsum("sncf,ndf->sncd", grad_up_pre, full_up, preferred_element_type=f32)
    ).astype(bf16)
    part_moe = jnp.einsum("sncr,sncd->srd", picks, grad_in, preferred_element_type=f32).astype(bf16)
    grad_normed_moe = lax.psum_scatter(
        part_moe.reshape(group_rows, width), "ctx", scatter_dimension=0, tiled=True
    ).astype(f32)

    out_rows = (
        jnp.einsum("sncf,nfd->sncd", hidden, full_down, preferred_element_type=f32) * slot_gate
    ).astype(bf16)
    part_mixed = jnp.einsum("sncr,sncd->srd", picks, out_rows, preferred_element_type=f32).astype(
        bf16
    )
    mixed = lax.psum_scatter(
        part_mixed.reshape(group_rows, width), "ctx", scatter_dimension=0, tiled=True
    ).astype(f32)
    output = (state + mixed).astype(bf16)

    grad_down = jnp.einsum("sncf,sncd->nfd", hidden, grad_rows, preferred_element_type=f32)
    grad_gate = jnp.einsum("sncd,sncf->ndf", expert_in, grad_gate_pre, preferred_element_type=f32)
    grad_up = jnp.einsum("sncd,sncf->ndf", expert_in, grad_up_pre, preferred_element_type=f32)

    def expert_sum(term):
        return lax.psum_scatter(term.astype(bf16), "dp", scatter_dimension=1, tiled=True).astype(f32)

    moe_gain_term = jnp.sum(grad_normed_moe * hat_state, axis=0)
    grad_state = cotangent.astype(f32) + rms_back(grad_normed_moe * gain_moe, hat_state, inv_state)
    grad_branch = grad_state.astype(bf16)
    grad_attn = lax.dot_general(grad_branch, full_wo, NT, preferred_element_type=f32).astype(bf16)
    grad_attn = grad_attn.reshape(count_rows, peers // rep, own_width).transpose(1, 0, 2)
    grad_attn = jnp.repeat(grad_attn, rep, axis=0)
    grad_attended = lax.all_to_all(
        grad_attn, "ctx", split_axis=0, concat_axis=0, tiled=True
    ).reshape(group_rows, own_width)
    grad_q, grad_k, grad_v = attention_backward(
        queries,
        keys,
        values,
        lse,
        attended,
        grad_attended,
        seg_col,
        seg_row,
        place,
        first_tile,
        tile,
        block_len,
        scale,
    )
    hat_q = raw[:, :own_width] * inv_qk[:, 0:1]
    hat_k = raw[:, own_width : 2 * own_width] * inv_qk[:, 1:2]
    query_gain_term = jnp.sum(grad_q * hat_q, axis=0)
    key_gain_term = jnp.sum(grad_k * hat_k, axis=0)
    means = jnp.stack(
        [
            jnp.sum(grad_q * gain_q * hat_q, axis=1),
            jnp.sum(grad_k * gain_k * hat_k, axis=1),
        ]
    )
    means = (lax.psum(means, "ctx") * (1.0 / (rep * width))).T
    grad_raw_q = inv_qk[:, 0:1] * (grad_q * gain_q - hat_q * means[:, 0:1])
    grad_raw_k = inv_qk[:, 1:2] * (grad_k * gain_k - hat_k * means[:, 1:2])
    grad_qkv = jnp.concatenate([grad_raw_q.astype(bf16), grad_raw_k.astype(bf16), grad_v], axis=1)
    part_normed = lax.dot_general(grad_qkv, w_own, NT, preferred_element_type=f32) * (1.0 / rep)
    grad_normed = lax.psum_scatter(
        part_normed.astype(bf16), "ctx", scatter_dimension=0, tiled=True
    ).astype(f32)
    attn_gain_term = jnp.sum(grad_normed * hat_in, axis=0)
    input_grad = (grad_state + rms_back(grad_normed * gain_attn, hat_in, inv_in)).astype(bf16)

    part_qkv = lax.dot_general(normed_all, grad_qkv, TN, preferred_element_type=f32).astype(bf16)
    part_qkv = lax.psum_scatter(part_qkv, "dp", scatter_dimension=0, tiled=True)
    qkv_total = lax.all_gather(part_qkv, "ctx", axis=0, tiled=False)[::rep]
    rows_dp = part_qkv.shape[0]
    qkv_total = (
        qkv_total.reshape(peers // rep, rows_dp, 3, own_width)
        .transpose(1, 2, 0, 3)
        .reshape(rows_dp, 3 * width)
        .astype(f32)
    )
    part_out = lax.dot_general(attn_low, grad_branch, TN, preferred_element_type=f32).astype(bf16)
    out_total = lax.psum(
        lax.psum_scatter(part_out, "dp", scatter_dimension=0, tiled=True), "ctx"
    ).astype(f32)

    own_terms = jnp.stack([query_gain_term, key_gain_term]) * (1.0 / rep)
    spread = lax.dynamic_update_slice_in_dim(
        jnp.zeros((2, width), f32), own_terms, first_head * head_dim, 1
    )
    gain_terms = jnp.concatenate([attn_gain_term[None], spread, moe_gain_term[None]], axis=0)
    gain_terms = lax.psum(gain_terms, ("dp", "ctx"))
    gain_terms = lax.dynamic_slice_in_dim(
        gain_terms, my_dp * (width // groups), width // groups, 1
    )
    return (
        output,
        input_grad,
        qkv_total,
        out_total,
        gain_terms[0],
        gain_terms[1],
        gain_terms[2],
        gain_terms[3],
        expert_sum(grad_gate),
        expert_sum(grad_up),
        expert_sum(grad_down),
    )


def solution(mesh):
    rows = P(("dp", "ctx"), None)
    expert = P("ctx", "dp", None)
    by_dp = P("dp", None)
    return jax.shard_map(
        on_device,
        mesh=mesh,
        in_specs=(
            rows,
            rows,
            by_dp,
            by_dp,
            P("dp"),
            P("dp"),
            P("dp"),
            P("dp"),
            expert,
            expert,
            expert,
            rows,
            rows,
            rows,
            by_dp,
            by_dp,
        ),
        out_specs=(
            rows,
            rows,
            by_dp,
            by_dp,
            P("dp"),
            P("dp"),
            P("dp"),
            P("dp"),
            expert,
            expert,
            expert,
        ),
        check_vma=False,
    )
```

time: 4260 us -> 2300 us (0.54)
  waiting for transfers between devices: 2050 us -> 1340 us
  matrix products: 1090 us -> 420 us
  blocking collectives: 455 us -> 174 us
  local copies, waits for them, and re-layouts: 318 us -> 108 us
  other arithmetic: 281 us -> 72.5 us
  Pallas kernels: 0 us -> 134 us
    all_to_all x4, waiting for transfers between devices: 1050 us -> 149 us  [the longest x1 87.7 us: on_device(): lax.all_to_all(attended.reshape(peers, count_rows, own_width), 'ctx', spl...]
    dot_general x53 -> x17, matrix products: 1060 us -> 390 us  [the longest x1 42.1 us: on_device(): jnp.einsum('sncr,sncd->srd', picks, grad_in, preferred_element_type=f32)]
    all_gather x6 -> x1, blocking collectives: 439 us -> 9.62 us  [on_device(): lax.all_gather(jnp.stack([attn_gain, query_gain, key_gain, moe_gain]), 'd...]
    reduce_scatter x3 -> x8, waiting for transfers between devices: 261 us -> 589 us  [the longest x3 201 us: expert_sum(): lax.psum_scatter(term.astype(bf16), 'dp', scatter_dimension=1, tiled=True)]
    unnamed x17 -> x18, waiting for transfers between devices: 204 us -> 3.93 us
    reduce_sum x9, other arithmetic: 189 us -> 24.5 us  [the longest x1 8.05 us: on_device(): query_gain_term = jnp.sum(grad_q * hat_q, axis=0)]
    all_gather x9, waiting for transfers between devices: 375 us -> 537 us  [the longest x1 153 us: on_device(): normed_all = lax.all_gather(normed, 'ctx', axis=0, tiled=True)]
    psum x1 -> x3, blocking collectives: 16.5 us -> 164 us  [the longest x1 63.1 us: on_device(): square = lax.psum(jnp.sum(square * square, axis=2).T, 'ctx') * (1.0 / rep)]
  transfers between devices with their start and end apart: 19 -> 22, of which waited for: 14 -> 18; matrix products, arithmetic and copies ran while one was open for 24% -> 20% of each run, Pallas kernels for 0% -> 6%
where the time goes in v1:
time: 2300 us; the launch traced here: 2290 us
  waiting for transfers between devices  1340 us (58%)
  matrix products  420 us (18%)
  blocking collectives  174 us (8%)
  Pallas kernels  134 us (6%)
  local copies, waits for them, and re-layouts  108 us (5%)
  other arithmetic  72.5 us (3%)
  starting transfers between devices  28.8 us (1%)
    reduce_scatter x3, waiting for transfers between devices, expert_sum(): lax.psum_scatter(term.astype(bf16), 'dp', scatter_dimension=1, tiled=True)  201 us
    reduce_scatter x1, waiting for transfers between devices, on_device(): lax.psum_scatter(part_mixed.reshape(group_rows, width), 'ctx', scatter_di...  164 us
    all_gather x1, waiting for transfers between devices, on_device(): normed_all = lax.all_gather(normed, 'ctx', axis=0, tiled=True)  153 us
    reduce_scatter x1, waiting for transfers between devices, on_device(): lax.psum_scatter(part_moe.reshape(group_rows, width), 'ctx', scatter_dime...  116 us
    reduce_scatter x1, waiting for transfers between devices, on_device(): lax.psum_scatter(part_normed.astype(bf16), 'ctx', scatter_dimension=0, ti...  108 us
    all_gather x1, waiting for transfers between devices, on_device(): lax.all_gather(normed_moe, 'ctx', axis=0, tiled=True)  99.8 us
    all_to_all x1, waiting for transfers between devices, on_device(): lax.all_to_all(attended.reshape(peers, count_rows, own_width), 'ctx', spl...  87.7 us
    pallas_call x1, Pallas kernels, attention_backward(): pl.pallas_call(functools.partial(backward_kernel, tile, prompt_tiles, blo...  70.7 us
  transfers between devices with their start and end apart: 22, of which 18 were waited for; matrix products, arithmetic and copies ran while one was open for 20% of the time, Pallas kernels for 6%

profile of v1, /device:TPU:0, one launch (start us, length us, event | category | flops | bytes accessed | tf_op | source)
XLA Modules:
  0.0 2293.5 jit_solution(3095794322906346769)
XLA Ops:
  36.7 29.0 %all-gather.13.cloned.1.call-done = bf16[2048,768]{1,0:T(8,128)(2,1)} async-done(((bf16[512,768]{1,0:T(8,128)(2,1)}), bf16[2048,768]{1,0:T(8,128)(2,1)}) %all-gather.13.cloned.1.call-update) | async-done | bytes 3145744 | tf_op jit(solution)/shard_map/all_gather | solution.py:408
  65.6 153.3 %all-gather.11.cloned.1.call-done = bf16[4096,2048]{1,0:T(8,128)(2,1)} async-done(((bf16[512,2048]{1,0:T(8,128)(2,1)}), bf16[4096,2048]{1,0:T(8,128)(2,1)}) %all-gather.11.cloned.1.call-update) | async-done | bytes 16777232 | tf_op jit(solution)/shard_map/all_gather | solution.py:404
  258.1 63.1 %psum.28 = f32[2,4096]{0,1:T(8,128)} all-reduce(f32[2,4096]{0,1:T(8,128)} %bitcast.177), channel_id=1, replica_groups=mesh['dp'=4,'ctx'=8] {'ctx'}, use_global_device_ids=true, to_apply=%region_4.5 | all-reduce | flops 8192 | bytes 65536 | tf_op jit(solution)/shard_map/psum | solution.py:411
  324.5 63.8 %attention_forward.1 = (bf16[4096,256]{1,0:T(8,128)(2,1)}, f32[2,8,512]{2,1,0:T(8,128)}, bf16[4096,256]{1,0:T(8,128)(2,1)}, bf16[4096,256]{1,0:T(8,128)(2,1)}, bf16[4096,256]{1,0:T(8,128)(2,1)}) custom-call(s32[16]{0:T(128)} %get-tuple-element.20.place, s32[8]{0:T(128)} %compare_select_fusion.first_tile, f32[4096,768]{1,0:T(8,128)} %copy.105.raw_q.raw_k.raw_v, ...), custom_call_target="tpu_custom_call" | custom-call | flops 17179869184 | bytes 33554432 | tf_op jit(solution)/shard_map/attention_forward/pallas_call | solution.py:235
  408.9 87.7 %all-to-all-done = bf16[8,512,256]{1,2,0:T(8,128)(2,1)} async-done(((bf16[8,512,256]{1,2,0:T(8,128)(2,1)}), bf16[8,512,256]{1,2,0:T(8,128)(2,1)}, u32[]{:S(2)}, u32[]{:S(2)}) %all-to-all-start) | async-done | bytes 2097184 | tf_op jit(solution)/shard_map/all_to_all | solution.py:416
  558.9 99.8 %all-gather.17.cloned.1.call-done = bf16[4096,2048]{1,0:T(8,128)(2,1)} async-done(((bf16[512,2048]{1,0:T(8,128)(2,1)}), bf16[4096,2048]{1,0:T(8,128)(2,1)}) %all-gather.17.cloned.1.call-update) | async-done | bytes 16777232 | tf_op jit(solution)/shard_map/all_gather | solution.py:450
  677.5 68.6 %all-gather.21.cloned.1.call-done = bf16[2,2048,1024]{2,1,0:T(8,128)(2,1)} async-done(((bf16[2,512,1024]{2,1,0:T(8,128)(2,1)}), bf16[2,2048,1024]{2,1,0:T(8,128)(2,1)}) %all-gather.21.cloned.1.call-update) | async-done | bytes 8388624 | tf_op jit(solution)/shard_map/all_gather | solution.py:441
  746.1 27.3 %fusion.20 = f32[2,8,288,1024]{3,2,1,0:T(8,128)} fusion(bf16[8,2,288,2048]{3,2,1,0:T(8,128)(2,1)} %convolution_convert_fusion.1, bf16[2,2048,1024]{2,1,0:T(8,128)(2,1)} %all-gather.21.cloned.1.call-done), kind=kOutput, calls=%fused_computation.33 | convolution fusion | flops 19327352832 | bytes 46137344 | tf_op jit(solution)/shard_map/sncd,ndf->sncf/dot_general | solution.py:457
  773.4 62.2 %all-gather.19.cloned.1.call-done = bf16[2,2048,1024]{2,1,0:T(8,128)(2,1)} async-done(((bf16[2,512,1024]{2,1,0:T(8,128)(2,1)}), bf16[2,2048,1024]{2,1,0:T(8,128)(2,1)}) %all-gather.19.cloned.1.call-update) | async-done | bytes 8388624 | tf_op jit(solution)/shard_map/all_gather | solution.py:440
  835.6 27.3 %fusion.22 = f32[2,8,288,1024]{3,2,1,0:T(8,128)} fusion(bf16[8,2,288,2048]{3,2,1,0:T(8,128)(2,1)} %convolution_convert_fusion.1, bf16[2,2048,1024]{2,1,0:T(8,128)(2,1)} %all-gather.19.cloned.1.call-done), kind=kOutput, calls=%fused_computation.35 | convolution fusion | flops 19327352832 | bytes 46137344 | tf_op jit(solution)/shard_map/sncd,ndf->sncf/dot_general | solution.py:456
  862.9 62.2 %all-gather.23.cloned.1.call-done = bf16[2,1024,2048]{2,1,0:T(8,128)(2,1)} async-done(((bf16[2,256,2048]{2,1,0:T(8,128)(2,1)}), bf16[2,1024,2048]{2,1,0:T(8,128)(2,1)}) %all-gather.23.cloned.1.call-update) | async-done | bytes 8388624 | tf_op jit(solution)/shard_map/all_gather | solution.py:442
  925.1 37.5 %fusion.9 = (bf16[8,2,288,1024]{3,2,0,1:T(8,128)(2,1)}, bf16[8,2,288,1024]{3,2,0,1:T(8,128)(2,1)}, bf16[8,2,288,1024]{3,2,0,1:T(8,128)(2,1)}) fusion(f32[2,8,288,1024]{3,2,1,0:T(8,128)} %fusion.22, f32[2,8,288,1024]{3,2,1,0:T(8,128)} %fusion.20, bf16[2,1024,2048]{2,1,0:T(8,128)(2,1)} %all-gather.23.cloned.1.call-done, ...), kind=kOutput, calls=%fused_computation.14 | convolution fusion | flops 19398131712 | bytes 93323264 | tf_op jit(solution)/shard_map/sncd,nfd->sncf/dot_general | solution.py:448
  962.6 29.8 %fusion.38 = f32[2,8,288,2048]{3,2,0,1:T(8,128)} fusion(bf16[2,2048,1024]{2,1,0:T(8,128)(2,1)} %all-gather.19.cloned.1.call-done, bf16[8,2,288,1024]{3,2,0,1:T(8,128)(2,1)} %get-tuple-element.77), kind=kOutput, calls=%fused_computation.50 | convolution fusion | flops 19327352832 | bytes 55574528 | tf_op jit(solution)/shard_map/sncf,ndf->sncd/dot_general | solution.py:466
  992.3 42.1 %bitcast_convert_fusion = bf16[8,512,2048]{2,1,0:T(8,128)(2,1)} fusion(f32[2,8,288,2048]{3,2,0,1:T(8,128)} %fusion.38, bf16[2,2048,1024]{2,1,0:T(8,128)(2,1)} %all-gather.21.cloned.1.call-done, bf16[8,2,288,1024]{3,2,0,1:T(8,128)(2,1)} %get-tuple-element.76, pred[8,2,288,512]{3,2,1,0:T(32,128)(4,1)S(1)} %copy-done.8), kind=kOutput, calls=%fused_computation.4 | convolution fusion | flops 29018292224 | bytes 74711040 | tf_op jit(solution)/shard_map/sncr,sncd->srd/dot_general | solution.py:469
  1034.6 29.2 %fusion.28 = f32[2,8,288,2048]{3,2,0,1:T(8,128)} fusion(bf16[8,2,288,1024]{3,2,0,1:T(8,128)(2,1)} %get-tuple-element.78, bf16[2,1024,2048]{2,1,0:T(8,128)(2,1)} %all-gather.23.cloned.1.call-done), kind=kOutput, calls=%fused_computation.39 | convolution fusion | flops 19327352832 | bytes 55574528 | tf_op jit(solution)/shard_map/sncf,nfd->sncd/dot_general | solution.py:475
  1063.8 23.4 %bitcast_convert_fusion.1 = bf16[8,512,2048]{2,1,0:T(8,128)(2,1)} fusion(f32[2,8,288,2048]{3,2,0,1:T(8,128)} %fusion.28, f32[8,2,288]{2,1,0:T(2,128)S(1)} %copy-done.26, s32[8,2,512]{2,1,0:T(2,128)S(1)} %copy-done.13), kind=kOutput, calls=%fused_computation.5 | convolution fusion | flops 9693298688 | bytes 54577152 | tf_op jit(solution)/shard_map/sncr,sncd->srd/dot_general | solution.py:477
  1087.3 115.6 %reduce-scatter.11.cloned.1.call-done = bf16[512,2048]{1,0:T(8,128)(2,1)} async-done(((bf16[4096,2048]{1,0:T(8,128)(2,1)}), bf16[512,2048]{1,0:T(8,128)(2,1)}) %reduce-scatter.11.cloned.1.call-update) | async-done | bytes 2097168 | tf_op jit(solution)/shard_map/reduce_scatter | solution.py:470
  1207.5 164.3 %reduce-scatter.9.cloned.1.call-done = bf16[512,2048]{1,0:T(8,128)(2,1)} async-done(((bf16[4096,2048]{1,0:T(8,128)(2,1)}), bf16[512,2048]{1,0:T(8,128)(2,1)}) %reduce-scatter.9.cloned.1.call-update) | async-done | bytes 2097168 | tf_op jit(solution)/shard_map/reduce_scatter | solution.py:480
  1404.4 47.3 %all-to-all-done.3 = bf16[8,512,256]{2,1,0:T(8,128)(2,1)} async-done(((bf16[8,512,256]{2,1,0:T(8,128)(2,1)}), bf16[8,512,256]{2,1,0:T(8,128)(2,1)}, u32[]{:S(2)}, u32[]{:S(2)}) %all-to-all-start.3) | async-done | bytes 2097184 | tf_op jit(solution)/shard_map/all_to_all | solution.py:498
  1451.7 70.7 %attention_backward.1 = (f32[4096,256]{1,0:T(8,128)}, f32[4096,256]{1,0:T(8,128)}, bf16[4096,256]{1,0:T(8,128)(2,1)}) custom-call(s32[16]{0:T(128)} %get-tuple-element.20.place, s32[8]{0:T(128)} %compare_select_fusion.first_tile, bf16[4096,256]{1,0:T(8,128)(2,1)} %get-tuple-element.22.queries, bf16[4096,256]{1,0:T(8,128)(2,1)} %get-tuple-element.23.keys, ...), custom_call_target="tpu_custom_call" | custom-call | flops 21474836480 | bytes 33554432 | tf_op jit(solution)/shard_map/attention_backward/pallas_call | solution.py:292
  1531.1 62.9 %psum.29 = f32[2,4096]{0,1:T(8,128)} all-reduce(f32[2,4096]{0,1:T(8,128)S(1)} %copy.120), channel_id=1, replica_groups=mesh['dp'=4,'ctx'=8] {'ctx'}, use_global_device_ids=true, to_apply=%region_16.17 | all-reduce | flops 8192 | bytes 65536 | tf_op jit(solution)/shard_map/psum | solution.py:526
  1625.1 27.0 %bitcast_convert_fusion.2 = bf16[2,1024,2048]{2,1,0:T(8,128)(2,1)} fusion(bf16[8,2,288,1024]{3,2,0,1:T(8,128)(2,1)} %get-tuple-element.78, bf16[8,2,288,2048]{3,2,1,0:T(8,128)(2,1)} %multiply_convert_fusion), kind=kOutput, calls=%fused_computation.25 | convolution fusion | flops 19331547136 | bytes 36700160 | tf_op jit(solution)/shard_map/sncf,sncd->nfd/dot_general | solution.py:485
  1652.1 27.3 %bitcast_convert_fusion.3 = bf16[2,2048,1024]{2,1,0:T(8,128)(2,1)} fusion(bf16[8,2,288,2048]{3,2,1,0:T(8,128)(2,1)} %convolution_convert_fusion.1, bf16[8,2,288,1024]{3,2,0,1:T(8,128)(2,1)} %get-tuple-element.76), kind=kOutput, calls=%fused_computation.26 | convolution fusion | flops 19331547136 | bytes 36700160 | tf_op jit(solution)/shard_map/sncd,sncf->ndf/dot_general | solution.py:487
  1679.5 27.1 %bitcast_convert_fusion.4 = bf16[2,2048,1024]{2,1,0:T(8,128)(2,1)} fusion(bf16[8,2,288,2048]{3,2,1,0:T(8,128)(2,1)} %convolution_convert_fusion.1, bf16[8,2,288,1024]{3,2,0,1:T(8,128)(2,1)} %get-tuple-element.77), kind=kOutput, calls=%fused_computation.27 | convolution fusion | flops 19331547136 | bytes 36700160 | tf_op jit(solution)/shard_map/sncd,sncf->ndf/dot_general | solution.py:486
  1728.1 29.6 %reduce-scatter.23.cloned.1.call-done = bf16[2,256,2048]{2,1,0:T(8,128)(2,1)} async-done(((bf16[2,1024,2048]{2,1,0:T(8,128)(2,1)}), bf16[2,256,2048]{2,1,0:T(8,128)(2,1)}) %reduce-scatter.23.cloned.1.call-update) | async-done | bytes 2097168 | tf_op jit(solution)/shard_map/reduce_scatter | solution.py:490
  1761.8 85.2 %reduce-scatter.21.cloned.1.call-done = bf16[2,512,1024]{2,1,0:T(8,128)(2,1)} async-done(((bf16[2,2048,1024]{2,1,0:T(8,128)(2,1)}), bf16[2,512,1024]{2,1,0:T(8,128)(2,1)}) %reduce-scatter.21.cloned.1.call-update) | async-done | bytes 2097168 | tf_op jit(solution)/shard_map/reduce_scatter | solution.py:490
  1851.1 86.1 %reduce-scatter.19.cloned.1.call-done = bf16[2,512,1024]{2,1,0:T(8,128)(2,1)} async-done(((bf16[2,2048,1024]{2,1,0:T(8,128)(2,1)}), bf16[2,512,1024]{2,1,0:T(8,128)(2,1)}) %reduce-scatter.19.cloned.1.call-update) | async-done | bytes 2097168 | tf_op jit(solution)/shard_map/reduce_scatter | solution.py:490
  1941.3 63.1 %all-reduce.3.cloned.1.call-done = bf16[512,2048]{1,0:T(8,128)(2,1)} async-done(((bf16[512,2048]{1,0:T(8,128)(2,1)}), bf16[512,2048]{1,0:T(8,128)(2,1)}) %all-reduce.3.cloned.1.call-update) | async-done | bytes 2097168 | tf_op jit(solution)/shard_map/psum | solution.py:548
  2008.5 61.8 %all-gather.27.cloned.1.call-done = bf16[4096,768]{1,0:T(8,128)(2,1)} async-done(((bf16[512,768]{1,0:T(8,128)(2,1)}), bf16[4096,768]{1,0:T(8,128)(2,1)}) %all-gather.27.cloned.1.call-update) | async-done | bytes 6291472 | tf_op jit(solution)/shard_map/all_gather | solution.py:539
  2080.4 21.7 copy.137
  2131.3 108.1 %reduce-scatter.13.cloned.1.call-done = bf16[512,2048]{1,0:T(8,128)(2,1)} async-done(((bf16[4096,2048]{1,0:T(8,128)(2,1)}), bf16[512,2048]{1,0:T(8,128)(2,1)}) %reduce-scatter.13.cloned.1.call-update) | async-done | bytes 2097168 | tf_op jit(solution)/shard_map/reduce_scatter | solution.py:531
  2242.4 37.9 %psum.31 = f32[4,2048]{1,0:T(4,128)S(1)} all-reduce(f32[4,2048]{1,0:T(4,128)S(1)} %pad_maximum_fusion.4), channel_id=1, replica_groups=mesh['dp'=4,'ctx'=8] {'dp','ctx'}, use_global_device_ids=true, to_apply=%region_26.27 | all-reduce | flops 8192 | bytes 65536 | tf_op jit(solution)/shard_map/psum | solution.py:557
  (197 shorter events, 336.5 us)
Async XLA Ops:
  7.2 58.5 %all-gather.13.cloned.1.call-start = ((), (), s32[]{:S(2)}) async-start(), calls=%async_computation.13 | async-start | bytes 3932160 | tf_op jit(solution)/shard_map/all_gather | solution.py:408
  18.8 200.1 %all-gather.11.cloned.1.call-start = ((), (), s32[]{:S(2)}) async-start(), calls=%async_computation.12 | async-start | bytes 18874368 | tf_op jit(solution)/shard_map/all_gather | solution.py:404
  29.1 475.5 %copy-start.15 = (f32[1,2048]{1,0:T(1,128)}, f32[1,2048]{1,0:T(1,128)S(1)}, u32[]{:S(2)}) copy-start(f32[1,2048]{1,0:T(1,128)S(1)} %get-tuple-element.87) | copy-start | bytes 24580
  31.0 377.9 %all-gather.15.cloned.1.call-start = ((), (), s32[]{:S(2)}) async-start(), calls=%async_computation.14 | async-start | bytes 10485760 | tf_op jit(solution)/shard_map/all_gather | solution.py:420
  31.8 508.2 %all-gather.25.cloned.1.call-start = ((), (), s32[]{:S(2)}) async-start(), calls=%async_computation.20 | async-start | bytes 18874368 | tf_op jit(solution)/shard_map/all_gather | solution.py:444
  32.4 207.0 %copy-start.24 = (s32[8,512]{1,0:T(8,128)}, s32[8,512]{1,0:T(8,128)S(1)}, u32[]{:S(2)}) copy-start(s32[8,512]{1,0:T(8,128)S(1)} %reshape.104.seg_row) | copy-start | bytes 49156
  392.2 104.5 %all-to-all-start = ((bf16[8,512,256]{1,2,0:T(8,128)(2,1)}), bf16[8,512,256]{1,2,0:T(8,128)(2,1)}, u32[]{:S(2)}, u32[]{:S(2)}) async-start(bf16[8,512,256]{1,2,0:T(8,128)(2,1)} %copy.109), calls=%async_computation | async-start | bytes 4194304 | tf_op jit(solution)/shard_map/all_to_all | solution.py:416
  396.8 261.8 %all-gather.17.cloned.1.call-start = ((), (), s32[]{:S(2)}) async-start(), calls=%async_computation.15 | async-start | bytes 18874368 | tf_op jit(solution)/shard_map/all_gather | solution.py:450
  508.4 237.7 %all-gather.21.cloned.1.call-start = ((), (), s32[]{:S(2)}) async-start(), calls=%async_computation.17 | async-start | bytes 10485760 | tf_op jit(solution)/shard_map/all_gather | solution.py:441
  509.0 326.6 %all-gather.19.cloned.1.call-start = ((), (), s32[]{:S(2)}) async-start(), calls=%async_computation.16 | async-start | bytes 10485760 | tf_op jit(solution)/shard_map/all_gather | solution.py:440
  513.9 13.0 all-to-all-start.1
  517.3 407.8 %all-gather.23.cloned.1.call-start = ((), (), s32[]{:S(2)}) async-start(), calls=%async_computation.18 | async-start | bytes 10485760 | tf_op jit(solution)/shard_map/all_gather | solution.py:442
  527.0 131.7 %copy-start.12 = (s32[8,2,512]{2,1,0:T(2,128)}, s32[8,2,512]{2,1,0:T(2,128)S(1)}, u32[]{:S(2)}) copy-start(s32[8,2,512]{2,1,0:T(2,128)S(1)} %all-to-all-done.1) | copy-start | bytes 98308
  527.0 11.8 all-to-all-start.2
  530.3 672.6 %reduce-scatter.11.cloned.1.call-start = ((), (), s32[]{:S(2)}) async-start(), calls=%async_computation.21 | async-start | bytes 18874368 | tf_op jit(solution)/shard_map/reduce_scatter | solution.py:470
  1034.5 337.3 %reduce-scatter.9.cloned.1.call-start = ((), (), s32[]{:S(2)}) async-start(), calls=%async_computation.19 | async-start | bytes 18874368 | tf_op jit(solution)/shard_map/reduce_scatter | solution.py:480
  1087.2 115.7 %copy-start.16 = (f32[1,2048]{1,0:T(1,128)S(1)}, f32[1,2048]{1,0:T(1,128)}, u32[]{:S(2)}) copy-start(f32[1,2048]{1,0:T(1,128)} %copy-done.15) | copy-start | bytes 24580
  1087.2 115.7 %copy-start.20 = (f32[512]{0:T(512)S(1)}, f32[512]{0:T(512)}, u32[]{:S(2)}) copy-start(f32[512]{0:T(512)} %copy-done.19) | copy-start | bytes 6148
  1087.2 284.5 %copy-start.7 = (bf16[512,2048]{1,0:T(8,128)(2,1)S(1)}, bf16[512,2048]{1,0:T(8,128)(2,1)}, u32[]{:S(2)}) copy-start(bf16[512,2048]{1,0:T(8,128)(2,1)} %param.17) | copy-start | bytes 6291460
  1087.2 619.5 %reduce-scatter.17.cloned.1.call-start = ((), (), s32[]{:S(2)}) async-start(), calls=%async_computation.24 | async-start | bytes 10485760 | tf_op jit(solution)/shard_map/reduce_scatter | solution.py:549
  1398.3 53.4 %all-to-all-start.3 = ((bf16[8,512,256]{2,1,0:T(8,128)(2,1)}), bf16[8,512,256]{2,1,0:T(8,128)(2,1)}, u32[]{:S(2)}, u32[]{:S(2)}) async-start(bf16[8,512,256]{2,1,0:T(8,128)(2,1)} %bitcast.176), calls=%async_computation.5 | async-start | bytes 4194304 | tf_op jit(solution)/shard_map/all_to_all | solution.py:498
  1402.6 304.6 %reduce-scatter.15.cloned.1.call-start = ((), (), s32[]{:S(2)}) async-start(), calls=%async_computation.23 | async-start | bytes 3932160 | tf_op jit(solution)/shard_map/reduce_scatter | solution.py:538
  1625.0 132.6 %reduce-scatter.23.cloned.1.call-start = ((), (), s32[]{:S(2)}) async-start(), calls=%async_computation.28 | async-start | bytes 10485760 | tf_op jit(solution)/shard_map/reduce_scatter | solution.py:490
  1652.1 194.9 %reduce-scatter.21.cloned.1.call-start = ((), (), s32[]{:S(2)}) async-start(), calls=%async_computation.27 | async-start | bytes 10485760 | tf_op jit(solution)/shard_map/reduce_scatter | solution.py:490
  1679.4 257.8 %reduce-scatter.19.cloned.1.call-start = ((), (), s32[]{:S(2)}) async-start(), calls=%async_computation.26 | async-start | bytes 10485760 | tf_op jit(solution)/shard_map/reduce_scatter | solution.py:490
  1706.6 297.8 %all-reduce.3.cloned.1.call-start = ((), (), s32[]{:S(2)}) async-start(), calls=%async_computation.25 | async-start | bytes 4194304 | tf_op jit(solution)/shard_map/psum | solution.py:548
  1707.2 363.1 %all-gather.27.cloned.1.call-start = ((), (), s32[]{:S(2)}) async-start(), calls=%async_computation.29 | async-start | bytes 7077888 | tf_op jit(solution)/shard_map/all_gather | solution.py:539
  1707.8 531.7 %reduce-scatter.13.cloned.1.call-start = ((), (), s32[]{:S(2)}) async-start(), calls=%async_computation.22 | async-start | bytes 18874368 | tf_op jit(solution)/shard_map/reduce_scatter | solution.py:531
  2118.5 120.9 %copy-start.2 = (bf16[512,2048]{1,0:T(8,128)(2,1)S(1)}, bf16[512,2048]{1,0:T(8,128)(2,1)}, u32[]{:S(2)}) copy-start(bf16[512,2048]{1,0:T(8,128)(2,1)} %param.16) | copy-start | bytes 6291460
  2118.5 120.9 %copy-start.18 = (f32[1,2048]{1,0:T(1,128)S(1)}, f32[1,2048]{1,0:T(1,128)}, u32[]{:S(2)}) copy-start(f32[1,2048]{1,0:T(1,128)} %copy-done.17) | copy-start | bytes 24580
  2118.5 120.9 %copy-start.23 = (f32[512]{0:T(512)S(1)}, f32[512]{0:T(512)}, u32[]{:S(2)}) copy-start(f32[512]{0:T(512)} %copy-done.22) | copy-start | bytes 6148
  2131.3 111.0 %copy-start.21 = (f32[2048]{0:T(1024)S(1)}, f32[2048]{0:T(1024)}, u32[]{:S(2)}) copy-start(f32[2048]{0:T(1024)} %get-tuple-element.68) | copy-start | bytes 24580
  (30 other events, 546.7 us)
Sparse Core Ops, SparseCore 0:
  18.9 46.6 all-gather.12
  67.8 151.0 all-gather.10
  220.8 85.8 all-gather.14
  308.1 195.8 all-gather.24
  508.5 150.0 all-gather.16
  660.4 85.7 all-gather.20
  748.0 87.6 all-gather.18
  837.5 87.5 all-gather.22
  1034.6 168.2 reduce-scatter.10
  1205.1 166.6 reduce-scatter.8
  1387.7 84.7 reduce-scatter.16
  1625.1 42.6 reduce-scatter.14
  1671.2 86.3 reduce-scatter.22
  1760.6 86.3 reduce-scatter.20
  1850.8 86.3 reduce-scatter.18
  1939.4 64.9 all-reduce.2
  2005.9 64.3 all-gather.26
  2072.5 166.8 reduce-scatter.12

commit v2 on v1

--- a/solution.py
+++ b/solution.py
@@ -217,13 +217,12 @@
 
 
 def attention_forward(
-    raw, inv, gain_q, gain_k, seg_col, seg_row, place, first_tile, tile, block_len, scale
+    raw, inv, gain_q, gain_k, seg_col, seg_row, place, first_tile, tile, prompt_tiles, block_len, scale
 ):
     group, width = raw.shape[0], raw.shape[1] // 3
     head_dim = 128
     heads = width // head_dim
     tiles = group // tile
-    prompt_tiles = tiles // 2
 
     def part(which):
         return pl.BlockSpec((group, head_dim), lambda h, *_: (0, which * heads + h))
@@ -277,13 +276,12 @@
 
 
 def attention_backward(
-    queries, keys, values, lse, out, grad_out, seg_col, seg_row, place, first_tile, tile, block_len, scale
+    queries, keys, values, lse, out, grad_out, seg_col, seg_row, place, first_tile, tile, prompt_tiles, block_len, scale
 ):
     group, width = queries.shape
     head_dim = 128
     heads = width // head_dim
     tiles = group // tile
-    prompt_tiles = tiles // 2
 
     def whole(shape):
         return pl.BlockSpec(shape, lambda h, *_: (0,) * len(shape))
@@ -339,6 +337,412 @@
     return (jnp.where(holds & (slot < capacity), slot, -1), gate)
 
 
+def tied(array, *after):
+    return lax.optimization_barrier((array, *after))[0]
+
+
+def barrier(*arrays):
+    return lax.optimization_barrier(arrays)
+
+
+class Line:
+    def __init__(self):
+        peers = lax.axis_size("ctx")
+        self.chips = peers // 2
+        self.chip = lax.axis_index("ctx") // 2
+        self.up = [(i, i + 2) for i in range(peers - 2)]
+        self.down = [(i + 2, i) for i in range(peers - 2)]
+        self.pair = [(i, i ^ 1) for i in range(peers)]
+        steps = range(1, self.chips)
+        every = [d for s in steps for d in (s, -s)]
+        self.orders = [
+            sorted((d for d in every if 0 <= z + d < self.chips), key=lambda d: (abs(d), -d))
+            for z in range(self.chips)
+        ]
+
+    def step(self, from_below, from_above):
+        return (
+            lax.ppermute(from_below, "ctx", self.up),
+            lax.ppermute(from_above, "ctx", self.down),
+        )
+
+    def other(self, rows):
+        return lax.ppermute(rows, "ctx", self.pair)
+
+    def take(self, turn, arrived):
+        offsets = [self.orders[z][turn - 1] for z in range(self.chips)]
+        offset = jnp.array(offsets, jnp.int32)[self.chip]
+        kinds = sorted(set(offsets))
+        chosen = arrived[kinds[0]]
+        for kind in kinds[1:]:
+            chosen = jnp.where(offset == kind, arrived[kind], chosen)
+        return chosen, self.chip + offset
+
+
+def swap_partners(groups, shift):
+    return [(i, i ^ shift) for i in range(groups)]
+
+
+def swap_dp(part, shift):
+    return lax.ppermute(part, "dp", swap_partners(lax.axis_size("dp"), shift))
+
+
+def first_dp(part):
+    return [swap_dp(part, 1), swap_dp(part, 2)]
+
+
+def second_dp(pieces, axis):
+    half = pieces[0].shape[axis] // 2
+    return [
+        swap_dp(lax.slice_in_dim(pieces[0], 0, half, axis=axis), 2),
+        swap_dp(lax.slice_in_dim(pieces[1], half, 2 * half, axis=axis), 1),
+    ]
+
+
+def join_dp(part, pieces, axis):
+    mine = lax.axis_index("dp")
+    size = part.shape[axis]
+    half = size // 2
+
+    def both(shift):
+        return [(mine ^ shift) * size, (mine ^ shift) * size + half]
+
+    parts = [
+        (part, both(0)),
+        (pieces[0], both(1)),
+        (pieces[1], both(2)),
+        (pieces[2], both(3)[:1]),
+        (pieces[3], both(3)[1:]),
+    ]
+    return join(parts, axis, size * lax.axis_size("dp"), half)
+
+
+def pick_dp(term, shift, axis):
+    size = term.shape[axis] // lax.axis_size("dp")
+    return lax.dynamic_slice_in_dim(term, (lax.axis_index("dp") ^ shift) * size, size, axis)
+
+
+def scatter_one(term, shift, axis):
+    return swap_dp(pick_dp(term, shift, axis), shift)
+
+
+def total_dp(term, pieces, axis):
+    groups = lax.axis_size("dp")
+    size = term.shape[axis] // groups
+    total = lax.dynamic_slice_in_dim(term, lax.axis_index("dp") * size, size, axis).astype(f32)
+    for piece in pieces:
+        total = total + piece.astype(f32)
+    return total
+
+
+def sum_small(array, axes="ctx"):
+    return jnp.sum(lax.all_gather(array, axes, axis=0, tiled=False), axis=0)
+
+
+def project_kernel(places, own, other, weight, gain, *rest):
+    normed, raw, square = rest[-3:]
+
+    def work(rows_ref):
+        rows = rows_ref[...].astype(f32)
+        hat = rows * lax.rsqrt(jnp.mean(rows * rows, axis=1, keepdims=True) + epsilon)
+        low = (hat * gain[...]).astype(bf16)
+        normed[...] = low
+        product = jnp.dot(low, weight[...], preferred_element_type=f32)
+        raw[...] = product
+        third = product.shape[1] // 3
+        for which in range(2):
+            part = product[:, which * third : (which + 1) * third]
+            square[which : which + 1, :] = jnp.sum((part * part).T, axis=0, keepdims=True)
+
+    pl.when(pl.program_id(0) == 0)(lambda: work(own))
+    pl.when(pl.program_id(0) == 1)(lambda: work(other))
+
+
+def project(unit_index, own, other, weight, gain, peers, kept=()):
+    rows, width = own.shape
+    columns = weight.shape[1]
+
+    def fixed(shape):
+        return pl.BlockSpec(shape, lambda s, *_: (0,) * len(shape))
+
+    return pl.pallas_call(
+        project_kernel,
+        grid_spec=pltpu.PrefetchScalarGridSpec(
+            num_scalar_prefetch=1,
+            grid=(2,),
+            in_specs=[
+                fixed((rows, width)),
+                fixed((rows, width)),
+                fixed((width, columns)),
+                fixed((1, width)),
+            ]
+            + [pl.BlockSpec(memory_space=pl.ANY)] * len(kept),
+            out_specs=[
+                pl.BlockSpec((rows, width), lambda s, at: (at[s], 0)),
+                pl.BlockSpec((rows, columns), lambda s, at: (at[s], 0)),
+                pl.BlockSpec((None, 2, rows), lambda s, at: (at[s], 0, 0)),
+            ],
+        ),
+        out_shape=[
+            jax.ShapeDtypeStruct((peers * rows, width), bf16),
+            jax.ShapeDtypeStruct((peers * rows, columns), f32),
+            jax.ShapeDtypeStruct((peers, 2, rows), f32),
+        ],
+        input_output_aliases={5 + i: i for i in range(len(kept))},
+        compiler_params=pltpu.CompilerParams(vmem_limit_bytes=56 * 2**20),
+        name="project",
+    )(unit_index, own, other, weight, gain, *kept)
+
+
+def join_kernel(axis, blocks, block, at, *refs):
+    out = refs[-1]
+    turn = 0
+    for ref, count in zip(refs[:-1], blocks):
+        for index in range(count):
+            here = (slice(None),) * axis + (slice(index * block, (index + 1) * block),)
+
+            @pl.when(pl.program_id(0) == turn)
+            def copy(ref=ref, here=here):
+                out[...] = ref[here]
+
+            turn += 1
+
+
+def join(parts, axis, length, block):
+    shape = list(parts[0][0].shape)
+    shape[axis] = block
+    blocks = [len(starts) for _, starts in parts]
+    at = jnp.stack([start // block for _, starts in parts for start in starts]).astype(jnp.int32)
+    rank = len(shape)
+
+    def target(turn, at):
+        return tuple(at[turn] if index == axis else 0 for index in range(rank))
+
+    def fixed(part):
+        return pl.BlockSpec(
+            part.shape, lambda turn, at: (0,) * rank, pipeline_mode=pl.Buffered(1)
+        )
+
+    return pl.pallas_call(
+        functools.partial(join_kernel, axis, blocks, block),
+        grid_spec=pltpu.PrefetchScalarGridSpec(
+            num_scalar_prefetch=1,
+            grid=(sum(blocks),),
+            in_specs=[fixed(part) for part, _ in parts],
+            out_specs=pl.BlockSpec(tuple(shape), target),
+        ),
+        out_shape=jax.ShapeDtypeStruct(
+            tuple(length if index == axis else size for index, size in enumerate(shape)),
+            parts[0][0].dtype,
+        ),
+        compiler_params=pltpu.CompilerParams(vmem_limit_bytes=40 * 2**20),
+        name="join",
+    )(at, *[part for part, _ in parts])
+
+
+def lay_kernel(at, own, other, *rest):
+    out = rest[-1]
+
+    def work(source):
+        out[...] = source[...].astype(f32)
+
+    pl.when(pl.program_id(0) == 0)(lambda: work(own))
+    pl.when(pl.program_id(0) == 1)(lambda: work(other))
+
+
+def lay(at, own, other, out_shape, pieces, index, kept=()):
+    rows, columns = own.shape
+    block = (rows, columns // pieces)
+    return pl.pallas_call(
+        lay_kernel,
+        grid_spec=pltpu.PrefetchScalarGridSpec(
+            num_scalar_prefetch=1,
+            grid=(2, pieces),
+            in_specs=[pl.BlockSpec(block, lambda s, t, at: (0, t))] * 2
+            + [pl.BlockSpec(memory_space=pl.ANY)] * len(kept),
+            out_specs=pl.BlockSpec(block, lambda s, t, at: index(at[s], t)),
+        ),
+        out_shape=jax.ShapeDtypeStruct(out_shape, f32),
+        input_output_aliases={3: 0} if kept else {},
+        name="lay",
+    )(at, own, other, *kept)
+
+
+def expert_kernel(
+    unit, own, other, cots, slots, gates, columns, w_gate, w_up, w_down, *rest
+):
+    expert_in, grad_rows, hidden, grad_gate, grad_up, part, total, ready = rest[-8:]
+    expert, piece = pl.program_id(0), pl.program_id(1)
+    last_expert = expert == pl.num_programs(0) - 1
+    last_piece = piece == pl.num_programs(1) - 1
+    room, width = expert_in.shape[1:]
+    rows = own.shape[0]
+    core = unit[1]
+
+    @pl.when(piece == 0)
+    def bring():
+        at = lax.broadcasted_iota(jnp.int32, (room, rows), 0)
+        for s in range(2):
+            found = at == slots[s, pl.ds(expert, 1), :]
+            picks = jnp.where(found, 1.0, 0.0).astype(bf16)
+            slot_gate = jnp.sum(
+                jnp.where(found, gates[s, pl.ds(expert, 1), :], 0.0), axis=1, keepdims=True
+            )
+            grad_rows[s] = (
+                jnp.dot(picks, cots[s], preferred_element_type=f32) * slot_gate
+            ).astype(bf16)
+
+            @pl.when(core == s)
+            def from_own():
+                expert_in[s] = jnp.dot(picks, own[...], preferred_element_type=f32).astype(bf16)
+
+            @pl.when(core != s)
+            def from_other():
+                expert_in[s] = jnp.dot(picks, other[...], preferred_element_type=f32).astype(bf16)
+
+    rows_in = expert_in[...].reshape(2 * room, width)
+    gate_pre = jnp.dot(rows_in, w_gate[...], preferred_element_type=f32)
+    up_pre = jnp.dot(rows_in, w_up[...], preferred_element_type=f32)
+    grad_hidden = lax.dot_general(
+        grad_rows[...].reshape(2 * room, width), w_down[...], NT, preferred_element_type=f32
+    )
+    sigmoid = 1.0 / (1.0 + jnp.exp(-gate_pre))
+    silu = gate_pre * sigmoid
+    hidden[...] = (silu * up_pre).astype(bf16).reshape(hidden.shape)
+    gate_here = (grad_hidden * up_pre * sigmoid * (1.0 + gate_pre * (1.0 - sigmoid))).astype(bf16)
+    up_here = (grad_hidden * silu).astype(bf16)
+    grad_gate[...] = gate_here.reshape(grad_gate.shape)
+    grad_up[...] = up_here.reshape(grad_up.shape)
+
+    def back():
+        return lax.dot_general(gate_here, w_gate[...], NT, preferred_element_type=f32) + lax.dot_general(
+            up_here, w_up[...], NT, preferred_element_type=f32
+        )
+
+    @pl.when(piece == 0)
+    def first():
+        total[...] = back()
+
+    @pl.when(piece != 0)
+    def later():
+        total[...] += back()
+
+    @pl.when(last_piece)
+    def keep():
+        for s in range(2):
+            ready[s, pl.ds(pl.multiple_of(expert * room, 16), room), :] = total[
+                s * room : (s + 1) * room, :
+            ].astype(bf16)
+
+    @pl.when(last_piece & last_expert)
+    def send():
+        for s in range(2):
+            at = lax.broadcasted_iota(jnp.int32, (rows, ready.shape[1]), 1)
+            here = columns[s]
+            found = at == here[:, 0:1]
+            for e in range(1, here.shape[1]):
+                found = found | (at == here[:, e : e + 1])
+            part[s] = jnp.dot(
+                jnp.where(found, 1.0, 0.0).astype(bf16), ready[s], preferred_element_type=f32
+            ).astype(bf16)
+
+
+def expert_unit(unit, own, other, cot_all, slots, gates, columns, w_gate, w_up, w_down, room, kept=(), piece=256):
+    rows, width = own.shape
+    experts, _, inner = w_gate.shape
+    peers = cot_all.shape[0]
+    wide_shape = (peers, experts, room, width)
+    thin_shape = (peers, experts, room, inner)
+    anywhere = pl.BlockSpec(memory_space=pl.ANY)
+    once = pl.Buffered(1)
+
+    def fixed(shape):
+        return pl.BlockSpec(shape, lambda e, f, u: (0,) * len(shape), pipeline_mode=once)
+
+    def chip(shape):
+        return pl.BlockSpec((2, *shape), lambda e, f, u: (u[0], 0, 0), pipeline_mode=once)
+
+    wide = pl.BlockSpec((2, None, room, width), lambda e, f, u: (u[0], e, 0, 0))
+    thin = pl.BlockSpec((2, None, room, piece), lambda e, f, u: (u[0], e, 0, f))
+    return pl.pallas_call(
+        expert_kernel,
+        grid_spec=pltpu.PrefetchScalarGridSpec(
+            num_scalar_prefetch=1,
+            grid=(experts, inner // piece),
+            in_specs=[
+                fixed((rows, width)), fixed((rows, width)), chip((rows, width)),
+                chip((experts, rows)), chip((experts, rows)), chip((rows, experts)),
+                pl.BlockSpec((None, width, piece), lambda e, f, u: (e, 0, f)),
+                pl.BlockSpec((None, width, piece), lambda e, f, u: (e, 0, f)),
+                pl.BlockSpec((None, piece, width), lambda e, f, u: (e, f, 0)),
+            ] + [anywhere] * len(kept),
+            out_specs=[wide, wide, thin, thin, thin,
+                pl.BlockSpec((2, rows, width), lambda e, f, u: (u[0], 0, 0))],
+            scratch_shapes=[
+                pltpu.VMEM((2 * room, width), f32),
+                pltpu.VMEM((2, experts * room, width), bf16),
+            ],
+        ),
+        out_shape=[
+            jax.ShapeDtypeStruct(shape, bf16)
+            for shape in [wide_shape] * 2 + [thin_shape] * 3 + [cot_all.shape]
+        ],
+        input_output_aliases={10 + i: i for i in range(len(kept))},
+        compiler_params=pltpu.CompilerParams(vmem_limit_bytes=60 * 2**20),
+        name="expert_unit",
+    )(unit, own, other, cot_all, slots, gates, columns, w_gate, w_up, w_down, *kept)
+
+
+def out_kernel(hidden, w_down, slots, gates, columns, part, ready):
+    expert = pl.program_id(1)
+    room = hidden.shape[1]
+    rows = slots.shape[2]
+    at = lax.broadcasted_iota(jnp.int32, (room, rows), 0)
+    product = jnp.dot(
+        hidden[...].reshape(2 * room, hidden.shape[2]), w_down[...], preferred_element_type=f32
+    )
+    for s in range(2):
+        found = at == slots[s, pl.ds(expert, 1), :]
+        slot_gate = jnp.sum(jnp.where(found, gates[s, pl.ds(expert, 1), :], 0.0), axis=1, keepdims=True)
+        ready[s, pl.ds(pl.multiple_of(expert * room, 16), room), :] = (
+            product[s * room : (s + 1) * room] * slot_gate
+        ).astype(bf16)
+
+    @pl.when(expert == pl.num_programs(1) - 1)
+    def send():
+        for s in range(2):
+            at = lax.broadcasted_iota(jnp.int32, (rows, ready.shape[1]), 1)
+            here = columns[s]
+            found = at == here[:, 0:1]
+            for e in range(1, here.shape[1]):
+                found = found | (at == here[:, e : e + 1])
+            part[s] = jnp.dot(
+                jnp.where(found, 1.0, 0.0).astype(bf16), ready[s], preferred_element_type=f32
+            ).astype(bf16)
+
+
+def expert_out(hidden, w_down, slots, gates, columns):
+    peers, experts, room, inner = hidden.shape
+    width = w_down.shape[2]
+    rows = slots.shape[2]
+    return pl.pallas_call(
+        out_kernel,
+        grid=(peers // 2, experts),
+        in_specs=[
+            pl.BlockSpec((2, None, room, inner), lambda c, e: (c, e, 0, 0)),
+            pl.BlockSpec((None, inner, width), lambda c, e: (e, 0, 0)),
+            pl.BlockSpec((2, experts, rows), lambda c, e: (c, 0, 0)),
+            pl.BlockSpec((2, experts, rows), lambda c, e: (c, 0, 0)),
+            pl.BlockSpec((2, rows, experts), lambda c, e: (c, 0, 0)),
+        ],
+        out_specs=pl.BlockSpec((2, rows, width), lambda c, e: (c, 0, 0)),
+        out_shape=jax.ShapeDtypeStruct((peers, rows, width), bf16),
+        scratch_shapes=[pltpu.VMEM((2, experts * room, width), bf16)],
+        compiler_params=pltpu.CompilerParams(vmem_limit_bytes=60 * 2**20),
+        name="expert_out",
+    )(hidden, w_down, slots, gates, columns)
+
+
 def on_device(
     tokens,
     cotangent,
@@ -363,6 +767,7 @@
     peers = lax.axis_size("ctx")
     groups = lax.axis_size("dp")
     me = lax.axis_index("ctx")
+    core = me % 2
     my_dp = lax.axis_index("dp")
     group_rows = count_rows * peers
     rep = max(1, peers // HEADS)
@@ -371,13 +776,10 @@
     first_head = (me // rep) * own_heads
     block_len = count_rows // BLK_DEV
     tile = 512
-
-    gain_all = lax.all_gather(
-        jnp.stack([attn_gain, query_gain, key_gain, moe_gain]), "dp", axis=1, tiled=True
-    ).astype(f32)
-    gain_attn, gain_moe = gain_all[0:1], gain_all[3:4]
-    gain_own = lax.dynamic_slice_in_dim(gain_all, first_head * head_dim, own_width, 1)
-    gain_q, gain_k = gain_own[1:2], gain_own[2:3]
+    line = Line()
+    turns = range(1, line.chips)
+
+    full_gate = lax.all_gather(w_gate, "dp", axis=1, tiled=True)
 
     assign = block_assign[0]
     count_blocks = assign.shape[0]
@@ -386,6 +788,7 @@
     ).astype(jnp.int32)
     cont = segment_ids[0]
     prompt_len = group_rows - cont.shape[0]
+    prompt_tiles = prompt_len // tile
     seg_logical = jnp.concatenate([jnp.full((prompt_len,), -1, jnp.int32), cont])
     tiles = group_rows // tile
     tile_seg = seg_logical.reshape(tiles, tile)[:, 0]
@@ -397,98 +800,182 @@
     seg_col = seg_logical[:, None]
     seg_row = seg_logical.reshape(tiles, tile)
 
+    local_experts = w_gate.shape[0]
+    count_experts = local_experts * peers
+    capacity = 9 * count_rows * TOP // (8 * count_experts)
+    room = (capacity + 15) // 16 * 16
+    slot, gate = slot_table(expert_ids, slot_order, gates, count_experts, capacity)
+    table = jnp.stack(
+        [
+            slot.reshape(peers, local_experts, count_rows).astype(f32),
+            gate.reshape(peers, local_experts, count_rows),
+        ],
+        axis=1,
+    )
+
     inputs = tokens.astype(f32)
-    inv_in = rms_scale(inputs)
-    hat_in = inputs * inv_in
-    normed = (hat_in * gain_attn).astype(bf16)
-    normed_all = lax.all_gather(normed, "ctx", axis=0, tiled=True)
-    w_own = lax.dynamic_slice_in_dim(
+    below, above = line.step(tokens, tokens)
+    other = line.other(tokens)
+    w_part = lax.dynamic_slice_in_dim(
         wqkv.reshape(wqkv.shape[0], 3, HEADS, head_dim), first_head, own_heads, 2
     ).reshape(wqkv.shape[0], 3 * own_width)
-    w_own = lax.all_gather(w_own, "dp", axis=0, tiled=True)
-    raw = jnp.dot(normed_all, w_own, preferred_element_type=f32)
-    square = raw[:, : 2 * own_width].reshape(group_rows, 2, own_width)
-    square = lax.psum(jnp.sum(square * square, axis=2).T, "ctx") * (1.0 / rep)
+    w_pieces = first_dp(w_part)
+    w_pieces = w_pieces + second_dp(w_pieces, 0)
+    gain_part = jnp.stack([attn_gain, query_gain, key_gain, moe_gain])
+    gain_all = jnp.zeros((4, width), bf16)
+    for shift in range(groups):
+        piece = swap_dp(gain_part, shift) if shift else gain_part
+        gain_all = lax.dynamic_update_slice_in_dim(
+            gain_all, piece, (my_dp ^ shift) * gain_part.shape[1], 1
+        )
+    gain_all = gain_all.astype(f32)
+    below, above, other, gain_all, table, wo, *w_pieces = barrier(
+        below, above, other, gain_all, table, wo, *w_pieces
+    )
+    w_own = join_dp(w_part, w_pieces, 0)
+    gain_attn, gain_moe = gain_all[0:1], gain_all[3:4]
+    gain_own = lax.dynamic_slice_in_dim(gain_all, first_head * head_dim, own_width, 1)
+    gain_q, gain_k = gain_own[1:2], gain_own[2:3]
+
+    half_rows = wo.shape[0] // 2
+    arrived = {-1: below, 1: above}
+    own, chip = tokens, line.chip
+    kept = ()
+    for turn in turns:
+        if turn + 1 < line.chips:
+            below, above = line.step(below, above)
+            arrived[-turn - 1], arrived[turn + 1] = below, above
+        next_own, next_chip = line.take(turn, arrived)
+        next_other = line.other(next_own)
+        at = jnp.stack([2 * chip + core, 2 * chip + 1 - core]).astype(jnp.int32)
+        kept = project(at, own, other, w_own, gain_attn, peers, kept)
+        travel = []
+        if turn == 1:
+            wo_half = lax.dynamic_slice_in_dim(wo, core * half_rows, half_rows, 0)
+            wo_pieces = first_dp(wo_half)
+            travel = wo_pieces + second_dp(wo_pieces, 0)
+        if turn == 2:
+            wo_pieces = [wo_half, *travelled[:2], jnp.concatenate(travelled[2:], axis=0)]
+            wo_mine = jnp.concatenate(wo_pieces, axis=0)
+            down_pieces = first_dp(w_down)
+            travel = [line.other(wo_mine), wo_mine, full_gate] + down_pieces
+            table = lax.all_to_all(table, "ctx", split_axis=0, concat_axis=0, tiled=True)
+            travel.append(table)
+        own, other, chip = next_own, next_other, next_chip
+        square = kept[2]
+        below, above, own, other, square, w_down, *travelled = barrier(
+            below, above, own, other, square, w_down, *travel
+        )
+        if turn == 2:
+            wo_theirs, wo_mine, full_gate, down_one, down_two, table = travelled
+        kept = (kept[0], kept[1], square)
+        if turn + 1 < line.chips:
+            arrived[-turn - 1], arrived[turn + 1] = below, above
+    cotangent_now, other = barrier(cotangent, other)
+    cot_all = lax.all_gather(cotangent_now, "ctx", axis=0, tiled=True).reshape(
+        peers, count_rows, width
+    )
+    down_pieces = [down_one, down_two] + second_dp([down_one, down_two], 1)
+    at = jnp.stack([2 * chip + core, 2 * chip + 1 - core]).astype(jnp.int32)
+    normed_all, raw, square = project(at, own, other, w_own, gain_attn, peers, kept)
+    square = sum_small(square.transpose(1, 0, 2).reshape(2, group_rows)) * (1.0 / rep)
     inv_qk = lax.rsqrt(square / width + epsilon).T
+    slot = table[:, 0].astype(jnp.int32)
+    gate_rows = table[:, 1]
+    offsets = (jnp.arange(local_experts, dtype=jnp.int32) * room)[None, :, None]
+    columns = jnp.where(slot >= 0, slot + offsets, -1).transpose(0, 2, 1)
+
+    inv_qk, w_up, columns, *down_pieces = barrier(inv_qk, w_up, columns, *down_pieces)
+    up_pieces = first_dp(w_up)
     attended, lse, queries, keys, values = attention_forward(
-        raw, inv_qk, gain_q, gain_k, seg_col, seg_row, place, first_tile, tile, block_len, scale
-    )
+        raw,
+        inv_qk,
+        gain_q,
+        gain_k,
+        seg_col,
+        seg_row,
+        place,
+        first_tile,
+        tile,
+        prompt_tiles,
+        block_len,
+        scale,
+    )
+    attended, *up_pieces = barrier(attended, *up_pieces)
+    up_pieces = up_pieces + second_dp(up_pieces, 1)
     attn_low = lax.all_to_all(
         attended.reshape(peers, count_rows, own_width), "ctx", split_axis=0, concat_axis=0, tiled=True
     )[::rep]
+    full_down = join_dp(w_down, down_pieces, 1)
+    starts = [(my_dp ^ shift) * wo.shape[0] for shift in range(groups)]
+    full_wo = join(
+        [
+            (wo_mine, [start + core * half_rows for start in starts]),
+            (wo_theirs, [start + (1 - core) * half_rows for start in starts]),
+        ],
+        0,
+        width,
+        half_rows,
+    )
+    attn_low, full_wo, full_down, *up_pieces = barrier(attn_low, full_wo, full_down, *up_pieces)
     attn_low = attn_low.transpose(1, 0, 2).reshape(count_rows, width)
-    full_wo = lax.all_gather(wo, "dp", axis=0, tiled=True)
     state = inputs + jnp.dot(attn_low, full_wo, preferred_element_type=f32)
     inv_state = rms_scale(state)
     hat_state = state * inv_state
     normed_moe = (hat_state * gain_moe).astype(bf16)
-
-    local_experts = w_gate.shape[0]
-    count_experts = local_experts * peers
-    capacity = 9 * count_rows * TOP // (8 * count_experts)
-    slot, gate = slot_table(expert_ids, slot_order, gates, count_experts, capacity)
-    slot = lax.all_to_all(
-        slot.reshape(peers, local_experts, count_rows), "ctx", split_axis=0, concat_axis=0, tiled=True
-    )
-    gate = lax.all_to_all(
-        gate.reshape(peers, local_experts, count_rows), "ctx", split_axis=0, concat_axis=0, tiled=True
-    )
-    picks = slot[:, :, None, :] == jnp.arange(capacity, dtype=jnp.int32)[:, None]
-    slot_gate = jnp.sum(jnp.where(picks, gate[:, :, None, :], 0.0), axis=3)[..., None]
-    picks = picks.astype(bf16)
-
-    full_gate = lax.all_gather(w_gate, "dp", axis=1, tiled=True)
-    full_up = lax.all_gather(w_up, "dp", axis=1, tiled=True)
-    full_down = lax.all_gather(w_down, "dp", axis=1, tiled=True)
-
-    cot_all = lax.all_gather(cotangent, "ctx", axis=0, tiled=True).reshape(peers, count_rows, width)
-    grad_rows = (
-        jnp.einsum("sncr,srd->sncd", picks, cot_all, preferred_element_type=f32) * slot_gate
-    ).astype(bf16)
-    grad_hidden = jnp.einsum("sncd,nfd->sncf", grad_rows, full_down, preferred_element_type=f32)
-
-    moe_all = lax.all_gather(normed_moe, "ctx", axis=0, tiled=True).reshape(
-        peers, count_rows, width
-    )
-    expert_in = jnp.einsum("sncr,srd->sncd", picks, moe_all, preferred_element_type=f32).astype(
-        bf16
-    )
-    gate_pre = jnp.einsum("sncd,ndf->sncf", expert_in, full_gate, preferred_element_type=f32)
-    up_pre = jnp.einsum("sncd,ndf->sncf", expert_in, full_up, preferred_element_type=f32)
-    sigmoid = jax.nn.sigmoid(gate_pre)
-    silu = gate_pre * sigmoid
-    hidden = (silu * up_pre).astype(bf16)
-    grad_gate_pre = (
-        grad_hidden * up_pre * sigmoid * (1.0 + gate_pre * (1.0 - sigmoid))
-    ).astype(bf16)
-    grad_up_pre = (grad_hidden * silu).astype(bf16)
-    grad_in = (
-        jnp.einsum("sncf,ndf->sncd", grad_gate_pre, full_gate, preferred_element_type=f32)
-        + jnp.einsum("sncf,ndf->sncd", grad_up_pre, full_up, preferred_element_type=f32)
-    ).astype(bf16)
-    part_moe = jnp.einsum("sncr,sncd->srd", picks, grad_in, preferred_element_type=f32).astype(bf16)
+    full_up = join_dp(w_up, up_pieces, 1)
+
+    normed_moe, full_up, cot_all = barrier(normed_moe, full_up, cot_all)
+    below, above = normed_moe, normed_moe
+    own, chip = normed_moe, line.chip
+    arrived = {}
+    kept = ()
+    for turn in range(line.chips):
+        if turn + 1 < line.chips:
+            below, above = line.step(below, above)
+            arrived[-turn - 1], arrived[turn + 1] = below, above
+        if turn > 0:
+            own, chip = line.take(turn, arrived)
+        other = line.other(own)
+        kept = expert_unit(
+            jnp.stack([chip, core]).astype(jnp.int32),
+            own,
+            other,
+            cot_all,
+            slot,
+            gate_rows,
+            columns,
+            full_gate,
+            full_up,
+            full_down,
+            room,
+            kept,
+        )
+        if turn + 1 < line.chips:
+            below, above, *kept = barrier(below, above, *kept)
+            arrived[-turn - 1], arrived[turn + 1] = below, above
+    expert_in, grad_rows, hidden, grad_gate_pre, grad_up_pre, part_moe = kept
     grad_normed_moe = lax.psum_scatter(
         part_moe.reshape(group_rows, width), "ctx", scatter_dimension=0, tiled=True
-    ).astype(f32)
-
-    out_rows = (
-        jnp.einsum("sncf,nfd->sncd", hidden, full_down, preferred_element_type=f32) * slot_gate
-    ).astype(bf16)
-    part_mixed = jnp.einsum("sncr,sncd->srd", picks, out_rows, preferred_element_type=f32).astype(
-        bf16
+    )
+
+    part_mixed = expert_out(hidden, full_down, slot, gate_rows, columns)
+    grad_down = jnp.einsum("sncf,sncd->nfd", hidden, grad_rows, preferred_element_type=f32)
+    grad_down = grad_down.astype(bf16)
+    part_mixed, grad_down, expert_in = barrier(part_mixed, grad_down, expert_in)
+    down_pieces = [scatter_one(grad_down, shift, 1) for shift in (1, 2, 3)]
+    grad_gate = jnp.einsum("sncd,sncf->ndf", expert_in, grad_gate_pre, preferred_element_type=f32)
+    grad_up = jnp.einsum("sncd,sncf->ndf", expert_in, grad_up_pre, preferred_element_type=f32)
+    grad_gate, grad_up = grad_gate.astype(bf16), grad_up.astype(bf16)
+    grad_normed_moe, part_mixed, grad_gate, grad_up, *down_pieces = barrier(
+        grad_normed_moe, part_mixed, grad_gate, grad_up, *down_pieces
     )
     mixed = lax.psum_scatter(
         part_mixed.reshape(group_rows, width), "ctx", scatter_dimension=0, tiled=True
-    ).astype(f32)
-    output = (state + mixed).astype(bf16)
-
-    grad_down = jnp.einsum("sncf,sncd->nfd", hidden, grad_rows, preferred_element_type=f32)
-    grad_gate = jnp.einsum("sncd,sncf->ndf", expert_in, grad_gate_pre, preferred_element_type=f32)
-    grad_up = jnp.einsum("sncd,sncf->ndf", expert_in, grad_up_pre, preferred_element_type=f32)
-
-    def expert_sum(term):
-        return lax.psum_scatter(term.astype(bf16), "dp", scatter_dimension=1, tiled=True).astype(f32)
-
+    )
+
+    gate_pieces = [scatter_one(grad_gate, shift, 1) for shift in (1, 2)]
+    grad_normed_moe = grad_normed_moe.astype(f32)
     moe_gain_term = jnp.sum(grad_normed_moe * hat_state, axis=0)
     grad_state = cotangent.astype(f32) + rms_back(grad_normed_moe * gain_moe, hat_state, inv_state)
     grad_branch = grad_state.astype(bf16)
@@ -498,6 +985,17 @@
     grad_attended = lax.all_to_all(
         grad_attn, "ctx", split_axis=0, concat_axis=0, tiled=True
     ).reshape(group_rows, own_width)
+    part_out = lax.dot_general(attn_low, grad_branch, TN, preferred_element_type=f32).astype(bf16)
+    part_out = part_out.reshape(groups, 2, half_rows, width)
+    out_theirs = line.other(lax.dynamic_index_in_dim(part_out, 1 - core, 1, keepdims=False))
+    part_out = lax.dynamic_index_in_dim(part_out, core, 1, keepdims=False).astype(f32)
+    part_out = (part_out + out_theirs.astype(f32)).astype(bf16)
+    down_sum = total_dp(grad_down, down_pieces, 1)
+    grad_attended, part_out, down_sum, *gate_pieces = barrier(
+        grad_attended, part_out, down_sum, *gate_pieces
+    )
+    gate_pieces.append(scatter_one(grad_gate, 3, 1))
+    out_pieces = [scatter_one(part_out, shift, 0) for shift in (1, 2)]
     grad_q, grad_k, grad_v = attention_backward(
         queries,
         keys,
@@ -510,9 +1008,13 @@
         place,
         first_tile,
         tile,
+        prompt_tiles,
         block_len,
         scale,
     )
+    grad_q, gate_last, *out_pieces = barrier(grad_q, gate_pieces[2], *out_pieces)
+    gate_pieces[2] = gate_last
+    out_pieces.append(scatter_one(part_out, 3, 0))
     hat_q = raw[:, :own_width] * inv_qk[:, 0:1]
     hat_k = raw[:, own_width : 2 * own_width] * inv_qk[:, 1:2]
     query_gain_term = jnp.sum(grad_q * hat_q, axis=0)
@@ -523,41 +1025,91 @@
             jnp.sum(grad_k * gain_k * hat_k, axis=1),
         ]
     )
-    means = (lax.psum(means, "ctx") * (1.0 / (rep * width))).T
+    means = (sum_small(means) * (1.0 / (rep * width))).T
     grad_raw_q = inv_qk[:, 0:1] * (grad_q * gain_q - hat_q * means[:, 0:1])
     grad_raw_k = inv_qk[:, 1:2] * (grad_k * gain_k - hat_k * means[:, 1:2])
     grad_qkv = jnp.concatenate([grad_raw_q.astype(bf16), grad_raw_k.astype(bf16), grad_v], axis=1)
     part_normed = lax.dot_general(grad_qkv, w_own, NT, preferred_element_type=f32) * (1.0 / rep)
-    grad_normed = lax.psum_scatter(
-        part_normed.astype(bf16), "ctx", scatter_dimension=0, tiled=True
-    ).astype(f32)
-    attn_gain_term = jnp.sum(grad_normed * hat_in, axis=0)
-    input_grad = (grad_state + rms_back(grad_normed * gain_attn, hat_in, inv_in)).astype(bf16)
-
+    part_normed = part_normed.astype(bf16)
+    part_normed, grad_qkv, mixed, *out_pieces = barrier(part_normed, grad_qkv, mixed, *out_pieces)
+    grad_normed = lax.psum_scatter(part_normed, "ctx", scatter_dimension=0, tiled=True)
+
+    out_sum = total_dp(part_out, out_pieces, 0).astype(bf16).reshape(half_rows, width)
+    out_share = half_rows // (peers // 2)
+    out_sum = lax.all_to_all(
+        out_sum.reshape(peers // 2, out_share, width),
+        "ctx",
+        split_axis=0,
+        concat_axis=0,
+        tiled=True,
+        axis_index_groups=[[2 * z + c for z in range(peers // 2)] for c in range(2)],
+    )
     part_qkv = lax.dot_general(normed_all, grad_qkv, TN, preferred_element_type=f32).astype(bf16)
-    part_qkv = lax.psum_scatter(part_qkv, "dp", scatter_dimension=0, tiled=True)
-    qkv_total = lax.all_gather(part_qkv, "ctx", axis=0, tiled=False)[::rep]
-    rows_dp = part_qkv.shape[0]
-    qkv_total = (
-        qkv_total.reshape(peers // rep, rows_dp, 3, own_width)
-        .transpose(1, 2, 0, 3)
-        .reshape(rows_dp, 3 * width)
-        .astype(f32)
-    )
-    part_out = lax.dot_general(attn_low, grad_branch, TN, preferred_element_type=f32).astype(bf16)
-    out_total = lax.psum(
-        lax.psum_scatter(part_out, "dp", scatter_dimension=0, tiled=True), "ctx"
-    ).astype(f32)
-
+    qkv_pieces = [scatter_one(part_qkv, shift, 0) for shift in (1, 2, 3)]
+    gate_sum = total_dp(grad_gate, gate_pieces, 1)
     own_terms = jnp.stack([query_gain_term, key_gain_term]) * (1.0 / rep)
     spread = lax.dynamic_update_slice_in_dim(
         jnp.zeros((2, width), f32), own_terms, first_head * head_dim, 1
     )
-    gain_terms = jnp.concatenate([attn_gain_term[None], spread, moe_gain_term[None]], axis=0)
-    gain_terms = lax.psum(gain_terms, ("dp", "ctx"))
-    gain_terms = lax.dynamic_slice_in_dim(
-        gain_terms, my_dp * (width // groups), width // groups, 1
-    )
+    gain_terms = jnp.concatenate([spread, moe_gain_term[None]], axis=0)
+    grad_up, gate_sum, gain_terms, out_sum, *qkv_pieces = barrier(
+        grad_up, gate_sum, gain_terms, out_sum, *qkv_pieces
+    )
+    up_pieces = [scatter_one(grad_up, shift, 1) for shift in (1, 2, 3)]
+    qkv_sum = total_dp(part_qkv, qkv_pieces, 0).astype(bf16)
+    out_sum = jnp.sum(out_sum.astype(f32), axis=0).astype(bf16)
+    rows_dp = qkv_sum.shape[0]
+    weights = jnp.concatenate([qkv_sum.reshape(out_share, -1), out_sum], axis=1)
+    qkv_columns = weights.shape[1] - width
+    below, above = weights, weights
+    own, chip = weights, line.chip
+    arrived = {}
+    qkv_kept, out_kept = (), ()
+    for turn in range(line.chips):
+        if turn + 1 < line.chips:
+            below, above = line.step(below, above)
+            arrived[-turn - 1], arrived[turn + 1] = below, above
+        if turn > 0:
+            own, chip = line.take(turn, arrived)
+        other = line.other(own)
+        at = jnp.stack([2 * chip + core, 2 * chip + 1 - core]).astype(jnp.int32)
+        qkv_kept = [
+            lay(
+                at // rep,
+                own[:, :qkv_columns].reshape(rows_dp, 3 * own_width),
+                other[:, :qkv_columns].reshape(rows_dp, 3 * own_width),
+                (rows_dp, 3 * width),
+                3,
+                lambda p, t: (0, t * (peers // rep) + p),
+                qkv_kept,
+            )
+        ]
+        at = jnp.stack([core * line.chips + chip, (1 - core) * line.chips + chip]).astype(jnp.int32)
+        out_kept = [
+            lay(
+                at,
+                own[:, qkv_columns:],
+                other[:, qkv_columns:],
+                (rows_dp, width),
+                1,
+                lambda p, t: (p, 0),
+                out_kept,
+            )
+        ]
+    qkv_total, out_total = qkv_kept[0], out_kept[0]
+    up_sum = total_dp(grad_up, up_pieces, 1)
+    output = (state + mixed.astype(f32)).astype(bf16)
+    out_total, qkv_total, up_sum, output, grad_normed = barrier(
+        out_total, qkv_total, up_sum, output, grad_normed
+    )
+
+    grad_normed = grad_normed.astype(f32)
+    inv_in = rms_scale(inputs)
+    hat_in = inputs * inv_in
+    attn_gain_term = jnp.sum(grad_normed * hat_in, axis=0)
+    input_grad = (grad_state + rms_back(grad_normed * gain_attn, hat_in, inv_in)).astype(bf16)
+    gain_terms = sum_small(jnp.concatenate([attn_gain_term[None], gain_terms], axis=0))
+    gain_terms = total_dp(gain_terms, [scatter_one(gain_terms, shift, 1) for shift in (1, 2, 3)], 1)
     return (
         output,
         input_grad,
@@ -567,9 +1119,9 @@
         gain_terms[1],
         gain_terms[2],
         gain_terms[3],
-        expert_sum(grad_gate),
-        expert_sum(grad_up),
-        expert_sum(grad_down),
+        gate_sum,
+        up_sum,
+        down_sum,
     )
 
 

time: 2300 us -> 1540 us (0.67)
  waiting for transfers between devices: 1340 us -> 469 us
  Pallas kernels: 134 us -> 480 us
  matrix products: 420 us -> 140 us
  blocking collectives: 174 us -> 47.8 us
  starting transfers between devices: 28.8 us -> 120 us
  other arithmetic: 72.5 us -> 118 us
  local copies, waits for them, and re-layouts: 108 us -> 132 us
    all_gather x8 -> x1, waiting for transfers between devices: 475 us -> 0.01 us  [on_device(): lax.all_gather(cotangent_now, 'ctx', axis=0, tiled=True)]
    ppermute x0 -> x69, waiting for transfers between devices: none -> 372 us  [the longest x37 246 us: swap_dp(): return lax.ppermute(part, 'dp', swap_partners(lax.axis_size('dp'), shift))]
    pallas_call x0 -> x21, Pallas kernels: none -> 346 us  [the longest x4 197 us: expert_unit(): pl.pallas_call(expert_kernel, grid_spec=pltpu.PrefetchScalarGridSpec(num_...]
    reduce_scatter x6 -> x1, waiting for transfers between devices: 309 us -> 0.01 us  [on_device(): lax.psum_scatter(part_normed, 'ctx', scatter_dimension=0, tiled=True)]
    dot_general x10 -> x0, matrix products: 275 us -> none  [the longest x1 42.1 us: on_device(): jnp.einsum('sncr,sncd->srd', picks, grad_in, preferred_element_type=f32)]
    reduce_scatter x1, waiting for transfers between devices: 164 us -> 0.02 us  [on_device(): lax.psum_scatter(part_mixed.reshape(group_rows, width), 'ctx', scatter_di...]
    psum x3 -> x0, blocking collectives: 164 us -> none  [the longest x1 63.1 us: on_device(): square = lax.psum(jnp.sum(square * square, axis=2).T, 'ctx') * (1.0 / rep)]
    reduce_scatter x1, waiting for transfers between devices: 116 us -> 0.01 us  [on_device(): lax.psum_scatter(part_moe.reshape(group_rows, width), 'ctx', scatter_dime...]
  transfers between devices with their start and end apart: 22 -> 78, of which waited for: 18 -> 27; matrix products, arithmetic and copies ran while one was open for 20% -> 24% of each run, Pallas kernels for 6% -> 28%
where the time goes in v2:
time: 1540 us; the launch traced here: 1530 us
  Pallas kernels  480 us (31%)
  waiting for transfers between devices  469 us (30%)
  matrix products  140 us (9%)
  local copies, waits for them, and re-layouts  132 us (9%)
  starting transfers between devices  120 us (8%)
  other arithmetic  118 us (8%)
  blocking collectives  47.8 us (3%)
  between operations  21.2 us (1%)
    ppermute x37, waiting for transfers between devices, swap_dp(): return lax.ppermute(part, 'dp', swap_partners(lax.axis_size('dp'), shift))  246 us
    pallas_call x4, Pallas kernels, expert_unit(): pl.pallas_call(expert_kernel, grid_spec=pltpu.PrefetchScalarGridSpec(num_...  197 us
    ppermute x9, waiting for transfers between devices, step(): lax.ppermute(from_below, 'ctx', self.up)  118 us
    pallas_call x1, Pallas kernels, attention_backward(): pl.pallas_call(functools.partial(backward_kernel, tile, prompt_tiles, blo...  70.4 us
    pallas_call x1, Pallas kernels, attention_forward(): pl.pallas_call(functools.partial(forward_kernel, tile, prompt_tiles, bloc...  63.8 us
    all_gather x3, blocking collectives, sum_small(): return jnp.sum(lax.all_gather(array, axes, axis=0, tiled=False), axis=0)  47.8 us
    ppermute x9, starting transfers between devices, step(): lax.ppermute(from_below, 'ctx', self.up)  45.4 us
    pallas_call x1, Pallas kernels, expert_out(): pl.pallas_call(out_kernel, grid=(peers // 2, experts), in_specs=[pl.Block...  45.1 us
  transfers between devices with their start and end apart: 78, of which 27 were waited for; matrix products, arithmetic and copies ran while one was open for 24% of the time, Pallas kernels for 28%

profile of v2, /device:TPU:0, one launch (start us, length us, event | category | flops | bytes accessed | tf_op | source)
XLA Modules:
  0.0 1529.3 jit_solution(2444514771084108215)
XLA Ops:
  39.7 24.5 %collective-permute-done.7.refs_2_ = bf16[512,768]{1,0:T(8,128)(2,1)S(1)} collective-permute-done((bf16[512,768]{1,0:T(8,128)(2,1)S(1)}, bf16[512,768]{1,0:T(8,128)(2,1)S(1)}, u32[]{:S(2)}, u32[]{:S(2)}) %collective-permute-start.7) | collective-permute-done | bytes 786464 | tf_op jit(solution)/shard_map/ppermute | solution.py:387
  76.6 10.9 collective-permute-done.9.refs_4_
  107.0 36.9 %collective-permute-done.14 = bf16[256,2048]{1,0:T(8,128)(2,1)} collective-permute-done((bf16[256,2048]{1,0:T(8,128)(2,1)}, bf16[256,2048]{1,0:T(8,128)(2,1)}, u32[]{:S(2)}, u32[]{:S(2)}) %collective-permute-start.14) | collective-permute-done | bytes 1048608 | tf_op jit(solution)/shard_map/ppermute | solution.py:387
  202.4 25.4 %all-to-all-done = f32[8,2,2,512]{3,2,1,0:T(2,128)S(1)} async-done(((f32[8,2,2,512]{3,2,1,0:T(2,128)}), f32[8,2,2,512]{3,2,1,0:T(2,128)S(1)}, u32[]{:S(2)}, u32[]{:S(2)}) %all-to-all-start) | async-done | bytes 65568 | tf_op jit(solution)/shard_map/all_to_all | solution.py:862
  231.2 10.7 project.6
  256.0 11.1 project.7
  267.1 17.8 %all_gather.22 = f32[8,2,4096]{2,1,0:T(2,128)S(1)} all-gather(f32[1,2,4096]{2,1,0:T(2,128)} %bitcast.152), channel_id=1, replica_groups=mesh['dp'=4,'ctx'=8] {'ctx'}, dimensions={0}, use_global_device_ids=true | all-gather | bytes 294912 | tf_op jit(solution)/shard_map/all_gather | solution.py:439
  291.5 63.8 %attention_forward.1 = (bf16[4096,256]{1,0:T(8,128)(2,1)}, f32[2,8,512]{2,1,0:T(8,128)}, bf16[4096,256]{1,0:T(8,128)(2,1)}, bf16[4096,256]{1,0:T(8,128)(2,1)}, bf16[4096,256]{1,0:T(8,128)(2,1)}) custom-call(s32[16]{0:T(128)} %get-tuple-element.220.place, s32[8]{0:T(128)} %compare_select_fusion.first_tile, f32[4096,768]{1,0:T(8,128)} %get-tuple-element.221.raw_q.raw_k.raw_v, ...), custom_call_target="tpu_custom_call" | custom-call | flops 17179869184 | bytes 33554432 | tf_op jit(solution)/shard_map/attention_forward/pallas_call | solution.py:234
  395.2 44.0 %all-to-all-done.1 = bf16[8,512,256]{1,2,0:T(8,128)(2,1)} async-done(((bf16[8,512,256]{1,2,0:T(8,128)(2,1)}), bf16[8,512,256]{1,2,0:T(8,128)(2,1)}, u32[]{:S(2)}, u32[]{:S(2)}) %all-to-all-start.1) | async-done | bytes 2097184 | tf_op jit(solution)/shard_map/all_to_all | solution.py:906
  473.2 49.1 %expert_unit.4 = (bf16[8,2,288,2048]{3,2,1,0:T(8,128)(2,1)}, bf16[8,2,288,2048]{3,2,1,0:T(8,128)(2,1)}, bf16[8,2,288,1024]{3,2,1,0:T(8,128)(2,1)}, bf16[8,2,288,...) custom-call(s32[2]{0:T(128)} %pad_add_fusion.6.unit, ...), custom_call_target="tpu_custom_call" | custom-call | tf_op jit(solution)/shard_map/expert_unit/pallas_call | solution.py:667
  532.1 49.4 %expert_unit.5 = (bf16[8,2,288,2048]{3,2,1,0:T(8,128)(2,1)}, bf16[8,2,288,2048]{3,2,1,0:T(8,128)(2,1)}, bf16[8,2,288,1024]{3,2,1,0:T(8,128)(2,1)}, bf16[8,2,288,...) custom-call(s32[2]{0:T(128)} %pad_add_fusion.7.unit, ...), custom_call_target="tpu_custom_call", output_to_operand_aliasing={{0}: (10, {}), {1}: (11, {}), {2}: (12, {}), {3}: (13, {}),... | custom-call | tf_op jit(solution)/shard_map/expert_unit/pallas_call | solution.py:667
  588.6 49.1 %expert_unit.6 = (bf16[8,2,288,2048]{3,2,1,0:T(8,128)(2,1)}, bf16[8,2,288,2048]{3,2,1,0:T(8,128)(2,1)}, bf16[8,2,288,1024]{3,2,1,0:T(8,128)(2,1)}, bf16[8,2,288,...) custom-call(s32[2]{0:T(128)} %pad_add_fusion.8.unit, ...), custom_call_target="tpu_custom_call", output_to_operand_aliasing={{0}: (10, {}), {1}: (11, {}), {2}: (12, {}), {3}: (13, {}),... | custom-call | tf_op jit(solution)/shard_map/expert_unit/pallas_call | solution.py:667
  644.8 49.1 %expert_unit.7 = (bf16[8,2,288,2048]{3,2,1,0:T(8,128)(2,1)}, bf16[8,2,288,2048]{3,2,1,0:T(8,128)(2,1)}, bf16[8,2,288,1024]{3,2,1,0:T(8,128)(2,1)}, bf16[8,2,288,...) custom-call(s32[2]{0:T(128)} %pad_add_fusion.5.unit, ...), custom_call_target="tpu_custom_call", output_to_operand_aliasing={{0}: (10, {}), {1}: (11, {}), {2}: (12, {}), {3}: (13, {}),... | custom-call | tf_op jit(solution)/shard_map/expert_unit/pallas_call | solution.py:667
  694.0 45.1 %expert_out.1 = bf16[8,512,2048]{2,1,0:T(8,128)(2,1)} custom-call(bf16[8,2,288,1024]{3,2,1,0:T(8,128)(2,1)} %get-tuple-element.294.hidden, bf16[2,1024,2048]{2,1,0:T(8,128)(2,1)} %join.6.w_down, s32[8,2,512]{2,1,0:T(2,128)} %copy.172.slots, f32[8,2,512]{2,1,0:T(2,128)} %slice_bitcast_fusion.gates, s32[8,512,2]{2,1,0:T(8,128)} %select_bitcast_fusion.columns), custom_call_target="tpu_custom_call" | custom-call | tf_op jit(solution)/shard_map/expert_out/pallas_call | solution.py:728
  739.1 26.9 %bitcast_convert_fusion.2 = bf16[2,1024,2048]{2,1,0:T(8,128)(2,1)} fusion(bf16[8,2,288,1024]{3,2,1,0:T(8,128)(2,1)} %get-tuple-element.294.hidden, bf16[8,2,288,2048]{3,2,1,0:T(8,128)(2,1)} %get-tuple-element.295), kind=kOutput, calls=%fused_computation.2 | convolution fusion | flops 19331547136 | bytes 36700160 | tf_op jit(solution)/shard_map/sncf,sncd->nfd/dot_general | solution.py:963
  773.3 27.6 %bitcast_convert_fusion = bf16[2,2048,1024]{2,1,0:T(8,128)(2,1)} fusion(bf16[8,2,288,2048]{3,2,1,0:T(8,128)(2,1)} %get-tuple-element.298, bf16[8,2,288,1024]{3,2,1,0:T(8,128)(2,1)} %get-tuple-element.300), kind=kOutput, calls=%fused_computation | convolution fusion | flops 19331547136 | bytes 36700160 | tf_op jit(solution)/shard_map/sncd,sncf->ndf/dot_general | solution.py:968
  801.0 24.9 %bitcast_convert_fusion.1 = bf16[2,2048,1024]{2,1,0:T(8,128)(2,1)} fusion(bf16[8,2,288,2048]{3,2,1,0:T(8,128)(2,1)} %get-tuple-element.298, bf16[8,2,288,1024]{3,2,1,0:T(8,128)(2,1)S(1)} %bitcast.138), kind=kOutput, calls=%fused_computation.1 | convolution fusion | flops 19331547136 | bytes 36700160 | tf_op jit(solution)/shard_map/sncd,sncf->ndf/dot_general | solution.py:967
  825.8 37.8 %collective-permute-done.41 = bf16[2,256,2048]{2,1,0:T(8,128)(2,1)} collective-permute-done((bf16[2,256,2048]{2,1,0:T(8,128)(2,1)S(1)}, bf16[2,256,2048]{2,1,0:T(8,128)(2,1)}, u32[]{:S(2)}, u32[]{:S(2)}) %collective-permute-start.41) | collective-permute-done | bytes 2097184 | tf_op jit(solution)/shard_map/ppermute | solution.py:387
  922.7 29.5 %collective-permute-done.45 = bf16[2,512,1024]{2,1,0:T(8,128)(2,1)} collective-permute-done((bf16[2,512,1024]{2,1,0:T(8,128)(2,1)}, bf16[2,512,1024]{2,1,0:T(8,128)(2,1)}, u32[]{:S(2)}, u32[]{:S(2)}) %collective-permute-start.45) | collective-permute-done | bytes 2097184 | tf_op jit(solution)/shard_map/ppermute | solution.py:387
  954.5 27.0 %all-to-all-done.2 = bf16[8,512,256]{2,1,0:T(8,128)(2,1)} async-done(((bf16[8,512,256]{2,1,0:T(8,128)(2,1)}), bf16[8,512,256]{2,1,0:T(8,128)(2,1)}, u32[]{:S(2)}, u32[]{:S(2)}) %all-to-all-start.2) | async-done | bytes 2097184 | tf_op jit(solution)/shard_map/all_to_all | solution.py:985
  988.3 70.4 %attention_backward.1 = (f32[4096,256]{1,0:T(8,128)}, f32[4096,256]{1,0:T(8,128)}, bf16[4096,256]{1,0:T(8,128)(2,1)}) custom-call(s32[16]{0:T(128)} %get-tuple-element.220.place, s32[8]{0:T(128)} %compare_select_fusion.first_tile, bf16[4096,256]{1,0:T(8,128)(2,1)} %get-tuple-element.222.queries, bf16[4096,256]{1,0:T(8,128)(2,1)} %get-tuple-element.223.keys, ...), custom_call_target="tpu_custom_call" | custom-call | flops 21474836480 | bytes 33554432 | tf_op jit(solution)/shard_map/attention_backward/pallas_call | solution.py:290
  1068.0 14.5 all-gather.2
  1091.5 19.7 %convolution_convert_fusion = bf16[4096,2048]{1,0:T(8,128)(2,1)} fusion(bf16[2048,768]{1,0:T(8,128)(2,1)S(1)} %copy-done.1, bf16[4096,256]{1,0:T(8,128)(2,1)} %get-tuple-element.312, bf16[4096,256]{1,0:T(8,128)(2,1)} %get-tuple-element.356, bf16[4096,256]{1,0:T(8,128)(2,1)} %get-tuple-element.355), kind=kOutput, calls=%fused_computation.4 | convolution fusion | flops 12912164864 | bytes 26214400 | tf_op jit(solution)/shard_map/dot_general | solution.py:1032
  1126.0 19.1 %convolution_convert_fusion.2 = bf16[2048,768]{1,0:T(8,128)(2,1)S(1)} fusion(bf16[4096,2048]{1,0:T(8,128)(2,1)} %get-tuple-element.214, bf16[4096,768]{1,0:T(8,128)(2,1)} %pad_maximum_fusion), kind=kOutput, calls=%fused_computation.46 | convolution fusion | flops 12886474752 | bytes 26214400 | tf_op jit(solution)/shard_map/dot_general | solution.py:1047
  1155.8 10.9 collective-permute-done.52
  1166.6 16.2 %collective-permute-done.51 = bf16[512,768]{1,0:T(8,128)(2,1)S(1)} collective-permute-done((bf16[512,768]{1,0:T(8,128)(2,1)S(1)}, bf16[512,768]{1,0:T(8,128)(2,1)S(1)}, u32[]{:S(2)}, u32[]{:S(2)}) %collective-permute-start.51) | collective-permute-done | bytes 786464 | tf_op jit(solution)/shard_map/ppermute | solution.py:387
  1194.8 43.4 %collective-permute-done.56 = bf16[64,8192]{1,0:T(8,128)(2,1)} collective-permute-done((bf16[64,8192]{1,0:T(8,128)(2,1)S(1)}, bf16[64,8192]{1,0:T(8,128)(2,1)}, u32[]{:S(2)}, u32[]{:S(2)}) %collective-permute-start.56) | collective-permute-done | bytes 1048608 | tf_op jit(solution)/shard_map/ppermute | solution.py:365
  1245.6 42.8 %collective-permute-done.57 = bf16[64,8192]{1,0:T(8,128)(2,1)} collective-permute-done((bf16[64,8192]{1,0:T(8,128)(2,1)}, bf16[64,8192]{1,0:T(8,128)(2,1)}, u32[]{:S(2)}, u32[]{:S(2)}) %collective-permute-start.57) | collective-permute-done | bytes 1048608 | tf_op jit(solution)/shard_map/ppermute | solution.py:365
  1306.9 31.5 %collective-permute-done.58 = bf16[64,8192]{1,0:T(8,128)(2,1)S(1)} collective-permute-done((bf16[64,8192]{1,0:T(8,128)(2,1)}, bf16[64,8192]{1,0:T(8,128)(2,1)S(1)}, u32[]{:S(2)}, u32[]{:S(2)}) %collective-permute-start.58) | collective-permute-done | bytes 1048608 | tf_op jit(solution)/shard_map/ppermute | solution.py:365
  1367.8 27.9 %collective-permute-done.65 = bf16[2,512,1024]{2,1,0:T(8,128)(2,1)} collective-permute-done((bf16[2,512,1024]{2,1,0:T(8,128)(2,1)}, bf16[2,512,1024]{2,1,0:T(8,128)(2,1)}, u32[]{:S(2)}, u32[]{:S(2)}) %collective-permute-start.65) | collective-permute-done | bytes 2097184 | tf_op jit(solution)/shard_map/ppermute | solution.py:387
  1395.7 33.1 %collective-permute-done.64 = bf16[2,512,1024]{2,1,0:T(8,128)(2,1)} collective-permute-done((bf16[2,512,1024]{2,1,0:T(8,128)(2,1)}, bf16[2,512,1024]{2,1,0:T(8,128)(2,1)}, u32[]{:S(2)}, u32[]{:S(2)}) %collective-permute-start.64) | collective-permute-done | bytes 2097184 | tf_op jit(solution)/shard_map/ppermute | solution.py:387
  1497.1 15.5 %all-gather.3 = f32[8,4,2048]{2,1,0:T(4,128)S(1)} all-gather(f32[1,4,2048]{2,1,0:T(4,128)S(1)} %maximum_bitcast_fusion.1), channel_id=3, replica_groups=mesh['dp'=4,'ctx'=8] {'ctx'}, dimensions={0}, use_global_device_ids=true | all-gather | bytes 294912 | tf_op jit(solution)/shard_map/all_gather | solution.py:439
  (435 shorter events, 502.4 us)
Async XLA Ops:
  7.2 221.4 %all-gather.7.cloned.1.call-start = ((), (), s32[]{:S(2)}) async-start(), calls=%async_computation.7 | async-start | bytes 10485760 | tf_op jit(solution)/shard_map/all_gather | solution.py:782
  7.9 81.8 %collective-permute-start.2 = (bf16[512,2048]{1,0:T(8,128)(2,1)}, bf16[512,2048]{1,0:T(8,128)(2,1)}, u32[]{:S(2)}, u32[]{:S(2)}) collective-permute-start(bf16[512,2048]{1,0:T(8,128)(2,1)} %own.1), channel_id=1, source_target_pairs={{0,1},{1,0},{2,3},{3,2},{4,5},{5,4},{6,7},{7,6},{8,9},{9,8},{10,11... | collective-permute-start | bytes 6291464 | tf_op jit(solution)/shard_map/ppermute | solution.py:370
  8.4 81.3 %collective-permute-start.1 = (bf16[512,2048]{1,0:T(8,128)(2,1)}, bf16[512,2048]{1,0:T(8,128)(2,1)}, u32[]{:S(2)}, u32[]{:S(2)}) collective-permute-start(bf16[512,2048]{1,0:T(8,128)(2,1)} %own.1), channel_id=1, source_target_pairs={{2,0},{3,1},{4,2},{5,3},{6,4},{7,5},{10,8},{11,9},{12,10},{13,11},... | collective-permute-start | bytes 6291464 | tf_op jit(solution)/shard_map/ppermute | solution.py:366
  9.7 80.0 %collective-permute-start = (bf16[512,2048]{1,0:T(8,128)(2,1)}, bf16[512,2048]{1,0:T(8,128)(2,1)}, u32[]{:S(2)}, u32[]{:S(2)}) collective-permute-start(bf16[512,2048]{1,0:T(8,128)(2,1)} %own.1), channel_id=1, source_target_pairs={{0,2},{1,3},{2,4},{3,5},{4,6},{5,7},{8,10},{9,11},{10,12},{11,13},... | collective-permute-start | bytes 6291464 | tf_op jit(solution)/shard_map/ppermute | solution.py:365
  92.9 69.9 %collective-permute-start.12 = (bf16[512,2048]{1,0:T(8,128)(2,1)}, bf16[512,2048]{1,0:T(8,128)(2,1)}, u32[]{:S(2)}, u32[]{:S(2)}) collective-permute-start(bf16[512,2048]{1,0:T(8,128)(2,1)} %broadcast_select_fusion.1.own), channel_id=1, source_target_pairs={{0,1},{1,0},{2,3},{3,2},{4,5},{5,4},{6,7},{7,6},{8,9},{9,8},{10,11... | collective-permute-start | bytes 6291464 | tf_op jit(solution)/shard_map/ppermute | solution.py:370
  92.9 69.9 %collective-permute-start.11 = (bf16[512,2048]{1,0:T(8,128)(2,1)}, bf16[512,2048]{1,0:T(8,128)(2,1)}, u32[]{:S(2)}, u32[]{:S(2)}) collective-permute-start(bf16[512,2048]{1,0:T(8,128)(2,1)} %collective-permute-done.1), channel_id=1, source_target_pairs={{2,0},{3,1},{4,2},{5,3},{6,4},{7,5},{10,8},{11,9},{12,10},{13,11},... | collective-permute-start | bytes 6291464 | tf_op jit(solution)/shard_map/ppermute | solution.py:366
  94.2 68.7 %collective-permute-start.10 = (bf16[512,2048]{1,0:T(8,128)(2,1)}, bf16[512,2048]{1,0:T(8,128)(2,1)}, u32[]{:S(2)}, u32[]{:S(2)}) collective-permute-start(bf16[512,2048]{1,0:T(8,128)(2,1)} %collective-permute-done), channel_id=1, source_target_pairs={{0,2},{1,3},{2,4},{3,5},{4,6},{5,7},{8,10},{9,11},{10,12},{11,13},... | collective-permute-start | bytes 6291464 | tf_op jit(solution)/shard_map/ppermute | solution.py:365
  172.4 56.1 %collective-permute-start.20 = (bf16[1024,2048]{1,0:T(8,128)(2,1)}, bf16[1024,2048]{1,0:T(8,128)(2,1)}, u32[]{:S(2)}, u32[]{:S(2)}) collective-permute-start(bf16[1024,2048]{1,0:T(8,128)(2,1)} %constant_dynamic-update-slice_fusion.refs_0_), channel_id=1, source_target_pairs={{0,1},{1,0},{2,3},{3,2},{4,5},{5,4},{6,7},{7,6},{8,9},{9,8},{10,11... | collective-permute-start | bytes 12582920 | tf_op jit(solution)/shard_map/ppermute | solution.py:370
  187.7 272.7 %all-gather.9.cloned.1.call-start = ((), (), s32[]{:S(2)}) async-start(), calls=%async_computation.8 | async-start | bytes 18874368 | tf_op jit(solution)/shard_map/all_gather | solution.py:875
  287.0 68.3 %collective-permute-start.27 = (bf16[2,512,1024]{2,1,0:T(8,128)(2,1)}, bf16[2,512,1024]{2,1,0:T(8,128)(2,1)}, u32[]{:S(2)}, u32[]{:S(2)}) collective-permute-start(bf16[2,512,1024]{2,1,0:T(8,128)(2,1)} %refs_0_.1), channel_id=1, source_target_pairs={{0,16},{8,24},{16,0},{24,8},{1,17},{9,25},{17,1},{25,9},{2,18},{10... | collective-permute-start | bytes 6291464 | tf_op jit(solution)/shard_map/ppermute | solution.py:387
  288.4 67.0 %collective-permute-start.26 = (bf16[2,512,1024]{2,1,0:T(8,128)(2,1)}, bf16[2,512,1024]{2,1,0:T(8,128)(2,1)}, u32[]{:S(2)}, u32[]{:S(2)}) collective-permute-start(bf16[2,512,1024]{2,1,0:T(8,128)(2,1)} %refs_0_.1), channel_id=1, source_target_pairs={{0,8},{8,0},{16,24},{24,16},{1,9},{9,1},{17,25},{25,17},{2,10},{10... | collective-permute-start | bytes 6291464 | tf_op jit(solution)/shard_map/ppermute | solution.py:387
  359.3 80.0 %all-to-all-start.1 = ((bf16[8,512,256]{1,2,0:T(8,128)(2,1)}), bf16[8,512,256]{1,2,0:T(8,128)(2,1)}, u32[]{:S(2)}, u32[]{:S(2)}) async-start(bf16[8,512,256]{1,2,0:T(8,128)(2,1)} %copy.170), calls=%async_computation.1 | async-start | bytes 4194304 | tf_op jit(solution)/shard_map/all_to_all | solution.py:906
  364.6 499.2 %reduce-scatter.4.cloned.1.call-start = ((), (), s32[]{:S(2)}) async-start(), calls=%async_computation.9 | async-start | bytes 18874368 | tf_op jit(solution)/shard_map/reduce_scatter | solution.py:958
  460.4 61.9 %collective-permute-start.31 = (bf16[512,2048]{1,0:T(8,128)(2,1)}, bf16[512,2048]{1,0:T(8,128)(2,1)}, u32[]{:S(2)}, u32[]{:S(2)}) collective-permute-start(bf16[512,2048]{1,0:T(8,128)(2,1)} %multiply_convert_fusion.2.own), channel_id=1, source_target_pairs={{2,0},{3,1},{4,2},{5,3},{6,4},{7,5},{10,8},{11,9},{12,10},{13,11},... | collective-permute-start | bytes 6291464 | tf_op jit(solution)/shard_map/ppermute | solution.py:366
  461.8 60.5 %collective-permute-start.30 = (bf16[512,2048]{1,0:T(8,128)(2,1)}, bf16[512,2048]{1,0:T(8,128)(2,1)}, u32[]{:S(2)}, u32[]{:S(2)}) collective-permute-start(bf16[512,2048]{1,0:T(8,128)(2,1)} %multiply_convert_fusion.2.own), channel_id=1, source_target_pairs={{0,2},{1,3},{2,4},{3,5},{4,6},{5,7},{8,10},{9,11},{10,12},{11,13},... | collective-permute-start | bytes 6291464 | tf_op jit(solution)/shard_map/ppermute | solution.py:365
  524.3 57.2 %collective-permute-start.34 = (bf16[512,2048]{1,0:T(8,128)(2,1)}, bf16[512,2048]{1,0:T(8,128)(2,1)}, u32[]{:S(2)}, u32[]{:S(2)}) collective-permute-start(bf16[512,2048]{1,0:T(8,128)(2,1)} %collective-permute-done.31), channel_id=1, source_target_pairs={{2,0},{3,1},{4,2},{5,3},{6,4},{7,5},{10,8},{11,9},{12,10},{13,11},... | collective-permute-start | bytes 6291464 | tf_op jit(solution)/shard_map/ppermute | solution.py:366
  694.0 423.6 %reduce-scatter.6.cloned.1.call-start = ((), (), s32[]{:S(2)}) async-start(), calls=%async_computation.10 | async-start | bytes 18874368 | tf_op jit(solution)/shard_map/reduce_scatter | solution.py:973
  769.8 56.1 %collective-permute-start.42 = (bf16[2,256,2048]{2,1,0:T(8,128)(2,1)S(1)}, bf16[2,256,2048]{2,1,0:T(8,128)(2,1)}, u32[]{:S(2)}, u32[]{:S(2)}) collective-permute-start(bf16[2,256,2048]{2,1,0:T(8,128)(2,1)S(1)} %get-tuple-element.363), channel_id=1, source_target_pairs={{0,24},{8,16},{16,8},{24,0},{1,25},{9,17},{17,9},{25,1},{2,26},{10... | collective-permute-start | bytes 6291464 | tf_op jit(solution)/shard_map/ppermute | solution.py:387
  772.3 91.4 %collective-permute-start.41 = (bf16[2,256,2048]{2,1,0:T(8,128)(2,1)S(1)}, bf16[2,256,2048]{2,1,0:T(8,128)(2,1)}, u32[]{:S(2)}, u32[]{:S(2)}) collective-permute-start(bf16[2,256,2048]{2,1,0:T(8,128)(2,1)S(1)} %get-tuple-element.364), channel_id=1, source_target_pairs={{0,16},{8,24},{16,0},{24,8},{1,17},{9,25},{17,1},{25,9},{2,18},{10... | collective-permute-start | bytes 6291464 | tf_op jit(solution)/shard_map/ppermute | solution.py:387
  772.8 91.0 %collective-permute-start.40 = (bf16[2,256,2048]{2,1,0:T(8,128)(2,1)S(1)}, bf16[2,256,2048]{2,1,0:T(8,128)(2,1)}, u32[]{:S(2)}, u32[]{:S(2)}) collective-permute-start(bf16[2,256,2048]{2,1,0:T(8,128)(2,1)S(1)} %get-tuple-element.365), channel_id=1, source_target_pairs={{0,8},{8,0},{16,24},{24,16},{1,9},{9,1},{17,25},{25,17},{2,10},{10... | collective-permute-start | bytes 6291464 | tf_op jit(solution)/shard_map/ppermute | solution.py:387
  893.3 88.1 %all-to-all-start.2 = ((bf16[8,512,256]{2,1,0:T(8,128)(2,1)}), bf16[8,512,256]{2,1,0:T(8,128)(2,1)}, u32[]{:S(2)}, u32[]{:S(2)}) async-start(bf16[8,512,256]{2,1,0:T(8,128)(2,1)} %bitcast.131), calls=%async_computation.3 | async-start | bytes 4194304 | tf_op jit(solution)/shard_map/all_to_all | solution.py:985
  897.7 596.5 %reduce-scatter.8.cloned.1.call-start = ((), (), s32[]{:S(2)}) async-start(), calls=%async_computation.11 | async-start | bytes 18874368 | tf_op jit(solution)/shard_map/reduce_scatter | solution.py:1035
  907.7 151.0 %collective-permute-start.46 = (bf16[2,512,1024]{2,1,0:T(8,128)(2,1)}, bf16[2,512,1024]{2,1,0:T(8,128)(2,1)S(1)}, u32[]{:S(2)}, u32[]{:S(2)}) collective-permute-start(bf16[2,512,1024]{2,1,0:T(8,128)(2,1)} %get-tuple-element.360), channel_id=1, source_target_pairs={{0,24},{8,16},{16,8},{24,0},{1,25},{9,17},{17,9},{25,1},{2,26},{10... | collective-permute-start | bytes 6291464 | tf_op jit(solution)/shard_map/ppermute | solution.py:387
  984.8 132.7 %collective-permute-start.49 = (bf16[1,256,2048]{2,1,0:T(8,128)(2,1)}, bf16[1,256,2048]{2,1,0:T(8,128)(2,1)}, u32[]{:S(2)}, u32[]{:S(2)}) collective-permute-start(bf16[1,256,2048]{2,1,0:T(8,128)(2,1)} %get-tuple-element.366), channel_id=1, source_target_pairs={{0,24},{8,16},{16,8},{24,0},{1,25},{9,17},{17,9},{25,1},{2,26},{10... | collective-permute-start | bytes 3145736 | tf_op jit(solution)/shard_map/ppermute | solution.py:387
  985.9 72.9 %collective-permute-start.48 = (bf16[1,256,2048]{2,1,0:T(8,128)(2,1)S(1)}, bf16[1,256,2048]{2,1,0:T(8,128)(2,1)S(1)}, u32[]{:S(2)}, u32[]{:S(2)}) collective-permute-start(bf16[1,256,2048]{2,1,0:T(8,128)(2,1)S(1)} %get-tuple-element.367), channel_id=1, source_target_pairs={{0,16},{8,24},{16,0},{24,8},{1,17},{9,25},{17,1},{25,9},{2,18},{10... | collective-permute-start | bytes 3145736 | tf_op jit(solution)/shard_map/ppermute | solution.py:387
  987.6 71.2 %collective-permute-start.47 = (bf16[1,256,2048]{2,1,0:T(8,128)(2,1)S(1)}, bf16[1,256,2048]{2,1,0:T(8,128)(2,1)S(1)}, u32[]{:S(2)}, u32[]{:S(2)}) collective-permute-start(bf16[1,256,2048]{2,1,0:T(8,128)(2,1)S(1)} %get-tuple-element.368), channel_id=1, source_target_pairs={{0,8},{8,0},{16,24},{24,16},{1,9},{9,1},{17,25},{25,17},{2,10},{10... | collective-permute-start | bytes 3145736 | tf_op jit(solution)/shard_map/ppermute | solution.py:387
  1122.2 61.5 %all-to-all-start.3 = ((bf16[4,64,2048]{2,1,0:T(8,128)(2,1)}), bf16[4,64,2048]{2,1,0:T(8,128)(2,1)S(1)}, u32[]{:S(2)}, u32[]{:S(2)}) async-start(bf16[4,64,2048]{2,1,0:T(8,128)(2,1)} %bitcast.81), calls=%async_computation.5 | async-start | bytes 2097152 | tf_op jit(solution)/shard_map/all_to_all | solution.py:1039
  1305.5 90.2 %collective-permute-start.65 = (bf16[2,512,1024]{2,1,0:T(8,128)(2,1)}, bf16[2,512,1024]{2,1,0:T(8,128)(2,1)}, u32[]{:S(2)}, u32[]{:S(2)}) collective-permute-start(bf16[2,512,1024]{2,1,0:T(8,128)(2,1)} %get-tuple-element.358), channel_id=1, source_target_pairs={{0,24},{8,16},{16,8},{24,0},{1,25},{9,17},{17,9},{25,1},{2,26},{10... | collective-permute-start | bytes 6291464 | tf_op jit(solution)/shard_map/ppermute | solution.py:387
  1338.4 90.4 %collective-permute-start.64 = (bf16[2,512,1024]{2,1,0:T(8,128)(2,1)}, bf16[2,512,1024]{2,1,0:T(8,128)(2,1)}, u32[]{:S(2)}, u32[]{:S(2)}) collective-permute-start(bf16[2,512,1024]{2,1,0:T(8,128)(2,1)} %get-tuple-element.359), channel_id=1, source_target_pairs={{0,16},{8,24},{16,0},{24,8},{1,17},{9,25},{17,1},{25,9},{2,18},{10... | collective-permute-start | bytes 6291464 | tf_op jit(solution)/shard_map/ppermute | solution.py:387
  1347.9 104.1 %collective-permute-start.60 = (bf16[64,8192]{1,0:T(8,128)(2,1)}, bf16[64,8192]{1,0:T(8,128)(2,1)}, u32[]{:S(2)}, u32[]{:S(2)}) collective-permute-start(bf16[64,8192]{1,0:T(8,128)(2,1)} %get-tuple-element.372), channel_id=1, source_target_pairs={{0,1},{1,0},{2,3},{3,2},{4,5},{5,4},{6,7},{7,6},{8,9},{9,8},{10,11... | collective-permute-start | bytes 3145736 | tf_op jit(solution)/shard_map/ppermute | solution.py:370
  1347.9 108.4 %collective-permute-start.59 = (bf16[64,8192]{1,0:T(8,128)(2,1)}, bf16[64,8192]{1,0:T(8,128)(2,1)}, u32[]{:S(2)}, u32[]{:S(2)}) collective-permute-start(bf16[64,8192]{1,0:T(8,128)(2,1)} %get-tuple-element.373), channel_id=1, source_target_pairs={{0,1},{1,0},{2,3},{3,2},{4,5},{5,4},{6,7},{7,6},{8,9},{9,8},{10,11... | collective-permute-start | bytes 3145736 | tf_op jit(solution)/shard_map/ppermute | solution.py:370
  1352.1 108.5 %collective-permute-start.61 = (bf16[64,8192]{1,0:T(8,128)(2,1)S(1)}, bf16[64,8192]{1,0:T(8,128)(2,1)}, u32[]{:S(2)}, u32[]{:S(2)}) collective-permute-start(bf16[64,8192]{1,0:T(8,128)(2,1)S(1)} %get-tuple-element.374), channel_id=1, source_target_pairs={{0,1},{1,0},{2,3},{3,2},{4,5},{5,4},{6,7},{7,6},{8,9},{9,8},{10,11... | collective-permute-start | bytes 3145736 | tf_op jit(solution)/shard_map/ppermute | solution.py:370
  (109 other events, 2971.7 us)
Sparse Core Ops, SparseCore 0:
  9.9 127.4 all-gather.6
  243.4 189.1 all-gather.8
  694.1 168.4 reduce-scatter.3
  864.8 199.3 reduce-scatter.5
  1117.7 250.4 reduce-scatter.7

commit v3 on v2

--- a/solution.py
+++ b/solution.py
@@ -350,8 +350,7 @@
         peers = lax.axis_size("ctx")
         self.chips = peers // 2
         self.chip = lax.axis_index("ctx") // 2
-        self.up = [(i, i + 2) for i in range(peers - 2)]
-        self.down = [(i + 2, i) for i in range(peers - 2)]
+        self.peers = peers
         self.pair = [(i, i ^ 1) for i in range(peers)]
         steps = range(1, self.chips)
         every = [d for s in steps for d in (s, -s)]
@@ -360,10 +359,12 @@
             for z in range(self.chips)
         ]
 
-    def step(self, from_below, from_above):
+    def step(self, turn, from_below, from_above):
+        up = [(i, i + 2) for i in range(2 * (turn - 1), self.peers - 2)]
+        down = [(i + 2, i) for i in range(self.peers - 2 * turn)]
         return (
-            lax.ppermute(from_below, "ctx", self.up),
-            lax.ppermute(from_above, "ctx", self.down),
+            lax.ppermute(from_below, "ctx", up),
+            lax.ppermute(from_above, "ctx", down),
         )
 
     def other(self, rows):
@@ -391,6 +392,10 @@
     return [swap_dp(part, 1), swap_dp(part, 2)]
 
 
+def send_dp(part):
+    return [swap_dp(part, shift) for shift in (1, 2, 3)]
+
+
 def second_dp(pieces, axis):
     half = pieces[0].shape[axis] // 2
     return [
@@ -407,13 +412,11 @@
     def both(shift):
         return [(mine ^ shift) * size, (mine ^ shift) * size + half]
 
-    parts = [
-        (part, both(0)),
-        (pieces[0], both(1)),
-        (pieces[1], both(2)),
-        (pieces[2], both(3)[:1]),
-        (pieces[3], both(3)[1:]),
-    ]
+    parts = [(part, both(0)), (pieces[0], both(1)), (pieces[1], both(2))]
+    if len(pieces) == 3:
+        parts.append((pieces[2], both(3)))
+    else:
+        parts += [(pieces[2], both(3)[:1]), (pieces[3], both(3)[1:])]
     return join(parts, axis, size * lax.axis_size("dp"), half)
 
 
@@ -435,8 +438,14 @@
     return total
 
 
-def sum_small(array, axes="ctx"):
-    return jnp.sum(lax.all_gather(array, axes, axis=0, tiled=False), axis=0)
+def sum_small(array):
+    peers = lax.axis_size("ctx")
+
+    def swap(rows, shift):
+        return lax.ppermute(rows, "ctx", [(i, i ^ shift) for i in range(peers)])
+
+    array = array + swap(array, 1)
+    return sum((swap(array, 2 * shift) for shift in range(1, peers // 2)), start=array)
 
 
 def project_kernel(places, own, other, weight, gain, *rest):
@@ -779,8 +788,6 @@
     line = Line()
     turns = range(1, line.chips)
 
-    full_gate = lax.all_gather(w_gate, "dp", axis=1, tiled=True)
-
     assign = block_assign[0]
     count_blocks = assign.shape[0]
     place = jnp.argmax(
@@ -814,13 +821,16 @@
     )
 
     inputs = tokens.astype(f32)
-    below, above = line.step(tokens, tokens)
+    below, above = line.step(1, tokens, tokens)
     other = line.other(tokens)
-    w_part = lax.dynamic_slice_in_dim(
-        wqkv.reshape(wqkv.shape[0], 3, HEADS, head_dim), first_head, own_heads, 2
-    ).reshape(wqkv.shape[0], 3 * own_width)
-    w_pieces = first_dp(w_part)
-    w_pieces = w_pieces + second_dp(w_pieces, 0)
+    w_part = jnp.concatenate(
+        [
+            lax.dynamic_slice_in_dim(wqkv, which * width + first_head * head_dim, own_width, 1)
+            for which in range(3)
+        ],
+        axis=1,
+    )
+    w_pieces = send_dp(w_part)
     gain_part = jnp.stack([attn_gain, query_gain, key_gain, moe_gain])
     gain_all = jnp.zeros((4, width), bf16)
     for shift in range(groups):
@@ -829,9 +839,10 @@
             gain_all, piece, (my_dp ^ shift) * gain_part.shape[1], 1
         )
     gain_all = gain_all.astype(f32)
-    below, above, other, gain_all, table, wo, *w_pieces = barrier(
-        below, above, other, gain_all, table, wo, *w_pieces
-    )
+    below, above, other, gain_all, table, wo, w_gate, *w_pieces = barrier(
+        below, above, other, gain_all, table, wo, w_gate, *w_pieces
+    )
+    full_gate = lax.all_gather(w_gate, "dp", axis=1, tiled=True)
     w_own = join_dp(w_part, w_pieces, 0)
     gain_attn, gain_moe = gain_all[0:1], gain_all[3:4]
     gain_own = lax.dynamic_slice_in_dim(gain_all, first_head * head_dim, own_width, 1)
@@ -840,34 +851,26 @@
     half_rows = wo.shape[0] // 2
     arrived = {-1: below, 1: above}
     own, chip = tokens, line.chip
-    kept = ()
+    kept, travelled = (), ()
     for turn in turns:
         if turn + 1 < line.chips:
-            below, above = line.step(below, above)
+            below, above = line.step(turn + 1, below, above)
             arrived[-turn - 1], arrived[turn + 1] = below, above
         next_own, next_chip = line.take(turn, arrived)
         next_other = line.other(next_own)
         at = jnp.stack([2 * chip + core, 2 * chip + 1 - core]).astype(jnp.int32)
         kept = project(at, own, other, w_own, gain_attn, peers, kept)
-        travel = []
+        travel = list(travelled)
         if turn == 1:
             wo_half = lax.dynamic_slice_in_dim(wo, core * half_rows, half_rows, 0)
-            wo_pieces = first_dp(wo_half)
-            travel = wo_pieces + second_dp(wo_pieces, 0)
+            travel = first_dp(wo_half)
         if turn == 2:
-            wo_pieces = [wo_half, *travelled[:2], jnp.concatenate(travelled[2:], axis=0)]
-            wo_mine = jnp.concatenate(wo_pieces, axis=0)
-            down_pieces = first_dp(w_down)
-            travel = [line.other(wo_mine), wo_mine, full_gate] + down_pieces
-            table = lax.all_to_all(table, "ctx", split_axis=0, concat_axis=0, tiled=True)
-            travel.append(table)
+            travel.append(swap_dp(wo_half, 3))
         own, other, chip = next_own, next_other, next_chip
         square = kept[2]
         below, above, own, other, square, w_down, *travelled = barrier(
             below, above, own, other, square, w_down, *travel
         )
-        if turn == 2:
-            wo_theirs, wo_mine, full_gate, down_one, down_two, table = travelled
         kept = (kept[0], kept[1], square)
         if turn + 1 < line.chips:
             arrived[-turn - 1], arrived[turn + 1] = below, above
@@ -875,7 +878,10 @@
     cot_all = lax.all_gather(cotangent_now, "ctx", axis=0, tiled=True).reshape(
         peers, count_rows, width
     )
-    down_pieces = [down_one, down_two] + second_dp([down_one, down_two], 1)
+    down_pieces = first_dp(w_down)
+    wo_mine = jnp.concatenate([wo_half, *travelled[:3]], axis=0)
+    wo_theirs = line.other(wo_mine)
+    table = lax.all_to_all(table, "ctx", split_axis=0, concat_axis=0, tiled=True)
     at = jnp.stack([2 * chip + core, 2 * chip + 1 - core]).astype(jnp.int32)
     normed_all, raw, square = project(at, own, other, w_own, gain_attn, peers, kept)
     square = sum_small(square.transpose(1, 0, 2).reshape(2, group_rows)) * (1.0 / rep)
@@ -885,7 +891,10 @@
     offsets = (jnp.arange(local_experts, dtype=jnp.int32) * room)[None, :, None]
     columns = jnp.where(slot >= 0, slot + offsets, -1).transpose(0, 2, 1)
 
-    inv_qk, w_up, columns, *down_pieces = barrier(inv_qk, w_up, columns, *down_pieces)
+    inv_qk, w_up, slot, gate_rows, columns, full_gate, wo_mine, wo_theirs, *down_pieces = barrier(
+        inv_qk, w_up, slot, gate_rows, columns, full_gate, wo_mine, wo_theirs, *down_pieces
+    )
+    down_pieces = down_pieces + second_dp(down_pieces, 1)
     up_pieces = first_dp(w_up)
     attended, lse, queries, keys, values = attention_forward(
         raw,
@@ -901,7 +910,8 @@
         block_len,
         scale,
     )
-    attended, *up_pieces = barrier(attended, *up_pieces)
+    attended, *pieces = barrier(attended, *up_pieces, *down_pieces)
+    up_pieces, down_pieces = pieces[:2], pieces[2:]
     up_pieces = up_pieces + second_dp(up_pieces, 1)
     attn_low = lax.all_to_all(
         attended.reshape(peers, count_rows, own_width), "ctx", split_axis=0, concat_axis=0, tiled=True
@@ -917,22 +927,22 @@
         width,
         half_rows,
     )
-    attn_low, full_wo, full_down, *up_pieces = barrier(attn_low, full_wo, full_down, *up_pieces)
+    full_up = join_dp(w_up, up_pieces, 1)
+    attn_low, full_wo, full_down, full_up = barrier(attn_low, full_wo, full_down, full_up)
     attn_low = attn_low.transpose(1, 0, 2).reshape(count_rows, width)
     state = inputs + jnp.dot(attn_low, full_wo, preferred_element_type=f32)
     inv_state = rms_scale(state)
     hat_state = state * inv_state
     normed_moe = (hat_state * gain_moe).astype(bf16)
-    full_up = join_dp(w_up, up_pieces, 1)
-
-    normed_moe, full_up, cot_all = barrier(normed_moe, full_up, cot_all)
+
+    normed_moe, cot_all = barrier(normed_moe, cot_all)
     below, above = normed_moe, normed_moe
     own, chip = normed_moe, line.chip
     arrived = {}
     kept = ()
     for turn in range(line.chips):
         if turn + 1 < line.chips:
-            below, above = line.step(below, above)
+            below, above = line.step(turn + 1, below, above)
             arrived[-turn - 1], arrived[turn + 1] = below, above
         if turn > 0:
             own, chip = line.take(turn, arrived)
@@ -985,7 +995,9 @@
     grad_attended = lax.all_to_all(
         grad_attn, "ctx", split_axis=0, concat_axis=0, tiled=True
     ).reshape(group_rows, own_width)
-    part_out = lax.dot_general(attn_low, grad_branch, TN, preferred_element_type=f32).astype(bf16)
+    part_out = lax.dot_general(
+        attn_low, tied(grad_branch, grad_attn), TN, preferred_element_type=f32
+    ).astype(bf16)
     part_out = part_out.reshape(groups, 2, half_rows, width)
     out_theirs = line.other(lax.dynamic_index_in_dim(part_out, 1 - core, 1, keepdims=False))
     part_out = lax.dynamic_index_in_dim(part_out, core, 1, keepdims=False).astype(f32)
@@ -1012,7 +1024,7 @@
         block_len,
         scale,
     )
-    grad_q, gate_last, *out_pieces = barrier(grad_q, gate_pieces[2], *out_pieces)
+    grad_q, gate_last, grad_up, *out_pieces = barrier(grad_q, gate_pieces[2], grad_up, *out_pieces)
     gate_pieces[2] = gate_last
     out_pieces.append(scatter_one(part_out, 3, 0))
     hat_q = raw[:, :own_width] * inv_qk[:, 0:1]
@@ -1031,7 +1043,9 @@
     grad_qkv = jnp.concatenate([grad_raw_q.astype(bf16), grad_raw_k.astype(bf16), grad_v], axis=1)
     part_normed = lax.dot_general(grad_qkv, w_own, NT, preferred_element_type=f32) * (1.0 / rep)
     part_normed = part_normed.astype(bf16)
-    part_normed, grad_qkv, mixed, *out_pieces = barrier(part_normed, grad_qkv, mixed, *out_pieces)
+    part_normed, grad_qkv, mixed, grad_up, *out_pieces = barrier(
+        part_normed, grad_qkv, mixed, grad_up, *out_pieces
+    )
     grad_normed = lax.psum_scatter(part_normed, "ctx", scatter_dimension=0, tiled=True)
 
     out_sum = total_dp(part_out, out_pieces, 0).astype(bf16).reshape(half_rows, width)
@@ -1051,33 +1065,37 @@
     spread = lax.dynamic_update_slice_in_dim(
         jnp.zeros((2, width), f32), own_terms, first_head * head_dim, 1
     )
-    gain_terms = jnp.concatenate([spread, moe_gain_term[None]], axis=0)
-    grad_up, gate_sum, gain_terms, out_sum, *qkv_pieces = barrier(
-        grad_up, gate_sum, gain_terms, out_sum, *qkv_pieces
-    )
-    up_pieces = [scatter_one(grad_up, shift, 1) for shift in (1, 2, 3)]
+    attn_gain_term = (
+        jnp.sum(part_normed.astype(f32) * normed_all.astype(f32), axis=0) / gain_attn[0]
+    )
+    gain_terms = jnp.concatenate([attn_gain_term[None], spread, moe_gain_term[None]], axis=0)
+    gate_sum, out_sum, gain_terms, grad_up, *qkv_pieces = barrier(
+        gate_sum, out_sum, gain_terms, grad_up, *qkv_pieces
+    )
+    up_pieces = [scatter_one(grad_up, shift, 1) for shift in (1, 2)]
+    gain_terms = sum_small(gain_terms)
+    gain_terms = total_dp(gain_terms, [scatter_one(gain_terms, shift, 1) for shift in (1, 2, 3)], 1)
     qkv_sum = total_dp(part_qkv, qkv_pieces, 0).astype(bf16)
     out_sum = jnp.sum(out_sum.astype(f32), axis=0).astype(bf16)
     rows_dp = qkv_sum.shape[0]
-    weights = jnp.concatenate([qkv_sum.reshape(out_share, -1), out_sum], axis=1)
-    qkv_columns = weights.shape[1] - width
-    below, above = weights, weights
-    own, chip = weights, line.chip
+    own, chip = [qkv_sum, out_sum], line.chip
+    below, above = own, own
     arrived = {}
     qkv_kept, out_kept = (), ()
     for turn in range(line.chips):
+        if turn > 0:
+            own, chips = zip(*[line.take(turn, {d: a[i] for d, a in arrived.items()}) for i in (0, 1)])
+            chip = chips[0]
         if turn + 1 < line.chips:
-            below, above = line.step(below, above)
-            arrived[-turn - 1], arrived[turn + 1] = below, above
-        if turn > 0:
-            own, chip = line.take(turn, arrived)
-        other = line.other(own)
-        at = jnp.stack([2 * chip + core, 2 * chip + 1 - core]).astype(jnp.int32)
+            steps = [line.step(turn + 1, b, a) for b, a in zip(below, above)]
+            below, above = [s[0] for s in steps], [s[1] for s in steps]
+        other = [line.other(part) for part in own]
+        at = jnp.stack([2 * chip + core, 2 * chip + 1 - core]).astype(jnp.int32) // rep
         qkv_kept = [
             lay(
-                at // rep,
-                own[:, :qkv_columns].reshape(rows_dp, 3 * own_width),
-                other[:, :qkv_columns].reshape(rows_dp, 3 * own_width),
+                at,
+                own[0],
+                other[0],
                 (rows_dp, 3 * width),
                 3,
                 lambda p, t: (0, t * (peers // rep) + p),
@@ -1086,30 +1104,27 @@
         ]
         at = jnp.stack([core * line.chips + chip, (1 - core) * line.chips + chip]).astype(jnp.int32)
         out_kept = [
-            lay(
-                at,
-                own[:, qkv_columns:],
-                other[:, qkv_columns:],
-                (rows_dp, width),
-                1,
-                lambda p, t: (p, 0),
-                out_kept,
-            )
+            lay(at, own[1], other[1], (rows_dp, width), 1, lambda p, t: (p, 0), out_kept)
         ]
+        if turn + 1 < line.chips:
+            *both, qkv_kept[0], out_kept[0], grad_up = barrier(
+                *below, *above, qkv_kept[0], out_kept[0], grad_up, *up_pieces
+            )[: len(below) + len(above) + 3]
+            below, above = both[:2], both[2:]
+            if turn == 0:
+                up_pieces.append(scatter_one(grad_up, 3, 1))
+            arrived[-turn - 1], arrived[turn + 1] = below, above
     qkv_total, out_total = qkv_kept[0], out_kept[0]
     up_sum = total_dp(grad_up, up_pieces, 1)
     output = (state + mixed.astype(f32)).astype(bf16)
-    out_total, qkv_total, up_sum, output, grad_normed = barrier(
-        out_total, qkv_total, up_sum, output, grad_normed
+    out_total, qkv_total, up_sum, output, gain_terms, grad_normed = barrier(
+        out_total, qkv_total, up_sum, output, gain_terms, grad_normed
     )
 
     grad_normed = grad_normed.astype(f32)
     inv_in = rms_scale(inputs)
     hat_in = inputs * inv_in
-    attn_gain_term = jnp.sum(grad_normed * hat_in, axis=0)
     input_grad = (grad_state + rms_back(grad_normed * gain_attn, hat_in, inv_in)).astype(bf16)
-    gain_terms = sum_small(jnp.concatenate([attn_gain_term[None], gain_terms], axis=0))
-    gain_terms = total_dp(gain_terms, [scatter_one(gain_terms, shift, 1) for shift in (1, 2, 3)], 1)
     return (
         output,
         input_grad,

time: 1540 us -> 1350 us (0.88)
  waiting for transfers between devices: 469 us -> 350 us
  local copies, waits for them, and re-layouts: 132 us -> 75.4 us
  blocking collectives: 47.8 us -> 0 us
  other arithmetic: 118 us -> 138 us
    ppermute x37 -> x35, waiting for transfers between devices: 246 us -> 189 us  [swap_dp(): return lax.ppermute(part, 'dp', swap_partners(lax.axis_size('dp'), shift))]
    all_gather x3 -> x0, blocking collectives: 47.8 us -> none  [sum_small(): return jnp.sum(lax.all_gather(array, axes, axis=0, tiled=False), axis=0)]
    all_to_all x1, waiting for transfers between devices: 25.4 us -> 0.01 us  [on_device(): lax.all_to_all(table, 'ctx', split_axis=0, concat_axis=0, tiled=True)]
    slice x14 -> x0, local copies, waits for them, and re-layouts: 22.1 us -> none  [the longest x4 6.67 us: on_device(): other[:, qkv_columns:]]
    ppermute x18 -> x36, waiting for transfers between devices: 123 us -> 102 us  [the longest x12 68 us: step(): lax.ppermute(from_above, 'ctx', down)]
    all_to_all x1, waiting for transfers between devices: 44 us -> 27.4 us  [on_device(): lax.all_to_all(attended.reshape(peers, count_rows, own_width), 'ctx', spl...]
    reshape x9 -> x0, local copies, waits for them, and re-layouts: 16.2 us -> none  [the longest x4 7.94 us: on_device(): other[:, :qkv_columns].reshape(rows_dp, 3 * own_width)]
    ppermute x18 -> x36, starting transfers between devices: 57.3 us -> 66.6 us  [the longest x12 33 us: step(): lax.ppermute(from_below, 'ctx', up)]
  transfers between devices with their start and end apart: 78 -> 98, of which waited for: 27 -> 26; matrix products, arithmetic and copies ran while one was open for 24% -> 24% of each run, Pallas kernels for 28% -> 32%
where the time goes in v3:
time: 1350 us; the launch traced here: 1340 us
  Pallas kernels  479 us (35%)
  waiting for transfers between devices  350 us (26%)
  matrix products  141 us (10%)
  other arithmetic  138 us (10%)
  starting transfers between devices  134 us (10%)
  local copies, waits for them, and re-layouts  75.4 us (6%)
  between operations  25 us (2%)
    pallas_call x4, Pallas kernels, expert_unit(): pl.pallas_call(expert_kernel, grid_spec=pltpu.PrefetchScalarGridSpec(num_...  196 us
    ppermute x35, waiting for transfers between devices, swap_dp(): return lax.ppermute(part, 'dp', swap_partners(lax.axis_size('dp'), shift))  189 us
    pallas_call x1, Pallas kernels, attention_backward(): pl.pallas_call(functools.partial(backward_kernel, tile, prompt_tiles, blo...  68.9 us
    ppermute x12, waiting for transfers between devices, step(): lax.ppermute(from_above, 'ctx', down)  68 us
    pallas_call x1, Pallas kernels, attention_forward(): pl.pallas_call(functools.partial(forward_kernel, tile, prompt_tiles, bloc...  62.2 us
    pallas_call x1, Pallas kernels, expert_out(): pl.pallas_call(out_kernel, grid=(peers // 2, experts), in_specs=[pl.Block...  45 us
    pallas_call x4, Pallas kernels, project(): pl.pallas_call(project_kernel, grid_spec=pltpu.PrefetchScalarGridSpec(num...  44.1 us
    ppermute x35, starting transfers between devices, swap_dp(): return lax.ppermute(part, 'dp', swap_partners(lax.axis_size('dp'), shift))  40.5 us
  transfers between devices with their start and end apart: 98, of which 26 were waited for; matrix products, arithmetic and copies ran while one was open for 24% of the time, Pallas kernels for 32%

profile of v3, /device:TPU:0, one launch (start us, length us, event | category | flops | bytes accessed | tf_op | source)
XLA Modules:
  0.0 1343.0 jit_solution(5861006394817417932)
XLA Ops:
  28.0 9.7 collective-permute-done.3
  45.6 15.2 %collective-permute-done.7.refs_2_ = bf16[512,768]{1,0:T(8,128)(2,1)} collective-permute-done((bf16[512,768]{1,0:T(8,128)(2,1)S(1)}, bf16[512,768]{1,0:T(8,128)(2,1)}, u32[]{:S(2)}, u32[]{:S(2)}) %collective-permute-start.7) | collective-permute-done | bytes 786464 | tf_op jit(solution)/shard_map/ppermute | solution.py:388
  81.1 10.6 project.4
  91.7 26.0 %collective-permute-done.13 = bf16[256,2048]{1,0:T(8,128)(2,1)S(1)} collective-permute-done((bf16[256,2048]{1,0:T(8,128)(2,1)}, bf16[256,2048]{1,0:T(8,128)(2,1)S(1)}, u32[]{:S(2)}, u32[]{:S(2)}) %collective-permute-start.13) | collective-permute-done | bytes 1048608 | tf_op jit(solution)/shard_map/ppermute | solution.py:388
  131.4 10.6 project.5
  142.0 33.2 %collective-permute-done.17 = bf16[256,2048]{1,0:T(8,128)(2,1)S(1)} collective-permute-done((bf16[256,2048]{1,0:T(8,128)(2,1)}, bf16[256,2048]{1,0:T(8,128)(2,1)S(1)}, u32[]{:S(2)}, u32[]{:S(2)}) %collective-permute-start.17) | collective-permute-done | bytes 1048608 | tf_op jit(solution)/shard_map/ppermute | solution.py:388
  178.4 11.2 project.6
  207.8 11.8 project.7
  256.7 62.2 %attention_forward.1 = (bf16[4096,256]{1,0:T(8,128)(2,1)}, f32[2,8,512]{2,1,0:T(8,128)}, bf16[4096,256]{1,0:T(8,128)(2,1)}, bf16[4096,256]{1,0:T(8,128)(2,1)}, bf16[4096,256]{1,0:T(8,128)(2,1)}) custom-call(s32[16]{0:T(128)} %get-tuple-element.248.place, s32[8]{0:T(128)} %compare_select_fusion.first_tile, f32[4096,768]{1,0:T(8,128)} %get-tuple-element.249.raw_q.raw_k.raw_v, ...), custom_call_target="tpu_custom_call" | custom-call | flops 17179869184 | bytes 33554432 | tf_op jit(solution)/shard_map/attention_forward/pallas_call | solution.py:234
  335.5 9.2 join.5
  368.8 27.4 %all-to-all-done.1 = bf16[8,512,256]{1,2,0:T(8,128)(2,1)} async-done(((bf16[8,512,256]{1,2,0:T(8,128)(2,1)}), bf16[8,512,256]{1,2,0:T(8,128)(2,1)}, u32[]{:S(2)}, u32[]{:S(2)}) %all-to-all-start.1) | async-done | bytes 2097184 | tf_op jit(solution)/shard_map/all_to_all | solution.py:916
  417.4 48.9 %expert_unit.4 = (bf16[8,2,288,2048]{3,2,1,0:T(8,128)(2,1)}, bf16[8,2,288,2048]{3,2,1,0:T(8,128)(2,1)}, bf16[8,2,288,1024]{3,2,1,0:T(8,128)(2,1)}, bf16[8,2,288,...) custom-call(s32[2]{0:T(128)} %pad_add_fusion.6.unit, ...), custom_call_target="tpu_custom_call" | custom-call | tf_op jit(solution)/shard_map/expert_unit/pallas_call | solution.py:676
  472.6 49.1 %expert_unit.5 = (bf16[8,2,288,2048]{3,2,1,0:T(8,128)(2,1)}, bf16[8,2,288,2048]{3,2,1,0:T(8,128)(2,1)}, bf16[8,2,288,1024]{3,2,1,0:T(8,128)(2,1)}, bf16[8,2,288,...) custom-call(s32[2]{0:T(128)} %pad_add_fusion.7.unit, ...), custom_call_target="tpu_custom_call", output_to_operand_aliasing={{0}: (10, {}), {1}: (11, {}), {2}: (12, {}), {3}: (13, {}),... | custom-call | tf_op jit(solution)/shard_map/expert_unit/pallas_call | solution.py:676
  528.8 49.0 %expert_unit.6 = (bf16[8,2,288,2048]{3,2,1,0:T(8,128)(2,1)}, bf16[8,2,288,2048]{3,2,1,0:T(8,128)(2,1)}, bf16[8,2,288,1024]{3,2,1,0:T(8,128)(2,1)}, bf16[8,2,288,...) custom-call(s32[2]{0:T(128)} %pad_add_fusion.8.unit, ...), custom_call_target="tpu_custom_call", output_to_operand_aliasing={{0}: (10, {}), {1}: (11, {}), {2}: (12, {}), {3}: (13, {}),... | custom-call | tf_op jit(solution)/shard_map/expert_unit/pallas_call | solution.py:676
  584.9 49.2 %expert_unit.7 = (bf16[8,2,288,2048]{3,2,1,0:T(8,128)(2,1)}, bf16[8,2,288,2048]{3,2,1,0:T(8,128)(2,1)}, bf16[8,2,288,1024]{3,2,1,0:T(8,128)(2,1)}, bf16[8,2,288,...) custom-call(s32[2]{0:T(128)} %pad_add_fusion.5.unit, ...), custom_call_target="tpu_custom_call", output_to_operand_aliasing={{0}: (10, {}), {1}: (11, {}), {2}: (12, {}), {3}: (13, {}),... | custom-call | tf_op jit(solution)/shard_map/expert_unit/pallas_call | solution.py:676
  634.2 45.0 %expert_out.1 = bf16[8,512,2048]{2,1,0:T(8,128)(2,1)} custom-call(bf16[8,2,288,1024]{3,2,1,0:T(8,128)(2,1)} %get-tuple-element.321.hidden, bf16[2,1024,2048]{2,1,0:T(8,128)(2,1)} %join.6.w_down, s32[8,2,512]{2,1,0:T(2,128)} %copy.198.slots, f32[8,2,512]{2,1,0:T(2,128)} %get-tuple-element.273.gates, s32[8,512,2]{2,1,0:T(8,128)} %select_bitcast_fusion.columns), custom_call_target="tpu_custom_call" | custom-call | tf_op jit(solution)/shard_map/expert_out/pallas_call | solution.py:737
  679.2 26.9 %bitcast_convert_fusion.2 = bf16[2,1024,2048]{2,1,0:T(8,128)(2,1)} fusion(bf16[8,2,288,1024]{3,2,1,0:T(8,128)(2,1)} %get-tuple-element.321.hidden, bf16[8,2,288,2048]{3,2,1,0:T(8,128)(2,1)} %get-tuple-element.322), kind=kOutput, calls=%fused_computation.3 | convolution fusion | flops 19331547136 | bytes 36700160 | tf_op jit(solution)/shard_map/sncf,sncd->nfd/dot_general | solution.py:973
  713.4 27.6 %bitcast_convert_fusion = bf16[2,2048,1024]{2,1,0:T(8,128)(2,1)} fusion(bf16[8,2,288,2048]{3,2,1,0:T(8,128)(2,1)} %get-tuple-element.325, bf16[8,2,288,1024]{3,2,1,0:T(8,128)(2,1)} %get-tuple-element.327), kind=kOutput, calls=%fused_computation.1 | convolution fusion | flops 19331547136 | bytes 36700160 | tf_op jit(solution)/shard_map/sncd,sncf->ndf/dot_general | solution.py:978
  741.0 24.9 %bitcast_convert_fusion.1 = bf16[2,2048,1024]{2,1,0:T(8,128)(2,1)} fusion(bf16[8,2,288,2048]{3,2,1,0:T(8,128)(2,1)} %get-tuple-element.325, bf16[8,2,288,1024]{3,2,1,0:T(8,128)(2,1)S(1)} %bitcast.143), kind=kOutput, calls=%fused_computation.2 | convolution fusion | flops 19331547136 | bytes 36700160 | tf_op jit(solution)/shard_map/sncd,sncf->ndf/dot_general | solution.py:977
  765.9 37.6 %collective-permute-done.43 = bf16[2,256,2048]{2,1,0:T(8,128)(2,1)} collective-permute-done((bf16[2,256,2048]{2,1,0:T(8,128)(2,1)S(1)}, bf16[2,256,2048]{2,1,0:T(8,128)(2,1)}, u32[]{:S(2)}, u32[]{:S(2)}) %collective-permute-start.43) | collective-permute-done | bytes 2097184 | tf_op jit(solution)/shard_map/ppermute | solution.py:388
  863.1 29.7 %collective-permute-done.47 = bf16[2,512,1024]{2,1,0:T(8,128)(2,1)} collective-permute-done((bf16[2,512,1024]{2,1,0:T(8,128)(2,1)}, bf16[2,512,1024]{2,1,0:T(8,128)(2,1)}, u32[]{:S(2)}, u32[]{:S(2)}) %collective-permute-start.47) | collective-permute-done | bytes 2097184 | tf_op jit(solution)/shard_map/ppermute | solution.py:388
  893.9 28.2 %all-to-all-done.2 = bf16[8,512,256]{2,1,0:T(8,128)(2,1)} async-done(((bf16[8,512,256]{2,1,0:T(8,128)(2,1)}), bf16[8,512,256]{2,1,0:T(8,128)(2,1)}, u32[]{:S(2)}, u32[]{:S(2)}) %all-to-all-start.2) | async-done | bytes 2097184 | tf_op jit(solution)/shard_map/all_to_all | solution.py:995
  927.6 68.9 %attention_backward.1 = (f32[4096,256]{1,0:T(8,128)}, f32[4096,256]{1,0:T(8,128)}, bf16[4096,256]{1,0:T(8,128)(2,1)}) custom-call(s32[16]{0:T(128)} %get-tuple-element.248.place, s32[8]{0:T(128)} %compare_select_fusion.first_tile, bf16[4096,256]{1,0:T(8,128)(2,1)} %get-tuple-element.250.queries, bf16[4096,256]{1,0:T(8,128)(2,1)} %get-tuple-element.251.keys, ...), custom_call_target="tpu_custom_call" | custom-call | flops 21474836480 | bytes 33554432 | tf_op jit(solution)/shard_map/attention_backward/pallas_call | solution.py:290
  996.5 9.1 multiply_reduce_fusion.2
  1021.7 20.1 %convolution_convert_fusion = bf16[4096,2048]{1,0:T(8,128)(2,1)} fusion(bf16[2048,768]{1,0:T(8,128)(2,1)S(1)} %copy-done.3, bf16[4096,256]{1,0:T(8,128)(2,1)} %get-tuple-element.341, bf16[4096,256]{1,0:T(8,128)(2,1)} %get-tuple-element.404, bf16[4096,256]{1,0:T(8,128)(2,1)} %get-tuple-element.403), kind=kOutput, calls=%fused_computation.5 | convolution fusion | flops 12912164864 | bytes 26214400 | tf_op jit(solution)/shard_map/dot_general | solution.py:1044
  1063.7 19.3 %convolution_convert_fusion.2 = bf16[2048,768]{1,0:T(8,128)(2,1)S(1)} fusion(bf16[4096,2048]{1,0:T(8,128)(2,1)} %get-tuple-element.239, bf16[4096,768]{1,0:T(8,128)(2,1)} %pad_maximum_fusion), kind=kOutput, calls=%fused_computation.46 | convolution fusion | flops 12886474752 | bytes 26214400 | tf_op jit(solution)/shard_map/dot_general | solution.py:1061
  1087.2 10.2 multiply_reduce_fusion
  1104.6 14.8 %collective-permute-done.57 = bf16[512,768]{1,0:T(8,128)(2,1)S(1)} collective-permute-done((bf16[512,768]{1,0:T(8,128)(2,1)S(1)}, bf16[512,768]{1,0:T(8,128)(2,1)S(1)}, u32[]{:S(2)}, u32[]{:S(2)}) %collective-permute-start.57) | collective-permute-done | bytes 786464 | tf_op jit(solution)/shard_map/ppermute | solution.py:388
  1133.2 14.6 %collective-permute-done.62 = bf16[64,2048]{1,0:T(8,128)(2,1)S(1)} collective-permute-done((bf16[64,2048]{1,0:T(8,128)(2,1)S(1)}, bf16[64,2048]{1,0:T(8,128)(2,1)S(1)}, u32[]{:S(2)}, u32[]{:S(2)}) %collective-permute-start.62) | collective-permute-done | bytes 262176 | tf_op jit(solution)/shard_map/ppermute | solution.py:367
  1163.6 31.1 %collective-permute-done.60 = bf16[64,2048]{1,0:T(8,128)(2,1)S(1)} collective-permute-done((bf16[64,2048]{1,0:T(8,128)(2,1)S(1)}, bf16[64,2048]{1,0:T(8,128)(2,1)S(1)}, u32[]{:S(2)}, u32[]{:S(2)}) %collective-permute-start.60) | collective-permute-done | bytes 262176 | tf_op jit(solution)/shard_map/ppermute | solution.py:366
  1228.6 42.6 %collective-permute-done.70 = bf16[64,2048]{1,0:T(8,128)(2,1)S(1)} collective-permute-done((bf16[64,2048]{1,0:T(8,128)(2,1)}, bf16[64,2048]{1,0:T(8,128)(2,1)S(1)}, u32[]{:S(2)}, u32[]{:S(2)}) %collective-permute-start.70) | collective-permute-done | bytes 262176 | tf_op jit(solution)/shard_map/ppermute | solution.py:367
  1296.1 10.5 collective-permute-done.76
  (491 shorter events, 433.5 us)
Async XLA Ops:
  7.2 242.0 %all-gather.3.cloned.1.call-start = ((), (), s32[]{:S(2)}) async-start(), calls=%async_computation.7 | async-start | bytes 10485760 | tf_op jit(solution)/shard_map/all_gather | solution.py:845
  7.3 54.8 %collective-permute-start.2 = (bf16[512,2048]{1,0:T(8,128)(2,1)}, bf16[512,2048]{1,0:T(8,128)(2,1)}, u32[]{:S(2)}, u32[]{:S(2)}) collective-permute-start(bf16[512,2048]{1,0:T(8,128)(2,1)} %own.1), channel_id=1, source_target_pairs={{0,1},{1,0},{2,3},{3,2},{4,5},{5,4},{6,7},{7,6},{8,9},{9,8},{10,11... | collective-permute-start | bytes 6291464 | tf_op jit(solution)/shard_map/ppermute | solution.py:371
  7.8 54.3 %collective-permute-start.1 = (bf16[512,2048]{1,0:T(8,128)(2,1)}, bf16[512,2048]{1,0:T(8,128)(2,1)}, u32[]{:S(2)}, u32[]{:S(2)}) collective-permute-start(bf16[512,2048]{1,0:T(8,128)(2,1)} %own.1), channel_id=1, source_target_pairs={{2,0},{3,1},{4,2},{5,3},{6,4},{7,5},{10,8},{11,9},{12,10},{13,11},... | collective-permute-start | bytes 6291464 | tf_op jit(solution)/shard_map/ppermute | solution.py:367
  62.1 344.4 %all-gather.5.cloned.1.call-start = ((), (), s32[]{:S(2)}) async-start(), calls=%async_computation.8 | async-start | bytes 18874368 | tf_op jit(solution)/shard_map/all_gather | solution.py:878
  194.2 55.0 %collective-permute-start.23 = (bf16[1024,2048]{1,0:T(8,128)(2,1)}, bf16[1024,2048]{1,0:T(8,128)(2,1)}, u32[]{:S(2)}, u32[]{:S(2)}) collective-permute-start(bf16[1024,2048]{1,0:T(8,128)(2,1)} %pad_maximum_fusion.1.refs_0_), channel_id=1, source_target_pairs={{0,1},{1,0},{2,3},{3,2},{4,5},{5,4},{6,7},{7,6},{8,9},{9,8},{10,11... | collective-permute-start | bytes 12582920 | tf_op jit(solution)/shard_map/ppermute | solution.py:371
  249.2 70.7 %collective-permute-start.27 = (bf16[2,512,1024]{2,1,0:T(8,128)(2,1)}, bf16[2,512,1024]{2,1,0:T(8,128)(2,1)}, u32[]{:S(2)}, u32[]{:S(2)}) collective-permute-start(bf16[2,512,1024]{2,1,0:T(8,128)(2,1)} %refs_0_.1), channel_id=1, source_target_pairs={{0,16},{8,24},{16,0},{24,8},{1,17},{9,25},{17,1},{25,9},{2,18},{10... | collective-permute-start | bytes 6291464 | tf_op jit(solution)/shard_map/ppermute | solution.py:388
  249.4 70.5 %collective-permute-start.26 = (bf16[2,512,1024]{2,1,0:T(8,128)(2,1)}, bf16[2,512,1024]{2,1,0:T(8,128)(2,1)}, u32[]{:S(2)}, u32[]{:S(2)}) collective-permute-start(bf16[2,512,1024]{2,1,0:T(8,128)(2,1)} %refs_0_.1), channel_id=1, source_target_pairs={{0,8},{8,0},{16,24},{24,16},{1,9},{9,1},{17,25},{25,17},{2,10},{10... | collective-permute-start | bytes 6291464 | tf_op jit(solution)/shard_map/ppermute | solution.py:388
  253.4 65.5 %collective-permute-start.29 = (bf16[2,128,2048]{2,1,0:T(8,128)(2,1)S(1)}, bf16[2,128,2048]{2,1,0:T(8,128)(2,1)S(1)}, u32[]{:S(2)}, u32[]{:S(2)}) collective-permute-start(bf16[2,128,2048]{2,1,0:T(8,128)(2,1)S(1)} %slice.73), channel_id=1, source_target_pairs={{0,8},{8,0},{16,24},{24,16},{1,9},{9,1},{17,25},{25,17},{2,10},{10... | collective-permute-start | bytes 3145736 | tf_op jit(solution)/shard_map/ppermute | solution.py:388
  254.8 64.1 %collective-permute-start.28 = (bf16[2,128,2048]{2,1,0:T(8,128)(2,1)S(1)}, bf16[2,128,2048]{2,1,0:T(8,128)(2,1)S(1)}, u32[]{:S(2)}, u32[]{:S(2)}) collective-permute-start(bf16[2,128,2048]{2,1,0:T(8,128)(2,1)S(1)} %slice.72), channel_id=1, source_target_pairs={{0,16},{8,24},{16,0},{24,8},{1,17},{9,25},{17,1},{25,9},{2,18},{10... | collective-permute-start | bytes 3145736 | tf_op jit(solution)/shard_map/ppermute | solution.py:388
  323.8 72.4 %all-to-all-start.1 = ((bf16[8,512,256]{1,2,0:T(8,128)(2,1)}), bf16[8,512,256]{1,2,0:T(8,128)(2,1)}, u32[]{:S(2)}, u32[]{:S(2)}) async-start(bf16[8,512,256]{1,2,0:T(8,128)(2,1)} %copy.197), calls=%async_computation.1 | async-start | bytes 4194304 | tf_op jit(solution)/shard_map/all_to_all | solution.py:916
  328.4 475.2 %reduce-scatter.4.cloned.1.call-start = ((), (), s32[]{:S(2)}) async-start(), calls=%async_computation.9 | async-start | bytes 18874368 | tf_op jit(solution)/shard_map/reduce_scatter | solution.py:968
  406.6 59.7 %collective-permute-start.33 = (bf16[512,2048]{1,0:T(8,128)(2,1)S(1)}, bf16[512,2048]{1,0:T(8,128)(2,1)}, u32[]{:S(2)}, u32[]{:S(2)}) collective-permute-start(bf16[512,2048]{1,0:T(8,128)(2,1)S(1)} %multiply_convert_fusion.2.own), channel_id=1, source_target_pairs={{2,0},{3,1},{4,2},{5,3},{6,4},{7,5},{10,8},{11,9},{12,10},{13,11},... | collective-permute-start | bytes 6291464 | tf_op jit(solution)/shard_map/ppermute | solution.py:367
  407.9 58.4 %collective-permute-start.32 = (bf16[512,2048]{1,0:T(8,128)(2,1)S(1)}, bf16[512,2048]{1,0:T(8,128)(2,1)}, u32[]{:S(2)}, u32[]{:S(2)}) collective-permute-start(bf16[512,2048]{1,0:T(8,128)(2,1)S(1)} %multiply_convert_fusion.2.own), channel_id=1, source_target_pairs={{0,2},{1,3},{2,4},{3,5},{4,6},{5,7},{8,10},{9,11},{10,12},{11,13},... | collective-permute-start | bytes 6291464 | tf_op jit(solution)/shard_map/ppermute | solution.py:366
  468.3 53.4 %collective-permute-start.36 = (bf16[512,2048]{1,0:T(8,128)(2,1)}, bf16[512,2048]{1,0:T(8,128)(2,1)}, u32[]{:S(2)}, u32[]{:S(2)}) collective-permute-start(bf16[512,2048]{1,0:T(8,128)(2,1)} %collective-permute-done.33), channel_id=1, source_target_pairs={{2,0},{3,1},{4,2},{5,3},{10,8},{11,9},{12,10},{13,11},{18,16},{19,... | collective-permute-start | bytes 6291464 | tf_op jit(solution)/shard_map/ppermute | solution.py:367
  634.1 414.1 %reduce-scatter.6.cloned.1.call-start = ((), (), s32[]{:S(2)}) async-start(), calls=%async_computation.10 | async-start | bytes 18874368 | tf_op jit(solution)/shard_map/reduce_scatter | solution.py:983
  709.8 56.1 %collective-permute-start.44 = (bf16[2,256,2048]{2,1,0:T(8,128)(2,1)S(1)}, bf16[2,256,2048]{2,1,0:T(8,128)(2,1)}, u32[]{:S(2)}, u32[]{:S(2)}) collective-permute-start(bf16[2,256,2048]{2,1,0:T(8,128)(2,1)S(1)} %get-tuple-element.410), channel_id=1, source_target_pairs={{0,24},{8,16},{16,8},{24,0},{1,25},{9,17},{17,9},{25,1},{2,26},{10... | collective-permute-start | bytes 6291464 | tf_op jit(solution)/shard_map/ppermute | solution.py:388
  711.0 92.6 %collective-permute-start.43 = (bf16[2,256,2048]{2,1,0:T(8,128)(2,1)S(1)}, bf16[2,256,2048]{2,1,0:T(8,128)(2,1)}, u32[]{:S(2)}, u32[]{:S(2)}) collective-permute-start(bf16[2,256,2048]{2,1,0:T(8,128)(2,1)S(1)} %get-tuple-element.411), channel_id=1, source_target_pairs={{0,16},{8,24},{16,0},{24,8},{1,17},{9,25},{17,1},{25,9},{2,18},{10... | collective-permute-start | bytes 6291464 | tf_op jit(solution)/shard_map/ppermute | solution.py:388
  712.2 91.3 %collective-permute-start.42 = (bf16[2,256,2048]{2,1,0:T(8,128)(2,1)S(1)}, bf16[2,256,2048]{2,1,0:T(8,128)(2,1)}, u32[]{:S(2)}, u32[]{:S(2)}) collective-permute-start(bf16[2,256,2048]{2,1,0:T(8,128)(2,1)S(1)} %get-tuple-element.412), channel_id=1, source_target_pairs={{0,8},{8,0},{16,24},{24,16},{1,9},{9,1},{17,25},{25,17},{2,10},{10... | collective-permute-start | bytes 6291464 | tf_op jit(solution)/shard_map/ppermute | solution.py:388
  832.1 89.9 %all-to-all-start.2 = ((bf16[8,512,256]{2,1,0:T(8,128)(2,1)}), bf16[8,512,256]{2,1,0:T(8,128)(2,1)}, u32[]{:S(2)}, u32[]{:S(2)}) async-start(bf16[8,512,256]{2,1,0:T(8,128)(2,1)} %bitcast.134), calls=%async_computation.3 | async-start | bytes 4194304 | tf_op jit(solution)/shard_map/all_to_all | solution.py:995
  838.3 488.5 %reduce-scatter.8.cloned.1.call-start = ((), (), s32[]{:S(2)}) async-start(), calls=%async_computation.11 | async-start | bytes 18874368 | tf_op jit(solution)/shard_map/reduce_scatter | solution.py:1049
  848.2 148.3 %collective-permute-start.48 = (bf16[2,512,1024]{2,1,0:T(8,128)(2,1)}, bf16[2,512,1024]{2,1,0:T(8,128)(2,1)S(1)}, u32[]{:S(2)}, u32[]{:S(2)}) collective-permute-start(bf16[2,512,1024]{2,1,0:T(8,128)(2,1)} %get-tuple-element.407), channel_id=1, source_target_pairs={{0,24},{8,16},{16,8},{24,0},{1,25},{9,17},{17,9},{25,1},{2,26},{10... | collective-permute-start | bytes 6291464 | tf_op jit(solution)/shard_map/ppermute | solution.py:388
  925.4 71.1 %collective-permute-start.50 = (bf16[1,256,2048]{2,1,0:T(8,128)(2,1)S(1)}, bf16[1,256,2048]{2,1,0:T(8,128)(2,1)S(1)}, u32[]{:S(2)}, u32[]{:S(2)}) collective-permute-start(bf16[1,256,2048]{2,1,0:T(8,128)(2,1)S(1)} %get-tuple-element.417), channel_id=1, source_target_pairs={{0,16},{8,24},{16,0},{24,8},{1,17},{9,25},{17,1},{25,9},{2,18},{10... | collective-permute-start | bytes 3145736 | tf_op jit(solution)/shard_map/ppermute | solution.py:388
  926.2 70.3 %collective-permute-start.49 = (bf16[1,256,2048]{2,1,0:T(8,128)(2,1)S(1)}, bf16[1,256,2048]{2,1,0:T(8,128)(2,1)S(1)}, u32[]{:S(2)}, u32[]{:S(2)}) collective-permute-start(bf16[1,256,2048]{2,1,0:T(8,128)(2,1)S(1)} %get-tuple-element.418), channel_id=1, source_target_pairs={{0,8},{8,0},{16,24},{24,16},{1,9},{9,1},{17,25},{25,17},{2,10},{10... | collective-permute-start | bytes 3145736 | tf_op jit(solution)/shard_map/ppermute | solution.py:388
  1059.9 60.8 %all-to-all-start.3 = ((bf16[4,64,2048]{2,1,0:T(8,128)(2,1)}), bf16[4,64,2048]{2,1,0:T(8,128)(2,1)S(1)}, u32[]{:S(2)}, u32[]{:S(2)}) async-start(bf16[4,64,2048]{2,1,0:T(8,128)(2,1)} %bitcast.79), calls=%async_computation.5 | async-start | bytes 2097152 | tf_op jit(solution)/shard_map/all_to_all | solution.py:1053
  1125.4 69.4 %collective-permute-start.66 = (bf16[2,512,1024]{2,1,0:T(8,128)(2,1)}, bf16[2,512,1024]{2,1,0:T(8,128)(2,1)}, u32[]{:S(2)}, u32[]{:S(2)}) collective-permute-start(bf16[2,512,1024]{2,1,0:T(8,128)(2,1)} %get-tuple-element.405), channel_id=1, source_target_pairs={{0,16},{8,24},{16,0},{24,8},{1,17},{9,25},{17,1},{25,9},{2,18},{10... | collective-permute-start | bytes 6291464 | tf_op jit(solution)/shard_map/ppermute | solution.py:388
  1126.7 68.1 %collective-permute-start.65 = (bf16[2,512,1024]{2,1,0:T(8,128)(2,1)}, bf16[2,512,1024]{2,1,0:T(8,128)(2,1)}, u32[]{:S(2)}, u32[]{:S(2)}) collective-permute-start(bf16[2,512,1024]{2,1,0:T(8,128)(2,1)} %get-tuple-element.406), channel_id=1, source_target_pairs={{0,8},{8,0},{16,24},{24,16},{1,9},{9,1},{17,25},{25,17},{2,10},{10... | collective-permute-start | bytes 6291464 | tf_op jit(solution)/shard_map/ppermute | solution.py:388
  1131.9 62.8 %collective-permute-start.61 = (bf16[512,768]{1,0:T(8,128)(2,1)}, bf16[512,768]{1,0:T(8,128)(2,1)}, u32[]{:S(2)}, u32[]{:S(2)}) collective-permute-start(bf16[512,768]{1,0:T(8,128)(2,1)} %add_convert_fusion.2.own), channel_id=1, source_target_pairs={{2,0},{3,1},{4,2},{5,3},{6,4},{7,5},{10,8},{11,9},{12,10},{13,11},... | collective-permute-start | bytes 2359304 | tf_op jit(solution)/shard_map/ppermute | solution.py:367
  1198.1 76.6 %collective-permute-start.73 = (bf16[2,512,1024]{2,1,0:T(8,128)(2,1)}, bf16[2,512,1024]{2,1,0:T(8,128)(2,1)}, u32[]{:S(2)}, u32[]{:S(2)}) collective-permute-start(bf16[2,512,1024]{2,1,0:T(8,128)(2,1)} %constant_dynamic-slice_fusion.4), channel_id=1, source_target_pairs={{0,24},{8,16},{16,8},{24,0},{1,25},{9,17},{17,9},{25,1},{2,26},{10... | collective-permute-start | bytes 6291464 | tf_op jit(solution)/shard_map/ppermute | solution.py:388
  1213.2 61.1 %collective-permute-start.69 = (bf16[512,768]{1,0:T(8,128)(2,1)}, bf16[512,768]{1,0:T(8,128)(2,1)}, u32[]{:S(2)}, u32[]{:S(2)}) collective-permute-start(bf16[512,768]{1,0:T(8,128)(2,1)} %collective-permute-done.61), channel_id=1, source_target_pairs={{2,0},{3,1},{4,2},{5,3},{10,8},{11,9},{12,10},{13,11},{18,16},{19,... | collective-permute-start | bytes 2359304 | tf_op jit(solution)/shard_map/ppermute | solution.py:367
  1214.5 60.2 %collective-permute-start.67 = (bf16[512,768]{1,0:T(8,128)(2,1)}, bf16[512,768]{1,0:T(8,128)(2,1)}, u32[]{:S(2)}, u32[]{:S(2)}) collective-permute-start(bf16[512,768]{1,0:T(8,128)(2,1)} %copy-done.29), channel_id=1, source_target_pairs={{2,4},{3,5},{4,6},{5,7},{10,12},{11,13},{12,14},{13,15},{18,20},{1... | collective-permute-start | bytes 2359304 | tf_op jit(solution)/shard_map/ppermute | solution.py:366
  1216.1 55.1 %collective-permute-start.70 = (bf16[64,2048]{1,0:T(8,128)(2,1)}, bf16[64,2048]{1,0:T(8,128)(2,1)S(1)}, u32[]{:S(2)}, u32[]{:S(2)}) collective-permute-start(bf16[64,2048]{1,0:T(8,128)(2,1)} %copy-done.55), channel_id=1, source_target_pairs={{2,0},{3,1},{4,2},{5,3},{10,8},{11,9},{12,10},{13,11},{18,16},{19,... | collective-permute-start | bytes 786440 | tf_op jit(solution)/shard_map/ppermute | solution.py:367
  1218.3 54.5 %collective-permute-start.68 = (bf16[64,2048]{1,0:T(8,128)(2,1)S(1)}, bf16[64,2048]{1,0:T(8,128)(2,1)}, u32[]{:S(2)}, u32[]{:S(2)}) collective-permute-start(bf16[64,2048]{1,0:T(8,128)(2,1)S(1)} %collective-permute-done.60), channel_id=1, source_target_pairs={{2,4},{3,5},{4,6},{5,7},{10,12},{11,13},{12,14},{13,15},{18,20},{1... | collective-permute-start | bytes 786440 | tf_op jit(solution)/shard_map/ppermute | solution.py:366
  (148 other events, 3232.7 us)
Sparse Core Ops, SparseCore 0:
  62.2 134.0 all-gather.2
  197.9 189.3 all-gather.4
  634.2 169.0 reduce-scatter.3
  805.6 200.0 reduce-scatter.5
  1048.4 225.8 reduce-scatter.7

commit v4 on v3

--- a/solution.py
+++ b/solution.py
@@ -11,6 +11,7 @@
 TOP = 8
 BLK_DEV = 2
 LOG2E = 1.4426950408889634
+HEAD_DIM = 128
 
 epsilon = 1e-06
 masked_value = -1e30
@@ -61,6 +62,7 @@
     group, width = raw_q.shape
     tiles = group // tile
     blocks = group // block_len
+    columns = [slice(first, first + HEAD_DIM) for first in range(0, width, HEAD_DIM)]
 
     def bring(block, carry):
         source = pl.ds(pl.multiple_of(place[block] * block_len, block_len), block_len)
@@ -79,39 +81,50 @@
 
     def query_tile(index, carry):
         first = pl.multiple_of(index * tile, tile)
-        query = queries[pl.ds(first, tile), :]
+        here = pl.ds(first, tile)
         seg_query = seg_row[pl.ds(index, 1), :]
 
-        def step(is_masked, at, state):
-            largest, total, running = state
+        def step(is_masked, at, states):
             key_first = pl.multiple_of(at * tile, tile)
-            scores = lax.dot_general(
-                keys[pl.ds(key_first, tile), :], query, NT, preferred_element_type=f32
-            ) * (scale * LOG2E)
+            there = pl.ds(key_first, tile)
             if is_masked:
-                allowed = tile_mask(seg_col[pl.ds(key_first, tile), :], seg_query, key_first, first)
-                scores = jnp.where(allowed, scores, masked_value)
-            new_largest = jnp.maximum(largest, jnp.max(scores, axis=0, keepdims=True))
-            shrink = jnp.exp2(largest - new_largest)
-            terms = jnp.exp2(scores - new_largest)
-            total = total * shrink + jnp.sum(terms, axis=0, keepdims=True)
-            running = running * shrink + jnp.dot(
-                values_t[:, pl.ds(key_first, tile)], terms.astype(bf16), preferred_element_type=f32
+                allowed = tile_mask(seg_col[there, :], seg_query, key_first, first)
+            every = [
+                lax.dot_general(
+                    keys[there, head], queries[here, head], NT, preferred_element_type=f32
+                )
+                for head in columns
+            ]
+            after = []
+            for scores, head, (largest, total, running) in zip(every, columns, states):
+                scores = scores * (scale * LOG2E)
+                if is_masked:
+                    scores = jnp.where(allowed, scores, masked_value)
+                new_largest = jnp.maximum(largest, jnp.max(scores, axis=0, keepdims=True))
+                shrink = jnp.exp2(largest - new_largest)
+                terms = jnp.exp2(scores - new_largest)
+                total = total * shrink + jnp.sum(terms, axis=0, keepdims=True)
+                running = running * shrink + jnp.dot(
+                    values_t[head, there], terms.astype(bf16), preferred_element_type=f32
+                )
+                after.append((new_largest, total, running))
+            return after
+
+        states = [
+            (
+                jnp.full((1, tile), masked_value, f32),
+                jnp.zeros((1, tile), f32),
+                jnp.zeros((HEAD_DIM, tile), f32),
             )
-            return (new_largest, total, running)
-
-        state = (
-            jnp.full((1, tile), masked_value, f32),
-            jnp.zeros((1, tile), f32),
-            jnp.zeros((width, tile), f32),
+            for _ in columns
+        ]
+        states = lax.fori_loop(
+            0, jnp.minimum(index, prompt_tiles), functools.partial(step, False), states
         )
-        state = lax.fori_loop(
-            0, jnp.minimum(index, prompt_tiles), functools.partial(step, False), state
-        )
-        state = lax.fori_loop(first_tile[index], index + 1, functools.partial(step, True), state)
-        largest, total, running = state
-        lse[pl.ds(index, 1), :] = largest + jnp.log2(total)
-        out_logical[pl.ds(first, tile), :] = (running / total).T
+        states = lax.fori_loop(first_tile[index], index + 1, functools.partial(step, True), states)
+        for which, (head, (largest, total, running)) in enumerate(zip(columns, states)):
+            lse[which, pl.ds(index, 1), :] = largest + jnp.log2(total)
+            out_logical[here, head] = (running / total).T.astype(bf16)
         return carry
 
     lax.fori_loop(0, tiles, query_tile, 0)
@@ -119,7 +132,7 @@
     def send(block, carry):
         target = pl.ds(pl.multiple_of(place[block] * block_len, block_len), block_len)
         source = pl.ds(pl.multiple_of(block * block_len, block_len), block_len)
-        out[target, :] = out_logical[source, :].astype(bf16)
+        out[target, :] = out_logical[source, :]
         return carry
 
     lax.fori_loop(0, blocks, send, 0)
@@ -153,6 +166,7 @@
     group, width = queries.shape
     tiles = group // tile
     blocks = group // block_len
+    columns = [slice(first, first + HEAD_DIM) for first in range(0, width, HEAD_DIM)]
 
     def bring(block, carry):
         source = pl.ds(pl.multiple_of(place[block] * block_len, block_len), block_len)
@@ -165,42 +179,59 @@
     for index in range(tiles):
         rows = slice(index * tile, (index + 1) * tile)
         keys_t[:, rows] = keys[rows, :].T
-        delta[index : index + 1, :] = jnp.sum(total_q[rows, :].T, axis=0, keepdims=True)
+        for which, head in enumerate(columns):
+            delta[which, index : index + 1, :] = jnp.sum(
+                total_q[rows, head].T, axis=0, keepdims=True
+            )
     total_k[...] = jnp.zeros_like(total_k)
     total_v[...] = jnp.zeros_like(total_v)
 
     def query_tile(index, carry):
         first = pl.multiple_of(index * tile, tile)
-        query = queries[pl.ds(first, tile), :]
-        grad_tile = grad_here[pl.ds(first, tile), :]
+        here = pl.ds(first, tile)
         seg_query = seg_row[pl.ds(index, 1), :]
-        lse_tile = lse[pl.ds(index, 1), :]
-        delta_tile = delta[pl.ds(index, 1), :]
-
-        def step(is_masked, at, running):
+
+        def step(is_masked, at, states):
             key_first = pl.multiple_of(at * tile, tile)
-            here = pl.ds(key_first, tile)
-            scores = lax.dot_general(keys[here, :], query, NT, preferred_element_type=f32) * (
-                scale * LOG2E
-            )
-            probs = jnp.exp2(scores - lse_tile)
+            there = pl.ds(key_first, tile)
             if is_masked:
-                allowed = tile_mask(seg_col[here, :], seg_query, key_first, first)
-                probs = jnp.where(allowed, probs, 0.0)
-            dprobs = lax.dot_general(values[here, :], grad_tile, NT, preferred_element_type=f32)
-            dscores = (probs * (dprobs - delta_tile)).astype(bf16)
-            total_v[here, :] += jnp.dot(probs.astype(bf16), grad_tile, preferred_element_type=f32)
-            total_k[here, :] += jnp.dot(dscores, query, preferred_element_type=f32)
-            return running + jnp.dot(keys_t[:, here], dscores, preferred_element_type=f32)
-
-        running = jnp.zeros((width, tile), f32)
-        running = lax.fori_loop(
-            0, jnp.minimum(index, prompt_tiles), functools.partial(step, False), running
+                allowed = tile_mask(seg_col[there, :], seg_query, key_first, first)
+            every = [
+                (
+                    lax.dot_general(
+                        keys[there, head], queries[here, head], NT, preferred_element_type=f32
+                    ),
+                    lax.dot_general(
+                        values[there, head], grad_here[here, head], NT, preferred_element_type=f32
+                    ),
+                )
+                for head in columns
+            ]
+            after = []
+            for which, (head, running) in enumerate(zip(columns, states)):
+                scores, dprobs = every[which]
+                probs = jnp.exp2(scores * (scale * LOG2E) - lse[which, pl.ds(index, 1), :])
+                if is_masked:
+                    probs = jnp.where(allowed, probs, 0.0)
+                dscores = (probs * (dprobs - delta[which, pl.ds(index, 1), :])).astype(bf16)
+                total_v[there, head] += jnp.dot(
+                    probs.astype(bf16), grad_here[here, head], preferred_element_type=f32
+                )
+                total_k[there, head] += jnp.dot(
+                    dscores, queries[here, head], preferred_element_type=f32
+                )
+                after.append(
+                    running + jnp.dot(keys_t[head, there], dscores, preferred_element_type=f32)
+                )
+            return after
+
+        states = [jnp.zeros((HEAD_DIM, tile), f32) for _ in columns]
+        states = lax.fori_loop(
+            0, jnp.minimum(index, prompt_tiles), functools.partial(step, False), states
         )
-        running = lax.fori_loop(
-            first_tile[index], index + 1, functools.partial(step, True), running
-        )
-        total_q[pl.ds(first, tile), :] = running.T
+        states = lax.fori_loop(first_tile[index], index + 1, functools.partial(step, True), states)
+        for head, running in zip(columns, states):
+            total_q[here, head] = running.T
         return carry
 
     lax.fori_loop(0, tiles, query_tile, 0)
@@ -220,42 +251,37 @@
     raw, inv, gain_q, gain_k, seg_col, seg_row, place, first_tile, tile, prompt_tiles, block_len, scale
 ):
     group, width = raw.shape[0], raw.shape[1] // 3
-    head_dim = 128
-    heads = width // head_dim
+    heads = width // HEAD_DIM
     tiles = group // tile
 
     def part(which):
-        return pl.BlockSpec((group, head_dim), lambda h, *_: (0, which * heads + h))
+        return pl.BlockSpec((group, width), lambda i, *_: (0, which), pipeline_mode=pl.Buffered(1))
 
     def whole(shape):
-        return pl.BlockSpec(shape, lambda h, *_: (0,) * len(shape))
-
-    head = pl.BlockSpec((group, head_dim), lambda h, *_: (0, h))
+        return pl.BlockSpec(
+            shape, lambda i, *_: (0,) * len(shape), pipeline_mode=pl.Buffered(1)
+        )
+
+    head = whole((group, width))
     return pl.pallas_call(
         functools.partial(forward_kernel, tile, prompt_tiles, block_len, scale),
         grid_spec=pltpu.PrefetchScalarGridSpec(
             num_scalar_prefetch=2,
-            grid=(heads,),
+            grid=(1,),
             in_specs=[
                 part(0),
                 part(1),
                 part(2),
                 whole((group, 2)),
-                pl.BlockSpec((1, head_dim), lambda h, *_: (0, h)),
-                pl.BlockSpec((1, head_dim), lambda h, *_: (0, h)),
+                whole((1, width)),
+                whole((1, width)),
                 whole((group, 1)),
                 whole((tiles, tile)),
             ],
-            out_specs=[
-                head,
-                pl.BlockSpec((None, tiles, tile), lambda h, *_: (h, 0, 0)),
-                head,
-                head,
-                head,
-            ],
+            out_specs=[head, whole((heads, tiles, tile)), head, head, head],
             scratch_shapes=[
-                pltpu.VMEM((head_dim, group), bf16),
-                pltpu.VMEM((group, head_dim), f32),
+                pltpu.VMEM((width, group), bf16),
+                pltpu.VMEM((group, width), bf16),
             ],
         ),
         out_shape=[
@@ -265,11 +291,9 @@
             jax.ShapeDtypeStruct((group, width), bf16),
             jax.ShapeDtypeStruct((group, width), bf16),
         ],
-        compiler_params=pltpu.CompilerParams(vmem_limit_bytes=56 * 2**20),
+        compiler_params=pltpu.CompilerParams(vmem_limit_bytes=60 * 2**20),
         cost_estimate=pl.CostEstimate(
-            flops=2 * heads * group * group * head_dim * 2,
-            bytes_accessed=32 * group * width,
-            transcendentals=0,
+            flops=4 * group * group * width, bytes_accessed=24 * group * width, transcendentals=0
         ),
         name="attention_forward",
     )(place, first_tile, raw, raw, raw, inv, gain_q, gain_k, seg_col, seg_row)
@@ -279,24 +303,25 @@
     queries, keys, values, lse, out, grad_out, seg_col, seg_row, place, first_tile, tile, prompt_tiles, block_len, scale
 ):
     group, width = queries.shape
-    head_dim = 128
-    heads = width // head_dim
+    heads = width // HEAD_DIM
     tiles = group // tile
 
     def whole(shape):
-        return pl.BlockSpec(shape, lambda h, *_: (0,) * len(shape))
-
-    head = pl.BlockSpec((group, head_dim), lambda h, *_: (0, h))
+        return pl.BlockSpec(
+            shape, lambda i, *_: (0,) * len(shape), pipeline_mode=pl.Buffered(1)
+        )
+
+    head = whole((group, width))
     return pl.pallas_call(
         functools.partial(backward_kernel, tile, prompt_tiles, block_len, scale),
         grid_spec=pltpu.PrefetchScalarGridSpec(
             num_scalar_prefetch=2,
-            grid=(heads,),
+            grid=(1,),
             in_specs=[
                 head,
                 head,
                 head,
-                pl.BlockSpec((None, tiles, tile), lambda h, *_: (h, 0, 0)),
+                whole((heads, tiles, tile)),
                 head,
                 head,
                 whole((group, 1)),
@@ -304,12 +329,12 @@
             ],
             out_specs=[head, head, head],
             scratch_shapes=[
-                pltpu.VMEM((head_dim, group), bf16),
-                pltpu.VMEM((group, head_dim), bf16),
-                pltpu.VMEM((tiles, tile), f32),
-                pltpu.VMEM((group, head_dim), f32),
-                pltpu.VMEM((group, head_dim), f32),
-                pltpu.VMEM((group, head_dim), f32),
+                pltpu.VMEM((width, group), bf16),
+                pltpu.VMEM((group, width), bf16),
+                pltpu.VMEM((heads, tiles, tile), f32),
+                pltpu.VMEM((group, width), f32),
+                pltpu.VMEM((group, width), f32),
+                pltpu.VMEM((group, width), f32),
             ],
         ),
         out_shape=[
@@ -317,11 +342,9 @@
             jax.ShapeDtypeStruct((group, width), f32),
             jax.ShapeDtypeStruct((group, width), bf16),
         ],
-        compiler_params=pltpu.CompilerParams(vmem_limit_bytes=56 * 2**20),
+        compiler_params=pltpu.CompilerParams(vmem_limit_bytes=60 * 2**20),
         cost_estimate=pl.CostEstimate(
-            flops=5 * heads * group * group * head_dim,
-            bytes_accessed=32 * group * width,
-            transcendentals=0,
+            flops=5 * group * group * width, bytes_accessed=24 * group * width, transcendentals=0
         ),
         name="attention_backward",
     )(place, first_tile, queries, keys, values, lse, out, grad_out, seg_col, seg_row)
@@ -335,10 +358,6 @@
     earlier = holds[:, None, :] & (order[:, None, :] < order[:, :, None])
     slot = jnp.sum(earlier.astype(jnp.int32), axis=2)
     return (jnp.where(holds & (slot < capacity), slot, -1), gate)
-
-
-def tied(array, *after):
-    return lax.optimization_barrier((array, *after))[0]
 
 
 def barrier(*arrays):
@@ -559,17 +578,16 @@
     pl.when(pl.program_id(0) == 1)(lambda: work(other))
 
 
-def lay(at, own, other, out_shape, pieces, index, kept=()):
-    rows, columns = own.shape
-    block = (rows, columns // pieces)
+def lay(at, own, other, out_shape, block_columns, first, pieces, index, kept=()):
+    block = (out_shape[0], block_columns)
     return pl.pallas_call(
         lay_kernel,
         grid_spec=pltpu.PrefetchScalarGridSpec(
             num_scalar_prefetch=1,
             grid=(2, pieces),
-            in_specs=[pl.BlockSpec(block, lambda s, t, at: (0, t))] * 2
+            in_specs=[pl.BlockSpec(block, lambda s, t, at: (0, first + t))] * 2
             + [pl.BlockSpec(memory_space=pl.ANY)] * len(kept),
-            out_specs=pl.BlockSpec(block, lambda s, t, at: index(at[s], t)),
+            out_specs=pl.BlockSpec(block, lambda s, t, at: (0, index(at[s], t))),
         ),
         out_shape=jax.ShapeDtypeStruct(out_shape, f32),
         input_output_aliases={3: 0} if kept else {},
@@ -995,19 +1013,16 @@
     grad_attended = lax.all_to_all(
         grad_attn, "ctx", split_axis=0, concat_axis=0, tiled=True
     ).reshape(group_rows, own_width)
-    part_out = lax.dot_general(
-        attn_low, tied(grad_branch, grad_attn), TN, preferred_element_type=f32
-    ).astype(bf16)
-    part_out = part_out.reshape(groups, 2, half_rows, width)
-    out_theirs = line.other(lax.dynamic_index_in_dim(part_out, 1 - core, 1, keepdims=False))
-    part_out = lax.dynamic_index_in_dim(part_out, core, 1, keepdims=False).astype(f32)
+    part_out = lax.dot_general(attn_low, grad_branch, TN, preferred_element_type=f32).astype(bf16)
+    half = width // 2
+    out_theirs = line.other(lax.dynamic_slice_in_dim(part_out, (1 - core) * half, half, 1))
+    part_out = lax.dynamic_slice_in_dim(part_out, core * half, half, 1).astype(f32)
     part_out = (part_out + out_theirs.astype(f32)).astype(bf16)
     down_sum = total_dp(grad_down, down_pieces, 1)
     grad_attended, part_out, down_sum, *gate_pieces = barrier(
         grad_attended, part_out, down_sum, *gate_pieces
     )
-    gate_pieces.append(scatter_one(grad_gate, 3, 1))
-    out_pieces = [scatter_one(part_out, shift, 0) for shift in (1, 2)]
+    out_pieces = [scatter_one(part_out, shift, 0) for shift in (1, 2, 3)]
     grad_q, grad_k, grad_v = attention_backward(
         queries,
         keys,
@@ -1024,9 +1039,12 @@
         block_len,
         scale,
     )
-    grad_q, gate_last, grad_up, *out_pieces = barrier(grad_q, gate_pieces[2], grad_up, *out_pieces)
-    gate_pieces[2] = gate_last
-    out_pieces.append(scatter_one(part_out, 3, 0))
+    grad_q, grad_gate, *out_pieces = barrier(grad_q, grad_gate, *out_pieces)
+    gate_pieces.append(scatter_one(grad_gate, 3, 1))
+    out_sum = total_dp(part_out, out_pieces, 0).astype(bf16)
+    rows_dp = out_sum.shape[0]
+    share = half // line.chips
+    out_sum = out_sum.reshape(rows_dp, line.chips, share).transpose(1, 0, 2)
     hat_q = raw[:, :own_width] * inv_qk[:, 0:1]
     hat_k = raw[:, own_width : 2 * own_width] * inv_qk[:, 1:2]
     query_gain_term = jnp.sum(grad_q * hat_q, axis=0)
@@ -1043,15 +1061,11 @@
     grad_qkv = jnp.concatenate([grad_raw_q.astype(bf16), grad_raw_k.astype(bf16), grad_v], axis=1)
     part_normed = lax.dot_general(grad_qkv, w_own, NT, preferred_element_type=f32) * (1.0 / rep)
     part_normed = part_normed.astype(bf16)
-    part_normed, grad_qkv, mixed, grad_up, *out_pieces = barrier(
-        part_normed, grad_qkv, mixed, grad_up, *out_pieces
-    )
+    part_normed, mixed, grad_up, out_sum = barrier(part_normed, mixed, grad_up, out_sum)
     grad_normed = lax.psum_scatter(part_normed, "ctx", scatter_dimension=0, tiled=True)
 
-    out_sum = total_dp(part_out, out_pieces, 0).astype(bf16).reshape(half_rows, width)
-    out_share = half_rows // (peers // 2)
     out_sum = lax.all_to_all(
-        out_sum.reshape(peers // 2, out_share, width),
+        out_sum,
         "ctx",
         split_axis=0,
         concat_axis=0,
@@ -1060,7 +1074,6 @@
     )
     part_qkv = lax.dot_general(normed_all, grad_qkv, TN, preferred_element_type=f32).astype(bf16)
     qkv_pieces = [scatter_one(part_qkv, shift, 0) for shift in (1, 2, 3)]
-    gate_sum = total_dp(grad_gate, gate_pieces, 1)
     own_terms = jnp.stack([query_gain_term, key_gain_term]) * (1.0 / rep)
     spread = lax.dynamic_update_slice_in_dim(
         jnp.zeros((2, width), f32), own_terms, first_head * head_dim, 1
@@ -1069,54 +1082,85 @@
         jnp.sum(part_normed.astype(f32) * normed_all.astype(f32), axis=0) / gain_attn[0]
     )
     gain_terms = jnp.concatenate([attn_gain_term[None], spread, moe_gain_term[None]], axis=0)
-    gate_sum, out_sum, gain_terms, grad_up, *qkv_pieces = barrier(
-        gate_sum, out_sum, gain_terms, grad_up, *qkv_pieces
-    )
-    up_pieces = [scatter_one(grad_up, shift, 1) for shift in (1, 2)]
-    gain_terms = sum_small(gain_terms)
-    gain_terms = total_dp(gain_terms, [scatter_one(gain_terms, shift, 1) for shift in (1, 2, 3)], 1)
+    gain_pieces = [scatter_one(gain_terms, shift, 1) for shift in (1, 2, 3)]
+    output = (state + mixed.astype(f32)).astype(bf16)
+    out_sum, gain_terms, grad_up, grad_gate, output, *pieces = barrier(
+        out_sum, gain_terms, grad_up, grad_gate, output, *qkv_pieces, *gain_pieces, *gate_pieces
+    )
+    qkv_pieces, gain_pieces, gate_pieces = pieces[:3], pieces[3:6], pieces[6:]
+    gate_sum = total_dp(grad_gate, gate_pieces, 1)
+    gain_terms = total_dp(gain_terms, gain_pieces, 1)
     qkv_sum = total_dp(part_qkv, qkv_pieces, 0).astype(bf16)
     out_sum = jnp.sum(out_sum.astype(f32), axis=0).astype(bf16)
-    rows_dp = qkv_sum.shape[0]
-    own, chip = [qkv_sum, out_sum], line.chip
+    own, chip = jnp.concatenate([qkv_sum, out_sum], axis=1), line.chip
+    gain_shape = gain_terms.shape
+    row = own.shape[1]
+    gain_terms = gain_terms.reshape(-1)
+    gain_rows = (gain_terms.size // row + 16) // 16 * 16
+    gain_size = gain_terms.size
+    gain_terms = jnp.pad(gain_terms, (0, gain_rows * row - gain_size)).reshape(gain_rows, row)
+    own = jnp.concatenate([own, gain_terms.astype(bf16)], axis=0)
+    gain_terms = jnp.zeros((gain_rows, row), f32)
     below, above = own, own
     arrived = {}
     qkv_kept, out_kept = (), ()
     for turn in range(line.chips):
+        if turn + 1 < line.chips:
+            below, above = line.step(turn + 1, below, above)
         if turn > 0:
-            own, chips = zip(*[line.take(turn, {d: a[i] for d, a in arrived.items()}) for i in (0, 1)])
-            chip = chips[0]
-        if turn + 1 < line.chips:
-            steps = [line.step(turn + 1, b, a) for b, a in zip(below, above)]
-            below, above = [s[0] for s in steps], [s[1] for s in steps]
-        other = [line.other(part) for part in own]
+            own, chip = line.take(turn, arrived)
+        other = line.other(own)
+        gain_terms = gain_terms + own[rows_dp:].astype(f32) + other[rows_dp:].astype(f32)
         at = jnp.stack([2 * chip + core, 2 * chip + 1 - core]).astype(jnp.int32) // rep
         qkv_kept = [
             lay(
                 at,
-                own[0],
-                other[0],
+                own,
+                other,
                 (rows_dp, 3 * width),
+                own_width,
+                0,
                 3,
-                lambda p, t: (0, t * (peers // rep) + p),
+                lambda p, t: t * (width // own_width) + p,
                 qkv_kept,
             )
         ]
         at = jnp.stack([core * line.chips + chip, (1 - core) * line.chips + chip]).astype(jnp.int32)
-        out_kept = [
-            lay(at, own[1], other[1], (rows_dp, width), 1, lambda p, t: (p, 0), out_kept)
-        ]
+        if share % HEAD_DIM == 0 and 3 * own_width % share == 0:
+            out_kept = [
+                lay(
+                    at,
+                    own,
+                    other,
+                    (rows_dp, width),
+                    share,
+                    3 * own_width // share,
+                    1,
+                    lambda p, t: p,
+                    out_kept,
+                )
+            ]
+        else:
+            out_kept = list(out_kept) or [jnp.zeros((rows_dp, width), f32)]
+            for which, part in enumerate((own, other)):
+                out_kept[0] = lax.dynamic_update_slice_in_dim(
+                    out_kept[0], part[:rows_dp, 3 * own_width :].astype(f32), at[which] * share, 1
+                )
+        if turn == 0:
+            up_pieces = [scatter_one(grad_up, shift, 1) for shift in (1, 2)]
+        if turn == 1:
+            up_pieces.append(scatter_one(grad_up, 3, 1))
+        if turn == 2:
+            grad_up = total_dp(grad_up, up_pieces, 1)
+            up_pieces = []
         if turn + 1 < line.chips:
-            *both, qkv_kept[0], out_kept[0], grad_up = barrier(
-                *below, *above, qkv_kept[0], out_kept[0], grad_up, *up_pieces
-            )[: len(below) + len(above) + 3]
-            below, above = both[:2], both[2:]
-            if turn == 0:
-                up_pieces.append(scatter_one(grad_up, 3, 1))
+            below, above, qkv_kept[0], out_kept[0], grad_up, gate_sum, *up_pieces = barrier(
+                below, above, qkv_kept[0], out_kept[0], grad_up, gate_sum, *up_pieces
+            )
             arrived[-turn - 1], arrived[turn + 1] = below, above
     qkv_total, out_total = qkv_kept[0], out_kept[0]
-    up_sum = total_dp(grad_up, up_pieces, 1)
-    output = (state + mixed.astype(f32)).astype(bf16)
+    up_sum = grad_up
+    gain_terms = gain_terms.reshape(-1)[:gain_size].reshape(gain_shape)
     out_total, qkv_total, up_sum, output, gain_terms, grad_normed = barrier(
         out_total, qkv_total, up_sum, output, gain_terms, grad_normed
     )

time: 1350 us -> 1330 us (0.985)
  starting transfers between devices: 134 us -> 118 us
    ppermute x12 -> x9, waiting for transfers between devices: 31.1 us -> 1.08 us  [step(): lax.ppermute(from_below, 'ctx', up)]
    ppermute x35, waiting for transfers between devices: 189 us -> 208 us  [swap_dp(): return lax.ppermute(part, 'dp', swap_partners(lax.axis_size('dp'), shift))]
    ppermute x12 -> x9, waiting for transfers between devices: 68 us -> 86.3 us  [step(): lax.ppermute(from_above, 'ctx', down)]
    ppermute x12 -> x9, starting transfers between devices: 33 us -> 28.8 us  [step(): lax.ppermute(from_below, 'ctx', up)]
  transfers between devices with their start and end apart: 98 -> 84, of which waited for: 26 -> 27; matrix products, arithmetic and copies ran while one was open for 24% -> 25% of each run, Pallas kernels for 32% -> 32%
where the time goes in v4:
time: 1330 us; the launch traced here: 1320 us
  Pallas kernels  468 us (35%)
  waiting for transfers between devices  360 us (27%)
  matrix products  140 us (11%)
  other arithmetic  128 us (10%)
  starting transfers between devices  118 us (9%)
  local copies, waits for them, and re-layouts  84.4 us (6%)
  between operations  21.5 us (2%)
    ppermute x35, waiting for transfers between devices, swap_dp(): return lax.ppermute(part, 'dp', swap_partners(lax.axis_size('dp'), shift))  208 us
    pallas_call x4, Pallas kernels, expert_unit(): pl.pallas_call(expert_kernel, grid_spec=pltpu.PrefetchScalarGridSpec(num_...  196 us
    ppermute x9, waiting for transfers between devices, step(): lax.ppermute(from_above, 'ctx', down)  86.3 us
    pallas_call x1, Pallas kernels, attention_backward(): pl.pallas_call(functools.partial(backward_kernel, tile, prompt_tiles, blo...  67.7 us
    pallas_call x1, Pallas kernels, attention_forward(): pl.pallas_call(functools.partial(forward_kernel, tile, prompt_tiles, bloc...  53.2 us
    pallas_call x1, Pallas kernels, expert_out(): pl.pallas_call(out_kernel, grid=(peers // 2, experts), in_specs=[pl.Block...  44.9 us
    pallas_call x4, Pallas kernels, project(): pl.pallas_call(project_kernel, grid_spec=pltpu.PrefetchScalarGridSpec(num...  44.2 us
    ppermute x35, starting transfers between devices, swap_dp(): return lax.ppermute(part, 'dp', swap_partners(lax.axis_size('dp'), shift))  38.2 us
  transfers between devices with their start and end apart: 84, of which 27 were waited for; matrix products, arithmetic and copies ran while one was open for 25% of the time, Pallas kernels for 32%

profile of v4, /device:TPU:0, one launch (start us, length us, event | category | flops | bytes accessed | tf_op | source)
XLA Modules:
  0.0 1319.8 jit_solution(15761826097820661662)
XLA Ops:
  28.0 9.7 collective-permute-done.3
  45.6 15.2 %collective-permute-done.7.refs_2_ = bf16[512,768]{1,0:T(8,128)(2,1)} collective-permute-done((bf16[512,768]{1,0:T(8,128)(2,1)S(1)}, bf16[512,768]{1,0:T(8,128)(2,1)}, u32[]{:S(2)}, u32[]{:S(2)}) %collective-permute-start.7) | collective-permute-done | bytes 786464 | tf_op jit(solution)/shard_map/ppermute | solution.py:407
  81.2 10.6 project.4
  91.8 26.0 %collective-permute-done.13 = bf16[256,2048]{1,0:T(8,128)(2,1)S(1)} collective-permute-done((bf16[256,2048]{1,0:T(8,128)(2,1)}, bf16[256,2048]{1,0:T(8,128)(2,1)S(1)}, u32[]{:S(2)}, u32[]{:S(2)}) %collective-permute-start.13) | collective-permute-done | bytes 1048608 | tf_op jit(solution)/shard_map/ppermute | solution.py:407
  131.7 10.6 project.5
  142.3 33.1 %collective-permute-done.17 = bf16[256,2048]{1,0:T(8,128)(2,1)S(1)} collective-permute-done((bf16[256,2048]{1,0:T(8,128)(2,1)}, bf16[256,2048]{1,0:T(8,128)(2,1)S(1)}, u32[]{:S(2)}, u32[]{:S(2)}) %collective-permute-start.17) | collective-permute-done | bytes 1048608 | tf_op jit(solution)/shard_map/ppermute | solution.py:407
  178.4 11.1 project.6
  207.6 11.8 project.7
  258.5 53.2 %attention_forward.1 = (bf16[4096,256]{1,0:T(8,128)(2,1)}, f32[2,8,512]{2,1,0:T(8,128)}, bf16[4096,256]{1,0:T(8,128)(2,1)}, bf16[4096,256]{1,0:T(8,128)(2,1)}, bf16[4096,256]{1,0:T(8,128)(2,1)}) custom-call(s32[16]{0:T(128)} %get-tuple-element.253.place, s32[8]{0:T(128)} %compare_select_fusion.first_tile, f32[4096,768]{1,0:T(8,128)} %get-tuple-element.254.raw_q.raw_k.raw_v, ...), custom_call_target="tpu_custom_call" | custom-call | flops 17179869184 | bytes 25165824 | tf_op jit(solution)/shard_map/attention_forward/pallas_call | solution.py:266
  334.3 9.0 join.5
  366.3 29.7 %all-to-all-done.1 = bf16[8,512,256]{1,2,0:T(8,128)(2,1)} async-done(((bf16[8,512,256]{1,2,0:T(8,128)(2,1)}), bf16[8,512,256]{1,2,0:T(8,128)(2,1)}, u32[]{:S(2)}, u32[]{:S(2)}) %all-to-all-start.1) | async-done | bytes 2097184 | tf_op jit(solution)/shard_map/all_to_all | solution.py:934
  417.2 48.9 %expert_unit.4 = (bf16[8,2,288,2048]{3,2,1,0:T(8,128)(2,1)}, bf16[8,2,288,2048]{3,2,1,0:T(8,128)(2,1)}, bf16[8,2,288,1024]{3,2,1,0:T(8,128)(2,1)}, bf16[8,2,288,...) custom-call(s32[2]{0:T(128)} %pad_add_fusion.6.unit, ...), custom_call_target="tpu_custom_call" | custom-call | tf_op jit(solution)/shard_map/expert_unit/pallas_call | solution.py:694
  472.3 49.0 %expert_unit.5 = (bf16[8,2,288,2048]{3,2,1,0:T(8,128)(2,1)}, bf16[8,2,288,2048]{3,2,1,0:T(8,128)(2,1)}, bf16[8,2,288,1024]{3,2,1,0:T(8,128)(2,1)}, bf16[8,2,288,...) custom-call(s32[2]{0:T(128)} %pad_add_fusion.7.unit, ...), custom_call_target="tpu_custom_call", output_to_operand_aliasing={{0}: (10, {}), {1}: (11, {}), {2}: (12, {}), {3}: (13, {}),... | custom-call | tf_op jit(solution)/shard_map/expert_unit/pallas_call | solution.py:694
  528.5 48.9 %expert_unit.6 = (bf16[8,2,288,2048]{3,2,1,0:T(8,128)(2,1)}, bf16[8,2,288,2048]{3,2,1,0:T(8,128)(2,1)}, bf16[8,2,288,1024]{3,2,1,0:T(8,128)(2,1)}, bf16[8,2,288,...) custom-call(s32[2]{0:T(128)} %pad_add_fusion.8.unit, ...), custom_call_target="tpu_custom_call", output_to_operand_aliasing={{0}: (10, {}), {1}: (11, {}), {2}: (12, {}), {3}: (13, {}),... | custom-call | tf_op jit(solution)/shard_map/expert_unit/pallas_call | solution.py:694
  584.4 49.1 %expert_unit.7 = (bf16[8,2,288,2048]{3,2,1,0:T(8,128)(2,1)}, bf16[8,2,288,2048]{3,2,1,0:T(8,128)(2,1)}, bf16[8,2,288,1024]{3,2,1,0:T(8,128)(2,1)}, bf16[8,2,288,...) custom-call(s32[2]{0:T(128)} %pad_add_fusion.5.unit, ...), custom_call_target="tpu_custom_call", output_to_operand_aliasing={{0}: (10, {}), {1}: (11, {}), {2}: (12, {}), {3}: (13, {}),... | custom-call | tf_op jit(solution)/shard_map/expert_unit/pallas_call | solution.py:694
  633.6 44.9 %expert_out.1 = bf16[8,512,2048]{2,1,0:T(8,128)(2,1)} custom-call(bf16[8,2,288,1024]{3,2,1,0:T(8,128)(2,1)} %get-tuple-element.326.hidden, bf16[2,1024,2048]{2,1,0:T(8,128)(2,1)} %join.6.w_down, s32[8,2,512]{2,1,0:T(2,128)} %copy.201.slots, f32[8,2,512]{2,1,0:T(2,128)} %get-tuple-element.278.gates, s32[8,512,2]{2,1,0:T(8,128)} %select_bitcast_fusion.columns), custom_call_target="tpu_custom_call" | custom-call | tf_op jit(solution)/shard_map/expert_out/pallas_call | solution.py:755
  678.5 26.9 %bitcast_convert_fusion.2 = bf16[2,1024,2048]{2,1,0:T(8,128)(2,1)} fusion(bf16[8,2,288,1024]{3,2,1,0:T(8,128)(2,1)} %get-tuple-element.326.hidden, bf16[8,2,288,2048]{3,2,1,0:T(8,128)(2,1)} %get-tuple-element.327), kind=kOutput, calls=%fused_computation.3 | convolution fusion | flops 19331547136 | bytes 36700160 | tf_op jit(solution)/shard_map/sncf,sncd->nfd/dot_general | solution.py:991
  712.7 27.6 %bitcast_convert_fusion = bf16[2,2048,1024]{2,1,0:T(8,128)(2,1)} fusion(bf16[8,2,288,2048]{3,2,1,0:T(8,128)(2,1)} %get-tuple-element.330, bf16[8,2,288,1024]{3,2,1,0:T(8,128)(2,1)} %get-tuple-element.332), kind=kOutput, calls=%fused_computation.1 | convolution fusion | flops 19331547136 | bytes 36700160 | tf_op jit(solution)/shard_map/sncd,sncf->ndf/dot_general | solution.py:996
  740.3 24.9 %bitcast_convert_fusion.1 = bf16[2,2048,1024]{2,1,0:T(8,128)(2,1)} fusion(bf16[8,2,288,2048]{3,2,1,0:T(8,128)(2,1)} %get-tuple-element.330, bf16[8,2,288,1024]{3,2,1,0:T(8,128)(2,1)S(1)} %bitcast.137), kind=kOutput, calls=%fused_computation.2 | convolution fusion | flops 19331547136 | bytes 36700160 | tf_op jit(solution)/shard_map/sncd,sncf->ndf/dot_general | solution.py:995
  765.2 37.6 %collective-permute-done.43 = bf16[2,256,2048]{2,1,0:T(8,128)(2,1)} collective-permute-done((bf16[2,256,2048]{2,1,0:T(8,128)(2,1)S(1)}, bf16[2,256,2048]{2,1,0:T(8,128)(2,1)}, u32[]{:S(2)}, u32[]{:S(2)}) %collective-permute-start.43) | collective-permute-done | bytes 2097184 | tf_op jit(solution)/shard_map/ppermute | solution.py:407
  810.9 10.0 convolution_convert_fusion.1
  860.7 30.7 %collective-permute-done.47 = bf16[2,512,1024]{2,1,0:T(8,128)(2,1)} collective-permute-done((bf16[2,512,1024]{2,1,0:T(8,128)(2,1)}, bf16[2,512,1024]{2,1,0:T(8,128)(2,1)}, u32[]{:S(2)}, u32[]{:S(2)}) %collective-permute-start.47) | collective-permute-done | bytes 2097184 | tf_op jit(solution)/shard_map/ppermute | solution.py:407
  891.9 29.9 %all-to-all-done.2 = bf16[8,512,256]{2,1,0:T(8,128)(2,1)} async-done(((bf16[8,512,256]{2,1,0:T(8,128)(2,1)}), bf16[8,512,256]{2,1,0:T(8,128)(2,1)}, u32[]{:S(2)}, u32[]{:S(2)}) %all-to-all-start.2) | async-done | bytes 2097184 | tf_op jit(solution)/shard_map/all_to_all | solution.py:1013
  928.8 67.7 %attention_backward.1 = (f32[4096,256]{1,0:T(8,128)}, f32[4096,256]{1,0:T(8,128)}, bf16[4096,256]{1,0:T(8,128)(2,1)}) custom-call(s32[16]{0:T(128)} %get-tuple-element.253.place, s32[8]{0:T(128)} %compare_select_fusion.first_tile, bf16[4096,256]{1,0:T(8,128)(2,1)} %get-tuple-element.255.queries, bf16[4096,256]{1,0:T(8,128)(2,1)} %get-tuple-element.256.keys, ...), custom_call_target="tpu_custom_call" | custom-call | flops 21474836480 | bytes 25165824 | tf_op jit(solution)/shard_map/attention_backward/pallas_call | solution.py:315
  1017.5 20.1 %convolution_convert_fusion = bf16[4096,2048]{1,0:T(8,128)(2,1)} fusion(bf16[2048,768]{1,0:T(8,128)(2,1)S(1)} %copy-done.3, bf16[4096,256]{1,0:T(8,128)(2,1)} %get-tuple-element.344, bf16[4096,256]{1,0:T(8,128)(2,1)} %get-tuple-element.414, bf16[4096,256]{1,0:T(8,128)(2,1)} %get-tuple-element.413), kind=kOutput, calls=%fused_computation.5 | convolution fusion | flops 12912164864 | bytes 26214400 | tf_op jit(solution)/shard_map/dot_general | solution.py:1062
  1042.6 18.0 %convolution_convert_fusion.2 = bf16[2048,768]{1,0:T(8,128)(2,1)S(1)} fusion(bf16[4096,2048]{1,0:T(8,128)(2,1)} %get-tuple-element.244, bf16[4096,256]{1,0:T(8,128)(2,1)} %get-tuple-element.344, bf16[4096,256]{1,0:T(8,128)(2,1)S(1)} %copy-done.39, bf16[4096,256]{1,0:T(8,128)(2,1)S(1)} %copy-done.38), kind=kOutput, calls=%fused_computation.44 | convolution fusion | flops 12905349120 | bytes 26214400 | tf_op jit(solution)/shard_map/dot_general | solution.py:1075
  1070.8 14.9 %multiply_reduce_fusion = f32[2048]{0:T(1024)S(1)} fusion(bf16[4096,2048]{1,0:T(8,128)(2,1)} %get-tuple-element.244, bf16[4096,2048]{1,0:T(8,128)(2,1)} %convolution_convert_fusion), kind=kLoop, calls=%fused_computation | loop fusion | flops 33552384 | bytes 33562624 | tf_op jit(solution)/shard_map/reduce_sum | solution.py:1082
  1088.1 19.6 %collective-permute-done.57 = bf16[512,768]{1,0:T(8,128)(2,1)} collective-permute-done((bf16[512,768]{1,0:T(8,128)(2,1)}, bf16[512,768]{1,0:T(8,128)(2,1)}, u32[]{:S(2)}, u32[]{:S(2)}) %collective-permute-start.57) | collective-permute-done | bytes 786464 | tf_op jit(solution)/shard_map/ppermute | solution.py:407
  1107.6 15.3 %collective-permute-done.56 = bf16[512,768]{1,0:T(8,128)(2,1)} collective-permute-done((bf16[512,768]{1,0:T(8,128)(2,1)}, bf16[512,768]{1,0:T(8,128)(2,1)}, u32[]{:S(2)}, u32[]{:S(2)}) %collective-permute-start.56) | collective-permute-done | bytes 786464 | tf_op jit(solution)/shard_map/ppermute | solution.py:407
  1160.4 28.0 %collective-permute-done.63 = bf16[528,1024]{1,0:T(8,128)(2,1)} collective-permute-done((bf16[528,1024]{1,0:T(8,128)(2,1)S(1)}, bf16[528,1024]{1,0:T(8,128)(2,1)}, u32[]{:S(2)}, u32[]{:S(2)}) %collective-permute-start.63) | collective-permute-done | bytes 1081376 | tf_op jit(solution)/shard_map/ppermute | solution.py:386
  1209.1 48.2 %collective-permute-done.68 = bf16[528,1024]{1,0:T(8,128)(2,1)} collective-permute-done((bf16[528,1024]{1,0:T(8,128)(2,1)}, bf16[528,1024]{1,0:T(8,128)(2,1)}, u32[]{:S(2)}, u32[]{:S(2)}) %collective-permute-start.68) | collective-permute-done | bytes 1081376 | tf_op jit(solution)/shard_map/ppermute | solution.py:386
  1279.8 9.8 collective-permute-done.72
  (447 shorter events, 408.0 us)
Async XLA Ops:
  7.2 241.9 %all-gather.3.cloned.1.call-start = ((), (), s32[]{:S(2)}) async-start(), calls=%async_computation.7 | async-start | bytes 10485760 | tf_op jit(solution)/shard_map/all_gather | solution.py:863
  7.3 54.8 %collective-permute-start.2 = (bf16[512,2048]{1,0:T(8,128)(2,1)}, bf16[512,2048]{1,0:T(8,128)(2,1)}, u32[]{:S(2)}, u32[]{:S(2)}) collective-permute-start(bf16[512,2048]{1,0:T(8,128)(2,1)} %own.1), channel_id=1, source_target_pairs={{0,1},{1,0},{2,3},{3,2},{4,5},{5,4},{6,7},{7,6},{8,9},{9,8},{10,11... | collective-permute-start | bytes 6291464 | tf_op jit(solution)/shard_map/ppermute | solution.py:390
  7.8 54.3 %collective-permute-start.1 = (bf16[512,2048]{1,0:T(8,128)(2,1)}, bf16[512,2048]{1,0:T(8,128)(2,1)}, u32[]{:S(2)}, u32[]{:S(2)}) collective-permute-start(bf16[512,2048]{1,0:T(8,128)(2,1)} %own.1), channel_id=1, source_target_pairs={{2,0},{3,1},{4,2},{5,3},{6,4},{7,5},{10,8},{11,9},{12,10},{13,11},... | collective-permute-start | bytes 6291464 | tf_op jit(solution)/shard_map/ppermute | solution.py:386
  62.1 344.2 %all-gather.5.cloned.1.call-start = ((), (), s32[]{:S(2)}) async-start(), calls=%async_computation.8 | async-start | bytes 18874368 | tf_op jit(solution)/shard_map/all_gather | solution.py:896
  194.2 55.0 %collective-permute-start.23 = (bf16[1024,2048]{1,0:T(8,128)(2,1)}, bf16[1024,2048]{1,0:T(8,128)(2,1)}, u32[]{:S(2)}, u32[]{:S(2)}) collective-permute-start(bf16[1024,2048]{1,0:T(8,128)(2,1)} %pad_maximum_fusion.1.refs_0_), channel_id=1, source_target_pairs={{0,1},{1,0},{2,3},{3,2},{4,5},{5,4},{6,7},{7,6},{8,9},{9,8},{10,11... | collective-permute-start | bytes 12582920 | tf_op jit(solution)/shard_map/ppermute | solution.py:390
  249.2 68.6 %collective-permute-start.27 = (bf16[2,512,1024]{2,1,0:T(8,128)(2,1)}, bf16[2,512,1024]{2,1,0:T(8,128)(2,1)}, u32[]{:S(2)}, u32[]{:S(2)}) collective-permute-start(bf16[2,512,1024]{2,1,0:T(8,128)(2,1)} %refs_0_.1), channel_id=1, source_target_pairs={{0,16},{8,24},{16,0},{24,8},{1,17},{9,25},{17,1},{25,9},{2,18},{10... | collective-permute-start | bytes 6291464 | tf_op jit(solution)/shard_map/ppermute | solution.py:407
  249.2 68.5 %collective-permute-start.26 = (bf16[2,512,1024]{2,1,0:T(8,128)(2,1)}, bf16[2,512,1024]{2,1,0:T(8,128)(2,1)}, u32[]{:S(2)}, u32[]{:S(2)}) collective-permute-start(bf16[2,512,1024]{2,1,0:T(8,128)(2,1)} %refs_0_.1), channel_id=1, source_target_pairs={{0,8},{8,0},{16,24},{24,16},{1,9},{9,1},{17,25},{25,17},{2,10},{10... | collective-permute-start | bytes 6291464 | tf_op jit(solution)/shard_map/ppermute | solution.py:407
  255.3 62.4 %collective-permute-start.29 = (bf16[2,128,2048]{2,1,0:T(8,128)(2,1)}, bf16[2,128,2048]{2,1,0:T(8,128)(2,1)S(1)}, u32[]{:S(2)}, u32[]{:S(2)}) collective-permute-start(bf16[2,128,2048]{2,1,0:T(8,128)(2,1)} %slice.98), channel_id=1, source_target_pairs={{0,8},{8,0},{16,24},{24,16},{1,9},{9,1},{17,25},{25,17},{2,10},{10... | collective-permute-start | bytes 3145736 | tf_op jit(solution)/shard_map/ppermute | solution.py:407
  256.6 61.2 %collective-permute-start.28 = (bf16[2,128,2048]{2,1,0:T(8,128)(2,1)}, bf16[2,128,2048]{2,1,0:T(8,128)(2,1)}, u32[]{:S(2)}, u32[]{:S(2)}) collective-permute-start(bf16[2,128,2048]{2,1,0:T(8,128)(2,1)} %slice.97), channel_id=1, source_target_pairs={{0,16},{8,24},{16,0},{24,8},{1,17},{9,25},{17,1},{25,9},{2,18},{10... | collective-permute-start | bytes 3145736 | tf_op jit(solution)/shard_map/ppermute | solution.py:407
  321.7 74.4 %all-to-all-start.1 = ((bf16[8,512,256]{1,2,0:T(8,128)(2,1)}), bf16[8,512,256]{1,2,0:T(8,128)(2,1)}, u32[]{:S(2)}, u32[]{:S(2)}) async-start(bf16[8,512,256]{1,2,0:T(8,128)(2,1)} %copy.200), calls=%async_computation.1 | async-start | bytes 4194304 | tf_op jit(solution)/shard_map/all_to_all | solution.py:934
  327.4 475.6 %reduce-scatter.4.cloned.1.call-start = ((), (), s32[]{:S(2)}) async-start(), calls=%async_computation.9 | async-start | bytes 18874368 | tf_op jit(solution)/shard_map/reduce_scatter | solution.py:986
  406.5 59.6 %collective-permute-start.33 = (bf16[512,2048]{1,0:T(8,128)(2,1)S(1)}, bf16[512,2048]{1,0:T(8,128)(2,1)}, u32[]{:S(2)}, u32[]{:S(2)}) collective-permute-start(bf16[512,2048]{1,0:T(8,128)(2,1)S(1)} %multiply_convert_fusion.2.own), channel_id=1, source_target_pairs={{2,0},{3,1},{4,2},{5,3},{6,4},{7,5},{10,8},{11,9},{12,10},{13,11},... | collective-permute-start | bytes 6291464 | tf_op jit(solution)/shard_map/ppermute | solution.py:386
  407.7 58.4 %collective-permute-start.32 = (bf16[512,2048]{1,0:T(8,128)(2,1)S(1)}, bf16[512,2048]{1,0:T(8,128)(2,1)}, u32[]{:S(2)}, u32[]{:S(2)}) collective-permute-start(bf16[512,2048]{1,0:T(8,128)(2,1)S(1)} %multiply_convert_fusion.2.own), channel_id=1, source_target_pairs={{0,2},{1,3},{2,4},{3,5},{4,6},{5,7},{8,10},{9,11},{10,12},{11,13},... | collective-permute-start | bytes 6291464 | tf_op jit(solution)/shard_map/ppermute | solution.py:385
  468.0 53.3 %collective-permute-start.36 = (bf16[512,2048]{1,0:T(8,128)(2,1)}, bf16[512,2048]{1,0:T(8,128)(2,1)}, u32[]{:S(2)}, u32[]{:S(2)}) collective-permute-start(bf16[512,2048]{1,0:T(8,128)(2,1)} %collective-permute-done.33), channel_id=1, source_target_pairs={{2,0},{3,1},{4,2},{5,3},{10,8},{11,9},{12,10},{13,11},{18,16},{19,... | collective-permute-start | bytes 6291464 | tf_op jit(solution)/shard_map/ppermute | solution.py:386
  633.5 404.1 %reduce-scatter.6.cloned.1.call-start = ((), (), s32[]{:S(2)}) async-start(), calls=%async_computation.10 | async-start | bytes 18874368 | tf_op jit(solution)/shard_map/reduce_scatter | solution.py:1001
  709.2 56.1 %collective-permute-start.44 = (bf16[2,256,2048]{2,1,0:T(8,128)(2,1)S(1)}, bf16[2,256,2048]{2,1,0:T(8,128)(2,1)}, u32[]{:S(2)}, u32[]{:S(2)}) collective-permute-start(bf16[2,256,2048]{2,1,0:T(8,128)(2,1)S(1)} %get-tuple-element.419), channel_id=1, source_target_pairs={{0,24},{8,16},{16,8},{24,0},{1,25},{9,17},{17,9},{25,1},{2,26},{10... | collective-permute-start | bytes 6291464 | tf_op jit(solution)/shard_map/ppermute | solution.py:407
  710.4 92.5 %collective-permute-start.43 = (bf16[2,256,2048]{2,1,0:T(8,128)(2,1)S(1)}, bf16[2,256,2048]{2,1,0:T(8,128)(2,1)}, u32[]{:S(2)}, u32[]{:S(2)}) collective-permute-start(bf16[2,256,2048]{2,1,0:T(8,128)(2,1)S(1)} %get-tuple-element.420), channel_id=1, source_target_pairs={{0,16},{8,24},{16,0},{24,8},{1,17},{9,25},{17,1},{25,9},{2,18},{10... | collective-permute-start | bytes 6291464 | tf_op jit(solution)/shard_map/ppermute | solution.py:407
  711.6 91.2 %collective-permute-start.42 = (bf16[2,256,2048]{2,1,0:T(8,128)(2,1)S(1)}, bf16[2,256,2048]{2,1,0:T(8,128)(2,1)}, u32[]{:S(2)}, u32[]{:S(2)}) collective-permute-start(bf16[2,256,2048]{2,1,0:T(8,128)(2,1)S(1)} %get-tuple-element.421), channel_id=1, source_target_pairs={{0,8},{8,0},{16,24},{24,16},{1,9},{9,1},{17,25},{25,17},{2,10},{10... | collective-permute-start | bytes 6291464 | tf_op jit(solution)/shard_map/ppermute | solution.py:407
  831.8 89.9 %all-to-all-start.2 = ((bf16[8,512,256]{2,1,0:T(8,128)(2,1)}), bf16[8,512,256]{2,1,0:T(8,128)(2,1)}, u32[]{:S(2)}, u32[]{:S(2)}) async-start(bf16[8,512,256]{2,1,0:T(8,128)(2,1)} %bitcast.126), calls=%async_computation.3 | async-start | bytes 4194304 | tf_op jit(solution)/shard_map/all_to_all | solution.py:1013
  838.0 466.7 %reduce-scatter.8.cloned.1.call-start = ((), (), s32[]{:S(2)}) async-start(), calls=%async_computation.11 | async-start | bytes 18874368 | tf_op jit(solution)/shard_map/reduce_scatter | solution.py:1065
  925.3 71.2 %collective-permute-start.50 = (bf16[512,1024]{1,0:T(8,128)(2,1)}, bf16[512,1024]{1,0:T(8,128)(2,1)S(1)}, u32[]{:S(2)}, u32[]{:S(2)}) collective-permute-start(bf16[512,1024]{1,0:T(8,128)(2,1)} %get-tuple-element.425), channel_id=1, source_target_pairs={{0,24},{8,16},{16,8},{24,0},{1,25},{9,17},{17,9},{25,1},{2,26},{10... | collective-permute-start | bytes 3145736 | tf_op jit(solution)/shard_map/ppermute | solution.py:407
  927.0 69.6 %collective-permute-start.49 = (bf16[512,1024]{1,0:T(8,128)(2,1)}, bf16[512,1024]{1,0:T(8,128)(2,1)S(1)}, u32[]{:S(2)}, u32[]{:S(2)}) collective-permute-start(bf16[512,1024]{1,0:T(8,128)(2,1)} %get-tuple-element.426), channel_id=1, source_target_pairs={{0,16},{8,24},{16,0},{24,8},{1,17},{9,25},{17,1},{25,9},{2,18},{10... | collective-permute-start | bytes 3145736 | tf_op jit(solution)/shard_map/ppermute | solution.py:407
  927.7 68.9 %collective-permute-start.48 = (bf16[512,1024]{1,0:T(8,128)(2,1)}, bf16[512,1024]{1,0:T(8,128)(2,1)S(1)}, u32[]{:S(2)}, u32[]{:S(2)}) collective-permute-start(bf16[512,1024]{1,0:T(8,128)(2,1)} %get-tuple-element.427), channel_id=1, source_target_pairs={{0,8},{8,0},{16,24},{24,16},{1,9},{9,1},{17,25},{25,17},{2,10},{10... | collective-permute-start | bytes 3145736 | tf_op jit(solution)/shard_map/ppermute | solution.py:407
  1040.9 84.1 %collective-permute-start.61 = (bf16[2,512,1024]{2,1,0:T(8,128)(2,1)}, bf16[2,512,1024]{2,1,0:T(8,128)(2,1)S(1)}, u32[]{:S(2)}, u32[]{:S(2)}) collective-permute-start(bf16[2,512,1024]{2,1,0:T(8,128)(2,1)} %constant_dynamic-slice_fusion.4), channel_id=1, source_target_pairs={{0,24},{8,16},{16,8},{24,0},{1,25},{9,17},{17,9},{25,1},{2,26},{10... | collective-permute-start | bytes 6291464 | tf_op jit(solution)/shard_map/ppermute | solution.py:407
  1065.7 57.2 %collective-permute-start.56 = (bf16[512,768]{1,0:T(8,128)(2,1)}, bf16[512,768]{1,0:T(8,128)(2,1)}, u32[]{:S(2)}, u32[]{:S(2)}) collective-permute-start(bf16[512,768]{1,0:T(8,128)(2,1)} %get-tuple-element.429), channel_id=1, source_target_pairs={{0,16},{8,24},{16,0},{24,8},{1,17},{9,25},{17,1},{25,9},{2,18},{10... | collective-permute-start | bytes 2359304 | tf_op jit(solution)/shard_map/ppermute | solution.py:407
  1065.7 59.3 %collective-permute-start.55 = (bf16[512,768]{1,0:T(8,128)(2,1)}, bf16[512,768]{1,0:T(8,128)(2,1)}, u32[]{:S(2)}, u32[]{:S(2)}) collective-permute-start(bf16[512,768]{1,0:T(8,128)(2,1)} %get-tuple-element.430), channel_id=1, source_target_pairs={{0,8},{8,0},{16,24},{24,16},{1,9},{9,1},{17,25},{25,17},{2,10},{10... | collective-permute-start | bytes 2359304 | tf_op jit(solution)/shard_map/ppermute | solution.py:407
  1067.3 59.3 %all-to-all-start.3 = ((bf16[4,512,256]{2,1,0:T(8,128)(2,1)}), bf16[4,512,256]{2,1,0:T(8,128)(2,1)S(1)}, u32[]{:S(2)}, u32[]{:S(2)}) async-start(bf16[4,512,256]{2,1,0:T(8,128)(2,1)} %bitcast.128), calls=%async_computation.5 | async-start | bytes 2097152 | tf_op jit(solution)/shard_map/all_to_all | solution.py:1067
  1131.3 58.2 %collective-permute-start.66 = (bf16[2,512,1024]{2,1,0:T(8,128)(2,1)}, bf16[2,512,1024]{2,1,0:T(8,128)(2,1)}, u32[]{:S(2)}, u32[]{:S(2)}) collective-permute-start(bf16[2,512,1024]{2,1,0:T(8,128)(2,1)} %get-tuple-element.415), channel_id=1, source_target_pairs={{0,16},{8,24},{16,0},{24,8},{1,17},{9,25},{17,1},{25,9},{2,18},{10... | collective-permute-start | bytes 6291464 | tf_op jit(solution)/shard_map/ppermute | solution.py:407
  1132.9 56.6 %collective-permute-start.65 = (bf16[2,512,1024]{2,1,0:T(8,128)(2,1)}, bf16[2,512,1024]{2,1,0:T(8,128)(2,1)}, u32[]{:S(2)}, u32[]{:S(2)}) collective-permute-start(bf16[2,512,1024]{2,1,0:T(8,128)(2,1)} %get-tuple-element.416), channel_id=1, source_target_pairs={{0,8},{8,0},{16,24},{24,16},{1,9},{9,1},{17,25},{25,17},{2,10},{10... | collective-permute-start | bytes 6291464 | tf_op jit(solution)/shard_map/ppermute | solution.py:407
  1193.0 64.3 %collective-permute-start.70 = (bf16[2,512,1024]{2,1,0:T(8,128)(2,1)}, bf16[2,512,1024]{2,1,0:T(8,128)(2,1)}, u32[]{:S(2)}, u32[]{:S(2)}) collective-permute-start(bf16[2,512,1024]{2,1,0:T(8,128)(2,1)} %constant_dynamic-slice_fusion), channel_id=1, source_target_pairs={{0,24},{8,16},{16,8},{24,0},{1,25},{9,17},{17,9},{25,1},{2,26},{10... | collective-permute-start | bytes 6291464 | tf_op jit(solution)/shard_map/ppermute | solution.py:407
  1195.6 61.7 %collective-permute-start.68 = (bf16[528,1024]{1,0:T(8,128)(2,1)}, bf16[528,1024]{1,0:T(8,128)(2,1)}, u32[]{:S(2)}, u32[]{:S(2)}) collective-permute-start(bf16[528,1024]{1,0:T(8,128)(2,1)} %collective-permute-done.63), channel_id=1, source_target_pairs={{2,0},{3,1},{4,2},{5,3},{10,8},{11,9},{12,10},{13,11},{18,16},{19,... | collective-permute-start | bytes 3244040 | tf_op jit(solution)/shard_map/ppermute | solution.py:386
  1196.9 60.4 %collective-permute-start.67 = (bf16[528,1024]{1,0:T(8,128)(2,1)}, bf16[528,1024]{1,0:T(8,128)(2,1)}, u32[]{:S(2)}, u32[]{:S(2)}) collective-permute-start(bf16[528,1024]{1,0:T(8,128)(2,1)} %copy-done.32), channel_id=1, source_target_pairs={{2,4},{3,5},{4,6},{5,7},{10,12},{11,13},{12,14},{13,15},{18,20},{1... | collective-permute-start | bytes 3244040 | tf_op jit(solution)/shard_map/ppermute | solution.py:385
  (122 other events, 2982.2 us)
Sparse Core Ops, SparseCore 0:
  62.2 133.9 all-gather.2
  197.9 189.2 all-gather.4
  633.7 169.2 reduce-scatter.3
  805.2 199.9 reduce-scatter.5
  1037.8 224.5 reduce-scatter.7

commit v5 on v4

--- a/solution.py
+++ b/solution.py
@@ -874,16 +874,16 @@
         if turn + 1 < line.chips:
             below, above = line.step(turn + 1, below, above)
             arrived[-turn - 1], arrived[turn + 1] = below, above
+        if turn + 1 == line.chips:
+            cotangent_now, arrived[turn] = barrier(cotangent, arrived[turn])
         next_own, next_chip = line.take(turn, arrived)
         next_other = line.other(next_own)
         at = jnp.stack([2 * chip + core, 2 * chip + 1 - core]).astype(jnp.int32)
         kept = project(at, own, other, w_own, gain_attn, peers, kept)
         travel = list(travelled)
-        if turn == 1:
+        if turn == 2:
             wo_half = lax.dynamic_slice_in_dim(wo, core * half_rows, half_rows, 0)
             travel = first_dp(wo_half)
-        if turn == 2:
-            travel.append(swap_dp(wo_half, 3))
         own, other, chip = next_own, next_other, next_chip
         square = kept[2]
         below, above, own, other, square, w_down, *travelled = barrier(
@@ -892,13 +892,11 @@
         kept = (kept[0], kept[1], square)
         if turn + 1 < line.chips:
             arrived[-turn - 1], arrived[turn + 1] = below, above
-    cotangent_now, other = barrier(cotangent, other)
     cot_all = lax.all_gather(cotangent_now, "ctx", axis=0, tiled=True).reshape(
         peers, count_rows, width
     )
     down_pieces = first_dp(w_down)
-    wo_mine = jnp.concatenate([wo_half, *travelled[:3]], axis=0)
-    wo_theirs = line.other(wo_mine)
+    wo_pieces = [wo_half, *travelled[:2]]
     table = lax.all_to_all(table, "ctx", split_axis=0, concat_axis=0, tiled=True)
     at = jnp.stack([2 * chip + core, 2 * chip + 1 - core]).astype(jnp.int32)
     normed_all, raw, square = project(at, own, other, w_own, gain_attn, peers, kept)
@@ -909,10 +907,10 @@
     offsets = (jnp.arange(local_experts, dtype=jnp.int32) * room)[None, :, None]
     columns = jnp.where(slot >= 0, slot + offsets, -1).transpose(0, 2, 1)
 
-    inv_qk, w_up, slot, gate_rows, columns, full_gate, wo_mine, wo_theirs, *down_pieces = barrier(
-        inv_qk, w_up, slot, gate_rows, columns, full_gate, wo_mine, wo_theirs, *down_pieces
-    )
-    down_pieces = down_pieces + second_dp(down_pieces, 1)
+    inv_qk, w_up, slot, gate_rows, columns, full_gate, wo_half, *down_pieces = barrier(
+        inv_qk, w_up, slot, gate_rows, columns, full_gate, wo_half, *down_pieces
+    )
+    wo_pieces.append(swap_dp(wo_half, 3))
     up_pieces = first_dp(w_up)
     attended, lse, queries, keys, values = attention_forward(
         raw,
@@ -928,13 +926,14 @@
         block_len,
         scale,
     )
-    attended, *pieces = barrier(attended, *up_pieces, *down_pieces)
-    up_pieces, down_pieces = pieces[:2], pieces[2:]
+    attended, wo_pieces[3], *up_pieces = barrier(attended, wo_pieces[3], *up_pieces)
+    wo_mine = jnp.concatenate(wo_pieces, axis=0)
+    wo_theirs = line.other(wo_mine)
+    down_pieces = down_pieces + second_dp(down_pieces, 1)
     up_pieces = up_pieces + second_dp(up_pieces, 1)
     attn_low = lax.all_to_all(
         attended.reshape(peers, count_rows, own_width), "ctx", split_axis=0, concat_axis=0, tiled=True
     )[::rep]
-    full_down = join_dp(w_down, down_pieces, 1)
     starts = [(my_dp ^ shift) * wo.shape[0] for shift in range(groups)]
     full_wo = join(
         [
@@ -945,15 +944,16 @@
         width,
         half_rows,
     )
-    full_up = join_dp(w_up, up_pieces, 1)
-    attn_low, full_wo, full_down, full_up = barrier(attn_low, full_wo, full_down, full_up)
+    full_down = join_dp(w_down, down_pieces, 1)
+    attn_low, full_wo, full_down = barrier(attn_low, full_wo, full_down)
     attn_low = attn_low.transpose(1, 0, 2).reshape(count_rows, width)
     state = inputs + jnp.dot(attn_low, full_wo, preferred_element_type=f32)
     inv_state = rms_scale(state)
     hat_state = state * inv_state
     normed_moe = (hat_state * gain_moe).astype(bf16)
 
-    normed_moe, cot_all = barrier(normed_moe, cot_all)
+    normed_moe, cot_all, *up_pieces = barrier(normed_moe, cot_all, *up_pieces)
+    full_up = join_dp(w_up, up_pieces, 1)
     below, above = normed_moe, normed_moe
     own, chip = normed_moe, line.chip
     arrived = {}
@@ -1018,11 +1018,14 @@
     out_theirs = line.other(lax.dynamic_slice_in_dim(part_out, (1 - core) * half, half, 1))
     part_out = lax.dynamic_slice_in_dim(part_out, core * half, half, 1).astype(f32)
     part_out = (part_out + out_theirs.astype(f32)).astype(bf16)
+    out_pieces = [scatter_one(part_out, shift, 0) for shift in (1, 2)]
     down_sum = total_dp(grad_down, down_pieces, 1)
-    grad_attended, part_out, down_sum, *gate_pieces = barrier(
-        grad_attended, part_out, down_sum, *gate_pieces
-    )
-    out_pieces = [scatter_one(part_out, shift, 0) for shift in (1, 2, 3)]
+    grad_attended, part_out, down_sum, grad_gate, *pieces = barrier(
+        grad_attended, part_out, down_sum, grad_gate, *gate_pieces, *out_pieces
+    )
+    gate_pieces, out_pieces = pieces[:2], pieces[2:]
+    out_pieces.append(scatter_one(part_out, 3, 0))
+    gate_pieces.append(scatter_one(grad_gate, 3, 1))
     grad_q, grad_k, grad_v = attention_backward(
         queries,
         keys,
@@ -1039,8 +1042,7 @@
         block_len,
         scale,
     )
-    grad_q, grad_gate, *out_pieces = barrier(grad_q, grad_gate, *out_pieces)
-    gate_pieces.append(scatter_one(grad_gate, 3, 1))
+    grad_q, out_pieces[2], gate_pieces[2] = barrier(grad_q, out_pieces[2], gate_pieces[2])
     out_sum = total_dp(part_out, out_pieces, 0).astype(bf16)
     rows_dp = out_sum.shape[0]
     share = half // line.chips
@@ -1084,10 +1086,10 @@
     gain_terms = jnp.concatenate([attn_gain_term[None], spread, moe_gain_term[None]], axis=0)
     gain_pieces = [scatter_one(gain_terms, shift, 1) for shift in (1, 2, 3)]
     output = (state + mixed.astype(f32)).astype(bf16)
-    out_sum, gain_terms, grad_up, grad_gate, output, *pieces = barrier(
-        out_sum, gain_terms, grad_up, grad_gate, output, *qkv_pieces, *gain_pieces, *gate_pieces
-    )
-    qkv_pieces, gain_pieces, gate_pieces = pieces[:3], pieces[3:6], pieces[6:]
+    out_sum, gain_terms, grad_up, output, *pieces = barrier(
+        out_sum, gain_terms, grad_up, output, *qkv_pieces, *gain_pieces
+    )
+    qkv_pieces, gain_pieces = pieces[:3], pieces[3:]
     gate_sum = total_dp(grad_gate, gate_pieces, 1)
     gain_terms = total_dp(gain_terms, gain_pieces, 1)
     qkv_sum = total_dp(part_qkv, qkv_pieces, 0).astype(bf16)

time: 1330 us -> 1320 us (level)
    ppermute x9, waiting for transfers between devices: 86.3 us -> 128 us  [step(): lax.ppermute(from_above, 'ctx', down)]
    all_to_all x1, waiting for transfers between devices: 29.7 us -> 0.01 us  [on_device(): lax.all_to_all(attended.reshape(peers, count_rows, own_width), 'ctx', spl...]
    ppermute x35, waiting for transfers between devices: 208 us -> 179 us  [swap_dp(): return lax.ppermute(part, 'dp', swap_partners(lax.axis_size('dp'), shift))]
  transfers between devices with their start and end apart: 84 -> 84, of which waited for: 27 -> 30; matrix products, arithmetic and copies ran while one was open for 25% -> 25% of each run, Pallas kernels for 32% -> 32%
where the time goes in v5:
time: 1320 us
  Pallas kernels  467 us (35%)
  waiting for transfers between devices  365 us (28%)
  matrix products  141 us (11%)
  other arithmetic  128 us (10%)
  starting transfers between devices  111 us (8%)
  local copies, waits for them, and re-layouts  81.4 us (6%)
  between operations  21.5 us (2%)
    pallas_call x4, Pallas kernels, expert_unit(): pl.pallas_call(expert_kernel, grid_spec=pltpu.PrefetchScalarGridSpec(num_...  196 us
    ppermute x35, waiting for transfers between devices, swap_dp(): return lax.ppermute(part, 'dp', swap_partners(lax.axis_size('dp'), shift))  179 us
    ppermute x9, waiting for transfers between devices, step(): lax.ppermute(from_above, 'ctx', down)  128 us
    pallas_call x1, Pallas kernels, attention_backward(): pl.pallas_call(functools.partial(backward_kernel, tile, prompt_tiles, blo...  67.7 us
    pallas_call x1, Pallas kernels, attention_forward(): pl.pallas_call(functools.partial(forward_kernel, tile, prompt_tiles, bloc...  53.2 us
    pallas_call x1, Pallas kernels, expert_out(): pl.pallas_call(out_kernel, grid=(peers // 2, experts), in_specs=[pl.Block...  44.9 us
    pallas_call x4, Pallas kernels, project(): pl.pallas_call(project_kernel, grid_spec=pltpu.PrefetchScalarGridSpec(num...  42.7 us
    ppermute x35, starting transfers between devices, swap_dp(): return lax.ppermute(part, 'dp', swap_partners(lax.axis_size('dp'), shift))  41.7 us
  transfers between devices with their start and end apart: 84, of which 30 were waited for; matrix products, arithmetic and copies ran while one was open for 25% of the time, Pallas kernels for 32%

profile of v5, /device:TPU:0, one launch (start us, length us, event | category | flops | bytes accessed | tf_op | source)
XLA Modules:
  0.0 1315.4 jit_solution(6544693794450292203)
XLA Ops:
  28.0 9.7 collective-permute-done.3
  45.6 15.2 %collective-permute-done.7.refs_2_ = bf16[512,768]{1,0:T(8,128)(2,1)} collective-permute-done((bf16[512,768]{1,0:T(8,128)(2,1)S(1)}, bf16[512,768]{1,0:T(8,128)(2,1)}, u32[]{:S(2)}, u32[]{:S(2)}) %collective-permute-start.7) | collective-permute-done | bytes 786464 | tf_op jit(solution)/shard_map/ppermute | solution.py:407
  79.4 10.6 project.4
  90.0 26.8 %collective-permute-done.10 = bf16[512,2048]{1,0:T(8,128)(2,1)} collective-permute-done((bf16[512,2048]{1,0:T(8,128)(2,1)}, bf16[512,2048]{1,0:T(8,128)(2,1)}, u32[]{:S(2)}, u32[]{:S(2)}) %collective-permute-start.10) | collective-permute-done | bytes 2097184 | tf_op jit(solution)/shard_map/ppermute | solution.py:386
  128.1 10.6 project.5
  138.7 33.8 %collective-permute-done.16 = bf16[256,2048]{1,0:T(8,128)(2,1)S(1)} collective-permute-done((bf16[256,2048]{1,0:T(8,128)(2,1)S(1)}, bf16[256,2048]{1,0:T(8,128)(2,1)S(1)}, u32[]{:S(2)}, u32[]{:S(2)}) %collective-permute-start.16) | collective-permute-done | bytes 1048608 | tf_op jit(solution)/shard_map/ppermute | solution.py:407
  177.9 10.8 project.6
  199.2 8.9 all-to-all-done
  210.7 10.7 project.7
  246.7 53.2 %attention_forward.1 = (bf16[4096,256]{1,0:T(8,128)(2,1)}, f32[2,8,512]{2,1,0:T(8,128)}, bf16[4096,256]{1,0:T(8,128)(2,1)}, bf16[4096,256]{1,0:T(8,128)(2,1)}, bf16[4096,256]{1,0:T(8,128)(2,1)}) custom-call(s32[16]{0:T(128)} %get-tuple-element.239.place, s32[8]{0:T(128)} %compare_select_fusion.first_tile, f32[4096,768]{1,0:T(8,128)} %get-tuple-element.240.raw_q.raw_k.raw_v, ...), custom_call_target="tpu_custom_call" | custom-call | flops 17179869184 | bytes 25165824 | tf_op jit(solution)/shard_map/attention_forward/pallas_call | solution.py:266
  299.9 12.4 collective-permute-done.24
  330.6 22.8 %collective-permute-done.29.refs_4_ = bf16[2,128,2048]{2,1,0:T(8,128)(2,1)S(1)} collective-permute-done((bf16[2,128,2048]{2,1,0:T(8,128)(2,1)}, bf16[2,128,2048]{2,1,0:T(8,128)(2,1)S(1)}, u32[]{:S(2)}, u32[]{:S(2)}) %collective-permute-start.29) | collective-permute-done | bytes 1048608 | tf_op jit(solution)/shard_map/ppermute | solution.py:407
  410.4 48.9 %expert_unit.4 = (bf16[8,2,288,2048]{3,2,1,0:T(8,128)(2,1)}, bf16[8,2,288,2048]{3,2,1,0:T(8,128)(2,1)}, bf16[8,2,288,1024]{3,2,1,0:T(8,128)(2,1)}, bf16[8,2,288,...) custom-call(s32[2]{0:T(128)} %pad_add_fusion.6.unit, ...), custom_call_target="tpu_custom_call" | custom-call | tf_op jit(solution)/shard_map/expert_unit/pallas_call | solution.py:694
  465.6 49.0 %expert_unit.5 = (bf16[8,2,288,2048]{3,2,1,0:T(8,128)(2,1)}, bf16[8,2,288,2048]{3,2,1,0:T(8,128)(2,1)}, bf16[8,2,288,1024]{3,2,1,0:T(8,128)(2,1)}, bf16[8,2,288,...) custom-call(s32[2]{0:T(128)} %pad_add_fusion.7.unit, ...), custom_call_target="tpu_custom_call", output_to_operand_aliasing={{0}: (10, {}), {1}: (11, {}), {2}: (12, {}), {3}: (13, {}),... | custom-call | tf_op jit(solution)/shard_map/expert_unit/pallas_call | solution.py:694
  521.7 48.9 %expert_unit.6 = (bf16[8,2,288,2048]{3,2,1,0:T(8,128)(2,1)}, bf16[8,2,288,2048]{3,2,1,0:T(8,128)(2,1)}, bf16[8,2,288,1024]{3,2,1,0:T(8,128)(2,1)}, bf16[8,2,288,...) custom-call(s32[2]{0:T(128)} %pad_add_fusion.8.unit, ...), custom_call_target="tpu_custom_call", output_to_operand_aliasing={{0}: (10, {}), {1}: (11, {}), {2}: (12, {}), {3}: (13, {}),... | custom-call | tf_op jit(solution)/shard_map/expert_unit/pallas_call | solution.py:694
  578.4 49.2 %expert_unit.7 = (bf16[8,2,288,2048]{3,2,1,0:T(8,128)(2,1)}, bf16[8,2,288,2048]{3,2,1,0:T(8,128)(2,1)}, bf16[8,2,288,1024]{3,2,1,0:T(8,128)(2,1)}, bf16[8,2,288,...) custom-call(s32[2]{0:T(128)} %pad_add_fusion.5.unit, ...), custom_call_target="tpu_custom_call", output_to_operand_aliasing={{0}: (10, {}), {1}: (11, {}), {2}: (12, {}), {3}: (13, {}),... | custom-call | tf_op jit(solution)/shard_map/expert_unit/pallas_call | solution.py:694
  627.7 44.9 %expert_out.1 = bf16[8,512,2048]{2,1,0:T(8,128)(2,1)} custom-call(bf16[8,2,288,1024]{3,2,1,0:T(8,128)(2,1)} %get-tuple-element.313.hidden, bf16[2,1024,2048]{2,1,0:T(8,128)(2,1)} %join.6.w_down, s32[8,2,512]{2,1,0:T(2,128)} %copy.201.slots, f32[8,2,512]{2,1,0:T(2,128)} %get-tuple-element.262.gates, s32[8,512,2]{2,1,0:T(8,128)} %select_bitcast_fusion.columns), custom_call_target="tpu_custom_call" | custom-call | tf_op jit(solution)/shard_map/expert_out/pallas_call | solution.py:755
  672.6 26.9 %bitcast_convert_fusion.2 = bf16[2,1024,2048]{2,1,0:T(8,128)(2,1)} fusion(bf16[8,2,288,1024]{3,2,1,0:T(8,128)(2,1)} %get-tuple-element.313.hidden, bf16[8,2,288,2048]{3,2,1,0:T(8,128)(2,1)} %get-tuple-element.314), kind=kOutput, calls=%fused_computation.3 | convolution fusion | flops 19331547136 | bytes 36700160 | tf_op jit(solution)/shard_map/sncf,sncd->nfd/dot_general | solution.py:991
  706.7 27.6 %bitcast_convert_fusion = bf16[2,2048,1024]{2,1,0:T(8,128)(2,1)} fusion(bf16[8,2,288,2048]{3,2,1,0:T(8,128)(2,1)} %get-tuple-element.317, bf16[8,2,288,1024]{3,2,1,0:T(8,128)(2,1)} %get-tuple-element.319), kind=kOutput, calls=%fused_computation.1 | convolution fusion | flops 19331547136 | bytes 36700160 | tf_op jit(solution)/shard_map/sncd,sncf->ndf/dot_general | solution.py:996
  734.4 24.8 %bitcast_convert_fusion.1 = bf16[2,2048,1024]{2,1,0:T(8,128)(2,1)} fusion(bf16[8,2,288,2048]{3,2,1,0:T(8,128)(2,1)} %get-tuple-element.317, bf16[8,2,288,1024]{3,2,1,0:T(8,128)(2,1)S(1)} %bitcast.137), kind=kOutput, calls=%fused_computation.2 | convolution fusion | flops 19331547136 | bytes 36700160 | tf_op jit(solution)/shard_map/sncd,sncf->ndf/dot_general | solution.py:995
  759.2 37.7 %collective-permute-done.43 = bf16[2,256,2048]{2,1,0:T(8,128)(2,1)} collective-permute-done((bf16[2,256,2048]{2,1,0:T(8,128)(2,1)S(1)}, bf16[2,256,2048]{2,1,0:T(8,128)(2,1)}, u32[]{:S(2)}, u32[]{:S(2)}) %collective-permute-start.43) | collective-permute-done | bytes 2097184 | tf_op jit(solution)/shard_map/ppermute | solution.py:407
  806.1 10.0 convolution_convert_fusion.1
  859.2 27.0 %collective-permute-done.47 = bf16[2,512,1024]{2,1,0:T(8,128)(2,1)} collective-permute-done((bf16[2,512,1024]{2,1,0:T(8,128)(2,1)}, bf16[2,512,1024]{2,1,0:T(8,128)(2,1)}, u32[]{:S(2)}, u32[]{:S(2)}) %collective-permute-start.47) | collective-permute-done | bytes 2097184 | tf_op jit(solution)/shard_map/ppermute | solution.py:407
  887.6 28.8 %all-to-all-done.2 = bf16[8,512,256]{2,1,0:T(8,128)(2,1)} async-done(((bf16[8,512,256]{2,1,0:T(8,128)(2,1)}), bf16[8,512,256]{2,1,0:T(8,128)(2,1)}, u32[]{:S(2)}, u32[]{:S(2)}) %all-to-all-start.2) | async-done | bytes 2097184 | tf_op jit(solution)/shard_map/all_to_all | solution.py:1013
  923.8 67.7 %attention_backward.1 = (f32[4096,256]{1,0:T(8,128)}, f32[4096,256]{1,0:T(8,128)}, bf16[4096,256]{1,0:T(8,128)(2,1)}) custom-call(s32[16]{0:T(128)} %get-tuple-element.239.place, s32[8]{0:T(128)} %compare_select_fusion.first_tile, bf16[4096,256]{1,0:T(8,128)(2,1)} %get-tuple-element.241.queries, bf16[4096,256]{1,0:T(8,128)(2,1)} %get-tuple-element.242.keys, ...), custom_call_target="tpu_custom_call" | custom-call | flops 21474836480 | bytes 25165824 | tf_op jit(solution)/shard_map/attention_backward/pallas_call | solution.py:315
  1014.1 20.2 %convolution_convert_fusion = bf16[4096,2048]{1,0:T(8,128)(2,1)} fusion(bf16[2048,768]{1,0:T(8,128)(2,1)S(1)} %copy-done.3, bf16[4096,256]{1,0:T(8,128)(2,1)} %get-tuple-element.332, bf16[4096,256]{1,0:T(8,128)(2,1)} %get-tuple-element.398, bf16[4096,256]{1,0:T(8,128)(2,1)} %get-tuple-element.397), kind=kOutput, calls=%fused_computation.5 | convolution fusion | flops 12912164864 | bytes 26214400 | tf_op jit(solution)/shard_map/dot_general | solution.py:1064
  1035.8 19.4 %convolution_convert_fusion.2 = bf16[2048,768]{1,0:T(8,128)(2,1)S(1)} fusion(bf16[4096,2048]{1,0:T(8,128)(2,1)} %get-tuple-element.233, bf16[4096,256]{1,0:T(8,128)(2,1)} %get-tuple-element.332, bf16[4096,256]{1,0:T(8,128)(2,1)} %get-tuple-element.398, bf16[4096,256]{1,0:T(8,128)(2,1)S(1)} %copy-done.35), kind=kOutput, calls=%fused_computation.44 | convolution fusion | flops 12905349120 | bytes 26214400 | tf_op jit(solution)/shard_map/dot_general | solution.py:1077
  1065.4 15.0 %multiply_reduce_fusion = f32[2048]{0:T(1024)S(1)} fusion(bf16[4096,2048]{1,0:T(8,128)(2,1)} %get-tuple-element.233, bf16[4096,2048]{1,0:T(8,128)(2,1)} %convolution_convert_fusion), kind=kLoop, calls=%fused_computation | loop fusion | flops 33552384 | bytes 33562624 | tf_op jit(solution)/shard_map/reduce_sum | solution.py:1084
  1095.3 12.6 all-to-all-done.3
  1141.2 28.0 %collective-permute-done.63 = bf16[528,1024]{1,0:T(8,128)(2,1)} collective-permute-done((bf16[528,1024]{1,0:T(8,128)(2,1)S(1)}, bf16[528,1024]{1,0:T(8,128)(2,1)}, u32[]{:S(2)}, u32[]{:S(2)}) %collective-permute-start.63) | collective-permute-done | bytes 1081376 | tf_op jit(solution)/shard_map/ppermute | solution.py:386
  1190.0 50.6 %collective-permute-done.68 = bf16[528,1024]{1,0:T(8,128)(2,1)} collective-permute-done((bf16[528,1024]{1,0:T(8,128)(2,1)}, bf16[528,1024]{1,0:T(8,128)(2,1)}, u32[]{:S(2)}, u32[]{:S(2)}) %collective-permute-start.68) | collective-permute-done | bytes 1081376 | tf_op jit(solution)/shard_map/ppermute | solution.py:386
  1263.3 22.0 %collective-permute-done.72 = bf16[528,1024]{1,0:T(8,128)(2,1)} collective-permute-done((bf16[528,1024]{1,0:T(8,128)(2,1)}, bf16[528,1024]{1,0:T(8,128)(2,1)}, u32[]{:S(2)}, u32[]{:S(2)}) %collective-permute-start.72) | collective-permute-done | bytes 1081376 | tf_op jit(solution)/shard_map/ppermute | solution.py:386
  (433 shorter events, 409.2 us)
Async XLA Ops:
  7.2 234.1 %all-gather.3.cloned.1.call-start = ((), (), s32[]{:S(2)}) async-start(), calls=%async_computation.7 | async-start | bytes 10485760 | tf_op jit(solution)/shard_map/all_gather | solution.py:863
  7.3 54.8 %collective-permute-start.2 = (bf16[512,2048]{1,0:T(8,128)(2,1)}, bf16[512,2048]{1,0:T(8,128)(2,1)}, u32[]{:S(2)}, u32[]{:S(2)}) collective-permute-start(bf16[512,2048]{1,0:T(8,128)(2,1)} %own.1), channel_id=1, source_target_pairs={{0,1},{1,0},{2,3},{3,2},{4,5},{5,4},{6,7},{7,6},{8,9},{9,8},{10,11... | collective-permute-start | bytes 6291464 | tf_op jit(solution)/shard_map/ppermute | solution.py:390
  7.8 54.3 %collective-permute-start.1 = (bf16[512,2048]{1,0:T(8,128)(2,1)}, bf16[512,2048]{1,0:T(8,128)(2,1)}, u32[]{:S(2)}, u32[]{:S(2)}) collective-permute-start(bf16[512,2048]{1,0:T(8,128)(2,1)} %own.1), channel_id=1, source_target_pairs={{2,0},{3,1},{4,2},{5,3},{6,4},{7,5},{10,8},{11,9},{12,10},{13,11},... | collective-permute-start | bytes 6291464 | tf_op jit(solution)/shard_map/ppermute | solution.py:386
  9.2 52.8 %collective-permute-start = (bf16[512,2048]{1,0:T(8,128)(2,1)}, bf16[512,2048]{1,0:T(8,128)(2,1)}, u32[]{:S(2)}, u32[]{:S(2)}) collective-permute-start(bf16[512,2048]{1,0:T(8,128)(2,1)} %own.1), channel_id=1, source_target_pairs={{0,2},{1,3},{2,4},{3,5},{4,6},{5,7},{8,10},{9,11},{10,12},{11,13},... | collective-permute-start | bytes 6291464 | tf_op jit(solution)/shard_map/ppermute | solution.py:385
  62.1 330.0 %all-gather.5.cloned.1.call-start = ((), (), s32[]{:S(2)}) async-start(), calls=%async_computation.8 | async-start | bytes 18874368 | tf_op jit(solution)/shard_map/all_gather | solution.py:895
  120.6 52.4 %collective-permute-start.12 = (bf16[512,2048]{1,0:T(8,128)(2,1)}, bf16[512,2048]{1,0:T(8,128)(2,1)}, u32[]{:S(2)}, u32[]{:S(2)}) collective-permute-start(bf16[512,2048]{1,0:T(8,128)(2,1)} %collective-permute-done.9), channel_id=1, source_target_pairs={{4,6},{5,7},{12,14},{13,15},{20,22},{21,23},{28,30},{29,31}} | collective-permute-start | bytes 6291464 | tf_op jit(solution)/shard_map/ppermute | solution.py:385
  188.7 52.6 %collective-permute-start.23 = (bf16[2,256,2048]{2,1,0:T(8,128)(2,1)}, bf16[2,256,2048]{2,1,0:T(8,128)(2,1)S(1)}, u32[]{:S(2)}, u32[]{:S(2)}) collective-permute-start(bf16[2,256,2048]{2,1,0:T(8,128)(2,1)} %refs_0_), channel_id=1, source_target_pairs={{0,16},{8,24},{16,0},{24,8},{1,17},{9,25},{17,1},{25,9},{2,18},{10... | collective-permute-start | bytes 6291464 | tf_op jit(solution)/shard_map/ppermute | solution.py:407
  241.3 71.0 %collective-permute-start.26 = (bf16[2,512,1024]{2,1,0:T(8,128)(2,1)}, bf16[2,512,1024]{2,1,0:T(8,128)(2,1)}, u32[]{:S(2)}, u32[]{:S(2)}) collective-permute-start(bf16[2,512,1024]{2,1,0:T(8,128)(2,1)} %refs_0_.1), channel_id=1, source_target_pairs={{0,16},{8,24},{16,0},{24,8},{1,17},{9,25},{17,1},{25,9},{2,18},{10... | collective-permute-start | bytes 6291464 | tf_op jit(solution)/shard_map/ppermute | solution.py:407
  242.7 69.7 %collective-permute-start.25 = (bf16[2,512,1024]{2,1,0:T(8,128)(2,1)}, bf16[2,512,1024]{2,1,0:T(8,128)(2,1)}, u32[]{:S(2)}, u32[]{:S(2)}) collective-permute-start(bf16[2,512,1024]{2,1,0:T(8,128)(2,1)} %refs_0_.1), channel_id=1, source_target_pairs={{0,8},{8,0},{16,24},{24,16},{1,9},{9,1},{17,25},{25,17},{2,10},{10... | collective-permute-start | bytes 6291464 | tf_op jit(solution)/shard_map/ppermute | solution.py:407
  245.5 66.8 %collective-permute-start.24 = (bf16[256,2048]{1,0:T(8,128)(2,1)S(1)}, bf16[256,2048]{1,0:T(8,128)(2,1)}, u32[]{:S(2)}, u32[]{:S(2)}) collective-permute-start(bf16[256,2048]{1,0:T(8,128)(2,1)S(1)} %constant_dynamic-slice_fusion.20), channel_id=1, source_target_pairs={{0,24},{8,16},{16,8},{24,0},{1,25},{9,17},{17,9},{25,1},{2,26},{10... | collective-permute-start | bytes 3145736 | tf_op jit(solution)/shard_map/ppermute | solution.py:407
  315.9 53.1 %collective-permute-start.27 = (bf16[1024,2048]{1,0:T(8,128)(2,1)}, bf16[1024,2048]{1,0:T(8,128)(2,1)}, u32[]{:S(2)}, u32[]{:S(2)}) collective-permute-start(bf16[1024,2048]{1,0:T(8,128)(2,1)} %pad_maximum_fusion.1.refs_0_), channel_id=1, source_target_pairs={{0,1},{1,0},{2,3},{3,2},{4,5},{5,4},{6,7},{7,6},{8,9},{9,8},{10,11... | collective-permute-start | bytes 12582920 | tf_op jit(solution)/shard_map/ppermute | solution.py:390
  319.9 57.9 %all-to-all-start.1 = ((bf16[8,512,256]{1,2,0:T(8,128)(2,1)}), bf16[8,512,256]{1,2,0:T(8,128)(2,1)}, u32[]{:S(2)}, u32[]{:S(2)}) async-start(bf16[8,512,256]{1,2,0:T(8,128)(2,1)} %copy.200), calls=%async_computation.1 | async-start | bytes 4194304 | tf_op jit(solution)/shard_map/all_to_all | solution.py:934
  324.2 474.0 %reduce-scatter.4.cloned.1.call-start = ((), (), s32[]{:S(2)}) async-start(), calls=%async_computation.9 | async-start | bytes 18874368 | tf_op jit(solution)/shard_map/reduce_scatter | solution.py:986
  392.1 67.3 %collective-permute-start.33 = (bf16[512,2048]{1,0:T(8,128)(2,1)}, bf16[512,2048]{1,0:T(8,128)(2,1)}, u32[]{:S(2)}, u32[]{:S(2)}) collective-permute-start(bf16[512,2048]{1,0:T(8,128)(2,1)} %multiply_convert_fusion.2.own), channel_id=1, source_target_pairs={{2,0},{3,1},{4,2},{5,3},{6,4},{7,5},{10,8},{11,9},{12,10},{13,11},... | collective-permute-start | bytes 6291464 | tf_op jit(solution)/shard_map/ppermute | solution.py:386
  393.3 66.0 %collective-permute-start.32 = (bf16[512,2048]{1,0:T(8,128)(2,1)}, bf16[512,2048]{1,0:T(8,128)(2,1)}, u32[]{:S(2)}, u32[]{:S(2)}) collective-permute-start(bf16[512,2048]{1,0:T(8,128)(2,1)} %multiply_convert_fusion.2.own), channel_id=1, source_target_pairs={{0,2},{1,3},{2,4},{3,5},{4,6},{5,7},{8,10},{9,11},{10,12},{11,13},... | collective-permute-start | bytes 6291464 | tf_op jit(solution)/shard_map/ppermute | solution.py:385
  461.3 53.3 %collective-permute-start.36 = (bf16[512,2048]{1,0:T(8,128)(2,1)}, bf16[512,2048]{1,0:T(8,128)(2,1)}, u32[]{:S(2)}, u32[]{:S(2)}) collective-permute-start(bf16[512,2048]{1,0:T(8,128)(2,1)} %collective-permute-done.33), channel_id=1, source_target_pairs={{2,0},{3,1},{4,2},{5,3},{10,8},{11,9},{12,10},{13,11},{18,16},{19,... | collective-permute-start | bytes 6291464 | tf_op jit(solution)/shard_map/ppermute | solution.py:386
  517.5 53.2 %collective-permute-start.38 = (bf16[512,2048]{1,0:T(8,128)(2,1)}, bf16[512,2048]{1,0:T(8,128)(2,1)}, u32[]{:S(2)}, u32[]{:S(2)}) collective-permute-start(bf16[512,2048]{1,0:T(8,128)(2,1)} %collective-permute-done.35), channel_id=1, source_target_pairs={{4,6},{5,7},{12,14},{13,15},{20,22},{21,23},{28,30},{29,31}} | collective-permute-start | bytes 6291464 | tf_op jit(solution)/shard_map/ppermute | solution.py:385
  627.6 406.6 %reduce-scatter.6.cloned.1.call-start = ((), (), s32[]{:S(2)}) async-start(), calls=%async_computation.10 | async-start | bytes 18874368 | tf_op jit(solution)/shard_map/reduce_scatter | solution.py:1001
  703.2 56.0 %collective-permute-start.44 = (bf16[2,256,2048]{2,1,0:T(8,128)(2,1)S(1)}, bf16[2,256,2048]{2,1,0:T(8,128)(2,1)}, u32[]{:S(2)}, u32[]{:S(2)}) collective-permute-start(bf16[2,256,2048]{2,1,0:T(8,128)(2,1)S(1)} %get-tuple-element.403), channel_id=1, source_target_pairs={{0,24},{8,16},{16,8},{24,0},{1,25},{9,17},{17,9},{25,1},{2,26},{10... | collective-permute-start | bytes 6291464 | tf_op jit(solution)/shard_map/ppermute | solution.py:407
  705.3 91.6 %collective-permute-start.43 = (bf16[2,256,2048]{2,1,0:T(8,128)(2,1)S(1)}, bf16[2,256,2048]{2,1,0:T(8,128)(2,1)}, u32[]{:S(2)}, u32[]{:S(2)}) collective-permute-start(bf16[2,256,2048]{2,1,0:T(8,128)(2,1)S(1)} %get-tuple-element.404), channel_id=1, source_target_pairs={{0,16},{8,24},{16,0},{24,8},{1,17},{9,25},{17,1},{25,9},{2,18},{10... | collective-permute-start | bytes 6291464 | tf_op jit(solution)/shard_map/ppermute | solution.py:407
  706.1 90.8 %collective-permute-start.42 = (bf16[2,256,2048]{2,1,0:T(8,128)(2,1)S(1)}, bf16[2,256,2048]{2,1,0:T(8,128)(2,1)}, u32[]{:S(2)}, u32[]{:S(2)}) collective-permute-start(bf16[2,256,2048]{2,1,0:T(8,128)(2,1)S(1)} %get-tuple-element.405), channel_id=1, source_target_pairs={{0,8},{8,0},{16,24},{24,16},{1,9},{9,1},{17,25},{25,17},{2,10},{10... | collective-permute-start | bytes 6291464 | tf_op jit(solution)/shard_map/ppermute | solution.py:407
  827.1 89.3 %all-to-all-start.2 = ((bf16[8,512,256]{2,1,0:T(8,128)(2,1)}), bf16[8,512,256]{2,1,0:T(8,128)(2,1)}, u32[]{:S(2)}, u32[]{:S(2)}) async-start(bf16[8,512,256]{2,1,0:T(8,128)(2,1)} %bitcast.126), calls=%async_computation.3 | async-start | bytes 4194304 | tf_op jit(solution)/shard_map/all_to_all | solution.py:1013
  832.5 467.8 %reduce-scatter.8.cloned.1.call-start = ((), (), s32[]{:S(2)}) async-start(), calls=%async_computation.11 | async-start | bytes 18874368 | tf_op jit(solution)/shard_map/reduce_scatter | solution.py:1067
  848.7 67.7 %collective-permute-start.49 = (bf16[512,1024]{1,0:T(8,128)(2,1)}, bf16[512,1024]{1,0:T(8,128)(2,1)}, u32[]{:S(2)}, u32[]{:S(2)}) collective-permute-start(bf16[512,1024]{1,0:T(8,128)(2,1)} %get-tuple-element.409), channel_id=1, source_target_pairs={{0,16},{8,24},{16,0},{24,8},{1,17},{9,25},{17,1},{25,9},{2,18},{10... | collective-permute-start | bytes 3145736 | tf_op jit(solution)/shard_map/ppermute | solution.py:407
  849.6 66.8 %collective-permute-start.48 = (bf16[512,1024]{1,0:T(8,128)(2,1)S(1)}, bf16[512,1024]{1,0:T(8,128)(2,1)}, u32[]{:S(2)}, u32[]{:S(2)}) collective-permute-start(bf16[512,1024]{1,0:T(8,128)(2,1)S(1)} %get-tuple-element.410), channel_id=1, source_target_pairs={{0,8},{8,0},{16,24},{24,16},{1,9},{9,1},{17,25},{25,17},{2,10},{10... | collective-permute-start | bytes 3145736 | tf_op jit(solution)/shard_map/ppermute | solution.py:407
  919.5 72.0 %collective-permute-start.51 = (bf16[2,512,1024]{2,1,0:T(8,128)(2,1)}, bf16[2,512,1024]{2,1,0:T(8,128)(2,1)S(1)}, u32[]{:S(2)}, u32[]{:S(2)}) collective-permute-start(bf16[2,512,1024]{2,1,0:T(8,128)(2,1)} %constant_dynamic-slice_fusion.10), channel_id=1, source_target_pairs={{0,24},{8,16},{16,8},{24,0},{1,25},{9,17},{17,9},{25,1},{2,26},{10... | collective-permute-start | bytes 6291464 | tf_op jit(solution)/shard_map/ppermute | solution.py:407
  922.8 68.7 %collective-permute-start.50 = (bf16[512,1024]{1,0:T(8,128)(2,1)S(1)}, bf16[512,1024]{1,0:T(8,128)(2,1)}, u32[]{:S(2)}, u32[]{:S(2)}) collective-permute-start(bf16[512,1024]{1,0:T(8,128)(2,1)S(1)} %constant_dynamic-slice_fusion.11), channel_id=1, source_target_pairs={{0,24},{8,16},{16,8},{24,0},{1,25},{9,17},{17,9},{25,1},{2,26},{10... | collective-permute-start | bytes 3145736 | tf_op jit(solution)/shard_map/ppermute | solution.py:407
  1112.7 57.7 %collective-permute-start.66 = (bf16[2,512,1024]{2,1,0:T(8,128)(2,1)}, bf16[2,512,1024]{2,1,0:T(8,128)(2,1)}, u32[]{:S(2)}, u32[]{:S(2)}) collective-permute-start(bf16[2,512,1024]{2,1,0:T(8,128)(2,1)} %get-tuple-element.399), channel_id=1, source_target_pairs={{0,16},{8,24},{16,0},{24,8},{1,17},{9,25},{17,1},{25,9},{2,18},{10... | collective-permute-start | bytes 6291464 | tf_op jit(solution)/shard_map/ppermute | solution.py:407
  1113.7 56.7 %collective-permute-start.65 = (bf16[2,512,1024]{2,1,0:T(8,128)(2,1)}, bf16[2,512,1024]{2,1,0:T(8,128)(2,1)}, u32[]{:S(2)}, u32[]{:S(2)}) collective-permute-start(bf16[2,512,1024]{2,1,0:T(8,128)(2,1)} %get-tuple-element.400), channel_id=1, source_target_pairs={{0,8},{8,0},{16,24},{24,16},{1,9},{9,1},{17,25},{25,17},{2,10},{10... | collective-permute-start | bytes 6291464 | tf_op jit(solution)/shard_map/ppermute | solution.py:407
  1173.9 66.7 %collective-permute-start.70 = (bf16[2,512,1024]{2,1,0:T(8,128)(2,1)}, bf16[2,512,1024]{2,1,0:T(8,128)(2,1)}, u32[]{:S(2)}, u32[]{:S(2)}) collective-permute-start(bf16[2,512,1024]{2,1,0:T(8,128)(2,1)} %constant_dynamic-slice_fusion), channel_id=1, source_target_pairs={{0,24},{8,16},{16,8},{24,0},{1,25},{9,17},{17,9},{25,1},{2,26},{10... | collective-permute-start | bytes 6291464 | tf_op jit(solution)/shard_map/ppermute | solution.py:407
  1176.5 64.1 %collective-permute-start.68 = (bf16[528,1024]{1,0:T(8,128)(2,1)}, bf16[528,1024]{1,0:T(8,128)(2,1)}, u32[]{:S(2)}, u32[]{:S(2)}) collective-permute-start(bf16[528,1024]{1,0:T(8,128)(2,1)} %collective-permute-done.63), channel_id=1, source_target_pairs={{2,0},{3,1},{4,2},{5,3},{10,8},{11,9},{12,10},{13,11},{18,16},{19,... | collective-permute-start | bytes 3244040 | tf_op jit(solution)/shard_map/ppermute | solution.py:386
  1177.8 62.8 %collective-permute-start.67 = (bf16[528,1024]{1,0:T(8,128)(2,1)}, bf16[528,1024]{1,0:T(8,128)(2,1)}, u32[]{:S(2)}, u32[]{:S(2)}) collective-permute-start(bf16[528,1024]{1,0:T(8,128)(2,1)} %copy-done.30), channel_id=1, source_target_pairs={{2,4},{3,5},{4,6},{5,7},{10,12},{11,13},{12,14},{13,15},{18,20},{1... | collective-permute-start | bytes 3244040 | tf_op jit(solution)/shard_map/ppermute | solution.py:385
  (115 other events, 2735.4 us)
Sparse Core Ops, SparseCore 0:
  62.2 111.7 all-gather.2
  175.5 154.8 all-gather.4
  627.7 170.4 reduce-scatter.3
  800.4 199.7 reduce-scatter.5
  1034.4 233.5 reduce-scatter.7

commit v6 on v5

--- a/solution.py
+++ b/solution.py
@@ -1155,6 +1155,12 @@
         if turn == 2:
             grad_up = total_dp(grad_up, up_pieces, 1)
             up_pieces = []
+        if turn + 2 == line.chips:
+            grad_normed = grad_normed.astype(f32)
+            inv_in = rms_scale(inputs)
+            hat_in = inputs * inv_in
+            input_grad = grad_state + rms_back(grad_normed * gain_attn, hat_in, inv_in)
+            up_pieces = [*up_pieces, input_grad.astype(bf16)]
         if turn + 1 < line.chips:
             below, above, qkv_kept[0], out_kept[0], grad_up, gate_sum, *up_pieces = barrier(
                 below, above, qkv_kept[0], out_kept[0], grad_up, gate_sum, *up_pieces
@@ -1162,15 +1168,8 @@
             arrived[-turn - 1], arrived[turn + 1] = below, above
     qkv_total, out_total = qkv_kept[0], out_kept[0]
     up_sum = grad_up
+    input_grad = up_pieces[-1]
     gain_terms = gain_terms.reshape(-1)[:gain_size].reshape(gain_shape)
-    out_total, qkv_total, up_sum, output, gain_terms, grad_normed = barrier(
-        out_total, qkv_total, up_sum, output, gain_terms, grad_normed
-    )
-
-    grad_normed = grad_normed.astype(f32)
-    inv_in = rms_scale(inputs)
-    hat_in = inputs * inv_in
-    input_grad = (grad_state + rms_back(grad_normed * gain_attn, hat_in, inv_in)).astype(bf16)
     return (
         output,
         input_grad,

time: 1320 us -> 1320 us (level)
  transfers between devices with their start and end apart: 84 -> 84, of which waited for: 30 -> 31; matrix products, arithmetic and copies ran while one was open for 25% -> 25% of each run, Pallas kernels for 32% -> 31%
where the time goes in v6:
time: 1320 us; the launch traced here: 1310 us
  Pallas kernels  467 us (35%)
  waiting for transfers between devices  359 us (27%)
  matrix products  141 us (11%)
  other arithmetic  127 us (10%)
  starting transfers between devices  115 us (9%)
  local copies, waits for them, and re-layouts  81.4 us (6%)
  between operations  21.1 us (2%)
    pallas_call x4, Pallas kernels, expert_unit(): pl.pallas_call(expert_kernel, grid_spec=pltpu.PrefetchScalarGridSpec(num_...  196 us
    ppermute x35, waiting for transfers between devices, swap_dp(): return lax.ppermute(part, 'dp', swap_partners(lax.axis_size('dp'), shift))  179 us
    ppermute x9, waiting for transfers between devices, step(): lax.ppermute(from_above, 'ctx', down)  118 us
    pallas_call x1, Pallas kernels, attention_backward(): pl.pallas_call(functools.partial(backward_kernel, tile, prompt_tiles, blo...  67.7 us
    pallas_call x1, Pallas kernels, attention_forward(): pl.pallas_call(functools.partial(forward_kernel, tile, prompt_tiles, bloc...  53.2 us
    pallas_call x1, Pallas kernels, expert_out(): pl.pallas_call(out_kernel, grid=(peers // 2, experts), in_specs=[pl.Block...  44.9 us
    pallas_call x4, Pallas kernels, project(): pl.pallas_call(project_kernel, grid_spec=pltpu.PrefetchScalarGridSpec(num...  42.8 us
    ppermute x35, starting transfers between devices, swap_dp(): return lax.ppermute(part, 'dp', swap_partners(lax.axis_size('dp'), shift))  41.7 us
  transfers between devices with their start and end apart: 84, of which 31 were waited for; matrix products, arithmetic and copies ran while one was open for 25% of the time, Pallas kernels for 31%

profile of v6, /device:TPU:0, one launch (start us, length us, event | category | flops | bytes accessed | tf_op | source)
XLA Modules:
  0.0 1312.3 jit_solution(16766006159329372137)
XLA Ops:
  28.0 9.7 collective-permute-done.3
  45.6 15.2 %collective-permute-done.7.refs_2_ = bf16[512,768]{1,0:T(8,128)(2,1)} collective-permute-done((bf16[512,768]{1,0:T(8,128)(2,1)S(1)}, bf16[512,768]{1,0:T(8,128)(2,1)}, u32[]{:S(2)}, u32[]{:S(2)}) %collective-permute-start.7) | collective-permute-done | bytes 786464 | tf_op jit(solution)/shard_map/ppermute | solution.py:407
  79.2 10.6 project.4
  89.8 27.0 %collective-permute-done.10 = bf16[512,2048]{1,0:T(8,128)(2,1)} collective-permute-done((bf16[512,2048]{1,0:T(8,128)(2,1)}, bf16[512,2048]{1,0:T(8,128)(2,1)}, u32[]{:S(2)}, u32[]{:S(2)}) %collective-permute-start.10) | collective-permute-done | bytes 2097184 | tf_op jit(solution)/shard_map/ppermute | solution.py:386
  128.0 10.6 project.5
  138.7 33.9 %collective-permute-done.16 = bf16[256,2048]{1,0:T(8,128)(2,1)S(1)} collective-permute-done((bf16[256,2048]{1,0:T(8,128)(2,1)S(1)}, bf16[256,2048]{1,0:T(8,128)(2,1)S(1)}, u32[]{:S(2)}, u32[]{:S(2)}) %collective-permute-start.16) | collective-permute-done | bytes 1048608 | tf_op jit(solution)/shard_map/ppermute | solution.py:407
  177.9 10.8 project.6
  199.3 8.8 all-to-all-done
  210.6 10.7 project.7
  246.6 53.2 %attention_forward.1 = (bf16[4096,256]{1,0:T(8,128)(2,1)}, f32[2,8,512]{2,1,0:T(8,128)}, bf16[4096,256]{1,0:T(8,128)(2,1)}, bf16[4096,256]{1,0:T(8,128)(2,1)}, bf16[4096,256]{1,0:T(8,128)(2,1)}) custom-call(s32[16]{0:T(128)} %get-tuple-element.233.place, s32[8]{0:T(128)} %compare_select_fusion.first_tile, f32[4096,768]{1,0:T(8,128)} %get-tuple-element.234.raw_q.raw_k.raw_v, ...), custom_call_target="tpu_custom_call" | custom-call | flops 17179869184 | bytes 25165824 | tf_op jit(solution)/shard_map/attention_forward/pallas_call | solution.py:266
  299.8 12.4 collective-permute-done.24
  330.6 22.8 %collective-permute-done.29.refs_4_ = bf16[2,128,2048]{2,1,0:T(8,128)(2,1)S(1)} collective-permute-done((bf16[2,128,2048]{2,1,0:T(8,128)(2,1)}, bf16[2,128,2048]{2,1,0:T(8,128)(2,1)S(1)}, u32[]{:S(2)}, u32[]{:S(2)}) %collective-permute-start.29) | collective-permute-done | bytes 1048608 | tf_op jit(solution)/shard_map/ppermute | solution.py:407
  410.4 49.0 %expert_unit.4 = (bf16[8,2,288,2048]{3,2,1,0:T(8,128)(2,1)}, bf16[8,2,288,2048]{3,2,1,0:T(8,128)(2,1)}, bf16[8,2,288,1024]{3,2,1,0:T(8,128)(2,1)}, bf16[8,2,288,...) custom-call(s32[2]{0:T(128)} %pad_add_fusion.5.unit, ...), custom_call_target="tpu_custom_call" | custom-call | tf_op jit(solution)/shard_map/expert_unit/pallas_call | solution.py:694
  465.6 48.9 %expert_unit.5 = (bf16[8,2,288,2048]{3,2,1,0:T(8,128)(2,1)}, bf16[8,2,288,2048]{3,2,1,0:T(8,128)(2,1)}, bf16[8,2,288,1024]{3,2,1,0:T(8,128)(2,1)}, bf16[8,2,288,...) custom-call(s32[2]{0:T(128)} %pad_add_fusion.6.unit, ...), custom_call_target="tpu_custom_call", output_to_operand_aliasing={{0}: (10, {}), {1}: (11, {}), {2}: (12, {}), {3}: (13, {}),... | custom-call | tf_op jit(solution)/shard_map/expert_unit/pallas_call | solution.py:694
  521.7 48.9 %expert_unit.6 = (bf16[8,2,288,2048]{3,2,1,0:T(8,128)(2,1)}, bf16[8,2,288,2048]{3,2,1,0:T(8,128)(2,1)}, bf16[8,2,288,1024]{3,2,1,0:T(8,128)(2,1)}, bf16[8,2,288,...) custom-call(s32[2]{0:T(128)} %pad_add_fusion.7.unit, ...), custom_call_target="tpu_custom_call", output_to_operand_aliasing={{0}: (10, {}), {1}: (11, {}), {2}: (12, {}), {3}: (13, {}),... | custom-call | tf_op jit(solution)/shard_map/expert_unit/pallas_call | solution.py:694
  578.4 49.1 %expert_unit.7 = (bf16[8,2,288,2048]{3,2,1,0:T(8,128)(2,1)}, bf16[8,2,288,2048]{3,2,1,0:T(8,128)(2,1)}, bf16[8,2,288,1024]{3,2,1,0:T(8,128)(2,1)}, bf16[8,2,288,...) custom-call(s32[2]{0:T(128)} %pad_add_fusion.4.unit, ...), custom_call_target="tpu_custom_call", output_to_operand_aliasing={{0}: (10, {}), {1}: (11, {}), {2}: (12, {}), {3}: (13, {}),... | custom-call | tf_op jit(solution)/shard_map/expert_unit/pallas_call | solution.py:694
  627.6 44.9 %expert_out.1 = bf16[8,512,2048]{2,1,0:T(8,128)(2,1)} custom-call(bf16[8,2,288,1024]{3,2,1,0:T(8,128)(2,1)} %get-tuple-element.307.hidden, bf16[2,1024,2048]{2,1,0:T(8,128)(2,1)} %join.6.w_down, s32[8,2,512]{2,1,0:T(2,128)} %copy.201.slots, f32[8,2,512]{2,1,0:T(2,128)} %get-tuple-element.256.gates, s32[8,512,2]{2,1,0:T(8,128)} %select_bitcast_fusion.columns), custom_call_target="tpu_custom_call" | custom-call | tf_op jit(solution)/shard_map/expert_out/pallas_call | solution.py:755
  672.5 26.9 %bitcast_convert_fusion.2 = bf16[2,1024,2048]{2,1,0:T(8,128)(2,1)} fusion(bf16[8,2,288,1024]{3,2,1,0:T(8,128)(2,1)} %get-tuple-element.307.hidden, bf16[8,2,288,2048]{3,2,1,0:T(8,128)(2,1)} %get-tuple-element.308), kind=kOutput, calls=%fused_computation.3 | convolution fusion | flops 19331547136 | bytes 36700160 | tf_op jit(solution)/shard_map/sncf,sncd->nfd/dot_general | solution.py:991
  706.6 27.6 %bitcast_convert_fusion = bf16[2,2048,1024]{2,1,0:T(8,128)(2,1)} fusion(bf16[8,2,288,2048]{3,2,1,0:T(8,128)(2,1)} %get-tuple-element.311, bf16[8,2,288,1024]{3,2,1,0:T(8,128)(2,1)} %get-tuple-element.313), kind=kOutput, calls=%fused_computation.1 | convolution fusion | flops 19331547136 | bytes 36700160 | tf_op jit(solution)/shard_map/sncd,sncf->ndf/dot_general | solution.py:996
  734.3 24.8 %bitcast_convert_fusion.1 = bf16[2,2048,1024]{2,1,0:T(8,128)(2,1)} fusion(bf16[8,2,288,2048]{3,2,1,0:T(8,128)(2,1)} %get-tuple-element.311, bf16[8,2,288,1024]{3,2,1,0:T(8,128)(2,1)S(1)} %bitcast.137), kind=kOutput, calls=%fused_computation.2 | convolution fusion | flops 19331547136 | bytes 36700160 | tf_op jit(solution)/shard_map/sncd,sncf->ndf/dot_general | solution.py:995
  759.1 37.7 %collective-permute-done.43 = bf16[2,256,2048]{2,1,0:T(8,128)(2,1)} collective-permute-done((bf16[2,256,2048]{2,1,0:T(8,128)(2,1)S(1)}, bf16[2,256,2048]{2,1,0:T(8,128)(2,1)}, u32[]{:S(2)}, u32[]{:S(2)}) %collective-permute-start.43) | collective-permute-done | bytes 2097184 | tf_op jit(solution)/shard_map/ppermute | solution.py:407
  806.1 10.0 convolution_convert_fusion.1
  859.2 26.9 %collective-permute-done.47 = bf16[2,512,1024]{2,1,0:T(8,128)(2,1)} collective-permute-done((bf16[2,512,1024]{2,1,0:T(8,128)(2,1)}, bf16[2,512,1024]{2,1,0:T(8,128)(2,1)}, u32[]{:S(2)}, u32[]{:S(2)}) %collective-permute-start.47) | collective-permute-done | bytes 2097184 | tf_op jit(solution)/shard_map/ppermute | solution.py:407
  887.6 28.7 %all-to-all-done.2 = bf16[8,512,256]{2,1,0:T(8,128)(2,1)} async-done(((bf16[8,512,256]{2,1,0:T(8,128)(2,1)}), bf16[8,512,256]{2,1,0:T(8,128)(2,1)}, u32[]{:S(2)}, u32[]{:S(2)}) %all-to-all-start.2) | async-done | bytes 2097184 | tf_op jit(solution)/shard_map/all_to_all | solution.py:1013
  923.7 67.7 %attention_backward.1 = (f32[4096,256]{1,0:T(8,128)}, f32[4096,256]{1,0:T(8,128)}, bf16[4096,256]{1,0:T(8,128)(2,1)}) custom-call(s32[16]{0:T(128)} %get-tuple-element.233.place, s32[8]{0:T(128)} %compare_select_fusion.first_tile, bf16[4096,256]{1,0:T(8,128)(2,1)} %get-tuple-element.235.queries, bf16[4096,256]{1,0:T(8,128)(2,1)} %get-tuple-element.236.keys, ...), custom_call_target="tpu_custom_call" | custom-call | flops 21474836480 | bytes 25165824 | tf_op jit(solution)/shard_map/attention_backward/pallas_call | solution.py:315
  1014.0 20.1 %convolution_convert_fusion = bf16[4096,2048]{1,0:T(8,128)(2,1)} fusion(bf16[2048,768]{1,0:T(8,128)(2,1)S(1)} %copy-done.3, bf16[4096,256]{1,0:T(8,128)(2,1)} %get-tuple-element.326, bf16[4096,256]{1,0:T(8,128)(2,1)} %get-tuple-element.388, bf16[4096,256]{1,0:T(8,128)(2,1)} %get-tuple-element.387), kind=kOutput, calls=%fused_computation.5 | convolution fusion | flops 12912164864 | bytes 26214400 | tf_op jit(solution)/shard_map/dot_general | solution.py:1064
  1035.7 19.4 %convolution_convert_fusion.2 = bf16[2048,768]{1,0:T(8,128)(2,1)S(1)} fusion(bf16[4096,2048]{1,0:T(8,128)(2,1)} %get-tuple-element.334, bf16[4096,256]{1,0:T(8,128)(2,1)} %get-tuple-element.326, bf16[4096,256]{1,0:T(8,128)(2,1)} %get-tuple-element.388, bf16[4096,256]{1,0:T(8,128)(2,1)S(1)} %copy-done.33), kind=kOutput, calls=%fused_computation.44 | convolution fusion | flops 12905349120 | bytes 26214400 | tf_op jit(solution)/shard_map/dot_general | solution.py:1077
  1065.3 15.0 %multiply_reduce_fusion = f32[2048]{0:T(1024)S(1)} fusion(bf16[4096,2048]{1,0:T(8,128)(2,1)} %get-tuple-element.334, bf16[4096,2048]{1,0:T(8,128)(2,1)} %convolution_convert_fusion), kind=kLoop, calls=%fused_computation | loop fusion | flops 33552384 | bytes 33562624 | tf_op jit(solution)/shard_map/reduce_sum | solution.py:1084
  1095.2 12.6 all-to-all-done.3
  1141.1 28.0 %collective-permute-done.63 = bf16[528,1024]{1,0:T(8,128)(2,1)} collective-permute-done((bf16[528,1024]{1,0:T(8,128)(2,1)S(1)}, bf16[528,1024]{1,0:T(8,128)(2,1)}, u32[]{:S(2)}, u32[]{:S(2)}) %collective-permute-start.63) | collective-permute-done | bytes 1081376 | tf_op jit(solution)/shard_map/ppermute | solution.py:386
  1189.8 50.7 %collective-permute-done.68 = bf16[528,1024]{1,0:T(8,128)(2,1)} collective-permute-done((bf16[528,1024]{1,0:T(8,128)(2,1)}, bf16[528,1024]{1,0:T(8,128)(2,1)}, u32[]{:S(2)}, u32[]{:S(2)}) %collective-permute-start.68) | collective-permute-done | bytes 1081376 | tf_op jit(solution)/shard_map/ppermute | solution.py:386
  1273.8 11.3 collective-permute-done.72
  (428 shorter events, 417.0 us)
Async XLA Ops:
  7.2 234.0 %all-gather.3.cloned.1.call-start = ((), (), s32[]{:S(2)}) async-start(), calls=%async_computation.7 | async-start | bytes 10485760 | tf_op jit(solution)/shard_map/all_gather | solution.py:863
  7.3 54.8 %collective-permute-start.2 = (bf16[512,2048]{1,0:T(8,128)(2,1)}, bf16[512,2048]{1,0:T(8,128)(2,1)}, u32[]{:S(2)}, u32[]{:S(2)}) collective-permute-start(bf16[512,2048]{1,0:T(8,128)(2,1)} %own.1), channel_id=1, source_target_pairs={{0,1},{1,0},{2,3},{3,2},{4,5},{5,4},{6,7},{7,6},{8,9},{9,8},{10,11... | collective-permute-start | bytes 6291464 | tf_op jit(solution)/shard_map/ppermute | solution.py:390
  7.8 54.3 %collective-permute-start.1 = (bf16[512,2048]{1,0:T(8,128)(2,1)}, bf16[512,2048]{1,0:T(8,128)(2,1)}, u32[]{:S(2)}, u32[]{:S(2)}) collective-permute-start(bf16[512,2048]{1,0:T(8,128)(2,1)} %own.1), channel_id=1, source_target_pairs={{2,0},{3,1},{4,2},{5,3},{6,4},{7,5},{10,8},{11,9},{12,10},{13,11},... | collective-permute-start | bytes 6291464 | tf_op jit(solution)/shard_map/ppermute | solution.py:386
  9.2 52.8 %collective-permute-start = (bf16[512,2048]{1,0:T(8,128)(2,1)}, bf16[512,2048]{1,0:T(8,128)(2,1)}, u32[]{:S(2)}, u32[]{:S(2)}) collective-permute-start(bf16[512,2048]{1,0:T(8,128)(2,1)} %own.1), channel_id=1, source_target_pairs={{0,2},{1,3},{2,4},{3,5},{4,6},{5,7},{8,10},{9,11},{10,12},{11,13},... | collective-permute-start | bytes 6291464 | tf_op jit(solution)/shard_map/ppermute | solution.py:385
  62.1 329.8 %all-gather.5.cloned.1.call-start = ((), (), s32[]{:S(2)}) async-start(), calls=%async_computation.8 | async-start | bytes 18874368 | tf_op jit(solution)/shard_map/all_gather | solution.py:895
  120.6 52.4 %collective-permute-start.14 = (bf16[512,2048]{1,0:T(8,128)(2,1)}, bf16[512,2048]{1,0:T(8,128)(2,1)}, u32[]{:S(2)}, u32[]{:S(2)}) collective-permute-start(bf16[512,2048]{1,0:T(8,128)(2,1)} %select_select_fusion.3.own), channel_id=1, source_target_pairs={{0,1},{1,0},{2,3},{3,2},{4,5},{5,4},{6,7},{7,6},{8,9},{9,8},{10,11... | collective-permute-start | bytes 6291464 | tf_op jit(solution)/shard_map/ppermute | solution.py:390
  188.7 52.5 %collective-permute-start.23 = (bf16[2,256,2048]{2,1,0:T(8,128)(2,1)}, bf16[2,256,2048]{2,1,0:T(8,128)(2,1)S(1)}, u32[]{:S(2)}, u32[]{:S(2)}) collective-permute-start(bf16[2,256,2048]{2,1,0:T(8,128)(2,1)} %refs_0_), channel_id=1, source_target_pairs={{0,16},{8,24},{16,0},{24,8},{1,17},{9,25},{17,1},{25,9},{2,18},{10... | collective-permute-start | bytes 6291464 | tf_op jit(solution)/shard_map/ppermute | solution.py:407
  241.2 71.1 %collective-permute-start.26 = (bf16[2,512,1024]{2,1,0:T(8,128)(2,1)}, bf16[2,512,1024]{2,1,0:T(8,128)(2,1)}, u32[]{:S(2)}, u32[]{:S(2)}) collective-permute-start(bf16[2,512,1024]{2,1,0:T(8,128)(2,1)} %refs_0_.1), channel_id=1, source_target_pairs={{0,16},{8,24},{16,0},{24,8},{1,17},{9,25},{17,1},{25,9},{2,18},{10... | collective-permute-start | bytes 6291464 | tf_op jit(solution)/shard_map/ppermute | solution.py:407
  242.6 69.7 %collective-permute-start.25 = (bf16[2,512,1024]{2,1,0:T(8,128)(2,1)}, bf16[2,512,1024]{2,1,0:T(8,128)(2,1)}, u32[]{:S(2)}, u32[]{:S(2)}) collective-permute-start(bf16[2,512,1024]{2,1,0:T(8,128)(2,1)} %refs_0_.1), channel_id=1, source_target_pairs={{0,8},{8,0},{16,24},{24,16},{1,9},{9,1},{17,25},{25,17},{2,10},{10... | collective-permute-start | bytes 6291464 | tf_op jit(solution)/shard_map/ppermute | solution.py:407
  245.5 66.7 %collective-permute-start.24 = (bf16[256,2048]{1,0:T(8,128)(2,1)S(1)}, bf16[256,2048]{1,0:T(8,128)(2,1)}, u32[]{:S(2)}, u32[]{:S(2)}) collective-permute-start(bf16[256,2048]{1,0:T(8,128)(2,1)S(1)} %constant_dynamic-slice_fusion.20), channel_id=1, source_target_pairs={{0,24},{8,16},{16,8},{24,0},{1,25},{9,17},{17,9},{25,1},{2,26},{10... | collective-permute-start | bytes 3145736 | tf_op jit(solution)/shard_map/ppermute | solution.py:407
  315.9 53.0 %collective-permute-start.27 = (bf16[1024,2048]{1,0:T(8,128)(2,1)}, bf16[1024,2048]{1,0:T(8,128)(2,1)}, u32[]{:S(2)}, u32[]{:S(2)}) collective-permute-start(bf16[1024,2048]{1,0:T(8,128)(2,1)} %pad_maximum_fusion.1.refs_0_), channel_id=1, source_target_pairs={{0,1},{1,0},{2,3},{3,2},{4,5},{5,4},{6,7},{7,6},{8,9},{9,8},{10,11... | collective-permute-start | bytes 12582920 | tf_op jit(solution)/shard_map/ppermute | solution.py:390
  319.8 57.8 %all-to-all-start.1 = ((bf16[8,512,256]{1,2,0:T(8,128)(2,1)}), bf16[8,512,256]{1,2,0:T(8,128)(2,1)}, u32[]{:S(2)}, u32[]{:S(2)}) async-start(bf16[8,512,256]{1,2,0:T(8,128)(2,1)} %copy.200), calls=%async_computation.1 | async-start | bytes 4194304 | tf_op jit(solution)/shard_map/all_to_all | solution.py:934
  324.2 474.0 %reduce-scatter.4.cloned.1.call-start = ((), (), s32[]{:S(2)}) async-start(), calls=%async_computation.9 | async-start | bytes 18874368 | tf_op jit(solution)/shard_map/reduce_scatter | solution.py:986
  391.9 67.5 %collective-permute-start.33 = (bf16[512,2048]{1,0:T(8,128)(2,1)}, bf16[512,2048]{1,0:T(8,128)(2,1)}, u32[]{:S(2)}, u32[]{:S(2)}) collective-permute-start(bf16[512,2048]{1,0:T(8,128)(2,1)} %multiply_convert_fusion.2.own), channel_id=1, source_target_pairs={{2,0},{3,1},{4,2},{5,3},{6,4},{7,5},{10,8},{11,9},{12,10},{13,11},... | collective-permute-start | bytes 6291464 | tf_op jit(solution)/shard_map/ppermute | solution.py:386
  393.2 66.2 %collective-permute-start.32 = (bf16[512,2048]{1,0:T(8,128)(2,1)}, bf16[512,2048]{1,0:T(8,128)(2,1)}, u32[]{:S(2)}, u32[]{:S(2)}) collective-permute-start(bf16[512,2048]{1,0:T(8,128)(2,1)} %multiply_convert_fusion.2.own), channel_id=1, source_target_pairs={{0,2},{1,3},{2,4},{3,5},{4,6},{5,7},{8,10},{9,11},{10,12},{11,13},... | collective-permute-start | bytes 6291464 | tf_op jit(solution)/shard_map/ppermute | solution.py:385
  461.3 53.2 %collective-permute-start.36 = (bf16[512,2048]{1,0:T(8,128)(2,1)}, bf16[512,2048]{1,0:T(8,128)(2,1)}, u32[]{:S(2)}, u32[]{:S(2)}) collective-permute-start(bf16[512,2048]{1,0:T(8,128)(2,1)} %collective-permute-done.33), channel_id=1, source_target_pairs={{2,0},{3,1},{4,2},{5,3},{10,8},{11,9},{12,10},{13,11},{18,16},{19,... | collective-permute-start | bytes 6291464 | tf_op jit(solution)/shard_map/ppermute | solution.py:386
  517.5 53.2 %collective-permute-start.38 = (bf16[512,2048]{1,0:T(8,128)(2,1)}, bf16[512,2048]{1,0:T(8,128)(2,1)}, u32[]{:S(2)}, u32[]{:S(2)}) collective-permute-start(bf16[512,2048]{1,0:T(8,128)(2,1)} %collective-permute-done.35), channel_id=1, source_target_pairs={{4,6},{5,7},{12,14},{13,15},{20,22},{21,23},{28,30},{29,31}} | collective-permute-start | bytes 6291464 | tf_op jit(solution)/shard_map/ppermute | solution.py:385
  627.5 406.6 %reduce-scatter.6.cloned.1.call-start = ((), (), s32[]{:S(2)}) async-start(), calls=%async_computation.10 | async-start | bytes 18874368 | tf_op jit(solution)/shard_map/reduce_scatter | solution.py:1001
  703.1 56.0 %collective-permute-start.44 = (bf16[2,256,2048]{2,1,0:T(8,128)(2,1)S(1)}, bf16[2,256,2048]{2,1,0:T(8,128)(2,1)}, u32[]{:S(2)}, u32[]{:S(2)}) collective-permute-start(bf16[2,256,2048]{2,1,0:T(8,128)(2,1)S(1)} %get-tuple-element.393), channel_id=1, source_target_pairs={{0,24},{8,16},{16,8},{24,0},{1,25},{9,17},{17,9},{25,1},{2,26},{10... | collective-permute-start | bytes 6291464 | tf_op jit(solution)/shard_map/ppermute | solution.py:407
  705.3 91.5 %collective-permute-start.43 = (bf16[2,256,2048]{2,1,0:T(8,128)(2,1)S(1)}, bf16[2,256,2048]{2,1,0:T(8,128)(2,1)}, u32[]{:S(2)}, u32[]{:S(2)}) collective-permute-start(bf16[2,256,2048]{2,1,0:T(8,128)(2,1)S(1)} %get-tuple-element.394), channel_id=1, source_target_pairs={{0,16},{8,24},{16,0},{24,8},{1,17},{9,25},{17,1},{25,9},{2,18},{10... | collective-permute-start | bytes 6291464 | tf_op jit(solution)/shard_map/ppermute | solution.py:407
  706.0 90.8 %collective-permute-start.42 = (bf16[2,256,2048]{2,1,0:T(8,128)(2,1)S(1)}, bf16[2,256,2048]{2,1,0:T(8,128)(2,1)}, u32[]{:S(2)}, u32[]{:S(2)}) collective-permute-start(bf16[2,256,2048]{2,1,0:T(8,128)(2,1)S(1)} %get-tuple-element.395), channel_id=1, source_target_pairs={{0,8},{8,0},{16,24},{24,16},{1,9},{9,1},{17,25},{25,17},{2,10},{10... | collective-permute-start | bytes 6291464 | tf_op jit(solution)/shard_map/ppermute | solution.py:407
  827.1 89.2 %all-to-all-start.2 = ((bf16[8,512,256]{2,1,0:T(8,128)(2,1)}), bf16[8,512,256]{2,1,0:T(8,128)(2,1)}, u32[]{:S(2)}, u32[]{:S(2)}) async-start(bf16[8,512,256]{2,1,0:T(8,128)(2,1)} %bitcast.126), calls=%async_computation.3 | async-start | bytes 4194304 | tf_op jit(solution)/shard_map/all_to_all | solution.py:1013
  832.4 434.3 %reduce-scatter.8.cloned.1.call-start = ((), (), s32[]{:S(2)}) async-start(), calls=%async_computation.11 | async-start | bytes 18874368 | tf_op jit(solution)/shard_map/reduce_scatter | solution.py:1067
  848.7 67.6 %collective-permute-start.49 = (bf16[512,1024]{1,0:T(8,128)(2,1)}, bf16[512,1024]{1,0:T(8,128)(2,1)}, u32[]{:S(2)}, u32[]{:S(2)}) collective-permute-start(bf16[512,1024]{1,0:T(8,128)(2,1)} %get-tuple-element.399), channel_id=1, source_target_pairs={{0,16},{8,24},{16,0},{24,8},{1,17},{9,25},{17,1},{25,9},{2,18},{10... | collective-permute-start | bytes 3145736 | tf_op jit(solution)/shard_map/ppermute | solution.py:407
  849.6 66.7 %collective-permute-start.48 = (bf16[512,1024]{1,0:T(8,128)(2,1)S(1)}, bf16[512,1024]{1,0:T(8,128)(2,1)}, u32[]{:S(2)}, u32[]{:S(2)}) collective-permute-start(bf16[512,1024]{1,0:T(8,128)(2,1)S(1)} %get-tuple-element.400), channel_id=1, source_target_pairs={{0,8},{8,0},{16,24},{24,16},{1,9},{9,1},{17,25},{25,17},{2,10},{10... | collective-permute-start | bytes 3145736 | tf_op jit(solution)/shard_map/ppermute | solution.py:407
  919.5 72.0 %collective-permute-start.51 = (bf16[2,512,1024]{2,1,0:T(8,128)(2,1)}, bf16[2,512,1024]{2,1,0:T(8,128)(2,1)S(1)}, u32[]{:S(2)}, u32[]{:S(2)}) collective-permute-start(bf16[2,512,1024]{2,1,0:T(8,128)(2,1)} %constant_dynamic-slice_fusion.10), channel_id=1, source_target_pairs={{0,24},{8,16},{16,8},{24,0},{1,25},{9,17},{17,9},{25,1},{2,26},{10... | collective-permute-start | bytes 6291464 | tf_op jit(solution)/shard_map/ppermute | solution.py:407
  922.8 68.7 %collective-permute-start.50 = (bf16[512,1024]{1,0:T(8,128)(2,1)S(1)}, bf16[512,1024]{1,0:T(8,128)(2,1)}, u32[]{:S(2)}, u32[]{:S(2)}) collective-permute-start(bf16[512,1024]{1,0:T(8,128)(2,1)S(1)} %constant_dynamic-slice_fusion.11), channel_id=1, source_target_pairs={{0,24},{8,16},{16,8},{24,0},{1,25},{9,17},{17,9},{25,1},{2,26},{10... | collective-permute-start | bytes 3145736 | tf_op jit(solution)/shard_map/ppermute | solution.py:407
  1112.6 57.7 %collective-permute-start.66 = (bf16[2,512,1024]{2,1,0:T(8,128)(2,1)}, bf16[2,512,1024]{2,1,0:T(8,128)(2,1)}, u32[]{:S(2)}, u32[]{:S(2)}) collective-permute-start(bf16[2,512,1024]{2,1,0:T(8,128)(2,1)} %get-tuple-element.389), channel_id=1, source_target_pairs={{0,16},{8,24},{16,0},{24,8},{1,17},{9,25},{17,1},{25,9},{2,18},{10... | collective-permute-start | bytes 6291464 | tf_op jit(solution)/shard_map/ppermute | solution.py:407
  1113.0 57.3 %collective-permute-start.65 = (bf16[2,512,1024]{2,1,0:T(8,128)(2,1)}, bf16[2,512,1024]{2,1,0:T(8,128)(2,1)}, u32[]{:S(2)}, u32[]{:S(2)}) collective-permute-start(bf16[2,512,1024]{2,1,0:T(8,128)(2,1)} %get-tuple-element.390), channel_id=1, source_target_pairs={{0,8},{8,0},{16,24},{24,16},{1,9},{9,1},{17,25},{25,17},{2,10},{10... | collective-permute-start | bytes 6291464 | tf_op jit(solution)/shard_map/ppermute | solution.py:407
  1173.8 66.7 %collective-permute-start.70 = (bf16[2,512,1024]{2,1,0:T(8,128)(2,1)}, bf16[2,512,1024]{2,1,0:T(8,128)(2,1)}, u32[]{:S(2)}, u32[]{:S(2)}) collective-permute-start(bf16[2,512,1024]{2,1,0:T(8,128)(2,1)} %constant_dynamic-slice_fusion), channel_id=1, source_target_pairs={{0,24},{8,16},{16,8},{24,0},{1,25},{9,17},{17,9},{25,1},{2,26},{10... | collective-permute-start | bytes 6291464 | tf_op jit(solution)/shard_map/ppermute | solution.py:407
  1176.4 64.1 %collective-permute-start.68 = (bf16[528,1024]{1,0:T(8,128)(2,1)}, bf16[528,1024]{1,0:T(8,128)(2,1)}, u32[]{:S(2)}, u32[]{:S(2)}) collective-permute-start(bf16[528,1024]{1,0:T(8,128)(2,1)} %collective-permute-done.63), channel_id=1, source_target_pairs={{2,0},{3,1},{4,2},{5,3},{10,8},{11,9},{12,10},{13,11},{18,16},{19,... | collective-permute-start | bytes 3244040 | tf_op jit(solution)/shard_map/ppermute | solution.py:386
  1177.7 62.8 %collective-permute-start.67 = (bf16[528,1024]{1,0:T(8,128)(2,1)}, bf16[528,1024]{1,0:T(8,128)(2,1)}, u32[]{:S(2)}, u32[]{:S(2)}) collective-permute-start(bf16[528,1024]{1,0:T(8,128)(2,1)} %copy-done.29), channel_id=1, source_target_pairs={{2,4},{3,5},{4,6},{5,7},{10,12},{11,13},{12,14},{13,15},{18,20},{1... | collective-permute-start | bytes 3244040 | tf_op jit(solution)/shard_map/ppermute | solution.py:385
  (112 other events, 2698.5 us)
Sparse Core Ops, SparseCore 0:
  62.2 111.6 all-gather.2
  175.5 154.8 all-gather.4
  627.6 170.5 reduce-scatter.3
  800.4 199.6 reduce-scatter.5
  1034.3 232.4 reduce-scatter.7

commit v7 on v6

--- a/solution.py
+++ b/solution.py
@@ -1084,6 +1084,7 @@
         jnp.sum(part_normed.astype(f32) * normed_all.astype(f32), axis=0) / gain_attn[0]
     )
     gain_terms = jnp.concatenate([attn_gain_term[None], spread, moe_gain_term[None]], axis=0)
+    gain_terms, out_sum = barrier(gain_terms, out_sum)
     gain_pieces = [scatter_one(gain_terms, shift, 1) for shift in (1, 2, 3)]
     output = (state + mixed.astype(f32)).astype(bf16)
     out_sum, gain_terms, grad_up, output, *pieces = barrier(

time: 1320 us -> 1320 us (level)
    all_to_all x1, waiting for transfers between devices: 12.6 us -> 28.3 us  [on_device(): lax.all_to_all(out_sum, 'ctx', split_axis=0, concat_axis=0, tiled=True, a...]
  transfers between devices with their start and end apart: 84 -> 84, of which waited for: 31 -> 28; matrix products, arithmetic and copies ran while one was open for 25% -> 25% of each run, Pallas kernels for 31% -> 31%
where the time goes in v7:
time: 1320 us; the launch traced here: 1310 us
  Pallas kernels  467 us (35%)
  waiting for transfers between devices  358 us (27%)
  matrix products  141 us (11%)
  other arithmetic  129 us (10%)
  starting transfers between devices  111 us (8%)
  local copies, waits for them, and re-layouts  81.1 us (6%)
  between operations  21.4 us (2%)
    pallas_call x4, Pallas kernels, expert_unit(): pl.pallas_call(expert_kernel, grid_spec=pltpu.PrefetchScalarGridSpec(num_...  196 us
    ppermute x35, waiting for transfers between devices, swap_dp(): return lax.ppermute(part, 'dp', swap_partners(lax.axis_size('dp'), shift))  170 us
    ppermute x9, waiting for transfers between devices, step(): lax.ppermute(from_above, 'ctx', down)  114 us
    pallas_call x1, Pallas kernels, attention_backward(): pl.pallas_call(functools.partial(backward_kernel, tile, prompt_tiles, blo...  67.7 us
    pallas_call x1, Pallas kernels, attention_forward(): pl.pallas_call(functools.partial(forward_kernel, tile, prompt_tiles, bloc...  53.2 us
    pallas_call x1, Pallas kernels, expert_out(): pl.pallas_call(out_kernel, grid=(peers // 2, experts), in_specs=[pl.Block...  44.9 us
    pallas_call x4, Pallas kernels, project(): pl.pallas_call(project_kernel, grid_spec=pltpu.PrefetchScalarGridSpec(num...  42.7 us
    ppermute x35, starting transfers between devices, swap_dp(): return lax.ppermute(part, 'dp', swap_partners(lax.axis_size('dp'), shift))  41.8 us
  transfers between devices with their start and end apart: 84, of which 28 were waited for; matrix products, arithmetic and copies ran while one was open for 25% of the time, Pallas kernels for 31%

profile of v7, /device:TPU:0, one launch (start us, length us, event | category | flops | bytes accessed | tf_op | source)
XLA Modules:
  0.0 1308.4 jit_solution(4781499372750886665)
XLA Ops:
  28.0 9.7 collective-permute-done.3
  45.6 15.2 %collective-permute-done.7.refs_2_ = bf16[512,768]{1,0:T(8,128)(2,1)} collective-permute-done((bf16[512,768]{1,0:T(8,128)(2,1)S(1)}, bf16[512,768]{1,0:T(8,128)(2,1)}, u32[]{:S(2)}, u32[]{:S(2)}) %collective-permute-start.7) | collective-permute-done | bytes 786464 | tf_op jit(solution)/shard_map/ppermute | solution.py:407
  79.3 10.6 project.4
  89.9 26.7 %collective-permute-done.10 = bf16[512,2048]{1,0:T(8,128)(2,1)} collective-permute-done((bf16[512,2048]{1,0:T(8,128)(2,1)}, bf16[512,2048]{1,0:T(8,128)(2,1)}, u32[]{:S(2)}, u32[]{:S(2)}) %collective-permute-start.10) | collective-permute-done | bytes 2097184 | tf_op jit(solution)/shard_map/ppermute | solution.py:386
  128.0 10.6 project.5
  138.6 33.8 %collective-permute-done.16 = bf16[256,2048]{1,0:T(8,128)(2,1)S(1)} collective-permute-done((bf16[256,2048]{1,0:T(8,128)(2,1)S(1)}, bf16[256,2048]{1,0:T(8,128)(2,1)S(1)}, u32[]{:S(2)}, u32[]{:S(2)}) %collective-permute-start.16) | collective-permute-done | bytes 1048608 | tf_op jit(solution)/shard_map/ppermute | solution.py:407
  177.8 10.7 project.6
  198.9 9.2 all-to-all-done
  210.8 10.7 project.7
  246.7 53.2 %attention_forward.1 = (bf16[4096,256]{1,0:T(8,128)(2,1)}, f32[2,8,512]{2,1,0:T(8,128)}, bf16[4096,256]{1,0:T(8,128)(2,1)}, bf16[4096,256]{1,0:T(8,128)(2,1)}, bf16[4096,256]{1,0:T(8,128)(2,1)}) custom-call(s32[16]{0:T(128)} %get-tuple-element.235.place, s32[8]{0:T(128)} %compare_select_fusion.first_tile, f32[4096,768]{1,0:T(8,128)} %get-tuple-element.236.raw_q.raw_k.raw_v, ...), custom_call_target="tpu_custom_call" | custom-call | flops 17179869184 | bytes 25165824 | tf_op jit(solution)/shard_map/attention_forward/pallas_call | solution.py:266
  299.9 12.5 collective-permute-done.24
  330.6 22.9 %collective-permute-done.29.refs_4_ = bf16[2,128,2048]{2,1,0:T(8,128)(2,1)S(1)} collective-permute-done((bf16[2,128,2048]{2,1,0:T(8,128)(2,1)}, bf16[2,128,2048]{2,1,0:T(8,128)(2,1)S(1)}, u32[]{:S(2)}, u32[]{:S(2)}) %collective-permute-start.29) | collective-permute-done | bytes 1048608 | tf_op jit(solution)/shard_map/ppermute | solution.py:407
  369.0 8.7 join.5
  410.5 48.9 %expert_unit.4 = (bf16[8,2,288,2048]{3,2,1,0:T(8,128)(2,1)}, bf16[8,2,288,2048]{3,2,1,0:T(8,128)(2,1)}, bf16[8,2,288,1024]{3,2,1,0:T(8,128)(2,1)}, bf16[8,2,288,...) custom-call(s32[2]{0:T(128)} %pad_add_fusion.5.unit, ...), custom_call_target="tpu_custom_call" | custom-call | tf_op jit(solution)/shard_map/expert_unit/pallas_call | solution.py:694
  465.7 49.0 %expert_unit.5 = (bf16[8,2,288,2048]{3,2,1,0:T(8,128)(2,1)}, bf16[8,2,288,2048]{3,2,1,0:T(8,128)(2,1)}, bf16[8,2,288,1024]{3,2,1,0:T(8,128)(2,1)}, bf16[8,2,288,...) custom-call(s32[2]{0:T(128)} %pad_add_fusion.6.unit, ...), custom_call_target="tpu_custom_call", output_to_operand_aliasing={{0}: (10, {}), {1}: (11, {}), {2}: (12, {}), {3}: (13, {}),... | custom-call | tf_op jit(solution)/shard_map/expert_unit/pallas_call | solution.py:694
  521.8 48.9 %expert_unit.6 = (bf16[8,2,288,2048]{3,2,1,0:T(8,128)(2,1)}, bf16[8,2,288,2048]{3,2,1,0:T(8,128)(2,1)}, bf16[8,2,288,1024]{3,2,1,0:T(8,128)(2,1)}, bf16[8,2,288,...) custom-call(s32[2]{0:T(128)} %pad_add_fusion.7.unit, ...), custom_call_target="tpu_custom_call", output_to_operand_aliasing={{0}: (10, {}), {1}: (11, {}), {2}: (12, {}), {3}: (13, {}),... | custom-call | tf_op jit(solution)/shard_map/expert_unit/pallas_call | solution.py:694
  578.4 49.1 %expert_unit.7 = (bf16[8,2,288,2048]{3,2,1,0:T(8,128)(2,1)}, bf16[8,2,288,2048]{3,2,1,0:T(8,128)(2,1)}, bf16[8,2,288,1024]{3,2,1,0:T(8,128)(2,1)}, bf16[8,2,288,...) custom-call(s32[2]{0:T(128)} %pad_add_fusion.4.unit, ...), custom_call_target="tpu_custom_call", output_to_operand_aliasing={{0}: (10, {}), {1}: (11, {}), {2}: (12, {}), {3}: (13, {}),... | custom-call | tf_op jit(solution)/shard_map/expert_unit/pallas_call | solution.py:694
  627.7 44.9 %expert_out.1 = bf16[8,512,2048]{2,1,0:T(8,128)(2,1)} custom-call(bf16[8,2,288,1024]{3,2,1,0:T(8,128)(2,1)} %get-tuple-element.309.hidden, bf16[2,1024,2048]{2,1,0:T(8,128)(2,1)} %join.6.w_down, s32[8,2,512]{2,1,0:T(2,128)} %copy.201.slots, f32[8,2,512]{2,1,0:T(2,128)} %get-tuple-element.258.gates, s32[8,512,2]{2,1,0:T(8,128)} %select_bitcast_fusion.columns), custom_call_target="tpu_custom_call" | custom-call | tf_op jit(solution)/shard_map/expert_out/pallas_call | solution.py:755
  672.6 26.9 %bitcast_convert_fusion.2 = bf16[2,1024,2048]{2,1,0:T(8,128)(2,1)} fusion(bf16[8,2,288,1024]{3,2,1,0:T(8,128)(2,1)} %get-tuple-element.309.hidden, bf16[8,2,288,2048]{3,2,1,0:T(8,128)(2,1)} %get-tuple-element.310), kind=kOutput, calls=%fused_computation.3 | convolution fusion | flops 19331547136 | bytes 36700160 | tf_op jit(solution)/shard_map/sncf,sncd->nfd/dot_general | solution.py:991
  706.7 27.6 %bitcast_convert_fusion = bf16[2,2048,1024]{2,1,0:T(8,128)(2,1)} fusion(bf16[8,2,288,2048]{3,2,1,0:T(8,128)(2,1)} %get-tuple-element.313, bf16[8,2,288,1024]{3,2,1,0:T(8,128)(2,1)} %get-tuple-element.315), kind=kOutput, calls=%fused_computation.1 | convolution fusion | flops 19331547136 | bytes 36700160 | tf_op jit(solution)/shard_map/sncd,sncf->ndf/dot_general | solution.py:996
  734.3 24.8 %bitcast_convert_fusion.1 = bf16[2,2048,1024]{2,1,0:T(8,128)(2,1)} fusion(bf16[8,2,288,2048]{3,2,1,0:T(8,128)(2,1)} %get-tuple-element.313, bf16[8,2,288,1024]{3,2,1,0:T(8,128)(2,1)S(1)} %bitcast.137), kind=kOutput, calls=%fused_computation.2 | convolution fusion | flops 19331547136 | bytes 36700160 | tf_op jit(solution)/shard_map/sncd,sncf->ndf/dot_general | solution.py:995
  759.2 37.7 %collective-permute-done.43 = bf16[2,256,2048]{2,1,0:T(8,128)(2,1)} collective-permute-done((bf16[2,256,2048]{2,1,0:T(8,128)(2,1)S(1)}, bf16[2,256,2048]{2,1,0:T(8,128)(2,1)}, u32[]{:S(2)}, u32[]{:S(2)}) %collective-permute-start.43) | collective-permute-done | bytes 2097184 | tf_op jit(solution)/shard_map/ppermute | solution.py:407
  806.1 10.0 convolution_convert_fusion.1
  859.1 27.0 %collective-permute-done.47 = bf16[2,512,1024]{2,1,0:T(8,128)(2,1)} collective-permute-done((bf16[2,512,1024]{2,1,0:T(8,128)(2,1)}, bf16[2,512,1024]{2,1,0:T(8,128)(2,1)}, u32[]{:S(2)}, u32[]{:S(2)}) %collective-permute-start.47) | collective-permute-done | bytes 2097184 | tf_op jit(solution)/shard_map/ppermute | solution.py:407
  887.5 28.8 %all-to-all-done.2 = bf16[8,512,256]{2,1,0:T(8,128)(2,1)} async-done(((bf16[8,512,256]{2,1,0:T(8,128)(2,1)}), bf16[8,512,256]{2,1,0:T(8,128)(2,1)}, u32[]{:S(2)}, u32[]{:S(2)}) %all-to-all-start.2) | async-done | bytes 2097184 | tf_op jit(solution)/shard_map/all_to_all | solution.py:1013
  923.7 67.7 %attention_backward.1 = (f32[4096,256]{1,0:T(8,128)}, f32[4096,256]{1,0:T(8,128)}, bf16[4096,256]{1,0:T(8,128)(2,1)}) custom-call(s32[16]{0:T(128)} %get-tuple-element.235.place, s32[8]{0:T(128)} %compare_select_fusion.first_tile, bf16[4096,256]{1,0:T(8,128)(2,1)} %get-tuple-element.237.queries, bf16[4096,256]{1,0:T(8,128)(2,1)} %get-tuple-element.238.keys, ...), custom_call_target="tpu_custom_call" | custom-call | flops 21474836480 | bytes 25165824 | tf_op jit(solution)/shard_map/attention_backward/pallas_call | solution.py:315
  1013.9 20.1 %convolution_convert_fusion = bf16[4096,2048]{1,0:T(8,128)(2,1)} fusion(bf16[2048,768]{1,0:T(8,128)(2,1)S(1)} %copy-done.3, bf16[4096,256]{1,0:T(8,128)(2,1)} %get-tuple-element.328, bf16[4096,256]{1,0:T(8,128)(2,1)} %get-tuple-element.392, bf16[4096,256]{1,0:T(8,128)(2,1)} %get-tuple-element.391), kind=kOutput, calls=%fused_computation.5 | convolution fusion | flops 12912164864 | bytes 26214400 | tf_op jit(solution)/shard_map/dot_general | solution.py:1064
  1035.6 19.4 %convolution_convert_fusion.2 = bf16[2048,768]{1,0:T(8,128)(2,1)S(1)} fusion(bf16[4096,2048]{1,0:T(8,128)(2,1)} %get-tuple-element.335, bf16[4096,256]{1,0:T(8,128)(2,1)} %get-tuple-element.328, bf16[4096,256]{1,0:T(8,128)(2,1)} %get-tuple-element.392, bf16[4096,256]{1,0:T(8,128)(2,1)S(1)} %copy-done.32), kind=kOutput, calls=%fused_computation.44 | convolution fusion | flops 12905349120 | bytes 26214400 | tf_op jit(solution)/shard_map/dot_general | solution.py:1077
  1065.1 13.5 %multiply_reduce_fusion = f32[2048]{0:T(1024)S(1)} fusion(bf16[4096,2048]{1,0:T(8,128)(2,1)} %get-tuple-element.335, bf16[4096,2048]{1,0:T(8,128)(2,1)} %convolution_convert_fusion), kind=kLoop, calls=%fused_computation | loop fusion | flops 33552384 | bytes 33562624 | tf_op jit(solution)/shard_map/reduce_sum | solution.py:1084
  1079.5 28.3 %all-to-all-done.3 = bf16[4,512,256]{2,1,0:T(8,128)(2,1)S(1)} async-done(((bf16[4,512,256]{2,1,0:T(8,128)(2,1)}), bf16[4,512,256]{2,1,0:T(8,128)(2,1)S(1)}, u32[]{:S(2)}, u32[]{:S(2)}) %all-to-all-start.3) | async-done | bytes 1048608 | tf_op jit(solution)/shard_map/all_to_all | solution.py:1069
  1149.2 28.0 %collective-permute-done.63 = bf16[528,1024]{1,0:T(8,128)(2,1)} collective-permute-done((bf16[528,1024]{1,0:T(8,128)(2,1)S(1)}, bf16[528,1024]{1,0:T(8,128)(2,1)}, u32[]{:S(2)}, u32[]{:S(2)}) %collective-permute-start.63) | collective-permute-done | bytes 1081376 | tf_op jit(solution)/shard_map/ppermute | solution.py:386
  1197.9 50.9 %collective-permute-done.68 = bf16[528,1024]{1,0:T(8,128)(2,1)} collective-permute-done((bf16[528,1024]{1,0:T(8,128)(2,1)}, bf16[528,1024]{1,0:T(8,128)(2,1)}, u32[]{:S(2)}, u32[]{:S(2)}) %collective-permute-start.68) | collective-permute-done | bytes 1081376 | tf_op jit(solution)/shard_map/ppermute | solution.py:386
  (426 shorter events, 400.9 us)
Async XLA Ops:
  7.2 234.1 %all-gather.3.cloned.1.call-start = ((), (), s32[]{:S(2)}) async-start(), calls=%async_computation.7 | async-start | bytes 10485760 | tf_op jit(solution)/shard_map/all_gather | solution.py:863
  7.3 54.8 %collective-permute-start.2 = (bf16[512,2048]{1,0:T(8,128)(2,1)}, bf16[512,2048]{1,0:T(8,128)(2,1)}, u32[]{:S(2)}, u32[]{:S(2)}) collective-permute-start(bf16[512,2048]{1,0:T(8,128)(2,1)} %own.1), channel_id=1, source_target_pairs={{0,1},{1,0},{2,3},{3,2},{4,5},{5,4},{6,7},{7,6},{8,9},{9,8},{10,11... | collective-permute-start | bytes 6291464 | tf_op jit(solution)/shard_map/ppermute | solution.py:390
  7.8 54.3 %collective-permute-start.1 = (bf16[512,2048]{1,0:T(8,128)(2,1)}, bf16[512,2048]{1,0:T(8,128)(2,1)}, u32[]{:S(2)}, u32[]{:S(2)}) collective-permute-start(bf16[512,2048]{1,0:T(8,128)(2,1)} %own.1), channel_id=1, source_target_pairs={{2,0},{3,1},{4,2},{5,3},{6,4},{7,5},{10,8},{11,9},{12,10},{13,11},... | collective-permute-start | bytes 6291464 | tf_op jit(solution)/shard_map/ppermute | solution.py:386
  9.2 52.8 %collective-permute-start = (bf16[512,2048]{1,0:T(8,128)(2,1)}, bf16[512,2048]{1,0:T(8,128)(2,1)}, u32[]{:S(2)}, u32[]{:S(2)}) collective-permute-start(bf16[512,2048]{1,0:T(8,128)(2,1)} %own.1), channel_id=1, source_target_pairs={{0,2},{1,3},{2,4},{3,5},{4,6},{5,7},{8,10},{9,11},{10,12},{11,13},... | collective-permute-start | bytes 6291464 | tf_op jit(solution)/shard_map/ppermute | solution.py:385
  62.1 329.9 %all-gather.5.cloned.1.call-start = ((), (), s32[]{:S(2)}) async-start(), calls=%async_computation.8 | async-start | bytes 18874368 | tf_op jit(solution)/shard_map/all_gather | solution.py:895
  241.3 71.1 %collective-permute-start.26 = (bf16[2,512,1024]{2,1,0:T(8,128)(2,1)}, bf16[2,512,1024]{2,1,0:T(8,128)(2,1)}, u32[]{:S(2)}, u32[]{:S(2)}) collective-permute-start(bf16[2,512,1024]{2,1,0:T(8,128)(2,1)} %refs_0_.1), channel_id=1, source_target_pairs={{0,16},{8,24},{16,0},{24,8},{1,17},{9,25},{17,1},{25,9},{2,18},{10... | collective-permute-start | bytes 6291464 | tf_op jit(solution)/shard_map/ppermute | solution.py:407
  242.7 69.7 %collective-permute-start.25 = (bf16[2,512,1024]{2,1,0:T(8,128)(2,1)}, bf16[2,512,1024]{2,1,0:T(8,128)(2,1)}, u32[]{:S(2)}, u32[]{:S(2)}) collective-permute-start(bf16[2,512,1024]{2,1,0:T(8,128)(2,1)} %refs_0_.1), channel_id=1, source_target_pairs={{0,8},{8,0},{16,24},{24,16},{1,9},{9,1},{17,25},{25,17},{2,10},{10... | collective-permute-start | bytes 6291464 | tf_op jit(solution)/shard_map/ppermute | solution.py:407
  245.5 66.9 %collective-permute-start.24 = (bf16[256,2048]{1,0:T(8,128)(2,1)S(1)}, bf16[256,2048]{1,0:T(8,128)(2,1)}, u32[]{:S(2)}, u32[]{:S(2)}) collective-permute-start(bf16[256,2048]{1,0:T(8,128)(2,1)S(1)} %constant_dynamic-slice_fusion.20), channel_id=1, source_target_pairs={{0,24},{8,16},{16,8},{24,0},{1,25},{9,17},{17,9},{25,1},{2,26},{10... | collective-permute-start | bytes 3145736 | tf_op jit(solution)/shard_map/ppermute | solution.py:407
  316.0 53.0 %collective-permute-start.27 = (bf16[1024,2048]{1,0:T(8,128)(2,1)}, bf16[1024,2048]{1,0:T(8,128)(2,1)}, u32[]{:S(2)}, u32[]{:S(2)}) collective-permute-start(bf16[1024,2048]{1,0:T(8,128)(2,1)} %pad_maximum_fusion.1.refs_0_), channel_id=1, source_target_pairs={{0,1},{1,0},{2,3},{3,2},{4,5},{5,4},{6,7},{7,6},{8,9},{9,8},{10,11... | collective-permute-start | bytes 12582920 | tf_op jit(solution)/shard_map/ppermute | solution.py:390
  319.9 57.7 %all-to-all-start.1 = ((bf16[8,512,256]{1,2,0:T(8,128)(2,1)}), bf16[8,512,256]{1,2,0:T(8,128)(2,1)}, u32[]{:S(2)}, u32[]{:S(2)}) async-start(bf16[8,512,256]{1,2,0:T(8,128)(2,1)} %copy.200), calls=%async_computation.1 | async-start | bytes 4194304 | tf_op jit(solution)/shard_map/all_to_all | solution.py:934
  324.3 473.9 %reduce-scatter.4.cloned.1.call-start = ((), (), s32[]{:S(2)}) async-start(), calls=%async_computation.9 | async-start | bytes 18874368 | tf_op jit(solution)/shard_map/reduce_scatter | solution.py:986
  392.0 67.4 %collective-permute-start.33 = (bf16[512,2048]{1,0:T(8,128)(2,1)}, bf16[512,2048]{1,0:T(8,128)(2,1)}, u32[]{:S(2)}, u32[]{:S(2)}) collective-permute-start(bf16[512,2048]{1,0:T(8,128)(2,1)} %multiply_convert_fusion.2.own), channel_id=1, source_target_pairs={{2,0},{3,1},{4,2},{5,3},{6,4},{7,5},{10,8},{11,9},{12,10},{13,11},... | collective-permute-start | bytes 6291464 | tf_op jit(solution)/shard_map/ppermute | solution.py:386
  393.3 66.2 %collective-permute-start.32 = (bf16[512,2048]{1,0:T(8,128)(2,1)}, bf16[512,2048]{1,0:T(8,128)(2,1)}, u32[]{:S(2)}, u32[]{:S(2)}) collective-permute-start(bf16[512,2048]{1,0:T(8,128)(2,1)} %multiply_convert_fusion.2.own), channel_id=1, source_target_pairs={{0,2},{1,3},{2,4},{3,5},{4,6},{5,7},{8,10},{9,11},{10,12},{11,13},... | collective-permute-start | bytes 6291464 | tf_op jit(solution)/shard_map/ppermute | solution.py:385
  461.4 53.3 %collective-permute-start.36 = (bf16[512,2048]{1,0:T(8,128)(2,1)}, bf16[512,2048]{1,0:T(8,128)(2,1)}, u32[]{:S(2)}, u32[]{:S(2)}) collective-permute-start(bf16[512,2048]{1,0:T(8,128)(2,1)} %collective-permute-done.33), channel_id=1, source_target_pairs={{2,0},{3,1},{4,2},{5,3},{10,8},{11,9},{12,10},{13,11},{18,16},{19,... | collective-permute-start | bytes 6291464 | tf_op jit(solution)/shard_map/ppermute | solution.py:386
  517.5 53.2 %collective-permute-start.38 = (bf16[512,2048]{1,0:T(8,128)(2,1)}, bf16[512,2048]{1,0:T(8,128)(2,1)}, u32[]{:S(2)}, u32[]{:S(2)}) collective-permute-start(bf16[512,2048]{1,0:T(8,128)(2,1)} %collective-permute-done.35), channel_id=1, source_target_pairs={{4,6},{5,7},{12,14},{13,15},{20,22},{21,23},{28,30},{29,31}} | collective-permute-start | bytes 6291464 | tf_op jit(solution)/shard_map/ppermute | solution.py:385
  627.6 406.5 %reduce-scatter.6.cloned.1.call-start = ((), (), s32[]{:S(2)}) async-start(), calls=%async_computation.10 | async-start | bytes 18874368 | tf_op jit(solution)/shard_map/reduce_scatter | solution.py:1001
  703.1 56.0 %collective-permute-start.44 = (bf16[2,256,2048]{2,1,0:T(8,128)(2,1)S(1)}, bf16[2,256,2048]{2,1,0:T(8,128)(2,1)}, u32[]{:S(2)}, u32[]{:S(2)}) collective-permute-start(bf16[2,256,2048]{2,1,0:T(8,128)(2,1)S(1)} %get-tuple-element.397), channel_id=1, source_target_pairs={{0,24},{8,16},{16,8},{24,0},{1,25},{9,17},{17,9},{25,1},{2,26},{10... | collective-permute-start | bytes 6291464 | tf_op jit(solution)/shard_map/ppermute | solution.py:407
  705.3 91.6 %collective-permute-start.43 = (bf16[2,256,2048]{2,1,0:T(8,128)(2,1)S(1)}, bf16[2,256,2048]{2,1,0:T(8,128)(2,1)}, u32[]{:S(2)}, u32[]{:S(2)}) collective-permute-start(bf16[2,256,2048]{2,1,0:T(8,128)(2,1)S(1)} %get-tuple-element.398), channel_id=1, source_target_pairs={{0,16},{8,24},{16,0},{24,8},{1,17},{9,25},{17,1},{25,9},{2,18},{10... | collective-permute-start | bytes 6291464 | tf_op jit(solution)/shard_map/ppermute | solution.py:407
  706.1 90.8 %collective-permute-start.42 = (bf16[2,256,2048]{2,1,0:T(8,128)(2,1)S(1)}, bf16[2,256,2048]{2,1,0:T(8,128)(2,1)}, u32[]{:S(2)}, u32[]{:S(2)}) collective-permute-start(bf16[2,256,2048]{2,1,0:T(8,128)(2,1)S(1)} %get-tuple-element.399), channel_id=1, source_target_pairs={{0,8},{8,0},{16,24},{24,16},{1,9},{9,1},{17,25},{25,17},{2,10},{10... | collective-permute-start | bytes 6291464 | tf_op jit(solution)/shard_map/ppermute | solution.py:407
  827.0 89.3 %all-to-all-start.2 = ((bf16[8,512,256]{2,1,0:T(8,128)(2,1)}), bf16[8,512,256]{2,1,0:T(8,128)(2,1)}, u32[]{:S(2)}, u32[]{:S(2)}) async-start(bf16[8,512,256]{2,1,0:T(8,128)(2,1)} %bitcast.126), calls=%async_computation.3 | async-start | bytes 4194304 | tf_op jit(solution)/shard_map/all_to_all | solution.py:1013
  832.4 438.8 %reduce-scatter.8.cloned.1.call-start = ((), (), s32[]{:S(2)}) async-start(), calls=%async_computation.11 | async-start | bytes 18874368 | tf_op jit(solution)/shard_map/reduce_scatter | solution.py:1067
  848.7 67.7 %collective-permute-start.49 = (bf16[512,1024]{1,0:T(8,128)(2,1)}, bf16[512,1024]{1,0:T(8,128)(2,1)}, u32[]{:S(2)}, u32[]{:S(2)}) collective-permute-start(bf16[512,1024]{1,0:T(8,128)(2,1)} %get-tuple-element.403), channel_id=1, source_target_pairs={{0,16},{8,24},{16,0},{24,8},{1,17},{9,25},{17,1},{25,9},{2,18},{10... | collective-permute-start | bytes 3145736 | tf_op jit(solution)/shard_map/ppermute | solution.py:407
  849.5 66.8 %collective-permute-start.48 = (bf16[512,1024]{1,0:T(8,128)(2,1)S(1)}, bf16[512,1024]{1,0:T(8,128)(2,1)}, u32[]{:S(2)}, u32[]{:S(2)}) collective-permute-start(bf16[512,1024]{1,0:T(8,128)(2,1)S(1)} %get-tuple-element.404), channel_id=1, source_target_pairs={{0,8},{8,0},{16,24},{24,16},{1,9},{9,1},{17,25},{25,17},{2,10},{10... | collective-permute-start | bytes 3145736 | tf_op jit(solution)/shard_map/ppermute | solution.py:407
  919.4 72.0 %collective-permute-start.51 = (bf16[2,512,1024]{2,1,0:T(8,128)(2,1)}, bf16[2,512,1024]{2,1,0:T(8,128)(2,1)S(1)}, u32[]{:S(2)}, u32[]{:S(2)}) collective-permute-start(bf16[2,512,1024]{2,1,0:T(8,128)(2,1)} %constant_dynamic-slice_fusion.10), channel_id=1, source_target_pairs={{0,24},{8,16},{16,8},{24,0},{1,25},{9,17},{17,9},{25,1},{2,26},{10... | collective-permute-start | bytes 6291464 | tf_op jit(solution)/shard_map/ppermute | solution.py:407
  922.7 68.7 %collective-permute-start.50 = (bf16[512,1024]{1,0:T(8,128)(2,1)S(1)}, bf16[512,1024]{1,0:T(8,128)(2,1)}, u32[]{:S(2)}, u32[]{:S(2)}) collective-permute-start(bf16[512,1024]{1,0:T(8,128)(2,1)S(1)} %constant_dynamic-slice_fusion.11), channel_id=1, source_target_pairs={{0,24},{8,16},{16,8},{24,0},{1,25},{9,17},{17,9},{25,1},{2,26},{10... | collective-permute-start | bytes 3145736 | tf_op jit(solution)/shard_map/ppermute | solution.py:407
  1060.2 55.3 %collective-permute-start.57 = (bf16[512,768]{1,0:T(8,128)(2,1)}, bf16[512,768]{1,0:T(8,128)(2,1)}, u32[]{:S(2)}, u32[]{:S(2)}) collective-permute-start(bf16[512,768]{1,0:T(8,128)(2,1)} %get-tuple-element.406), channel_id=1, source_target_pairs={{0,16},{8,24},{16,0},{24,8},{1,17},{9,25},{17,1},{25,9},{2,18},{10... | collective-permute-start | bytes 2359304 | tf_op jit(solution)/shard_map/ppermute | solution.py:407
  1060.8 54.6 %collective-permute-start.56 = (bf16[512,768]{1,0:T(8,128)(2,1)}, bf16[512,768]{1,0:T(8,128)(2,1)}, u32[]{:S(2)}, u32[]{:S(2)}) collective-permute-start(bf16[512,768]{1,0:T(8,128)(2,1)} %get-tuple-element.407), channel_id=1, source_target_pairs={{0,8},{8,0},{16,24},{24,16},{1,9},{9,1},{17,25},{25,17},{2,10},{10... | collective-permute-start | bytes 2359304 | tf_op jit(solution)/shard_map/ppermute | solution.py:407
  1120.2 58.2 %collective-permute-start.66 = (bf16[2,512,1024]{2,1,0:T(8,128)(2,1)}, bf16[2,512,1024]{2,1,0:T(8,128)(2,1)}, u32[]{:S(2)}, u32[]{:S(2)}) collective-permute-start(bf16[2,512,1024]{2,1,0:T(8,128)(2,1)} %get-tuple-element.393), channel_id=1, source_target_pairs={{0,16},{8,24},{16,0},{24,8},{1,17},{9,25},{17,1},{25,9},{2,18},{10... | collective-permute-start | bytes 6291464 | tf_op jit(solution)/shard_map/ppermute | solution.py:407
  1120.7 57.7 %collective-permute-start.65 = (bf16[2,512,1024]{2,1,0:T(8,128)(2,1)}, bf16[2,512,1024]{2,1,0:T(8,128)(2,1)}, u32[]{:S(2)}, u32[]{:S(2)}) collective-permute-start(bf16[2,512,1024]{2,1,0:T(8,128)(2,1)} %get-tuple-element.394), channel_id=1, source_target_pairs={{0,8},{8,0},{16,24},{24,16},{1,9},{9,1},{17,25},{25,17},{2,10},{10... | collective-permute-start | bytes 6291464 | tf_op jit(solution)/shard_map/ppermute | solution.py:407
  1181.9 66.8 %collective-permute-start.70 = (bf16[2,512,1024]{2,1,0:T(8,128)(2,1)}, bf16[2,512,1024]{2,1,0:T(8,128)(2,1)}, u32[]{:S(2)}, u32[]{:S(2)}) collective-permute-start(bf16[2,512,1024]{2,1,0:T(8,128)(2,1)} %constant_dynamic-slice_fusion), channel_id=1, source_target_pairs={{0,24},{8,16},{16,8},{24,0},{1,25},{9,17},{17,9},{25,1},{2,26},{10... | collective-permute-start | bytes 6291464 | tf_op jit(solution)/shard_map/ppermute | solution.py:407
  1184.6 64.2 %collective-permute-start.68 = (bf16[528,1024]{1,0:T(8,128)(2,1)}, bf16[528,1024]{1,0:T(8,128)(2,1)}, u32[]{:S(2)}, u32[]{:S(2)}) collective-permute-start(bf16[528,1024]{1,0:T(8,128)(2,1)} %collective-permute-done.63), channel_id=1, source_target_pairs={{2,0},{3,1},{4,2},{5,3},{10,8},{11,9},{12,10},{13,11},{18,16},{19,... | collective-permute-start | bytes 3244040 | tf_op jit(solution)/shard_map/ppermute | solution.py:386
  1185.9 62.9 %collective-permute-start.67 = (bf16[528,1024]{1,0:T(8,128)(2,1)}, bf16[528,1024]{1,0:T(8,128)(2,1)}, u32[]{:S(2)}, u32[]{:S(2)}) collective-permute-start(bf16[528,1024]{1,0:T(8,128)(2,1)} %copy-done.28), channel_id=1, source_target_pairs={{2,4},{3,5},{4,6},{5,7},{10,12},{11,13},{12,14},{13,15},{18,20},{1... | collective-permute-start | bytes 3244040 | tf_op jit(solution)/shard_map/ppermute | solution.py:385
  (111 other events, 2717.3 us)
Sparse Core Ops, SparseCore 0:
  62.2 111.6 all-gather.2
  175.5 154.9 all-gather.4
  627.7 170.4 reduce-scatter.3
  800.4 199.7 reduce-scatter.5
  1034.2 224.2 reduce-scatter.7
